TPU v7x, 32 devices: a whole 2x2x4 slice. The times are simulated.
32 devices in a mesh: batch: 8 (over z, x), head: 4 (over y, core).
Axes of the slice: x: 2, y: 2, z: 4, core: 2. Of those that a mesh axis runs over, the one named last changes fastest.
Arguments:
- low_patches: bfloat16 [16, 196, 768], P('batch')
- high_patches: bfloat16 [16, 576, 768], P('batch')
- interp: bfloat16 [576, 196], replicated, may hold values from 0 to 2
- labels: int32 [32], P('batch'), may hold values from 0 to 999
- partner: int32 [32], P('batch'), may hold values from 0 to 31, as said below
- pair_count: int32 [1], replicated, may hold values from 32 to 64
- w_patch: float32 [768, 768], P('batch'), may hold values from -0.21875 to 0.21875
- pos_table: float32 [197, 768], P(None, 'batch'), may hold values from -3 to 3
- vectors: float32 [10, 768], P(None, 'batch')
- head_w: float32 [768, 1256], P('batch'), may hold values from -0.4375 to 0.4375
- w_qkv: float32 [768, 2304], P('batch', 'head'), may hold values from -0.21875 to 0.21875
- w_out: float32 [768, 768], P('batch', 'head'), may hold values from -0.21875 to 0.21875
- w_up: float32 [768, 3072], P('batch', 'head'), may hold values from -0.21875 to 0.21875
- w_down: float32 [768, 3072], P('batch', 'head'), may hold values from -0.109375 to 0.109375
- mom_qkv: float32 [768, 2304], P('batch', 'head'), may hold values from -0.00067453353 to 0.00067453353
- mom_out: float32 [768, 768], P('batch', 'head'), may hold values from -0.00067453353 to 0.00067453353
- mom_up: float32 [768, 3072], P('batch', 'head'), may hold values from -0.00067453353 to 0.00067453353
- mom_down: float32 [768, 3072], P('batch', 'head'), may hold values from -0.00067453353 to 0.00067453353
- first_patch: float32 [768, 768], P('batch'), may hold values from -3.0517578e-05 to 3.0517578e-05
- second_patch: float32 [768, 768], P('batch'), may hold values from 1.4218609e-12 to 1.1374887e-11
- first_pos: float32 [197, 768], P(None, 'batch'), may hold values from -2.9802322e-07 to 2.9802322e-07
- second_pos: float32 [197, 768], P(None, 'batch'), may hold values from 2.637893e-16 to 1.0258472e-15
- first_vec: float32 [10, 768], P(None, 'batch'), may hold values from -0.00015258789 to 0.00015258789
- second_vec: float32 [10, 768], P(None, 'batch'), may hold values from 3.412466e-11 to 2.843722e-10
- first_head: float32 [768, 1256], P('batch'), may hold values from -3.0517578e-05 to 3.0517578e-05
- second_head: float32 [768, 1256], P('batch'), may hold values from 1.4218609e-12 to 1.1374887e-11
Outputs:
- new_patch: float32 [768, 768], P('batch')
- new_pos: float32 [197, 768], P(None, 'batch')
- new_vectors: float32 [10, 768], P(None, 'batch')
- new_head: float32 [768, 1256], P('batch')
- new_qkv: float32 [768, 2304], P('batch', 'head')
- new_out: float32 [768, 768], P('batch', 'head')
- new_up: float32 [768, 3072], P('batch', 'head')
- new_down: float32 [768, 3072], P('batch', 'head')
- moment_qkv: float32 [768, 2304], P('batch', 'head')
- moment_out: float32 [768, 768], P('batch', 'head')
- moment_up: float32 [768, 3072], P('batch', 'head')
- moment_down: float32 [768, 3072], P('batch', 'head')
- new_first_patch: float32 [768, 768], P('batch')
- new_first_pos: float32 [197, 768], P(None, 'batch')
- new_first_vec: float32 [10, 768], P(None, 'batch')
- new_first_head: float32 [768, 1256], P('batch')
- new_second_patch: float32 [768, 768], P('batch')
- new_second_pos: float32 [197, 768], P(None, 'batch')
- new_second_vec: float32 [10, 768], P(None, 'batch')
- new_second_head: float32 [768, 1256], P('batch')
- losses: float32 [2], replicated
- grad_norm: float32 [1], replicated
- moment_logs: float32 [4], replicated
Inputs may be any that keep to these rules, and one draw needn't show every extreme that they name: partner[partner[i]] == i and partner[i] != i: the images fall into pairs of two views.
All inputs are finite; a program needn't handle non-finite values.
Results may differ from a plain program's by a relative error of at most 0.02.
Values may be sent and summed in bfloat16 or wider, within the bound.
No kernel may reach another device: no remote copies, remote signals or barrier semaphores. Data moves between devices by JAX's collectives and lax.ppermute only.
A program may use at most 192 MiB of HBM per device.

v0:
```python
from functools import partial
import math

import jax
import jax.numpy as jnp
from jax import lax
from jax.sharding import PartitionSpec as P

D = 768
HD = 64
CLS = 1000
NS_STEPS = 3
STEP = 10


PRECISE = lax.Precision.HIGHEST
POLY_ONE = 3.4445
POLY_TWO = -4.775
POLY_THREE = 2.0315
SOFTMAX_TEMP = 0.05
CLIP_NORM = 0.05
MOMENTUM = 0.95
MUON_RATE = 0.2
DECAY_RATE = 0.05
BETA_FIRST = 0.9
BETA_SECOND = 0.99
ADAM_FLOOR = 1e-08
ADAM_RATES = (0.08, 0.3, 0.5, 0.15)
ADAM_DECAYS = (0.05, 0.05, 0.0, 0.05)


def for_sending(shard):

    def short(part):
        return part.astype(jnp.bfloat16) if part.dtype == jnp.float32 else part

    return jax.tree.map(short, shard)


def matrix_product(left_side, right_side):
    return jnp.dot(left_side, right_side, preferred_element_type=jnp.float32)


def product_transposed_right(left_side, right_side, precision=None):
    contract = (((left_side.ndim - 1,), (right_side.ndim - 1,)), ((), ()))
    return lax.dot_general(
        left_side, right_side, contract, precision=precision, preferred_element_type=jnp.float32
    )


def row_product_result(left_side, right_side):
    flat_left = left_side.reshape(-1, left_side.shape[-1])
    flat_right = right_side.reshape(-1, right_side.shape[-1])
    return lax.dot_general(
        flat_left, flat_right, (((0,), (0,)), ((), ())), preferred_element_type=jnp.float32
    )


def precise(left_side, right_side):
    return jnp.dot(left_side, right_side, precision=PRECISE)


def layer_norm(values, gain_row, shift_row):
    centred = values - jnp.mean(values, -1, keepdims=True)
    return (
        centred * lax.rsqrt(jnp.mean(centred * centred, -1, keepdims=True) + 1e-06) * gain_row
        + shift_row
    )


def unit_norm(projected):
    return projected * lax.rsqrt(jnp.sum(projected * projected, -1, keepdims=True) + 1e-06)


def exact_gelu(values):
    return jax.nn.gelu(values, approximate=False)


def class_sum(logits, labels):
    picked = jnp.take_along_axis(logits, labels[:, None], 1)[:, 0]
    return jnp.sum(jax.nn.logsumexp(logits, -1) - picked)


def keep_all(values):
    return values


def adam_update(weight, gradient, first, second, rate, decay):
    first = BETA_FIRST * first + (1.0 - BETA_FIRST) * gradient
    second = BETA_SECOND * second + (1.0 - BETA_SECOND) * gradient * gradient
    direction = (
        first
        / (1.0 - BETA_FIRST**STEP)
        / (jnp.sqrt(second / (1.0 - BETA_SECOND**STEP)) + ADAM_FLOOR)
    )
    return (weight - rate * (direction + decay * weight), first, second)


def encode_group(patches, pos_rows, weights):
    w_patch, vectors, w_qkv, w_out, w_up, w_down = weights
    images_here = patches.shape[0]
    length = patches.shape[1] + 1
    group_heads = w_qkv.shape[1] // (3 * HD)
    embedded = matrix_product(patches, w_patch) + vectors[6]
    class_rows = jnp.broadcast_to(vectors[9], (images_here, 1, D))
    initial = jnp.concatenate([class_rows, embedded], 1) + pos_rows
    normed, norm_back = jax.vjp(layer_norm, initial, vectors[0], vectors[1])
    normed_low = normed.astype(jnp.bfloat16)
    packed = (
        matrix_product(normed_low, w_qkv)
        .reshape(images_here, length, group_heads, 3, HD)
        .astype(jnp.bfloat16)
    )
    queries = packed[:, :, :, 0]
    key_rows = packed[:, :, :, 1]
    value_rows = packed[:, :, :, 2]
    scores = jnp.einsum(
        "nqhd,nkhd->nhqk", queries, key_rows, preferred_element_type=jnp.float32
    ) * HD ** (-0.5)
    log_total = jax.nn.logsumexp(scores, -1)
    soft_low = jnp.exp(scores - log_total[..., None]).astype(jnp.bfloat16)
    blended = jnp.einsum(
        "nhqk,nkhd->nqhd", soft_low, value_rows, preferred_element_type=jnp.float32
    )
    blended = blended.reshape(images_here, length, group_heads * HD).astype(jnp.bfloat16)
    branch = lax.psum(product_transposed_right(blended, w_out).astype(jnp.bfloat16), "head").astype(
        jnp.float32
    )
    middle = initial + vectors[7] + branch
    normed_two, norm_two_back = jax.vjp(layer_norm, middle, vectors[2], vectors[3])
    normed_two_low = normed_two.astype(jnp.bfloat16)
    upward = matrix_product(normed_two_low, w_up)
    active, gelu_back = jax.vjp(exact_gelu, upward)
    active_low = active.astype(jnp.bfloat16)
    branch_two = lax.psum(
        product_transposed_right(active_low, w_down).astype(jnp.bfloat16), "head"
    ).astype(jnp.float32)
    pooled = jnp.mean(middle + vectors[8] + branch_two, 1)
    kept = (
        patches,
        normed_low,
        norm_back,
        queries,
        key_rows,
        value_rows,
        log_total,
        soft_low,
        blended,
        normed_two_low,
        norm_two_back,
        gelu_back,
        active_low,
    )
    return (pooled, kept)


def backward_group(grad_pooled, kept, weights, picker):
    (
        patches,
        normed_low,
        norm_back,
        queries,
        key_rows,
        value_rows,
        log_total,
        soft_low,
        blended,
        normed_two_low,
        norm_two_back,
        gelu_back,
        active_low,
    ) = kept
    w_patch, vectors, w_qkv, w_out, w_up, w_down = weights
    images_here, length = (normed_low.shape[0], normed_low.shape[1])
    group_heads = w_qkv.shape[1] // (3 * HD)
    grad_final = jnp.broadcast_to(grad_pooled[:, None, :] / length, (images_here, length, D))
    grad_final_low = grad_final.astype(jnp.bfloat16)
    grad_down = row_product_result(grad_final_low, active_low)
    grad_active = matrix_product(grad_final_low, w_down)
    grad_upward = gelu_back(grad_active)[0].astype(jnp.bfloat16)
    grad_up = row_product_result(normed_two_low, grad_upward)
    grad_normed_two = lax.psum(
        product_transposed_right(grad_upward, w_up).astype(jnp.bfloat16), "head"
    ).astype(jnp.float32)
    grad_middle, gain_two, shift_two = norm_two_back(grad_normed_two)
    grad_middle = grad_middle + grad_final
    grad_middle_low = grad_middle.astype(jnp.bfloat16)
    grad_out = row_product_result(grad_middle_low, blended)
    grad_blend = (
        matrix_product(grad_middle_low, w_out)
        .reshape(images_here, length, group_heads, HD)
        .astype(jnp.bfloat16)
    )
    grad_values = jnp.einsum(
        "nhqk,nqhd->nkhd", soft_low, grad_blend, preferred_element_type=jnp.float32
    )
    grad_soft = jnp.einsum(
        "nqhd,nkhd->nhqk", grad_blend, value_rows, preferred_element_type=jnp.float32
    )
    scale = HD ** (-0.5)
    scores = (
        jnp.einsum("nqhd,nkhd->nhqk", queries, key_rows, preferred_element_type=jnp.float32) * scale
    )
    probs = jnp.exp(scores - log_total[..., None])
    grad_scores = probs * (grad_soft - jnp.sum(probs * grad_soft, -1, keepdims=True))
    grad_scores = grad_scores.astype(jnp.bfloat16)
    grad_queries = (
        jnp.einsum("nhqk,nkhd->nqhd", grad_scores, key_rows, preferred_element_type=jnp.float32)
        * scale
    )
    grad_keys = (
        jnp.einsum("nhqk,nqhd->nkhd", grad_scores, queries, preferred_element_type=jnp.float32)
        * scale
    )
    grad_packed = jnp.stack([grad_queries, grad_keys, grad_values], 3).astype(jnp.bfloat16)
    grad_packed = grad_packed.reshape(images_here, length, 3 * group_heads * HD)
    grad_qkv = row_product_result(normed_low, grad_packed)
    grad_normed = lax.psum(
        product_transposed_right(grad_packed, w_qkv).astype(jnp.bfloat16), "head"
    ).astype(jnp.float32)
    grad_initial, gain_one, shift_one = norm_back(grad_normed)
    grad_initial = grad_initial + grad_middle
    grad_embed = grad_initial[:, 1:]
    grad_patch = row_product_result(patches, picker(grad_embed.astype(jnp.bfloat16)))
    zero_row = jnp.zeros((D,), jnp.float32)
    vector_grads = jnp.stack(
        [
            gain_one,
            shift_one,
            gain_two,
            shift_two,
            zero_row,
            zero_row,
            jnp.sum(grad_embed, (0, 1)),
            jnp.sum(grad_middle, (0, 1)),
            jnp.sum(grad_final, (0, 1)),
            jnp.sum(grad_initial[:, 0], 0),
        ]
    )
    grad_pos = jnp.sum(grad_initial, 0)
    return (grad_patch, grad_pos, vector_grads, (grad_qkv, grad_out, grad_up, grad_down))


def body(
    low_patches,
    high_patches,
    interp,
    labels,
    partner,
    pair_count,
    w_patch,
    pos_table,
    vectors,
    head_w,
    w_qkv,
    w_out,
    w_up,
    w_down,
    mom_qkv,
    mom_out,
    mom_up,
    mom_down,
    first_patch,
    second_patch,
    first_pos,
    second_pos,
    first_vec,
    second_vec,
    first_head,
    second_head,
):
    gathered = (
        lax.all_gather(w_patch.astype(jnp.bfloat16), "batch", axis=0, tiled=True),
        lax.all_gather(head_w.astype(jnp.bfloat16), "batch", axis=0, tiled=True),
        lax.all_gather(w_qkv.astype(jnp.bfloat16), "batch", axis=0, tiled=True),
        lax.all_gather(w_out.astype(jnp.bfloat16), "batch", axis=0, tiled=True),
        lax.all_gather(w_up.astype(jnp.bfloat16), "batch", axis=0, tiled=True),
        lax.all_gather(w_down.astype(jnp.bfloat16), "batch", axis=0, tiled=True),
        lax.all_gather(pos_table.astype(jnp.bfloat16), "batch", axis=1, tiled=True),
        lax.all_gather(vectors.astype(jnp.bfloat16), "batch", axis=1, tiled=True),
    )
    full_patch, full_head, full_qkv, full_out, full_up, full_down, full_pos, full_vec = gathered
    vector_rows = full_vec.astype(jnp.float32)
    pos_rows = full_pos.astype(jnp.float32)
    interp_rows = interp.astype(jnp.float32)
    pos_high = jnp.concatenate([pos_rows[:1], precise(interp_rows, pos_rows[1:])], 0)
    weights = (full_patch, vector_rows, full_qkv, full_out, full_up, full_down)
    pooled_low, kept_low = encode_group(low_patches, pos_rows, weights)
    pooled_high, kept_high = encode_group(high_patches, pos_high, weights)
    pooled = jnp.concatenate([pooled_low, pooled_high], 0)
    features, final_back = jax.vjp(layer_norm, pooled, vector_rows[4], vector_rows[5])
    features_low = features.astype(jnp.bfloat16)
    outputs = matrix_product(features_low, full_head)
    logits = outputs[:, :CLS]
    projected = outputs[:, CLS:]
    images_here = labels.shape[0]
    images_all = images_here * lax.axis_size("batch")
    class_terms, class_back = jax.vjp(partial(class_sum, labels=labels), logits)
    normalized_rows, unit_back = jax.vjp(unit_norm, projected)
    low_resolution_unit = normalized_rows.astype(jnp.bfloat16)
    all_unit_vectors = lax.all_gather(low_resolution_unit, "batch", axis=0, tiled=True)
    similarity_scores = (
        product_transposed_right(low_resolution_unit, all_unit_vectors) / SOFTMAX_TEMP
    )
    own_ids = lax.axis_index("batch") * images_here + jnp.arange(images_here, dtype=jnp.int32)
    column_ids = jnp.arange(images_all, dtype=jnp.int32)
    masked = jnp.where(own_ids[:, None] == column_ids[None, :], -1e30, similarity_scores)
    log_total = jax.nn.logsumexp(masked, -1)
    target = column_ids[None, :] == partner[:, None]
    pair_terms = jnp.sum(log_total - jnp.sum(jnp.where(target, similarity_scores, 0.0), -1))
    count = pair_count[0].astype(jnp.float32)
    similarity_gradient = (
        jnp.exp(masked - log_total[:, None]) - target.astype(jnp.float32)
    ) / count
    similarity_gradient = similarity_gradient.astype(jnp.bfloat16)
    other_device_rows = row_product_result(similarity_gradient, low_resolution_unit) / SOFTMAX_TEMP
    unit_vector_gradient = matrix_product(
        similarity_gradient, all_unit_vectors
    ) / SOFTMAX_TEMP + lax.psum_scatter(other_device_rows, "batch", scatter_dimension=0, tiled=True)
    unit_vector_gradient = lax.optimization_barrier(
        unit_vector_gradient.astype(jnp.bfloat16)
    ).astype(jnp.float32)
    grad_projected = unit_back(unit_vector_gradient)[0]
    grad_logits = class_back(jnp.float32(1.0 / images_all))[0]
    grad_outputs = jnp.concatenate([grad_logits, grad_projected], 1).astype(jnp.bfloat16)
    grad_head = row_product_result(features_low, keep_all(grad_outputs))
    grad_features = product_transposed_right(grad_outputs, full_head)
    grad_pooled, gain_final, shift_final = final_back(grad_features)
    low_count = low_patches.shape[0]
    patch_low, pos_low, vec_low, matrices_low = backward_group(
        grad_pooled[:low_count], kept_low, weights, keep_all
    )
    patch_high, pos_from_high, vec_high, matrices_high = backward_group(
        grad_pooled[low_count:], kept_high, weights, keep_all
    )
    grad_patch = patch_low + patch_high
    grad_pos = pos_low + jnp.concatenate(
        [pos_from_high[:1], precise(interp_rows.T, pos_from_high[1:])], 0
    )
    grad_vec = (vec_low + vec_high).at[4].set(gain_final).at[5].set(shift_final)
    reduced = (
        lax.psum_scatter(grad_patch, "batch", scatter_dimension=0, tiled=True),
        lax.psum_scatter(grad_head, "batch", scatter_dimension=0, tiled=True),
        lax.psum_scatter(
            matrices_low[0] + matrices_high[0], "batch", scatter_dimension=0, tiled=True
        ),
        lax.psum_scatter(
            matrices_low[1] + matrices_high[1], "batch", scatter_dimension=0, tiled=True
        ),
        lax.psum_scatter(
            matrices_low[2] + matrices_high[2], "batch", scatter_dimension=0, tiled=True
        ),
        lax.psum_scatter(
            matrices_low[3] + matrices_high[3], "batch", scatter_dimension=0, tiled=True
        ),
        lax.psum_scatter(grad_pos, "batch", scatter_dimension=1, tiled=True),
        lax.psum_scatter(grad_vec, "batch", scatter_dimension=1, tiled=True),
    )
    reduced_patch, reduced_head = (reduced[0], reduced[1])
    heads_count = lax.axis_size("head")
    adam_grads = (reduced_patch, reduced[6], reduced[7], reduced_head)
    adam_squares = sum((jnp.sum(gradient * gradient) for gradient in adam_grads))
    muon_squares = sum((jnp.sum(reduced[index] * reduced[index]) for index in range(2, 6)))
    totals = lax.psum(
        (
            muon_squares + adam_squares / heads_count,
            pair_terms / heads_count,
            class_terms / heads_count,
        ),
        ("batch", "head"),
    )
    norm = jnp.sqrt(totals[0])
    factor = jnp.minimum(1.0, CLIP_NORM / norm)
    losses = jnp.stack([totals[1], totals[2]])
    adam_weights = (w_patch, pos_table, vectors, head_w)
    firsts = (first_patch, first_pos, first_vec, first_head)
    seconds = (second_patch, second_pos, second_vec, second_head)
    adam_new = [
        adam_update(
            adam_weights[index],
            factor * adam_grads[index],
            firsts[index],
            seconds[index],
            ADAM_RATES[index],
            ADAM_DECAYS[index],
        )
        for index in range(4)
    ]
    old_moments = (mom_qkv, mom_out, mom_up, mom_down)
    old_weights = (w_qkv, w_out, w_up, w_down)
    moments = [MOMENTUM * old_moments[index] + factor * reduced[2 + index] for index in range(4)]
    squares = [jnp.sum(moment * moment) for moment in moments]
    totals_moment = lax.psum((squares[0], squares[1], squares[2], squares[3]), ("batch", "head"))
    moment_logs = jnp.log(
        jnp.stack([totals_moment[0], totals_moment[1], totals_moment[2], totals_moment[3]])
    )
    iterates = [moments[index] / (jnp.sqrt(totals_moment[index]) + 1e-07) for index in range(4)]
    for sweep in range(NS_STEPS):
        fulls = (
            lax.all_gather(for_sending(iterates[0]), "batch", axis=0, tiled=True),
            lax.all_gather(for_sending(iterates[1]), "batch", axis=0, tiled=True),
            lax.all_gather(for_sending(iterates[2]), "batch", axis=0, tiled=True),
            lax.all_gather(for_sending(iterates[3]), "batch", axis=0, tiled=True),
        )
        pieces = [
            product_transposed_right(iterates[index], fulls[index], PRECISE) for index in range(4)
        ]
        gram_rows = (
            lax.psum(pieces[0].astype(jnp.bfloat16), "head").astype(jnp.float32),
            lax.psum(pieces[1].astype(jnp.bfloat16), "head").astype(jnp.float32),
            lax.psum(pieces[2].astype(jnp.bfloat16), "head").astype(jnp.float32),
            lax.psum(pieces[3].astype(jnp.bfloat16), "head").astype(jnp.float32),
        )
        gram_full = (
            lax.all_gather(gram_rows[0].astype(jnp.bfloat16), "batch", axis=0, tiled=True).astype(
                jnp.float32
            ),
            lax.all_gather(gram_rows[1].astype(jnp.bfloat16), "batch", axis=0, tiled=True).astype(
                jnp.float32
            ),
            lax.all_gather(gram_rows[2].astype(jnp.bfloat16), "batch", axis=0, tiled=True).astype(
                jnp.float32
            ),
            lax.all_gather(gram_rows[3].astype(jnp.bfloat16), "batch", axis=0, tiled=True).astype(
                jnp.float32
            ),
        )
        iterates = [
            POLY_ONE * iterates[index]
            + precise(
                POLY_TWO * gram_rows[index]
                + POLY_THREE * precise(gram_rows[index], gram_full[index]),
                fulls[index],
            )
            for index in range(4)
        ]
    new_muon = []
    for index in range(4):
        weight = old_weights[index]
        full_columns = weight.shape[1] * heads_count
        scale = 0.2 * math.sqrt(max(D, full_columns))
        new_muon.append(weight - MUON_RATE * (scale * iterates[index] + DECAY_RATE * weight))
    return (
        adam_new[0][0],
        adam_new[1][0],
        adam_new[2][0],
        adam_new[3][0],
        new_muon[0],
        new_muon[1],
        new_muon[2],
        new_muon[3],
        moments[0],
        moments[1],
        moments[2],
        moments[3],
        adam_new[0][1],
        adam_new[1][1],
        adam_new[2][1],
        adam_new[3][1],
        adam_new[0][2],
        adam_new[1][2],
        adam_new[2][2],
        adam_new[3][2],
        losses,
        norm[None],
        moment_logs,
    )


def solution(mesh):
    placed = (
        P("batch", None, None),
        P("batch", None, None),
        P(),
        P("batch"),
        P("batch"),
        P(),
        P("batch", None),
        P(None, "batch"),
        P(None, "batch"),
        P("batch", None),
        P("batch", "head"),
        P("batch", "head"),
        P("batch", "head"),
        P("batch", "head"),
        P("batch", "head"),
        P("batch", "head"),
        P("batch", "head"),
        P("batch", "head"),
        P("batch", None),
        P("batch", None),
        P(None, "batch"),
        P(None, "batch"),
        P(None, "batch"),
        P(None, "batch"),
        P("batch", None),
        P("batch", None),
    )
    return jax.shard_map(
        body,
        mesh=mesh,
        in_specs=placed,
        out_specs=(
            P("batch", None),
            P(None, "batch"),
            P(None, "batch"),
            P("batch", None),
            P("batch", "head"),
            P("batch", "head"),
            P("batch", "head"),
            P("batch", "head"),
            P("batch", "head"),
            P("batch", "head"),
            P("batch", "head"),
            P("batch", "head"),
            P("batch", None),
            P(None, "batch"),
            P(None, "batch"),
            P("batch", None),
            P("batch", None),
            P(None, "batch"),
            P(None, "batch"),
            P("batch", None),
            P(),
            P(),
            P(),
        ),
        check_vma=False,
    )
```

profile of v0, /device:TPU:0, one launch (start us, length us, event | category | flops | bytes accessed | tf_op | source)
XLA Modules:
  0.0 2237.0 jit_solution(3375398994074332347)
XLA Ops:
  10.1 33.4 %all_gather.101 = bf16[197,768]{0,1:T(8,128)(2,1)S(1)} all-gather(bf16[197,96]{0,1:T(8,128)(2,1)S(1)} %convert_element_type.391), channel_id=1, replica_groups=mesh['batch'=8,'head'=4] {'batch'}, dimensions={1}, use_global_device_ids=true | all-gather | bytes 340416 | tf_op jit(solution)/shard_map/all_gather | solution.py:279
  44.5 30.4 %all-gather = bf16[8,96,10]{1,2,0:T(8,128)(2,1)S(1)} all-gather(bf16[1,96,10]{1,2,0:T(8,128)(2,1)S(1)} %convert_bitcast_fusion), channel_id=1, replica_groups=mesh['batch'=8,'head'=4] {'batch'}, dimensions={0}, use_global_device_ids=true | all-gather | bytes 17280 | tf_op jit(solution)/shard_map/all_gather | solution.py:280
  75.7 31.1 %all_gather.103 = bf16[768,192]{1,0:T(8,128)(2,1)S(1)} all-gather(bf16[96,192]{1,0:T(8,128)(2,1)S(1)} %convert_element_type.402), channel_id=1, replica_groups=mesh['batch'=8,'head'=4] {'batch'}, dimensions={0}, use_global_device_ids=true | all-gather | bytes 331776 | tf_op jit(solution)/shard_map/all_gather | solution.py:276
  108.7 34.4 %all_gather.102 = bf16[768,576]{1,0:T(8,128)(2,1)} all-gather(bf16[96,576]{1,0:T(8,128)(2,1)S(1)} %convert_element_type.395), channel_id=1, replica_groups=mesh['batch'=8,'head'=4] {'batch'}, dimensions={0}, use_global_device_ids=true | all-gather | bytes 995328 | tf_op jit(solution)/shard_map/all_gather | solution.py:275
  174.9 54.5 %all-reduce.29.cloned.1.call-done = (bf16[2,577,768]{2,1,0:T(8,128)(2,1)}, bf16[2,197,768]{2,1,0:T(8,128)(2,1)}) async-done(((bf16[2,577,768]{2,1,0:T(8,128)(2,1)}, bf16[2,197,768]{2,1,0:T(8,128)(2,1)}), (bf16[2,577,768]{2,1,0:T(8,128)(2,1)}, bf16[2,197,768]{2,1,0:T(8,128)(2,1)})) %all-reduce.29.cloned.1.call-update) | async-done | bytes 2377744 | tf_op jit(solution)/shard_map/psum | solution.py:126
  235.9 37.6 %all-gather.27.cloned.1.call-done = bf16[768,768]{1,0:T(8,128)(2,1)} async-done(((bf16[96,768]{1,0:T(8,128)(2,1)}), bf16[768,768]{1,0:T(8,128)(2,1)}) %all-gather.27.cloned.1.call-update) | async-done | bytes 1179664 | tf_op jit(solution)/shard_map/all_gather | solution.py:277
  285.6 9.2 multiply_convert_fusion.1
  294.9 21.4 all-gather.29.cloned.1.call-done
  329.0 50.2 %all-reduce.27.cloned.1.call-done = (bf16[2,577,768]{2,1,0:T(8,128)(2,1)}, bf16[2,197,768]{2,1,0:T(8,128)(2,1)}) async-done(((bf16[2,577,768]{2,1,0:T(8,128)(2,1)}, bf16[2,197,768]{2,1,0:T(8,128)(2,1)}), (bf16[2,577,768]{2,1,0:T(8,128)(2,1)}, bf16[2,197,768]{2,1,0:T(8,128)(2,1)})) %all-reduce.27.cloned.1.call-update) | async-done | bytes 2377744 | tf_op jit(solution)/shard_map/psum | solution.py:135
  384.3 45.1 %all-gather.31.cloned.1.call-done = bf16[768,1256]{1,0:T(8,128)(2,1)} async-done(((bf16[96,1256]{1,0:T(8,128)(2,1)}), bf16[768,1256]{1,0:T(8,128)(2,1)}) %all-gather.31.cloned.1.call-update) | async-done | bytes 1929232 | tf_op jit(solution)/shard_map/all_gather | solution.py:274
  432.8 26.0 %all-gather.1 = bf16[8,4,256]{2,1,0:T(4,128)(2,1)S(1)} all-gather(bf16[1,4,256]{2,1,0:T(4,128)(2,1)S(1)} %fusion.292), channel_id=1, replica_groups=mesh['batch'=8,'head'=4] {'batch'}, dimensions={0}, use_global_device_ids=true | all-gather | bytes 18432 | tf_op jit(solution)/shard_map/all_gather | solution.py:301
  465.4 35.1 %all-reduce = f32[32,256]{1,0:T(8,128)} all-reduce(f32[32,256]{1,0:T(8,128)} %convolution_multiply_fusion.17), channel_id=2, replica_groups=mesh['batch'=8,'head'=4] {'batch'}, use_global_device_ids=true, to_apply=%region_25.26.clone | all-reduce | flops 8192 | bytes 65536
  520.8 54.1 %all-reduce.25.cloned.1.call-done = (bf16[2,577,768]{2,1,0:T(8,128)(2,1)}, bf16[2,197,768]{2,1,0:T(8,128)(2,1)}) async-done(((bf16[2,577,768]{2,1,0:T(8,128)(2,1)}, bf16[2,197,768]{2,1,0:T(8,128)(2,1)}), (bf16[2,577,768]{2,1,0:T(8,128)(2,1)}, bf16[2,197,768]{2,1,0:T(8,128)(2,1)})) %all-reduce.25.cloned.1.call-update) | async-done | bytes 2377744 | tf_op jit(solution)/shard_map/psum | solution.py:182
  598.6 10.1 multiply_convert_fusion
  633.4 45.9 %all-reduce.23.cloned.1.call-done = (bf16[2,577,768]{2,1,0:T(8,128)(2,1)}, bf16[2,197,768]{2,1,0:T(8,128)(2,1)}) async-done(((bf16[2,577,768]{2,1,0:T(8,128)(2,1)}, bf16[2,197,768]{2,1,0:T(8,128)(2,1)}), (bf16[2,577,768]{2,1,0:T(8,128)(2,1)}, bf16[2,197,768]{2,1,0:T(8,128)(2,1)})) %all-reduce.23.cloned.1.call-update) | async-done | bytes 2377744 | tf_op jit(solution)/shard_map/psum | solution.py:218
  748.8 60.8 %reduce-scatter.27.cloned.1.call-done = f32[96,10]{1,0:T(8,128)} async-done(((f32[768,10]{1,0:T(8,128)}), f32[96,10]{1,0:T(8,128)}) %reduce-scatter.27.cloned.1.call-update) | async-done | bytes 3856
  811.0 63.8 %reduce-scatter.25.cloned.1.call-done = f32[96,197]{1,0:T(8,128)} async-done(((f32[768,197]{1,0:T(8,128)}), f32[96,197]{1,0:T(8,128)}) %reduce-scatter.25.cloned.1.call-update) | async-done | bytes 75664
  876.4 69.7 %reduce-scatter.17.cloned.1.call-done = f32[96,768]{1,0:T(8,128)} async-done(((f32[768,768]{1,0:T(8,128)}), f32[96,768]{1,0:T(8,128)}) %reduce-scatter.17.cloned.1.call-update) | async-done | bytes 294928 | tf_op jit(solution)/shard_map/reduce_scatter | solution.py:350
  947.9 69.8 %reduce-scatter.19.cloned.1.call-done = f32[96,768]{1,0:T(8,128)} async-done(((f32[768,768]{1,0:T(8,128)}), f32[96,768]{1,0:T(8,128)}) %reduce-scatter.19.cloned.1.call-update) | async-done | bytes 294928 | tf_op jit(solution)/shard_map/reduce_scatter | solution.py:353
  1019.4 67.4 %reduce-scatter.13.cloned.1.call-done = f32[96,576]{1,0:T(8,128)} async-done(((f32[768,576]{1,0:T(8,128)}), f32[96,576]{1,0:T(8,128)}) %reduce-scatter.13.cloned.1.call-update) | async-done | bytes 221200 | tf_op jit(solution)/shard_map/reduce_scatter | solution.py:344
  1091.1 67.5 %reduce-scatter.21.cloned.1.call-done = f32[96,768]{1,0:T(8,128)} async-done(((f32[768,768]{1,0:T(8,128)}), f32[96,768]{1,0:T(8,128)}) %reduce-scatter.21.cloned.1.call-update) | async-done | bytes 294928 | tf_op jit(solution)/shard_map/reduce_scatter | solution.py:342
  1162.2 83.8 %reduce-scatter.23.cloned.1.call-done = f32[96,1256]{1,0:T(8,128)} async-done(((f32[768,1256]{1,0:T(8,128)}), f32[96,1256]{1,0:T(8,128)}) %reduce-scatter.23.cloned.1.call-update) | async-done | bytes 482320 | tf_op jit(solution)/shard_map/reduce_scatter | solution.py:343
  1249.0 40.3 %psum.197 = f32[]{:T(128)} all-reduce(f32[]{:T(128)S(6)} %add.632), channel_id=1, replica_groups=mesh['batch'=8,'head'=4] {'batch','head'}, use_global_device_ids=true, to_apply=%region_79.80 | all-reduce | flops 1 | bytes 8 | tf_op jit(solution)/shard_map/psum | solution.py:364
  1294.9 40.6 %all-reduce.1 = (f32[]{:T(128)}, f32[]{:T(128)}, f32[]{:T(128)}, f32[]{:T(128)}, f32[1]{0:T(128)}, /*index=5*/f32[1]{0:T(128)}) all-reduce(f32[]{:T(128)} %get-tuple-element.210, f32[]{:T(128)} %get-tuple-element.208, f32[]{:T(128)} %get-tuple-element.206, ...), channel_id=1, replica_groups=mesh['batch'=8,'head'=4] {'batch','head'}, use_global_device_ids=true, to_apply=%region_81.82 | all-reduce | flops 6 | bytes 48 | tf_op jit(solution)/shard_map/psum | solution.py:393
  1339.7 31.7 %all_gather.114 = bf16[768,192]{1,0:T(8,128)(2,1)S(1)} all-gather(bf16[96,192]{1,0:T(8,128)(2,1)S(1)} %fusion.155), channel_id=1, replica_groups=mesh['batch'=8,'head'=4] {'batch'}, dimensions={0}, use_global_device_ids=true | all-gather | bytes 331776 | tf_op jit(solution)/shard_map/all_gather | solution.py:401
  1372.7 32.8 %all_gather.108 = bf16[768,576]{1,0:T(8,128)(2,1)S(1)} all-gather(bf16[96,576]{1,0:T(8,128)(2,1)S(1)} %fusion.157), channel_id=1, replica_groups=mesh['batch'=8,'head'=4] {'batch'}, dimensions={0}, use_global_device_ids=true | all-gather | bytes 995328 | tf_op jit(solution)/shard_map/all_gather | solution.py:400
  1411.3 16.8 all-gather.57.cloned.1.call-done
  1431.3 33.2 %all-reduce.21.cloned.1.call-done = (bf16[96,768]{1,0:T(8,128)(2,1)}, bf16[96,768]{1,0:T(8,128)(2,1)}, bf16[96,768]{1,0:T(8,128)(2,1)}, bf16[96,768]{1,0:T(8,128)(2,1)}) async-done(((bf16[96,768]{1,0:T(8,128)(2,1)}, bf16[96,768]{1,0:T(8,128)(2,1)}, bf16[96,768]{1,0:T(8,128)(2,1)}, bf16[96,768]{1,0:T(8,128)(2,1)}), (bf16[96,768]{1,0:T(8,128)(2,1)}, bf16[96,768]{1,0:T(8,128)(2,1)}, bf16[96,768]{1,0:T(8,128)(2,1)}, ...) | async-done | bytes 589840 | tf_op jit(solution)/shard_map/psum | solution.py:409
  1466.8 40.8 %all-gather.59.cloned.1.call-done = bf16[768,768]{1,0:T(8,128)(2,1)} async-done(((bf16[96,768]{1,0:T(8,128)(2,1)}), bf16[768,768]{1,0:T(8,128)(2,1)}) %all-gather.59.cloned.1.call-update) | async-done | bytes 1179664 | tf_op jit(solution)/shard_map/all_gather | solution.py:424
  1510.8 38.8 %all-gather.47.cloned.1.call-done = bf16[768,768]{1,0:T(8,128)(2,1)} async-done(((bf16[96,768]{1,0:T(8,128)(2,1)}), bf16[768,768]{1,0:T(8,128)(2,1)}) %all-gather.47.cloned.1.call-update) | async-done | bytes 1179664 | tf_op jit(solution)/shard_map/all_gather | solution.py:421
  1553.0 38.7 %all-gather.39.cloned.1.call-done = bf16[768,768]{1,0:T(8,128)(2,1)} async-done(((bf16[96,768]{1,0:T(8,128)(2,1)}), bf16[768,768]{1,0:T(8,128)(2,1)}) %all-gather.39.cloned.1.call-update) | async-done | bytes 1179664 | tf_op jit(solution)/shard_map/all_gather | solution.py:418
  1593.7 31.2 %all_gather.116 = bf16[768,192]{1,0:T(8,128)(2,1)S(1)} all-gather(bf16[96,192]{1,0:T(8,128)(2,1)S(1)} %get-tuple-element.275), channel_id=1, replica_groups=mesh['batch'=8,'head'=4] {'batch'}, dimensions={0}, use_global_device_ids=true | all-gather | bytes 331776 | tf_op jit(solution)/shard_map/all_gather | solution.py:401
  1626.1 8.8 all-gather.33.cloned.1.call-done
  1637.2 34.3 %all_gather.110 = bf16[768,576]{1,0:T(8,128)(2,1)S(1)} all-gather(bf16[96,576]{1,0:T(8,128)(2,1)S(1)} %get-tuple-element.273), channel_id=1, replica_groups=mesh['batch'=8,'head'=4] {'batch'}, dimensions={0}, use_global_device_ids=true | all-gather | bytes 995328 | tf_op jit(solution)/shard_map/all_gather | solution.py:400
  1683.7 39.5 %all-gather.49.cloned.1.call-done = bf16[768,768]{1,0:T(8,128)(2,1)} async-done(((bf16[96,768]{1,0:T(8,128)(2,1)}), bf16[768,768]{1,0:T(8,128)(2,1)}) %all-gather.49.cloned.1.call-update) | async-done | bytes 1179664 | tf_op jit(solution)/shard_map/all_gather | solution.py:402
  1726.5 33.5 %all-reduce.19.cloned.1.call-done = (bf16[96,768]{1,0:T(8,128)(2,1)}, bf16[96,768]{1,0:T(8,128)(2,1)}, bf16[96,768]{1,0:T(8,128)(2,1)}, bf16[96,768]{1,0:T(8,128)(2,1)}) async-done(((bf16[96,768]{1,0:T(8,128)(2,1)}, bf16[96,768]{1,0:T(8,128)(2,1)}, bf16[96,768]{1,0:T(8,128)(2,1)}, bf16[96,768]{1,0:T(8,128)(2,1)}), (bf16[96,768]{1,0:T(8,128)(2,1)}, bf16[96,768]{1,0:T(8,128)(2,1)}, bf16[96,768]{1,0:T(8,128)(2,1)}, ...) | async-done | bytes 589840 | tf_op jit(solution)/shard_map/psum | solution.py:409
  1762.1 41.0 %all-gather.63.cloned.1.call-done = bf16[768,768]{1,0:T(8,128)(2,1)} async-done(((bf16[96,768]{1,0:T(8,128)(2,1)}), bf16[768,768]{1,0:T(8,128)(2,1)}) %all-gather.63.cloned.1.call-update) | async-done | bytes 1179664 | tf_op jit(solution)/shard_map/all_gather | solution.py:424
  1807.2 37.9 %all-gather.51.cloned.1.call-done = bf16[768,768]{1,0:T(8,128)(2,1)} async-done(((bf16[96,768]{1,0:T(8,128)(2,1)}), bf16[768,768]{1,0:T(8,128)(2,1)}) %all-gather.51.cloned.1.call-update) | async-done | bytes 1179664 | tf_op jit(solution)/shard_map/all_gather | solution.py:421
  1848.5 38.7 %all-gather.41.cloned.1.call-done = bf16[768,768]{1,0:T(8,128)(2,1)} async-done(((bf16[96,768]{1,0:T(8,128)(2,1)}), bf16[768,768]{1,0:T(8,128)(2,1)}) %all-gather.41.cloned.1.call-update) | async-done | bytes 1179664 | tf_op jit(solution)/shard_map/all_gather | solution.py:418
  1889.2 31.2 %all_gather.118 = bf16[768,192]{1,0:T(8,128)(2,1)S(1)} all-gather(bf16[96,192]{1,0:T(8,128)(2,1)S(1)} %get-tuple-element.283), channel_id=1, replica_groups=mesh['batch'=8,'head'=4] {'batch'}, dimensions={0}, use_global_device_ids=true | all-gather | bytes 331776 | tf_op jit(solution)/shard_map/all_gather | solution.py:401
  1921.6 8.7 all-gather.35.cloned.1.call-done
  1932.7 34.2 %all_gather.112 = bf16[768,576]{1,0:T(8,128)(2,1)S(1)} all-gather(bf16[96,576]{1,0:T(8,128)(2,1)S(1)} %get-tuple-element.281), channel_id=1, replica_groups=mesh['batch'=8,'head'=4] {'batch'}, dimensions={0}, use_global_device_ids=true | all-gather | bytes 995328 | tf_op jit(solution)/shard_map/all_gather | solution.py:400
  1979.3 39.4 %all-gather.53.cloned.1.call-done = bf16[768,768]{1,0:T(8,128)(2,1)} async-done(((bf16[96,768]{1,0:T(8,128)(2,1)}), bf16[768,768]{1,0:T(8,128)(2,1)}) %all-gather.53.cloned.1.call-update) | async-done | bytes 1179664 | tf_op jit(solution)/shard_map/all_gather | solution.py:402
  2022.1 33.5 %all-reduce.17.cloned.1.call-done = (bf16[96,768]{1,0:T(8,128)(2,1)}, bf16[96,768]{1,0:T(8,128)(2,1)}, bf16[96,768]{1,0:T(8,128)(2,1)}, bf16[96,768]{1,0:T(8,128)(2,1)}) async-done(((bf16[96,768]{1,0:T(8,128)(2,1)}, bf16[96,768]{1,0:T(8,128)(2,1)}, bf16[96,768]{1,0:T(8,128)(2,1)}, bf16[96,768]{1,0:T(8,128)(2,1)}), (bf16[96,768]{1,0:T(8,128)(2,1)}, bf16[96,768]{1,0:T(8,128)(2,1)}, bf16[96,768]{1,0:T(8,128)(2,1)}, ...) | async-done | bytes 589840 | tf_op jit(solution)/shard_map/psum | solution.py:409
  2080.0 18.9 all-gather.43.cloned.1.call-done
  2101.5 39.3 %all-gather.37.cloned.1.call-done = bf16[768,768]{1,0:T(8,128)(2,1)} async-done(((bf16[96,768]{1,0:T(8,128)(2,1)}), bf16[768,768]{1,0:T(8,128)(2,1)}) %all-gather.37.cloned.1.call-update) | async-done | bytes 1179664 | tf_op jit(solution)/shard_map/all_gather | solution.py:415
  2143.2 39.5 %all-gather.55.cloned.1.call-done = bf16[768,768]{1,0:T(8,128)(2,1)} async-done(((bf16[96,768]{1,0:T(8,128)(2,1)}), bf16[768,768]{1,0:T(8,128)(2,1)}) %all-gather.55.cloned.1.call-update) | async-done | bytes 1179664 | tf_op jit(solution)/shard_map/all_gather | solution.py:421
  2188.3 36.3 %all-gather.67.cloned.1.call-done = bf16[768,768]{1,0:T(8,128)(2,1)} async-done(((bf16[96,768]{1,0:T(8,128)(2,1)}), bf16[768,768]{1,0:T(8,128)(2,1)}) %all-gather.67.cloned.1.call-update) | async-done | bytes 1179664 | tf_op jit(solution)/shard_map/all_gather | solution.py:424
  (667 shorter events, 346.4 us)
Async XLA Ops:
  7.2 135.9 %all-gather.25.cloned.1.call-start = ((), (), s32[]{:S(2)}) async-start(), calls=%async_computation.8 | async-start | bytes 1327104 | tf_op jit(solution)/shard_map/all_gather | solution.py:273
  9.1 220.4 %all-reduce.29.cloned.1.call-start = ((), (), s32[]{:S(2)}) async-start(), calls=%async_computation.44 | async-start | bytes 4816896 | tf_op jit(solution)/shard_map/psum | solution.py:126
  171.5 102.1 %all-gather.27.cloned.1.call-start = ((), (), s32[]{:S(2)}) async-start(), calls=%async_computation.9 | async-start | bytes 1327104 | tf_op jit(solution)/shard_map/all_gather | solution.py:277
  173.2 143.1 %all-gather.29.cloned.1.call-start = ((), (), s32[]{:S(2)}) async-start(), calls=%async_computation.10 | async-start | bytes 1327104 | tf_op jit(solution)/shard_map/all_gather | solution.py:278
  174.9 204.4 %all-reduce.27.cloned.1.call-start = ((), (), s32[]{:S(2)}) async-start(), calls=%async_computation.43 | async-start | bytes 4816896 | tf_op jit(solution)/shard_map/psum | solution.py:135
  230.9 346.7 %copy-start.118 = (f32[2,197]{1,0:T(2,128)}, f32[2,197]{1,0:T(2,128)S(1)}, u32[]{:S(2)}) copy-start(f32[2,197]{1,0:T(2,128)S(1)} %broadcast_multiply_fusion.4) | copy-start | bytes 4732
  232.0 345.6 %copy-start.128 = (f32[2,197]{1,0:T(2,128)}, f32[2,197]{1,0:T(2,128)S(1)}, u32[]{:S(2)}) copy-start(f32[2,197]{1,0:T(2,128)S(1)} %fusion.140) | copy-start | bytes 4732
  235.9 350.0 %copy-start.109 = (f32[2,577]{1,0:T(2,128)}, f32[2,577]{1,0:T(2,128)S(1)}, u32[]{:S(2)}) copy-start(f32[2,577]{1,0:T(2,128)S(1)} %fusion.135) | copy-start | bytes 13852
  323.5 105.9 %all-gather.31.cloned.1.call-start = ((), (), s32[]{:S(2)}) async-start(), calls=%async_computation.11 | async-start | bytes 2211840 | tf_op jit(solution)/shard_map/all_gather | solution.py:274
  325.3 249.5 %all-reduce.25.cloned.1.call-start = ((), (), s32[]{:S(2)}) async-start(), calls=%async_computation.42 | async-start | bytes 4816896 | tf_op jit(solution)/shard_map/psum | solution.py:182
  520.7 158.5 %all-reduce.23.cloned.1.call-start = ((), (), s32[]{:S(2)}) async-start(), calls=%async_computation.41 | async-start | bytes 4816896 | tf_op jit(solution)/shard_map/psum | solution.py:218
  622.3 124.9 %reduce-scatter.15.cloned.1.call-start = ((), (), s32[]{:S(2)}) async-start(), calls=%async_computation.13 | async-start | bytes 884736 | tf_op jit(solution)/shard_map/reduce_scatter | solution.py:347
  633.3 176.2 %reduce-scatter.27.cloned.1.call-start = ((), (), s32[]{:S(2)}) async-start(), calls=%async_computation.37 | async-start | bytes 442368
  697.0 177.7 %reduce-scatter.25.cloned.1.call-start = ((), (), s32[]{:S(2)}) async-start(), calls=%async_computation.36 | async-start | bytes 884736
  700.5 245.7 %reduce-scatter.17.cloned.1.call-start = ((), (), s32[]{:S(2)}) async-start(), calls=%async_computation.14 | async-start | bytes 2654208 | tf_op jit(solution)/shard_map/reduce_scatter | solution.py:350
  708.0 309.7 %reduce-scatter.19.cloned.1.call-start = ((), (), s32[]{:S(2)}) async-start(), calls=%async_computation.15 | async-start | bytes 2654208 | tf_op jit(solution)/shard_map/reduce_scatter | solution.py:353
  713.9 373.0 %reduce-scatter.13.cloned.1.call-start = ((), (), s32[]{:S(2)}) async-start(), calls=%async_computation.12 | async-start | bytes 2211840 | tf_op jit(solution)/shard_map/reduce_scatter | solution.py:344
  736.7 421.9 %reduce-scatter.21.cloned.1.call-start = ((), (), s32[]{:S(2)}) async-start(), calls=%async_computation.16 | async-start | bytes 2654208 | tf_op jit(solution)/shard_map/reduce_scatter | solution.py:342
  743.1 502.9 %reduce-scatter.23.cloned.1.call-start = ((), (), s32[]{:S(2)}) async-start(), calls=%async_computation.17 | async-start | bytes 4423680 | tf_op jit(solution)/shard_map/reduce_scatter | solution.py:343
  746.4 543.7 %copy-start.99 = (f32[96,768]{1,0:T(8,128)S(1)}, f32[96,768]{1,0:T(8,128)}, u32[]{:S(2)}) copy-start(f32[96,768]{1,0:T(8,128)} %param.47) | copy-start | bytes 884740
  746.5 661.6 %all-gather.45.cloned.1.call-start = ((), (), s32[]{:S(2)}) async-start(), calls=%async_computation.24 | async-start | bytes 1327104 | tf_op jit(solution)/shard_map/all_gather | solution.py:402
  946.1 344.7 %copy-start.73 = (f32[96,768]{1,0:T(8,128)S(1)}, f32[96,768]{1,0:T(8,128)}, u32[]{:S(2)}) copy-start(f32[96,768]{1,0:T(8,128)} %reduce-scatter.17.cloned.1.call-done) | copy-start | bytes 884740
  1017.7 272.4 %copy-start.74 = (f32[96,768]{1,0:T(8,128)S(1)}, f32[96,768]{1,0:T(8,128)}, u32[]{:S(2)}) copy-start(f32[96,768]{1,0:T(8,128)} %reduce-scatter.19.cloned.1.call-done) | copy-start | bytes 884740
  1019.4 273.2 %copy-start.96 = (f32[96,192]{1,0:T(8,128)S(1)}, f32[96,192]{1,0:T(8,128)}, u32[]{:S(2)}) copy-start(f32[96,192]{1,0:T(8,128)} %reduce-scatter.15.cloned.1.call-done) | copy-start | bytes 221188
  1019.4 273.2 %copy-start.100 = (f32[96,192]{1,0:T(8,128)S(1)}, f32[96,192]{1,0:T(8,128)}, u32[]{:S(2)}) copy-start(f32[96,192]{1,0:T(8,128)} %param.45) | copy-start | bytes 221188
  1088.5 204.7 %copy-start.80 = (f32[96,576]{1,0:T(8,128)S(1)}, f32[96,576]{1,0:T(8,128)}, u32[]{:S(2)}) copy-start(f32[96,576]{1,0:T(8,128)} %reduce-scatter.13.cloned.1.call-done) | copy-start | bytes 663556
  1293.2 300.1 %copy-start.67 = (f32[96,192]{1,0:T(8,128)}, f32[96,192]{1,0:T(8,128)S(1)}, u32[]{:S(2)}) copy-start(f32[96,192]{1,0:T(8,128)S(1)} %get-tuple-element.209) | copy-start | bytes 221188
  1336.9 91.2 %all-gather.57.cloned.1.call-start = ((), (), s32[]{:S(2)}) async-start(), calls=%async_computation.30 | async-start | bytes 1327104 | tf_op jit(solution)/shard_map/all_gather | solution.py:403
  1338.3 126.1 %all-reduce.21.cloned.1.call-start = ((), (), s32[]{:S(2)}) async-start(), calls=%async_computation.40 | async-start | bytes 1179648 | tf_op jit(solution)/shard_map/psum | solution.py:409
  1431.3 76.3 %all-gather.59.cloned.1.call-start = ((), (), s32[]{:S(2)}) async-start(), calls=%async_computation.31 | async-start | bytes 1327104 | tf_op jit(solution)/shard_map/all_gather | solution.py:424
  1464.5 85.1 %all-gather.47.cloned.1.call-start = ((), (), s32[]{:S(2)}) async-start(), calls=%async_computation.25 | async-start | bytes 1327104 | tf_op jit(solution)/shard_map/all_gather | solution.py:421
  1465.2 126.4 %all-gather.39.cloned.1.call-start = ((), (), s32[]{:S(2)}) async-start(), calls=%async_computation.21 | async-start | bytes 1327104 | tf_op jit(solution)/shard_map/all_gather | solution.py:418
  1466.0 168.9 %all-gather.33.cloned.1.call-start = ((), (), s32[]{:S(2)}) async-start(), calls=%async_computation.18 | async-start | bytes 1327104 | tf_op jit(solution)/shard_map/all_gather | solution.py:415
  1466.7 213.8 %all-gather.61.cloned.1.call-start = ((), (), s32[]{:S(2)}) async-start(), calls=%async_computation.32 | async-start | bytes 1327104 | tf_op jit(solution)/shard_map/all_gather | solution.py:403
  1510.8 169.8 %copy-start.42 = (f32[96,768]{1,0:T(8,128)}, f32[96,768]{1,0:T(8,128)S(1)}, u32[]{:S(2)}) copy-start(f32[96,768]{1,0:T(8,128)S(1)} %get-tuple-element.280) | copy-start | bytes 884740
  1510.8 212.4 %all-gather.49.cloned.1.call-start = ((), (), s32[]{:S(2)}) async-start(), calls=%async_computation.26 | async-start | bytes 1327104 | tf_op jit(solution)/shard_map/all_gather | solution.py:402
  1552.9 207.1 %all-reduce.19.cloned.1.call-start = ((), (), s32[]{:S(2)}) async-start(), calls=%async_computation.39 | async-start | bytes 1179648 | tf_op jit(solution)/shard_map/psum | solution.py:409
  1726.4 76.7 %all-gather.63.cloned.1.call-start = ((), (), s32[]{:S(2)}) async-start(), calls=%async_computation.33 | async-start | bytes 1327104 | tf_op jit(solution)/shard_map/all_gather | solution.py:424
  1760.0 85.1 %all-gather.51.cloned.1.call-start = ((), (), s32[]{:S(2)}) async-start(), calls=%async_computation.27 | async-start | bytes 1327104 | tf_op jit(solution)/shard_map/all_gather | solution.py:421
  1760.8 126.4 %all-gather.41.cloned.1.call-start = ((), (), s32[]{:S(2)}) async-start(), calls=%async_computation.22 | async-start | bytes 1327104 | tf_op jit(solution)/shard_map/all_gather | solution.py:418
  1761.5 168.9 %all-gather.35.cloned.1.call-start = ((), (), s32[]{:S(2)}) async-start(), calls=%async_computation.19 | async-start | bytes 1327104 | tf_op jit(solution)/shard_map/all_gather | solution.py:415
  1762.1 214.1 %all-gather.65.cloned.1.call-start = ((), (), s32[]{:S(2)}) async-start(), calls=%async_computation.34 | async-start | bytes 1327104 | tf_op jit(solution)/shard_map/all_gather | solution.py:403
  1807.2 211.6 %all-gather.53.cloned.1.call-start = ((), (), s32[]{:S(2)}) async-start(), calls=%async_computation.28 | async-start | bytes 1327104 | tf_op jit(solution)/shard_map/all_gather | solution.py:402
  1848.4 207.2 %all-reduce.17.cloned.1.call-start = ((), (), s32[]{:S(2)}) async-start(), calls=%async_computation.38 | async-start | bytes 1179648 | tf_op jit(solution)/shard_map/psum | solution.py:409
  2022.1 76.8 %all-gather.43.cloned.1.call-start = ((), (), s32[]{:S(2)}) async-start(), calls=%async_computation.23 | async-start | bytes 1327104 | tf_op jit(solution)/shard_map/all_gather | solution.py:418
  2055.6 85.3 %all-gather.37.cloned.1.call-start = ((), (), s32[]{:S(2)}) async-start(), calls=%async_computation.20 | async-start | bytes 1327104 | tf_op jit(solution)/shard_map/all_gather | solution.py:415
  2056.3 126.4 %all-gather.55.cloned.1.call-start = ((), (), s32[]{:S(2)}) async-start(), calls=%async_computation.29 | async-start | bytes 1327104 | tf_op jit(solution)/shard_map/all_gather | solution.py:421
  2056.9 167.7 %all-gather.67.cloned.1.call-start = ((), (), s32[]{:S(2)}) async-start(), calls=%async_computation.35 | async-start | bytes 1327104 | tf_op jit(solution)/shard_map/all_gather | solution.py:424
  (157 other events, 2266.3 us)
Sparse Core Ops, SparseCore 0:
  10.8 44.2 all-gather.24
  171.6 57.8 all-reduce.28
  232.5 41.0 all-gather.26
  276.4 39.8 all-gather.28
  323.6 55.5 all-reduce.26
  381.9 47.4 all-gather.30
  520.9 53.9 all-reduce.24
  622.4 56.7 all-reduce.22
  682.6 62.4 reduce-scatter.14
  749.1 60.3 reduce-scatter.26
  813.2 61.5 reduce-scatter.24
  878.1 67.9 reduce-scatter.16
  949.6 68.0 reduce-scatter.18
  1021.0 65.7 reduce-scatter.12
  1090.6 67.9 reduce-scatter.20
  1162.6 83.3 reduce-scatter.22
  1337.0 48.0 all-gather.44
  1387.7 40.3 all-gather.56
  1431.8 32.6 all-reduce.20
  1466.5 41.0 all-gather.58
  1509.8 39.8 all-gather.46
  1551.8 39.8 all-gather.38
  1593.9 40.9 all-gather.32
  1637.5 43.0 all-gather.60
  1683.3 39.8 all-gather.48
  1727.3 32.6 all-reduce.18
  1762.0 41.0 all-gather.62
  1805.3 39.8 all-gather.50
  1847.3 39.8 all-gather.40
  1889.2 41.0 all-gather.34
  1933.1 43.0 all-gather.64
  1979.0 39.7 all-gather.52
  2022.9 32.6 all-reduce.16
  2057.8 41.0 all-gather.42
  2101.0 39.8 all-gather.36
  2142.9 39.8 all-gather.54
  2184.8 39.8 all-gather.66
where the time goes:
time: 2250 us; the launch traced here: 2240 us
  waiting for transfers between devices  1400 us (62%)
  blocking collectives  467 us (21%)
  matrix products  170 us (8%)
  other arithmetic  106 us (5%)
  local copies, waits for them, and re-layouts  66.1 us (3%)
  between operations  29.5 us (1%)
    unnamed x39, waiting for transfers between devices  130 us
    all_gather x3, waiting for transfers between devices, body(): lax.all_gather(gram_rows[3].astype(jnp.bfloat16), 'batch', axis=0, tiled=...  118 us
    all_gather x3, waiting for transfers between devices, body(): lax.all_gather(gram_rows[2].astype(jnp.bfloat16), 'batch', axis=0, tiled=...  116 us
    all_gather x3, blocking collectives, body(): lax.all_gather(for_sending(iterates[0]), 'batch', axis=0, tiled=True)  101 us
    psum x3, waiting for transfers between devices, body(): lax.psum(pieces[0].astype(jnp.bfloat16), 'head').astype(jnp.float32)  100 us
    all_gather x3, waiting for transfers between devices, body(): lax.all_gather(gram_rows[1].astype(jnp.bfloat16), 'batch', axis=0, tiled=...  96.3 us
    all_gather x3, blocking collectives, body(): lax.all_gather(for_sending(iterates[1]), 'batch', axis=0, tiled=True)  94.2 us
    reduce_scatter x1, waiting for transfers between devices, body(): lax.psum_scatter(grad_head, 'batch', scatter_dimension=0, tiled=True)  83.8 us
  transfers between devices with their start and end apart: 37, of which 34 were waited for; matrix products, arithmetic and copies ran while one was open for 9% of the time, Pallas kernels for 0%

commit v1 on v0

v1 whole, which is shorter than its diff:
```python
import math

import jax
import jax.numpy as jnp
from jax import lax
from jax.sharding import PartitionSpec as P

D = 768
HD = 64
CLS = 1000
NS_STEPS = 3
STEP = 10

POLY_ONE = 3.4445
POLY_TWO = -4.775
POLY_THREE = 2.0315
SOFTMAX_TEMP = 0.05
CLIP_NORM = 0.05
MOMENTUM = 0.95
MUON_RATE = 0.2
DECAY_RATE = 0.05
BETA_FIRST = 0.9
BETA_SECOND = 0.99
ADAM_FLOOR = 1e-08
ADAM_RATES = (0.08, 0.3, 0.5, 0.15)
ADAM_DECAYS = (0.05, 0.05, 0.0, 0.05)

BF = jnp.bfloat16
F32 = jnp.float32


def up_to(size, step):
    return -(-size // step) * step


def dot(left, right, left_dim=1, right_dim=0, precision=None):
    return lax.dot_general(
        left,
        right,
        (((left_dim,), (right_dim,)), ((), ())),
        precision=precision,
        preferred_element_type=F32,
    )


def at(stacked, index):
    return lax.dynamic_index_in_dim(stacked, index, 0, keepdims=False)


def swap(values, axis, mask):
    count = lax.axis_size(axis)
    return lax.ppermute(values, axis, [(index, index ^ mask) for index in range(count)])


def swap_core(values):
    return swap(values, "head", 1)


def swap_side(values):
    return swap(values, "head", 2)


def swap_x(values):
    return swap(values, "batch", 1)


def pair_sum(values):
    low = values.astype(BF)
    return low.astype(F32) + swap_core(low).astype(F32)


def gather_rows(shard):
    rows, columns = shard.shape
    count = lax.axis_size("batch")
    if count != 8:
        own = lax.all_gather(shard, "batch", axis=0, tiled=True)
        return own, swap_side(own)
    here = lax.axis_index("batch")
    z, x = here // 2, here % 2
    half = rows // 2
    lines = jnp.stack([shard] + [swap(shard, "batch", 2 * mask) for mask in (1, 2, 3)])
    first, second = lines[:, :half], lines[:, half:]
    first = jnp.stack([first, swap_x(first)])
    second = jnp.stack([second, swap_side(second)])
    first = jnp.stack([first, swap_side(first)])
    second = jnp.stack([second, swap_x(second)])
    first = first.reshape(2, 8, half, columns)
    groups = []
    for side in range(2):
        pieces = []
        for z_to in range(4):
            for x_to in range(2):
                x_from, z_from = x ^ x_to, z ^ z_to
                pieces.append(at(first[side], x_from * 4 + z_from))
                pieces.append(at(second[:, side].reshape(8, half, columns), x_from * 4 + z_from))
        groups.append(jnp.concatenate(pieces, 0))
    return groups


def reduce_rows(own, other):
    count = lax.axis_size("batch")
    columns = own.shape[1]
    rows = own.shape[0] // count
    if count != 8:
        total = own + swap_side(other.astype(BF)).astype(F32)
        return lax.psum_scatter(total, "batch", scatter_dimension=0, tiled=True)
    here = lax.axis_index("batch")
    z, x = here // 2, here % 2
    half = rows // 2

    def pick_x(blocks, index):
        return lax.dynamic_index_in_dim(blocks, index, 1, keepdims=False)

    own = own.reshape(4, 2, rows, columns)
    other = other.reshape(4, 2, rows, columns)
    first = own[:, :, :half] + swap_side(other[:, :, :half].astype(BF)).astype(F32)
    first = pick_x(first, x) + swap_x(pick_x(first, 1 - x).astype(BF)).astype(F32)
    second = jnp.stack([own[:, :, half:], other[:, :, half:]])
    second = second.transpose(1, 2, 0, 3, 4)
    second = pick_x(second, x) + swap_x(pick_x(second, 1 - x).astype(BF)).astype(F32)
    second = second[:, 0] + swap_side(second[:, 1].astype(BF)).astype(F32)
    both = jnp.concatenate([first, second], 1)
    total = at(both, z)
    for mask in (1, 2, 3):
        total = total + swap(at(both, z ^ mask).astype(BF), "batch", 2 * mask).astype(F32)
    return total


def in_order(stacked, here, bits):
    tail = stacked.shape[1:]
    stacked = stacked.reshape((2,) * bits + tail)
    for bit in range(bits):
        axis = bits - 1 - bit
        flag = (here >> bit) % 2 == 1
        stacked = jnp.where(flag, jnp.flip(stacked, axis), stacked)
    return stacked.reshape((2**bits,) + tail)


def gather_small(values):
    count = lax.axis_size("batch")
    if count != 8:
        return lax.all_gather(values, "batch", axis=0, tiled=False)
    pair = jnp.stack([values, swap_x(values)])
    lines = jnp.stack([pair] + [swap(pair, "batch", 2 * mask) for mask in (1, 2, 3)])
    return in_order(lines.reshape((8,) + values.shape), lax.axis_index("batch"), 3)


def sum_everywhere(values):
    for axis in ("head", "batch"):
        mask = 1
        while mask < lax.axis_size(axis):
            values = values + swap(values, axis, mask)
            mask *= 2
    return values


def sum_over_head(values):
    mask = 1
    while mask < lax.axis_size("head"):
        values = values + swap(values, "head", mask)
        mask *= 2
    return values


def all_quarters(own, other):
    pair = jnp.stack([own, other])
    four = jnp.concatenate([pair, swap_core(pair)])
    head = lax.axis_index("head")
    places = (0, 2, 1, 3)
    table = jnp.array(places, jnp.int32)
    return [at(four, table[head ^ index]) for index in range(4)]


def normalize(values):
    centred = values - jnp.mean(values, -1, keepdims=True)
    scale = lax.rsqrt(jnp.mean(centred * centred, -1, keepdims=True) + 1e-06)
    return centred * scale, scale


def normalize_back(grad, unit, scale, gain):
    grad_unit = grad * gain
    return scale * (
        grad_unit
        - jnp.mean(grad_unit, -1, keepdims=True)
        - unit * jnp.mean(grad_unit * unit, -1, keepdims=True)
    )


def attend(packed, length):
    tokens = packed.shape[0]
    queries, keys, values = packed[:, :, 0], packed[:, :, 1], packed[:, :, 2]
    scores = jnp.einsum("qhd,khd->hqk", queries, keys, preferred_element_type=F32)
    scores = scores * HD ** (-0.5)
    scores = jnp.where(jnp.arange(tokens) < length, scores, -1e30)
    top = jnp.max(scores, -1, keepdims=True)
    log_total = top + jnp.log(jnp.sum(jnp.exp(scores - top), -1, keepdims=True))
    soft = jnp.exp(scores - log_total).astype(BF)
    blended = jnp.einsum("hqk,khd->qhd", soft, values, preferred_element_type=F32)
    return blended.astype(BF), log_total, soft


def attend_back(packed, length, log_total, soft, grad):
    tokens = packed.shape[0]
    queries, keys, values = packed[:, :, 0], packed[:, :, 1], packed[:, :, 2]
    scale = HD ** (-0.5)
    grad_values = jnp.einsum("hqk,qhd->khd", soft, grad, preferred_element_type=F32)
    grad_soft = jnp.einsum("qhd,khd->hqk", grad, values, preferred_element_type=F32)
    scores = jnp.einsum("qhd,khd->hqk", queries, keys, preferred_element_type=F32) * scale
    scores = jnp.where(jnp.arange(tokens) < length, scores, -1e30)
    probs = jnp.exp(scores - log_total)
    grad_scores = probs * (grad_soft - jnp.sum(probs * grad_soft, -1, keepdims=True))
    grad_scores = grad_scores.astype(BF)
    grad_queries = (
        jnp.einsum("hqk,khd->qhd", grad_scores, keys, preferred_element_type=F32) * scale
    )
    grad_keys = (
        jnp.einsum("hqk,qhd->khd", grad_scores, queries, preferred_element_type=F32) * scale
    )
    return jnp.stack([grad_queries, grad_keys, grad_values], 2).astype(BF)


def adam_update(weight, gradient, first, second, rate, decay):
    first = BETA_FIRST * first + (1.0 - BETA_FIRST) * gradient
    second = BETA_SECOND * second + (1.0 - BETA_SECOND) * gradient * gradient
    direction = (
        first
        / (1.0 - BETA_FIRST**STEP)
        / (jnp.sqrt(second / (1.0 - BETA_SECOND**STEP)) + ADAM_FLOOR)
    )
    return (weight - rate * (direction + decay * weight), first, second)


def gram_blocks(matrix):
    step = D // 3
    rows = [matrix[index * step : (index + 1) * step] for index in range(3)]
    top = dot(rows[0], matrix, 1, 1)
    middle = dot(rows[1], matrix[step:], 1, 1)
    last = dot(rows[2], rows[2], 1, 1)
    return jnp.stack(
        [
            top[:, :step],
            top[:, step : 2 * step],
            top[:, 2 * step :],
            middle[:, :step],
            middle[:, step:],
            last,
        ]
    )


def whole_gram(blocks):
    aa, ab, ac, bb, bc, cc = [blocks[index] for index in range(6)]
    return jnp.concatenate(
        [
            jnp.concatenate([aa, ab, ac], 1),
            jnp.concatenate([ab.T, bb, bc], 1),
            jnp.concatenate([ac.T, bc.T, cc], 1),
        ],
        0,
    )


def body(
    low_patches,
    high_patches,
    interp,
    labels,
    partner,
    pair_count,
    w_patch,
    pos_table,
    vectors,
    head_w,
    w_qkv,
    w_out,
    w_up,
    w_down,
    mom_qkv,
    mom_out,
    mom_up,
    mom_down,
    first_patch,
    second_patch,
    first_pos,
    second_pos,
    first_vec,
    second_vec,
    first_head,
    second_head,
):
    batch = lax.axis_index("batch")
    head = lax.axis_index("head")
    side = head // 2
    batch_size = lax.axis_size("batch")
    head_size = lax.axis_size("head")
    rows_here = w_patch.shape[0]
    grid_low, grid_high = low_patches.shape[1], high_patches.shape[1]
    low_rows = up_to(grid_low + 1, 16)
    high_rows = up_to(grid_high + 1, 16)
    tokens = low_rows + high_rows
    qkv_width, out_width = w_qkv.shape[1], w_out.shape[1]
    hidden = w_up.shape[1]
    patch_width = D // head_size
    extra_width = 64
    head_columns = head_w.shape[1]
    head_padded = up_to(head_columns, 64 * head_size)
    head_width = head_padded // head_size
    table_rows = extra_width * head_size

    table = jnp.concatenate([pos_table[1:], pos_table[:1], vectors], 0).astype(BF)
    table = jnp.pad(table, ((0, table_rows - table.shape[0]), (0, 0))).T
    quarter_patch = lax.dynamic_slice_in_dim(w_patch, head * patch_width, patch_width, 1)
    quarter_table = lax.dynamic_slice_in_dim(table, head * extra_width, extra_width, 1)
    padded_head = jnp.pad(head_w.astype(BF), ((0, 0), (0, head_padded - head_columns)))
    quarter_head = lax.dynamic_slice_in_dim(padded_head, head * head_width, head_width, 1)
    chunk_one = jnp.concatenate(
        [quarter_patch.astype(BF), quarter_table, w_qkv.astype(BF), w_out.astype(BF)], 1
    )
    chunk_two = w_up.astype(BF)
    chunk_three = jnp.concatenate([w_down.astype(BF), quarter_head], 1)
    one = gather_rows(chunk_one)
    two = gather_rows(chunk_two)
    three = gather_rows(chunk_three)
    small = patch_width + extra_width
    quarters = all_quarters(one[0][:, :small], one[1][:, :small])
    full_patch = jnp.concatenate([quarter[:, :patch_width] for quarter in quarters], 1)
    table = jnp.concatenate([quarter[:, patch_width:] for quarter in quarters], 1).T
    full_qkv = jnp.concatenate([part[:, small : small + qkv_width] for part in one], 1)
    full_out = jnp.concatenate([part[:, small + qkv_width :] for part in one], 1)
    full_up = jnp.concatenate(two, 1)
    full_down = jnp.concatenate([part[:, :hidden] for part in three], 1)
    quarters = all_quarters(three[0][:, hidden:], three[1][:, hidden:])
    full_head = jnp.concatenate(quarters, 1)[:, :head_columns]

    class_row = grid_low
    vec = table[grid_low + 1 : grid_low + 11].astype(F32)
    pos_low = table[:low_rows].astype(F32)
    pos_high = dot(interp, table[:grid_low])
    row_low = jnp.arange(low_rows)[:, None]
    row_high = jnp.arange(high_rows)[:, None]
    class_add = table[class_row].astype(F32) + vec[9]
    add_low = jnp.where(
        row_low < grid_low, pos_low + vec[6], jnp.where(row_low == grid_low, class_add, 0.0)
    )
    pos_high = jnp.pad(pos_high, ((0, high_rows - grid_high), (0, 0)))
    add_high = jnp.where(
        row_high < grid_high, pos_high + vec[6], jnp.where(row_high == grid_high, class_add, 0.0)
    )
    added = jnp.concatenate([add_low, add_high], 0)
    is_patch = jnp.concatenate([row_low < grid_low, row_high < grid_high], 0)
    is_token = jnp.concatenate([row_low <= grid_low, row_high <= grid_high], 0)
    patches = jnp.concatenate(
        [
            jnp.pad(at(low_patches, side), ((0, low_rows - grid_low), (0, 0))),
            jnp.pad(at(high_patches, side), ((0, high_rows - grid_high), (0, 0))),
        ],
        0,
    )
    initial = dot(patches, full_patch) + added
    unit_one, scale_one = normalize(initial)
    normed = (unit_one * vec[0] + vec[1]).astype(BF)
    group_heads = 2 * qkv_width // (3 * HD)
    packed = dot(normed, full_qkv).astype(BF).reshape(tokens, group_heads, 3, HD)
    blend_low, logs_low, soft_low = attend(packed[:low_rows], grid_low + 1)
    blend_high, logs_high, soft_high = attend(packed[low_rows:], grid_high + 1)
    blended = jnp.concatenate([blend_low, blend_high], 0).reshape(tokens, group_heads * HD)
    middle = initial + vec[7] + pair_sum(dot(blended, full_out, 1, 1))
    unit_two, scale_two = normalize(middle)
    normed_two = (unit_two * vec[2] + vec[3]).astype(BF)
    upward = dot(normed_two, full_up)
    cumulative = 0.5 * (1.0 + lax.erf(upward * (0.5**0.5)))
    active = (upward * cumulative).astype(BF).astype(F32)
    slope = cumulative + upward * jnp.exp(-0.5 * upward * upward) * (2.0 * math.pi) ** (-0.5)

    def per_image(values):
        values = jnp.where(is_token, values, 0.0)
        return jnp.stack([jnp.sum(values[:low_rows], 0), jnp.sum(values[low_rows:], 0)])

    lengths = jnp.array([[grid_low + 1.0], [grid_high + 1.0]], F32)
    active_sums = per_image(active)
    active_means = active_sums / lengths
    means_high = active_means.astype(BF)
    means_low = (active_means - means_high.astype(F32)).astype(BF)
    down_parts = dot(jnp.concatenate([means_high, means_low]), full_down, 1, 1)
    down_part = down_parts[:2] + down_parts[2:]
    down_part = down_part + swap_core(down_part)
    pooled_own = per_image(middle) / lengths + vec[8] + down_part

    ids = jnp.stack([side, low_patches.shape[0] + side])
    tags = jnp.stack([labels[ids], partner[ids]], 1).astype(F32)
    sent = jnp.concatenate([pooled_own, jnp.pad(tags, ((0, 0), (0, 126)))], 1)
    both_sides = in_order(jnp.stack([sent, swap_side(sent)]), side, 1)
    everyone = gather_small(both_sides.transpose(1, 0, 2))
    images = batch_size * 4
    everyone = everyone.reshape(images, D + 128)
    pooled = everyone[:, :D]
    all_labels = everyone[:, D].astype(jnp.int32)
    all_partners = everyone[:, D + 1].astype(jnp.int32)
    unit_final, scale_final = normalize(pooled)
    features = (unit_final * vec[4] + vec[5]).astype(BF)
    outputs = dot(features, full_head)
    logits, projected = outputs[:, :CLS], outputs[:, CLS:]
    picked = jnp.arange(CLS)[None, :] == all_labels[:, None]
    logit_top = jnp.max(logits, -1, keepdims=True)
    logit_log = logit_top + jnp.log(jnp.sum(jnp.exp(logits - logit_top), -1, keepdims=True))
    class_total = jnp.sum(logit_log[:, 0] - jnp.sum(jnp.where(picked, logits, 0.0), -1))
    grad_logits = (jnp.exp(logits - logit_log) - picked.astype(F32)) * (1.0 / images)
    length_inverse = lax.rsqrt(jnp.sum(projected * projected, -1, keepdims=True) + 1e-06)
    embedded = (projected * length_inverse).astype(BF)
    similar = dot(embedded, embedded, 1, 1) / SOFTMAX_TEMP
    image_ids = jnp.arange(images, dtype=jnp.int32)
    masked = jnp.where(image_ids[:, None] == image_ids[None, :], -1e30, similar)
    similar_top = jnp.max(masked, -1, keepdims=True)
    similar_log = similar_top + jnp.log(jnp.sum(jnp.exp(masked - similar_top), -1, keepdims=True))
    target = image_ids[None, :] == all_partners[:, None]
    pair_total = jnp.sum(similar_log[:, 0] - jnp.sum(jnp.where(target, similar, 0.0), -1))
    count = pair_count[0].astype(F32)
    grad_similar = ((jnp.exp(masked - similar_log) - target.astype(F32)) / count).astype(BF)
    grad_embedded = (dot(grad_similar, embedded) + dot(grad_similar, embedded, 0, 0)) / SOFTMAX_TEMP
    grad_embedded = grad_embedded.astype(BF).astype(F32)
    grad_projected = length_inverse * grad_embedded - projected * (
        length_inverse**3 * jnp.sum(grad_embedded * projected, -1, keepdims=True)
    )
    grad_outputs = jnp.concatenate([grad_logits, grad_projected], 1).astype(BF)
    features_here = lax.dynamic_slice_in_dim(features, batch * rows_here, rows_here, 1)
    grad_head = dot(features_here, grad_outputs, 0, 0)
    grad_features = dot(grad_outputs, full_head, 1, 1)
    grad_pooled = normalize_back(grad_features, unit_final, scale_final, vec[4])
    complete_rows = jnp.stack(
        [
            jnp.sum(grad_features * unit_final, 0),
            jnp.sum(grad_features, 0),
            jnp.sum(grad_pooled, 0),
        ]
    )
    is_low = (image_ids % 4) < 2
    grad_token = grad_pooled / jnp.where(is_low, grid_low + 1.0, grid_high + 1.0)[:, None]
    own_rows = [batch * 4 + side, batch * 4 + 2 + side]
    grad_own = jnp.stack([at(grad_token, index) for index in own_rows])
    grad_own_low = grad_own.astype(BF)

    def spread(pair, mask):
        rows = jnp.concatenate(
            [
                jnp.broadcast_to(pair[0], (low_rows, pair.shape[1])),
                jnp.broadcast_to(pair[1], (high_rows, pair.shape[1])),
            ],
            0,
        )
        return jnp.where(mask, rows, 0.0)

    grad_active = dot(grad_own_low, full_down)
    grad_upward = (spread(grad_active, is_token) * slope).astype(BF)
    grad_up = dot(normed_two, grad_upward, 0, 0)
    grad_normed_two = pair_sum(dot(grad_upward, full_up, 1, 1))
    gain_two = jnp.sum(grad_normed_two * unit_two, 0)
    shift_two = jnp.sum(grad_normed_two, 0)
    grad_middle = normalize_back(grad_normed_two, unit_two, scale_two, vec[2])
    grad_middle = grad_middle + spread(grad_own, is_token)
    grad_middle_low = grad_middle.astype(BF)
    grad_out = dot(grad_middle_low, blended, 0, 0)
    grad_blend = dot(grad_middle_low, full_out).astype(BF).reshape(tokens, group_heads, HD)
    grad_packed = jnp.concatenate(
        [
            attend_back(packed[:low_rows], grid_low + 1, logs_low, soft_low, grad_blend[:low_rows]),
            attend_back(
                packed[low_rows:], grid_high + 1, logs_high, soft_high, grad_blend[low_rows:]
            ),
        ],
        0,
    ).reshape(tokens, 2 * qkv_width)
    grad_qkv = dot(normed, grad_packed, 0, 0)
    grad_normed = pair_sum(dot(grad_packed, full_qkv, 1, 1))
    gain_one = jnp.sum(grad_normed * unit_one, 0)
    shift_one = jnp.sum(grad_normed, 0)
    grad_initial = normalize_back(grad_normed, unit_one, scale_one, vec[0]) + grad_middle
    grad_embed = jnp.where(is_patch, grad_initial, 0.0)
    grad_embed_low = grad_embed.astype(BF)
    initial_low = grad_initial.astype(BF)
    grad_low_tokens = grad_initial[: grid_low + 1]
    from_high = dot(interp, initial_low[low_rows : low_rows + grid_high], 0, 0)
    class_high = grad_initial[low_rows + grid_high][None]
    zero_row = jnp.zeros((1, D), F32)
    class_both = grad_low_tokens[grid_low:] + class_high
    table_grad = jnp.concatenate(
        [
            grad_low_tokens[:grid_low] + from_high,
            class_both,
            gain_one[None],
            shift_one[None],
            gain_two[None],
            shift_two[None],
            zero_row,
            zero_row,
            jnp.sum(grad_embed, 0)[None],
            jnp.sum(grad_middle, 0)[None],
            zero_row,
            class_both,
            jnp.zeros((table_rows - grid_low - 11, D), F32),
        ],
        0,
    ).T

    def quarter_grads(index):
        columns = lax.dynamic_slice_in_dim(grad_embed_low, index * patch_width, patch_width, 1)
        return [
            dot(patches, columns, 0, 0),
            lax.dynamic_slice_in_dim(table_grad, index * extra_width, extra_width, 1),
        ]

    def group(values, width, index):
        return values[:, index * width : (index + 1) * width]

    reduced_up = reduce_rows(group(grad_up, hidden, 0), group(grad_up, hidden, 1))
    tails = [
        jnp.concatenate(
            [
                group(grad_qkv, qkv_width, index),
                group(grad_out, out_width, index),
            ]
            + quarter_grads(owner),
            1,
        )
        for index, owner in ((0, head), (1, head ^ 2))
    ]
    reduced_tail = reduce_rows(tails[0], tails[1])
    own_width = qkv_width + out_width
    reduced_qkv = reduced_tail[:, :qkv_width]
    reduced_out = reduced_tail[:, qkv_width:own_width]
    quarter = reduced_tail[:, own_width:].astype(BF)
    quarters = all_quarters(quarter, swap_side(quarter))
    reduced_patch = jnp.concatenate([part[:, :patch_width] for part in quarters], 1).astype(F32)
    reduced_table = (
        jnp.concatenate([part[:, patch_width:] for part in quarters], 1).T.astype(F32)
    )
    reduced_pos = jnp.concatenate(
        [reduced_table[grid_low : grid_low + 1], reduced_table[:grid_low]], 0
    )
    complete_here = lax.dynamic_slice_in_dim(complete_rows, batch * rows_here, rows_here, 1)
    partial_vec = reduced_table[grid_low + 1 : grid_low + 11]
    reduced_vec = jnp.concatenate(
        [partial_vec[:4], complete_here[:2], partial_vec[6:8], complete_here[2:], partial_vec[9:]],
        0,
    )
    side_sums = jnp.stack([active_sums[:, :hidden], swap_side(active_sums[:, hidden:])])
    all_sums = gather_small(in_order(side_sums, side, 1).transpose(1, 0, 2)).reshape(images, hidden)
    sums_high = all_sums.astype(BF)
    sums_low = (all_sums - sums_high.astype(F32)).astype(BF)
    grad_token_low = grad_token.astype(BF)
    full_grad_down = dot(
        jnp.concatenate([grad_token_low, grad_token_low]),
        jnp.concatenate([sums_high, sums_low]),
        0,
        0,
    )
    reduced_down = lax.dynamic_slice_in_dim(full_grad_down, batch * rows_here, rows_here, 0)

    muon_grads = (reduced_qkv, reduced_out, reduced_up, reduced_down)
    adam_grads = (reduced_patch, reduced_pos, reduced_vec, grad_head)
    squares = sum(jnp.sum(gradient * gradient) for gradient in muon_grads)
    squares = squares + sum(jnp.sum(gradient * gradient) for gradient in adam_grads) / head_size
    norm = jnp.sqrt(sum_everywhere(jnp.broadcast_to(squares, (8, 128)))[0, 0])
    factor = jnp.minimum(1.0, CLIP_NORM / norm)
    losses = jnp.stack([pair_total, class_total])
    adam_weights = (w_patch, pos_table, vectors, head_w)
    firsts = (first_patch, first_pos, first_vec, first_head)
    seconds = (second_patch, second_pos, second_vec, second_head)
    adam_new = [
        adam_update(
            adam_weights[index],
            factor * adam_grads[index],
            firsts[index],
            seconds[index],
            ADAM_RATES[index],
            ADAM_DECAYS[index],
        )
        for index in range(4)
    ]

    old_moments = (mom_qkv, mom_out, mom_up, mom_down)
    old_weights = (w_qkv, w_out, w_up, w_down)
    moments = [MOMENTUM * old_moments[index] + factor * muon_grads[index] for index in range(4)]
    held = jnp.concatenate(old_moments, 1).astype(BF)
    held, _ = lax.optimization_barrier((held, full_up))
    full_old = lax.all_gather(held, "batch", axis=0, tiled=True)
    sent = jnp.concatenate([reduced_qkv, reduced_out, reduced_up], 1).astype(BF)
    full_grads = lax.all_gather(sent, "batch", axis=0, tiled=True)
    starts = (0, qkv_width, own_width, own_width + hidden, own_width + 2 * hidden)
    full_moments = []
    for index in range(4):
        low, top = starts[index], starts[index + 1]
        gradient = full_grad_down if index == 3 else full_grads[:, low:top].astype(F32)
        full_moments.append(
            (MOMENTUM * full_old[:, low:top].astype(F32) + factor * gradient)
        )
    own_squares = jnp.stack([jnp.sum(moment * moment) for moment in full_moments])
    totals = sum_over_head(jnp.broadcast_to(own_squares[:, None], (4, 128)))[:, 0]
    moment_logs = jnp.log(totals)
    inverse = 1.0 / (jnp.sqrt(totals) + 1e-07)
    full_moments = [moment.astype(BF) for moment in full_moments]
    blocks = jnp.stack([gram_blocks(moment) for moment in full_moments])
    kept = jnp.stack([at(blocks, head), at(blocks, head ^ 2)])
    given = jnp.stack([at(blocks, head ^ 1), at(blocks, head ^ 3)])
    kept = kept + swap_core(given.astype(BF)).astype(F32)
    mine = kept[0] + swap_side(kept[1].astype(BF)).astype(F32)
    inverse_here = at(inverse, head)
    gram = whole_gram(mine * (inverse_here * inverse_here))
    row_start = batch * rows_here

    def fine(left, right):
        return jnp.dot(left, right, precision=lax.Precision.HIGH)

    eye = jnp.eye(D, dtype=F32)
    polynomials = []
    for sweep in range(NS_STEPS):
        last = sweep == NS_STEPS - 1
        if last:
            gram_rows = lax.dynamic_slice_in_dim(gram, row_start, rows_here, 0)
            eye_rows = lax.dynamic_slice_in_dim(eye, row_start, rows_here, 0)
            rows = (
                POLY_ONE * eye_rows + POLY_TWO * gram_rows + POLY_THREE * fine(gram_rows, gram)
            )
        else:
            factor_here = POLY_ONE * eye + POLY_TWO * gram + POLY_THREE * fine(gram, gram)
            polynomials.append(factor_here)
            gram = fine(fine(gram, factor_here), factor_here)
    for polynomial in polynomials[::-1]:
        rows = fine(rows, polynomial)
    rows = rows.astype(BF)
    pair = jnp.stack([rows, swap_side(rows)])
    four = jnp.concatenate([pair, swap_core(pair)])
    order = jnp.array((0, 2, 1, 3), jnp.int32)
    new_muon = []
    for index in range(4):
        weight = old_weights[index]
        scale = 0.2 * math.sqrt(max(D, weight.shape[1] * head_size))
        iterate = dot(at(four, order[head ^ index]), full_moments[index]) * inverse[index]
        new_muon.append(weight - MUON_RATE * (scale * iterate + DECAY_RATE * weight))
    return (
        adam_new[0][0],
        adam_new[1][0],
        adam_new[2][0],
        adam_new[3][0],
        new_muon[0],
        new_muon[1],
        new_muon[2],
        new_muon[3],
        moments[0],
        moments[1],
        moments[2],
        moments[3],
        adam_new[0][1],
        adam_new[1][1],
        adam_new[2][1],
        adam_new[3][1],
        adam_new[0][2],
        adam_new[1][2],
        adam_new[2][2],
        adam_new[3][2],
        losses,
        norm[None],
        moment_logs,
    )


def solution(mesh):
    placed = (
        P("batch", None, None),
        P("batch", None, None),
        P(),
        P("batch"),
        P("batch"),
        P(),
        P("batch", None),
        P(None, "batch"),
        P(None, "batch"),
        P("batch", None),
        P("batch", "head"),
        P("batch", "head"),
        P("batch", "head"),
        P("batch", "head"),
        P("batch", "head"),
        P("batch", "head"),
        P("batch", "head"),
        P("batch", "head"),
        P("batch", None),
        P("batch", None),
        P(None, "batch"),
        P(None, "batch"),
        P(None, "batch"),
        P(None, "batch"),
        P("batch", None),
        P("batch", None),
    )
    return jax.shard_map(
        body,
        mesh=mesh,
        in_specs=placed,
        out_specs=(
            P("batch", None),
            P(None, "batch"),
            P(None, "batch"),
            P("batch", None),
            P("batch", "head"),
            P("batch", "head"),
            P("batch", "head"),
            P("batch", "head"),
            P("batch", "head"),
            P("batch", "head"),
            P("batch", "head"),
            P("batch", "head"),
            P("batch", None),
            P(None, "batch"),
            P(None, "batch"),
            P("batch", None),
            P("batch", None),
            P(None, "batch"),
            P(None, "batch"),
            P("batch", None),
            P(),
            P(),
            P(),
        ),
        check_vma=False,
    )
```

time: 2250 us -> 662 us (0.29)
  waiting for transfers between devices: 1400 us -> 183 us
  blocking collectives: 467 us -> 0 us
  local copies, waits for them, and re-layouts: 66.1 us -> 170 us
  matrix products: 170 us -> 92.5 us
  starting transfers between devices: 2.65 us -> 69.8 us
    all_gather x22 -> x2, waiting for transfers between devices: 602 us -> 74.7 us  [the longest x1 66.5 us: body(): full_old = lax.all_gather(held, 'batch', axis=0, tiled=True)]
    reduce_scatter x6 -> x0, waiting for transfers between devices: 358 us -> none  [the longest x1 83.8 us: body(): lax.psum_scatter(grad_head, 'batch', scatter_dimension=0, tiled=True)]
    all_gather x11 -> x0, blocking collectives: 351 us -> none  [the longest x3 101 us: body(): lax.all_gather(for_sending(iterates[0]), 'batch', axis=0, tiled=True)]
    psum x7 -> x0, waiting for transfers between devices: 305 us -> none  [the longest x3 100 us: body(): lax.psum(pieces[0].astype(jnp.bfloat16), 'head').astype(jnp.float32)]
    unnamed x39 -> x2, waiting for transfers between devices: 130 us -> 0.03 us
    ppermute x0 -> x64, waiting for transfers between devices: none -> 108 us  [swap(): lax.ppermute(values, axis, [(index, index ^ mask) for index in range(coun...]
    psum x2 -> x0, blocking collectives: 81 us -> none  [the longest x1 40.6 us: body(): lax.psum((squares[0], squares[1], squares[2], squares[3]), ('batch', 'hea...]
    dot_general x84 -> x60, matrix products: 170 us -> 92.5 us  [the longest x39 45.9 us: dot(): lax.dot_general(left, right, (((left_dim,), (right_dim,)), ((), ())), pre...]
  transfers between devices with their start and end apart: 37 -> 66, of which waited for: 34 -> 25; matrix products, arithmetic and copies ran while one was open for 9% -> 38% of each run, Pallas kernels for 0% -> 0%
where the time goes in v1:
time: 662 us; the launch traced here: 652 us
  waiting for transfers between devices  183 us (28%)
  local copies, waits for them, and re-layouts  170 us (26%)
  other arithmetic  102 us (15%)
  matrix products  92.5 us (14%)
  starting transfers between devices  69.8 us (11%)
  between operations  35.1 us (5%)
    ppermute x64, waiting for transfers between devices, swap(): lax.ppermute(values, axis, [(index, index ^ mask) for index in range(coun...  108 us
    unnamed x438, local copies, waits for them, and re-layouts  76.5 us
    ppermute x64, starting transfers between devices, swap(): lax.ppermute(values, axis, [(index, index ^ mask) for index in range(coun...  69.6 us
    all_gather x1, waiting for transfers between devices, body(): full_old = lax.all_gather(held, 'batch', axis=0, tiled=True)  66.5 us
    dot_general x39, matrix products, dot(): lax.dot_general(left, right, (((left_dim,), (right_dim,)), ((), ())), pre...  45.9 us
    dynamic_slice x41, local copies, waits for them, and re-layouts, at(): return lax.dynamic_index_in_dim(stacked, index, 0, keepdims=False)  32.8 us
    dot_general x9, matrix products, fine(): return jnp.dot(left, right, precision=lax.Precision.HIGH)  26.2 us
    concatenate x5, local copies, waits for them, and re-layouts, gather_rows(): groups.append(jnp.concatenate(pieces, 0))  21.8 us
  transfers between devices with their start and end apart: 66, of which 25 were waited for; matrix products, arithmetic and copies ran while one was open for 38% of the time, Pallas kernels for 0%

profile of v1, /device:TPU:0, one launch (start us, length us, event | category | flops | bytes accessed | tf_op | source)
XLA Modules:
  0.0 651.5 jit_solution(13792345455427160131)
XLA Ops:
  13.1 5.0 collective-permute-start.2
  47.9 2.5 collective-permute-start.18
  60.1 7.5 %collective-permute-done.17 = bf16[96,1088]{1,0:T(8,128)(2,1)S(1)} collective-permute-done((bf16[96,1088]{1,0:T(8,128)(2,1)}, bf16[96,1088]{1,0:T(8,128)(2,1)S(1)}, u32[]{:S(2)}, u32[]{:S(2)}) %collective-permute-start.17) | collective-permute-done | bytes 208928 | tf_op jit(solution)/shard_map/ppermute | solution.py:52
  74.6 5.0 collective-permute-done.3
  109.3 2.3 fusion.272
  142.0 5.2 concatenate.180
  155.8 4.6 concatenate.179
  186.0 5.7 concatenate.195
  191.7 5.4 concatenate.194
  217.1 2.6 fusion.7
  234.4 2.9 copy-done.7
  239.5 4.6 convert_select_fusion
  256.3 2.8 collective-permute-start.26
  272.8 3.7 fusion.6
  276.6 3.1 convolution_convert_fusion.3
  279.7 3.0 fusion.276
  289.7 12.4 %collective-permute-done.47 = f32[2,2,768]{2,1,0:T(2,128)S(1)} collective-permute-done((f32[2,2,768]{2,1,0:T(2,128)S(1)}, f32[2,2,768]{2,1,0:T(2,128)S(1)}, u32[]{:S(2)}, u32[]{:S(2)}) %collective-permute-start.47) | collective-permute-done | bytes 12320 | tf_op jit(solution)/shard_map/ppermute | solution.py:52
  313.9 3.5 multiply_reduce_fusion.1
  317.7 3.4 fusion.289
  326.4 4.7 fusion.39
  331.1 5.6 multiply_reduce_fusion
  336.7 3.0 multiply_convert_fusion
  352.7 3.1 fusion.32
  355.8 2.5 fusion.293
  360.4 2.6 select_convert_fusion
  368.6 2.3 fusion.105
  378.8 19.1 %collective-permute-done.40 = bf16[4,48,768]{2,1,0:T(8,128)(2,1)S(1)} collective-permute-done((bf16[4,48,768]{2,1,0:T(8,128)(2,1)S(1)}, bf16[4,48,768]{2,1,0:T(8,128)(2,1)S(1)}, u32[]{:S(2)}, u32[]{:S(2)}) %collective-permute-start.40) | collective-permute-done | bytes 294944 | tf_op jit(solution)/shard_map/ppermute | solution.py:52
  405.1 3.5 collective-permute-done.35
  414.8 10.2 %collective-permute-done.44 = bf16[96,768]{1,0:T(8,128)(2,1)S(1)} collective-permute-done((bf16[96,768]{1,0:T(8,128)(2,1)S(1)}, bf16[96,768]{1,0:T(8,128)(2,1)S(1)}, u32[]{:S(2)}, u32[]{:S(2)}) %collective-permute-start.44) | collective-permute-done | bytes 147488 | tf_op jit(solution)/shard_map/ppermute | solution.py:52
  425.1 6.7 %collective-permute-done.37 = bf16[96,1024]{1,0:T(8,128)(2,1)S(1)} collective-permute-done((bf16[96,1024]{1,0:T(8,128)(2,1)S(1)}, bf16[96,1024]{1,0:T(8,128)(2,1)S(1)}, u32[]{:S(2)}, u32[]{:S(2)}) %collective-permute-start.37) | collective-permute-done | bytes 196640 | tf_op jit(solution)/shard_map/ppermute | solution.py:52
  435.9 2.4 multiply_reduce_fusion.12
  440.3 2.8 collective-permute-done.51
  454.3 3.0 collective-permute-done.54
  460.8 3.8 collective-permute-done.56
  465.0 4.3 collective-permute-done.57
  475.4 8.2 %all-gather.5.cloned.1.call-done = bf16[768,1536]{1,0:T(8,128)(2,1)} async-done(((bf16[96,1536]{1,0:T(8,128)(2,1)}), bf16[768,1536]{1,0:T(8,128)(2,1)}) %all-gather.5.cloned.1.call-update) | async-done | bytes 2359312 | tf_op jit(solution)/shard_map/all_gather | solution.py:587
  483.6 66.5 %all-gather.3.cloned.1.call-done = bf16[768,2304]{1,0:T(8,128)(2,1)} async-done(((bf16[96,2304]{1,0:T(8,128)(2,1)}), bf16[768,2304]{1,0:T(8,128)(2,1)}) %all-gather.3.cloned.1.call-update) | async-done | bytes 3538960 | tf_op jit(solution)/shard_map/all_gather | solution.py:585
  550.1 4.4 multiply_reduce_fusion.8
  559.8 2.3 multiply_reduce_fusion.9
  569.1 2.7 pad_maximum_fusion.61
  580.1 14.7 %collective-permute-done.59 = bf16[6,256,256]{2,1,0:T(8,128)(2,1)S(1)} collective-permute-done((bf16[6,256,256]{2,1,0:T(8,128)(2,1)S(1)}, bf16[6,256,256]{2,1,0:T(8,128)(2,1)S(1)}, u32[]{:S(2)}, u32[]{:S(2)}) %collective-permute-start.59) | collective-permute-done | bytes 786464 | tf_op jit(solution)/shard_map/ppermute | solution.py:52
  602.7 6.4 fusion.11
  609.1 3.2 fusion.101
  612.3 3.4 fusion.303
  615.8 3.3 fusion.12
  619.1 3.2 fusion.304
  622.2 3.2 fusion.305
  631.3 3.1 collective-permute-done.62
  (926 shorter events, 326.9 us)
Async XLA Ops:
  7.3 476.3 %all-gather.5.cloned.1.call-start = ((), (), s32[]{:S(2)}) async-start(), calls=%async_computation.1 | async-start | bytes 2654208 | tf_op jit(solution)/shard_map/all_gather | solution.py:587
  13.1 38.5 %collective-permute-start.2 = (bf16[96,1024]{1,0:T(8,128)(2,1)}, bf16[96,1024]{1,0:T(8,128)(2,1)}, u32[]{:S(2)}, u32[]{:S(2)}) collective-permute-start(bf16[96,1024]{1,0:T(8,128)(2,1)} %pad_maximum_fusion.46), channel_id=1, source_target_pairs={{0,24},{4,28},{8,16},{12,20},{16,8},{20,12},{24,0},{28,4},{1,25},{... | collective-permute-start | bytes 589832 | tf_op jit(solution)/shard_map/ppermute | solution.py:52
  18.1 35.4 %collective-permute-start.1 = (bf16[96,1024]{1,0:T(8,128)(2,1)}, bf16[96,1024]{1,0:T(8,128)(2,1)}, u32[]{:S(2)}, u32[]{:S(2)}) collective-permute-start(bf16[96,1024]{1,0:T(8,128)(2,1)} %pad_maximum_fusion.46), channel_id=1, source_target_pairs={{0,16},{4,20},{8,24},{12,28},{16,0},{20,4},{24,8},{28,12},{1,17},{... | collective-permute-start | bytes 589832 | tf_op jit(solution)/shard_map/ppermute | solution.py:52
  19.7 24.7 %collective-permute-start.11 = (bf16[96,768]{1,0:T(8,128)(2,1)}, bf16[96,768]{1,0:T(8,128)(2,1)}, u32[]{:S(2)}, u32[]{:S(2)}) collective-permute-start(bf16[96,768]{1,0:T(8,128)(2,1)} %convert_element_type.391), channel_id=1, source_target_pairs={{0,24},{4,28},{8,16},{12,20},{16,8},{20,12},{24,0},{28,4},{1,25},{... | collective-permute-start | bytes 442376 | tf_op jit(solution)/shard_map/ppermute | solution.py:52
  21.7 26.2 %collective-permute-start.10 = (bf16[96,768]{1,0:T(8,128)(2,1)}, bf16[96,768]{1,0:T(8,128)(2,1)}, u32[]{:S(2)}, u32[]{:S(2)}) collective-permute-start(bf16[96,768]{1,0:T(8,128)(2,1)} %convert_element_type.391), channel_id=1, source_target_pairs={{0,16},{4,20},{8,24},{12,28},{16,0},{20,4},{24,8},{28,12},{1,17},{... | collective-permute-start | bytes 442376 | tf_op jit(solution)/shard_map/ppermute | solution.py:52
  22.7 27.7 %collective-permute-start.9 = (bf16[96,768]{1,0:T(8,128)(2,1)}, bf16[96,768]{1,0:T(8,128)(2,1)}, u32[]{:S(2)}, u32[]{:S(2)}) collective-permute-start(bf16[96,768]{1,0:T(8,128)(2,1)} %convert_element_type.391), channel_id=1, source_target_pairs={{0,8},{4,12},{8,0},{12,4},{16,24},{20,28},{24,16},{28,20},{1,9},{5... | collective-permute-start | bytes 442376 | tf_op jit(solution)/shard_map/ppermute | solution.py:52
  44.5 10.5 %collective-permute-start = (bf16[96,1024]{1,0:T(8,128)(2,1)}, bf16[96,1024]{1,0:T(8,128)(2,1)S(1)}, u32[]{:S(2)}, u32[]{:S(2)}) collective-permute-start(bf16[96,1024]{1,0:T(8,128)(2,1)} %pad_maximum_fusion.46), channel_id=1, source_target_pairs={{0,8},{4,12},{8,0},{12,4},{16,24},{20,28},{24,16},{28,20},{1,9},{5... | collective-permute-start | bytes 589832 | tf_op jit(solution)/shard_map/ppermute | solution.py:52
  47.9 10.9 %collective-permute-start.18 = (bf16[96,1088]{1,0:T(8,128)(2,1)}, bf16[96,1088]{1,0:T(8,128)(2,1)S(1)}, u32[]{:S(2)}, u32[]{:S(2)}) collective-permute-start(bf16[96,1088]{1,0:T(8,128)(2,1)} %get-tuple-element.279), channel_id=1, source_target_pairs={{0,24},{4,28},{8,16},{12,20},{16,8},{20,12},{24,0},{28,4},{1,25},{... | collective-permute-start | bytes 626696 | tf_op jit(solution)/shard_map/ppermute | solution.py:52
  50.3 17.2 %collective-permute-start.17 = (bf16[96,1088]{1,0:T(8,128)(2,1)}, bf16[96,1088]{1,0:T(8,128)(2,1)S(1)}, u32[]{:S(2)}, u32[]{:S(2)}) collective-permute-start(bf16[96,1088]{1,0:T(8,128)(2,1)} %get-tuple-element.279), channel_id=1, source_target_pairs={{0,16},{4,20},{8,24},{12,28},{16,0},{20,4},{24,8},{28,12},{1,17},{... | collective-permute-start | bytes 626696 | tf_op jit(solution)/shard_map/ppermute | solution.py:52
  51.6 17.5 %collective-permute-start.16 = (bf16[96,1088]{1,0:T(8,128)(2,1)}, bf16[96,1088]{1,0:T(8,128)(2,1)S(1)}, u32[]{:S(2)}, u32[]{:S(2)}) collective-permute-start(bf16[96,1088]{1,0:T(8,128)(2,1)} %get-tuple-element.279), channel_id=1, source_target_pairs={{0,8},{4,12},{8,0},{12,4},{16,24},{20,28},{24,16},{28,20},{1,9},{5... | collective-permute-start | bytes 626696 | tf_op jit(solution)/shard_map/ppermute | solution.py:52
  53.5 18.3 %collective-permute-start.12 = (bf16[4,48,768]{2,1,0:T(8,128)(2,1)S(1)}, bf16[4,48,768]{2,1,0:T(8,128)(2,1)S(1)}, u32[]{:S(2)}, u32[]{:S(2)}) collective-permute-start(bf16[4,48,768]{2,1,0:T(8,128)(2,1)S(1)} %get-tuple-element.271), channel_id=1, source_target_pairs={{0,4},{4,0},{8,12},{12,8},{16,20},{20,16},{24,28},{28,24},{1,5},{5... | collective-permute-start | bytes 884744 | tf_op jit(solution)/shard_map/ppermute | solution.py:52
  55.0 17.4 %collective-permute-start.13 = (bf16[4,48,768]{2,1,0:T(8,128)(2,1)S(1)}, bf16[4,48,768]{2,1,0:T(8,128)(2,1)S(1)}, u32[]{:S(2)}, u32[]{:S(2)}) collective-permute-start(bf16[4,48,768]{2,1,0:T(8,128)(2,1)S(1)} %get-tuple-element.270), channel_id=1, source_target_pairs={{0,2},{1,3},{2,0},{3,1},{4,6},{5,7},{6,4},{7,5},{8,10},{9,11},{10,... | collective-permute-start | bytes 884744 | tf_op jit(solution)/shard_map/ppermute | solution.py:52
  58.8 29.3 %collective-permute-start.4 = (bf16[4,48,1024]{2,1,0:T(8,128)(2,1)}, bf16[4,48,1024]{2,1,0:T(8,128)(2,1)}, u32[]{:S(2)}, u32[]{:S(2)}) collective-permute-start(bf16[4,48,1024]{2,1,0:T(8,128)(2,1)} %get-tuple-element.264), channel_id=1, source_target_pairs={{0,2},{1,3},{2,0},{3,1},{4,6},{5,7},{6,4},{7,5},{8,10},{9,11},{10,... | collective-permute-start | bytes 1179656 | tf_op jit(solution)/shard_map/ppermute | solution.py:52
  67.6 12.1 %collective-permute-start.3 = (bf16[4,48,1024]{2,1,0:T(8,128)(2,1)S(1)}, bf16[4,48,1024]{2,1,0:T(8,128)(2,1)S(1)}, u32[]{:S(2)}, u32[]{:S(2)}) collective-permute-start(bf16[4,48,1024]{2,1,0:T(8,128)(2,1)S(1)} %get-tuple-element.265), channel_id=1, source_target_pairs={{0,4},{4,0},{8,12},{12,8},{16,20},{20,16},{24,28},{28,24},{1,5},{5... | collective-permute-start | bytes 1179656 | tf_op jit(solution)/shard_map/ppermute | solution.py:52
  70.3 38.4 %collective-permute-start.20 = (bf16[4,48,1088]{2,1,0:T(8,128)(2,1)}, bf16[4,48,1088]{2,1,0:T(8,128)(2,1)}, u32[]{:S(2)}, u32[]{:S(2)}) collective-permute-start(bf16[4,48,1088]{2,1,0:T(8,128)(2,1)} %get-tuple-element.224), channel_id=1, source_target_pairs={{0,2},{1,3},{2,0},{3,1},{4,6},{5,7},{6,4},{7,5},{8,10},{9,11},{10,... | collective-permute-start | bytes 1253384 | tf_op jit(solution)/shard_map/ppermute | solution.py:52
  71.8 19.8 %collective-permute-start.19 = (bf16[4,48,1088]{2,1,0:T(8,128)(2,1)}, bf16[4,48,1088]{2,1,0:T(8,128)(2,1)}, u32[]{:S(2)}, u32[]{:S(2)}) collective-permute-start(bf16[4,48,1088]{2,1,0:T(8,128)(2,1)} %get-tuple-element.225), channel_id=1, source_target_pairs={{0,4},{4,0},{8,12},{12,8},{16,20},{20,16},{24,28},{28,24},{1,5},{5... | collective-permute-start | bytes 1253384 | tf_op jit(solution)/shard_map/ppermute | solution.py:52
  72.4 50.8 %collective-permute-start.15 = (bf16[2,4,48,768]{3,2,1,0:T(8,128)(2,1)S(1)}, bf16[2,4,48,768]{3,2,1,0:T(8,128)(2,1)}, u32[]{:S(2)}, u32[]{:S(2)}) collective-permute-start(bf16[2,4,48,768]{3,2,1,0:T(8,128)(2,1)S(1)} %pad_maximum_fusion.35), channel_id=1, source_target_pairs={{0,2},{1,3},{2,0},{3,1},{4,6},{5,7},{6,4},{7,5},{8,10},{9,11},{10,... | collective-permute-start | bytes 1769480 | tf_op jit(solution)/shard_map/ppermute | solution.py:52
  79.6 32.0 %collective-permute-start.14 = (bf16[2,4,48,768]{3,2,1,0:T(8,128)(2,1)}, bf16[2,4,48,768]{3,2,1,0:T(8,128)(2,1)}, u32[]{:S(2)}, u32[]{:S(2)}) collective-permute-start(bf16[2,4,48,768]{3,2,1,0:T(8,128)(2,1)} %get-tuple-element.267), channel_id=1, source_target_pairs={{0,4},{4,0},{8,12},{12,8},{16,20},{20,16},{24,28},{28,24},{1,5},{5... | collective-permute-start | bytes 1769480 | tf_op jit(solution)/shard_map/ppermute | solution.py:52
  88.1 41.0 %collective-permute-start.6 = (bf16[2,4,48,1024]{3,2,1,0:T(8,128)(2,1)S(1)}, bf16[2,4,48,1024]{3,2,1,0:T(8,128)(2,1)}, u32[]{:S(2)}, u32[]{:S(2)}) collective-permute-start(bf16[2,4,48,1024]{3,2,1,0:T(8,128)(2,1)S(1)} %pad_maximum_fusion.27), channel_id=1, source_target_pairs={{0,2},{1,3},{2,0},{3,1},{4,6},{5,7},{6,4},{7,5},{8,10},{9,11},{10,... | collective-permute-start | bytes 2359304 | tf_op jit(solution)/shard_map/ppermute | solution.py:52
  91.7 35.2 %collective-permute-start.5 = (bf16[2,4,48,1024]{3,2,1,0:T(8,128)(2,1)}, bf16[2,4,48,1024]{3,2,1,0:T(8,128)(2,1)}, u32[]{:S(2)}, u32[]{:S(2)}) collective-permute-start(bf16[2,4,48,1024]{3,2,1,0:T(8,128)(2,1)} %get-tuple-element.261), channel_id=1, source_target_pairs={{0,4},{4,0},{8,12},{12,8},{16,20},{20,16},{24,28},{28,24},{1,5},{5... | collective-permute-start | bytes 2359304 | tf_op jit(solution)/shard_map/ppermute | solution.py:52
  108.7 56.0 %collective-permute-start.22 = (bf16[2,4,48,1088]{3,2,1,0:T(8,128)(2,1)}, bf16[2,4,48,1088]{3,2,1,0:T(8,128)(2,1)}, u32[]{:S(2)}, u32[]{:S(2)}) collective-permute-start(bf16[2,4,48,1088]{3,2,1,0:T(8,128)(2,1)} %pad_maximum_fusion.23), channel_id=1, source_target_pairs={{0,2},{1,3},{2,0},{3,1},{4,6},{5,7},{6,4},{7,5},{8,10},{9,11},{10,... | collective-permute-start | bytes 2506760 | tf_op jit(solution)/shard_map/ppermute | solution.py:52
  111.6 51.7 %collective-permute-start.21 = (bf16[2,4,48,1088]{3,2,1,0:T(8,128)(2,1)}, bf16[2,4,48,1088]{3,2,1,0:T(8,128)(2,1)}, u32[]{:S(2)}, u32[]{:S(2)}) collective-permute-start(bf16[2,4,48,1088]{3,2,1,0:T(8,128)(2,1)} %get-tuple-element.221), channel_id=1, source_target_pairs={{0,4},{4,0},{8,12},{12,8},{16,20},{20,16},{24,28},{28,24},{1,5},{5... | collective-permute-start | bytes 2506760 | tf_op jit(solution)/shard_map/ppermute | solution.py:52
  163.3 35.5 %collective-permute-start.7 = (bf16[2,768,256]{1,2,0:T(8,128)(2,1)}, bf16[2,768,256]{1,2,0:T(8,128)(2,1)}, u32[]{:S(2)}, u32[]{:S(2)}) collective-permute-start(bf16[2,768,256]{1,2,0:T(8,128)(2,1)} %pad_maximum_fusion.29), channel_id=1, source_target_pairs={{0,1},{1,0},{2,3},{3,2},{4,5},{5,4},{6,7},{7,6},{8,9},{9,8},{10,11... | collective-permute-start | bytes 2359304 | tf_op jit(solution)/shard_map/ppermute | solution.py:52
  254.7 6.5 %collective-permute-start.28 = (f32[2,2,2,896]{3,1,2,0:T(2,128)S(1)}, f32[2,2,2,896]{3,1,2,0:T(2,128)S(1)}, u32[]{:S(2)}, u32[]{:S(2)}) collective-permute-start(f32[2,2,2,896]{3,1,2,0:T(2,128)S(1)} %get-tuple-element.295), channel_id=1, source_target_pairs={{0,24},{4,28},{8,16},{12,20},{16,8},{20,12},{24,0},{28,4},{1,25},{... | collective-permute-start | bytes 86024 | tf_op jit(solution)/shard_map/ppermute | solution.py:52
  259.7 26.8 %collective-permute-start.46 = (f32[2,768]{1,0:T(2,128)}, f32[2,768]{1,0:T(2,128)}, u32[]{:S(2)}, u32[]{:S(2)}) collective-permute-start(f32[2,768]{1,0:T(2,128)} %get-tuple-element.303), channel_id=1, source_target_pairs={{0,2},{1,3},{2,0},{3,1},{4,6},{5,7},{6,4},{7,5},{8,10},{9,11},{10,... | collective-permute-start | bytes 18440 | tf_op jit(solution)/shard_map/ppermute | solution.py:52
  282.7 31.3 %collective-permute-start.30 = (bf16[800,768]{1,0:T(8,128)(2,1)}, bf16[800,768]{1,0:T(8,128)(2,1)}, u32[]{:S(2)}, u32[]{:S(2)}) collective-permute-start(bf16[800,768]{1,0:T(8,128)(2,1)} %convolution_convert_fusion.3), channel_id=1, source_target_pairs={{0,1},{1,0},{2,3},{3,2},{4,5},{5,4},{6,7},{7,6},{8,9},{9,8},{10,11... | collective-permute-start | bytes 3686408 | tf_op jit(solution)/shard_map/ppermute | solution.py:52
  286.0 23.5 %collective-permute-start.41 = (bf16[4,2,48,768]{3,2,0,1:T(8,128)(2,1)}, bf16[4,2,48,768]{3,2,0,1:T(8,128)(2,1)}, u32[]{:S(2)}, u32[]{:S(2)}) collective-permute-start(bf16[4,2,48,768]{3,2,0,1:T(8,128)(2,1)} %fusion.99), channel_id=1, source_target_pairs={{0,4},{4,0},{8,12},{12,8},{16,20},{20,16},{24,28},{28,24},{1,5},{5... | collective-permute-start | bytes 1769480 | tf_op jit(solution)/shard_map/ppermute | solution.py:52
  287.5 14.7 %collective-permute-start.47 = (f32[2,2,768]{2,1,0:T(2,128)S(1)}, f32[2,2,768]{2,1,0:T(2,128)S(1)}, u32[]{:S(2)}, u32[]{:S(2)}) collective-permute-start(f32[2,2,768]{2,1,0:T(2,128)S(1)} %get-tuple-element.299), channel_id=1, source_target_pairs={{0,4},{4,0},{8,12},{12,8},{16,20},{20,16},{24,28},{28,24},{1,5},{5... | collective-permute-start | bytes 36872 | tf_op jit(solution)/shard_map/ppermute | solution.py:52
  302.8 71.4 %collective-permute-start.50 = (f32[2,2,2,768]{3,2,1,0:T(2,128)}, f32[2,2,2,768]{3,2,1,0:T(2,128)}, u32[]{:S(2)}, u32[]{:S(2)}) collective-permute-start(f32[2,2,2,768]{3,2,1,0:T(2,128)} %get-tuple-element.297), channel_id=1, source_target_pairs={{0,24},{4,28},{8,16},{12,20},{16,8},{20,12},{24,0},{28,4},{1,25},{... | collective-permute-start | bytes 73736 | tf_op jit(solution)/shard_map/ppermute | solution.py:52
  304.9 70.4 %collective-permute-start.49 = (f32[2,2,2,768]{3,2,1,0:T(2,128)}, f32[2,2,2,768]{3,2,1,0:T(2,128)}, u32[]{:S(2)}, u32[]{:S(2)}) collective-permute-start(f32[2,2,2,768]{3,2,1,0:T(2,128)} %get-tuple-element.297), channel_id=1, source_target_pairs={{0,16},{4,20},{8,24},{12,28},{16,0},{20,4},{24,8},{28,12},{1,17},{... | collective-permute-start | bytes 73736 | tf_op jit(solution)/shard_map/ppermute | solution.py:52
  306.0 69.3 %collective-permute-start.48 = (f32[2,2,2,768]{3,2,1,0:T(2,128)}, f32[2,2,2,768]{3,2,1,0:T(2,128)}, u32[]{:S(2)}, u32[]{:S(2)}) collective-permute-start(f32[2,2,2,768]{3,2,1,0:T(2,128)} %get-tuple-element.297), channel_id=1, source_target_pairs={{0,8},{4,12},{8,0},{12,4},{16,24},{20,28},{24,16},{28,20},{1,9},{5... | collective-permute-start | bytes 73736 | tf_op jit(solution)/shard_map/ppermute | solution.py:52
  309.4 62.4 %collective-permute-start.39 = (bf16[4,2,48,768]{3,2,0,1:T(8,128)(2,1)}, bf16[4,2,48,768]{3,2,0,1:T(8,128)(2,1)}, u32[]{:S(2)}, u32[]{:S(2)}) collective-permute-start(bf16[4,2,48,768]{3,2,0,1:T(8,128)(2,1)} %copy.426), channel_id=1, source_target_pairs={{0,2},{1,3},{2,0},{3,1},{4,6},{5,7},{6,4},{7,5},{8,10},{9,11},{10,... | collective-permute-start | bytes 1769480 | tf_op jit(solution)/shard_map/ppermute | solution.py:52
  349.6 8.7 %collective-permute-start.31 = (bf16[800,768]{1,0:T(8,128)(2,1)S(1)}, bf16[800,768]{1,0:T(8,128)(2,1)S(1)}, u32[]{:S(2)}, u32[]{:S(2)}) collective-permute-start(bf16[800,768]{1,0:T(8,128)(2,1)S(1)} %convolution_convert_fusion.1), channel_id=1, source_target_pairs={{0,1},{1,0},{2,3},{3,2},{4,5},{5,4},{6,7},{7,6},{8,9},{9,8},{10,11... | collective-permute-start | bytes 3686408 | tf_op jit(solution)/shard_map/ppermute | solution.py:52
  358.3 19.4 %collective-permute-start.42 = (bf16[4,48,768]{2,1,0:T(8,128)(2,1)}, bf16[4,48,768]{2,1,0:T(8,128)(2,1)}, u32[]{:S(2)}, u32[]{:S(2)}) collective-permute-start(bf16[4,48,768]{2,1,0:T(8,128)(2,1)} %fusion.142), channel_id=1, source_target_pairs={{0,2},{1,3},{2,0},{3,1},{4,6},{5,7},{6,4},{7,5},{8,10},{9,11},{10,... | collective-permute-start | bytes 884744 | tf_op jit(solution)/shard_map/ppermute | solution.py:52
  371.9 26.0 %collective-permute-start.34 = (bf16[4,2,48,1024]{3,2,0,1:T(8,128)(2,1)S(1)}, bf16[4,2,48,1024]{3,2,0,1:T(8,128)(2,1)S(1)}, u32[]{:S(2)}, u32[]{:S(2)}) collective-permute-start(bf16[4,2,48,1024]{3,2,0,1:T(8,128)(2,1)S(1)} %fusion.86), channel_id=1, source_target_pairs={{0,4},{4,0},{8,12},{12,8},{16,20},{20,16},{24,28},{28,24},{1,5},{5... | collective-permute-start | bytes 2359304 | tf_op jit(solution)/shard_map/ppermute | solution.py:52
  374.2 23.6 %collective-permute-start.40 = (bf16[4,48,768]{2,1,0:T(8,128)(2,1)S(1)}, bf16[4,48,768]{2,1,0:T(8,128)(2,1)S(1)}, u32[]{:S(2)}, u32[]{:S(2)}) collective-permute-start(bf16[4,48,768]{2,1,0:T(8,128)(2,1)S(1)} %fusion.141), channel_id=1, source_target_pairs={{0,4},{4,0},{8,12},{12,8},{16,20},{20,16},{24,28},{28,24},{1,5},{5... | collective-permute-start | bytes 884744 | tf_op jit(solution)/shard_map/ppermute | solution.py:52
  376.3 23.4 %collective-permute-start.32 = (bf16[4,2,48,1024]{3,2,0,1:T(8,128)(2,1)S(1)}, bf16[4,2,48,1024]{3,2,0,1:T(8,128)(2,1)S(1)}, u32[]{:S(2)}, u32[]{:S(2)}) collective-permute-start(bf16[4,2,48,1024]{3,2,0,1:T(8,128)(2,1)S(1)} %copy.425), channel_id=1, source_target_pairs={{0,2},{1,3},{2,0},{3,1},{4,6},{5,7},{6,4},{7,5},{8,10},{9,11},{10,... | collective-permute-start | bytes 2359304 | tf_op jit(solution)/shard_map/ppermute | solution.py:52
  398.2 10.4 %collective-permute-start.35 = (bf16[4,48,1024]{2,1,0:T(8,128)(2,1)S(1)}, bf16[4,48,1024]{2,1,0:T(8,128)(2,1)S(1)}, u32[]{:S(2)}, u32[]{:S(2)}) collective-permute-start(bf16[4,48,1024]{2,1,0:T(8,128)(2,1)S(1)} %fusion.110), channel_id=1, source_target_pairs={{0,2},{1,3},{2,0},{3,1},{4,6},{5,7},{6,4},{7,5},{8,10},{9,11},{10,... | collective-permute-start | bytes 1179656 | tf_op jit(solution)/shard_map/ppermute | solution.py:52
  400.0 10.1 %collective-permute-start.33 = (bf16[4,48,1024]{2,1,0:T(8,128)(2,1)S(1)}, bf16[4,48,1024]{2,1,0:T(8,128)(2,1)S(1)}, u32[]{:S(2)}, u32[]{:S(2)}) collective-permute-start(bf16[4,48,1024]{2,1,0:T(8,128)(2,1)S(1)} %fusion.109), channel_id=1, source_target_pairs={{0,4},{4,0},{8,12},{12,8},{16,20},{20,16},{24,28},{28,24},{1,5},{5... | collective-permute-start | bytes 1179656 | tf_op jit(solution)/shard_map/ppermute | solution.py:52
  400.6 12.0 %collective-permute-start.45 = (bf16[96,768]{1,0:T(8,128)(2,1)S(1)}, bf16[96,768]{1,0:T(8,128)(2,1)S(1)}, u32[]{:S(2)}, u32[]{:S(2)}) collective-permute-start(bf16[96,768]{1,0:T(8,128)(2,1)S(1)} %get-tuple-element.183), channel_id=1, source_target_pairs={{0,24},{4,28},{8,16},{12,20},{16,8},{20,12},{24,0},{28,4},{1,25},{... | collective-permute-start | bytes 442376 | tf_op jit(solution)/shard_map/ppermute | solution.py:52
  402.8 22.2 %collective-permute-start.44 = (bf16[96,768]{1,0:T(8,128)(2,1)S(1)}, bf16[96,768]{1,0:T(8,128)(2,1)S(1)}, u32[]{:S(2)}, u32[]{:S(2)}) collective-permute-start(bf16[96,768]{1,0:T(8,128)(2,1)S(1)} %get-tuple-element.182), channel_id=1, source_target_pairs={{0,16},{4,20},{8,24},{12,28},{16,0},{20,4},{24,8},{28,12},{1,17},{... | collective-permute-start | bytes 442376 | tf_op jit(solution)/shard_map/ppermute | solution.py:52
  403.0 21.9 %collective-permute-start.43 = (bf16[96,768]{1,0:T(8,128)(2,1)S(1)}, bf16[96,768]{1,0:T(8,128)(2,1)S(1)}, u32[]{:S(2)}, u32[]{:S(2)}) collective-permute-start(bf16[96,768]{1,0:T(8,128)(2,1)S(1)} %get-tuple-element.181), channel_id=1, source_target_pairs={{0,8},{4,12},{8,0},{12,4},{16,24},{20,28},{24,16},{28,20},{1,9},{5... | collective-permute-start | bytes 442376 | tf_op jit(solution)/shard_map/ppermute | solution.py:52
  410.3 14.7 %collective-permute-start.38 = (bf16[96,1024]{1,0:T(8,128)(2,1)S(1)}, bf16[96,1024]{1,0:T(8,128)(2,1)S(1)}, u32[]{:S(2)}, u32[]{:S(2)}) collective-permute-start(bf16[96,1024]{1,0:T(8,128)(2,1)S(1)} %get-tuple-element.174), channel_id=1, source_target_pairs={{0,24},{4,28},{8,16},{12,20},{16,8},{20,12},{24,0},{28,4},{1,25},{... | collective-permute-start | bytes 589832 | tf_op jit(solution)/shard_map/ppermute | solution.py:52
  412.4 19.4 %collective-permute-start.37 = (bf16[96,1024]{1,0:T(8,128)(2,1)S(1)}, bf16[96,1024]{1,0:T(8,128)(2,1)S(1)}, u32[]{:S(2)}, u32[]{:S(2)}) collective-permute-start(bf16[96,1024]{1,0:T(8,128)(2,1)S(1)} %get-tuple-element.173), channel_id=1, source_target_pairs={{0,16},{4,20},{8,24},{12,28},{16,0},{20,4},{24,8},{28,12},{1,17},{... | collective-permute-start | bytes 589832 | tf_op jit(solution)/shard_map/ppermute | solution.py:52
  412.7 19.1 %collective-permute-start.36 = (bf16[96,1024]{1,0:T(8,128)(2,1)S(1)}, bf16[96,1024]{1,0:T(8,128)(2,1)S(1)}, u32[]{:S(2)}, u32[]{:S(2)}) collective-permute-start(bf16[96,1024]{1,0:T(8,128)(2,1)S(1)} %get-tuple-element.172), channel_id=1, source_target_pairs={{0,8},{4,12},{8,0},{12,4},{16,24},{20,28},{24,16},{28,20},{1,9},{5... | collective-permute-start | bytes 589832 | tf_op jit(solution)/shard_map/ppermute | solution.py:52
  432.7 117.4 %all-gather.3.cloned.1.call-start = ((), (), s32[]{:S(2)}) async-start(), calls=%async_computation | async-start | bytes 3981312 | tf_op jit(solution)/shard_map/all_gather | solution.py:585
  566.1 8.5 %collective-permute-start.58 = (bf16[2,6,256,256]{3,2,1,0:T(8,128)(2,1)S(1)}, bf16[2,6,256,256]{3,2,1,0:T(8,128)(2,1)S(1)}, u32[]{:S(2)}, u32[]{:S(2)}) collective-permute-start(bf16[2,6,256,256]{3,2,1,0:T(8,128)(2,1)S(1)} %pad_maximum_fusion.12), channel_id=1, source_target_pairs={{0,1},{1,0},{2,3},{3,2},{4,5},{5,4},{6,7},{7,6},{8,9},{9,8},{10,11... | collective-permute-start | bytes 4718600 | tf_op jit(solution)/shard_map/ppermute | solution.py:52
  575.1 19.7 %collective-permute-start.59 = (bf16[6,256,256]{2,1,0:T(8,128)(2,1)S(1)}, bf16[6,256,256]{2,1,0:T(8,128)(2,1)S(1)}, u32[]{:S(2)}, u32[]{:S(2)}) collective-permute-start(bf16[6,256,256]{2,1,0:T(8,128)(2,1)S(1)} %fusion.85), channel_id=1, source_target_pairs={{0,2},{1,3},{2,0},{3,1},{4,6},{5,7},{6,4},{7,5},{8,10},{9,11},{10,... | collective-permute-start | bytes 2359304 | tf_op jit(solution)/shard_map/ppermute | solution.py:52
  (194 other events, 1277.8 us)
Sparse Core Ops, SparseCore 0:
  432.8 50.6 all-gather.4
  486.3 63.7 all-gather.2

commit v2 on v1

--- a/solution.py
+++ b/solution.py
@@ -3,6 +3,8 @@
 import jax
 import jax.numpy as jnp
 from jax import lax
+from jax.experimental import pallas as pl
+from jax.experimental.pallas import tpu as pltpu
 from jax.sharding import PartitionSpec as P
 
 D = 768
@@ -69,57 +71,142 @@
     return low.astype(F32) + swap_core(low).astype(F32)
 
 
-def gather_rows(shard):
-    rows, columns = shard.shape
+def place_kernel(splits, position, own, own_x, own_side, near, far, *outs):
+    x = position[1]
+    corner = jnp.where((position[0] ^ pl.program_id(0)) < 2, near[...], far[...])
+    parts = ((own[...], x, 0), (own_x[...], 1 - x, 0), (own_side[...], x, 1), (corner, 1 - x, 1))
+    for part, where, group in parts:
+        start = 0
+        for width, out in zip(splits, outs):
+            out[0, pl.ds(where, 1), :, group * width : (group + 1) * width] = part[
+                :, :, start : start + width
+            ]
+            start += width
+
+
+def place(parts, splits):
+    here = lax.axis_index("batch")
+    position = jnp.stack([here // 2, here % 2]).astype(jnp.int32)
+    _, rows, columns = parts[0].shape
+
+    def block(pick_line):
+        return pl.BlockSpec(
+            (1, rows, columns), lambda step, spot: (pick_line(spot[0] ^ step), 0, 0)
+        )
+
+    whole = block(lambda line: line)
+    near, far = block(lambda line: line & 1), block(lambda line: line & 1)
+    outs = pl.pallas_call(
+        lambda *refs: place_kernel(splits, *refs),
+        grid_spec=pltpu.PrefetchScalarGridSpec(
+            num_scalar_prefetch=1,
+            grid=(4,),
+            in_specs=[whole, whole, whole, near, far],
+            out_specs=[
+                pl.BlockSpec((1, 2, rows, 2 * width), lambda step, spot: (step, 0, 0, 0))
+                for width in splits
+            ],
+        ),
+        out_shape=[
+            jax.ShapeDtypeStruct((4, 2, rows, 2 * width), parts[0].dtype) for width in splits
+        ],
+        compiler_params=pltpu.CompilerParams(vmem_limit_bytes=32 * 1024 * 1024),
+    )(position, *parts)
+    return [out.reshape(8 * rows, out.shape[-1]) for out in outs]
+
+
+def tie(*values):
+    return lax.optimization_barrier(values)
+
+
+def gather_lines(shard):
+    if lax.axis_size("batch") != 8:
+        return lax.all_gather(shard, "batch", axis=0, tiled=True)
+    return jnp.stack([shard] + [swap(shard, "batch", 2 * mask) for mask in (1, 2, 3)])
+
+
+def gather_batch(lines):
+    if lax.axis_size("batch") != 8:
+        return lines
+    here = lax.axis_index("batch")
+    position = jnp.stack([here // 2, here % 2]).astype(jnp.int32)
+    _, rows, columns = lines.shape
+
+    def kernel(spot, own, own_x, out):
+        out[0, pl.ds(spot[1], 1)] = own[...]
+        out[0, pl.ds(1 - spot[1], 1)] = own_x[...]
+
+    line = pl.BlockSpec((1, rows, columns), lambda step, spot: (spot[0] ^ step, 0, 0))
+    out = pl.pallas_call(
+        kernel,
+        grid_spec=pltpu.PrefetchScalarGridSpec(
+            num_scalar_prefetch=1,
+            grid=(4,),
+            in_specs=[line, line],
+            out_specs=pl.BlockSpec((1, 2, rows, columns), lambda step, spot: (step, 0, 0, 0)),
+        ),
+        out_shape=jax.ShapeDtypeStruct((4, 2, rows, columns), lines.dtype),
+        compiler_params=pltpu.CompilerParams(vmem_limit_bytes=32 * 1024 * 1024),
+    )(position, lines, swap_x(lines))
+    return out.reshape(8 * rows, columns)
+
+
+def gather_planes(lines):
+    if lax.axis_size("batch") != 8:
+        return lines, swap_side(lines)
+    return lines, swap_x(lines), swap_side(lines)
+
+
+def gather_ends(planes):
+    if lax.axis_size("batch") != 8:
+        return ()
+    return swap_side(planes[1][:2]), swap_x(planes[2][2:])
+
+
+def gather_last(planes, ends, splits):
+    if lax.axis_size("batch") != 8:
+        own, other = planes
+        outs, start = [], 0
+        for width in splits:
+            pair = [own[:, start : start + width], other[:, start : start + width]]
+            outs.append(jnp.concatenate(pair, 1))
+            start += width
+        return outs
+    return place([*planes, *ends], splits)
+
+
+def pick(blocks, index, axis):
+    return lax.dynamic_index_in_dim(blocks, index, axis, keepdims=False)
+
+
+def reduce_start(own, other):
     count = lax.axis_size("batch")
     if count != 8:
-        own = lax.all_gather(shard, "batch", axis=0, tiled=True)
-        return own, swap_side(own)
-    here = lax.axis_index("batch")
-    z, x = here // 2, here % 2
+        return own.astype(F32) + swap_side(other).astype(F32), own
+    rows, columns = own.shape[0] // count, own.shape[1]
     half = rows // 2
-    lines = jnp.stack([shard] + [swap(shard, "batch", 2 * mask) for mask in (1, 2, 3)])
-    first, second = lines[:, :half], lines[:, half:]
-    first = jnp.stack([first, swap_x(first)])
-    second = jnp.stack([second, swap_side(second)])
-    first = jnp.stack([first, swap_side(first)])
-    second = jnp.stack([second, swap_x(second)])
-    first = first.reshape(2, 8, half, columns)
-    groups = []
-    for side in range(2):
-        pieces = []
-        for z_to in range(4):
-            for x_to in range(2):
-                x_from, z_from = x ^ x_to, z ^ z_to
-                pieces.append(at(first[side], x_from * 4 + z_from))
-                pieces.append(at(second[:, side].reshape(8, half, columns), x_from * 4 + z_from))
-        groups.append(jnp.concatenate(pieces, 0))
-    return groups
-
-
-def reduce_rows(own, other):
-    count = lax.axis_size("batch")
-    columns = own.shape[1]
-    rows = own.shape[0] // count
-    if count != 8:
-        total = own + swap_side(other.astype(BF)).astype(F32)
-        return lax.psum_scatter(total, "batch", scatter_dimension=0, tiled=True)
-    here = lax.axis_index("batch")
-    z, x = here // 2, here % 2
-    half = rows // 2
-
-    def pick_x(blocks, index):
-        return lax.dynamic_index_in_dim(blocks, index, 1, keepdims=False)
-
+    x = lax.axis_index("batch") % 2
     own = own.reshape(4, 2, rows, columns)
     other = other.reshape(4, 2, rows, columns)
-    first = own[:, :, :half] + swap_side(other[:, :, :half].astype(BF)).astype(F32)
-    first = pick_x(first, x) + swap_x(pick_x(first, 1 - x).astype(BF)).astype(F32)
-    second = jnp.stack([own[:, :, half:], other[:, :, half:]])
-    second = second.transpose(1, 2, 0, 3, 4)
-    second = pick_x(second, x) + swap_x(pick_x(second, 1 - x).astype(BF)).astype(F32)
+    first = own[:, :, :half].astype(F32) + swap_side(other[:, :, :half]).astype(F32)
+    second = jnp.stack([own[:, :, half:], other[:, :, half:]], 2)
+    second = pick(second, x, 1).astype(F32) + swap_x(pick(second, 1 - x, 1)).astype(F32)
+    return first, second
+
+
+def reduce_middle(first, second):
+    if lax.axis_size("batch") != 8:
+        return first
+    x = lax.axis_index("batch") % 2
+    first = pick(first, x, 1) + swap_x(pick(first, 1 - x, 1).astype(BF)).astype(F32)
     second = second[:, 0] + swap_side(second[:, 1].astype(BF)).astype(F32)
-    both = jnp.concatenate([first, second], 1)
+    return jnp.concatenate([first, second], 1)
+
+
+def reduce_end(both):
+    if lax.axis_size("batch") != 8:
+        return lax.psum_scatter(both, "batch", scatter_dimension=0, tiled=True)
+    z = lax.axis_index("batch") // 2
     total = at(both, z)
     for mask in (1, 2, 3):
         total = total + swap(at(both, z ^ mask).astype(BF), "batch", 2 * mask).astype(F32)
@@ -162,13 +249,38 @@
     return values
 
 
-def all_quarters(own, other):
-    pair = jnp.stack([own, other])
-    four = jnp.concatenate([pair, swap_core(pair)])
+def order_kernel(turned, position, mine, theirs, *outs):
+    core, side = position[0], position[1]
+    width = mine.shape[1] // 2
+    plain = width - turned
+    for index in range(4):
+        same_core = core == index % 2
+        same_side = side == index // 2
+        kept = jnp.where(same_core, mine[:, :width], theirs[:, :width])
+        other = jnp.where(same_core, mine[:, width:], theirs[:, width:])
+        quarter = jnp.where(same_side, kept, other)
+        outs[0][:, index * plain : (index + 1) * plain] = quarter[:, :plain]
+        if turned:
+            outs[1][index * turned : (index + 1) * turned, :] = (
+                quarter[:, plain:].astype(F32).T.astype(BF)
+            )
+
+
+def all_quarters(mine, turned=0):
     head = lax.axis_index("head")
-    places = (0, 2, 1, 3)
-    table = jnp.array(places, jnp.int32)
-    return [at(four, table[head ^ index]) for index in range(4)]
+    theirs = swap_core(mine)
+    rows, both = mine.shape
+    shapes = [jax.ShapeDtypeStruct((rows, 2 * both - 4 * turned), BF)]
+    if turned:
+        shapes.append(jax.ShapeDtypeStruct((4 * turned, rows), BF))
+    return pl.pallas_call(
+        lambda *refs: order_kernel(turned, *refs),
+        in_specs=[pl.BlockSpec(memory_space=pltpu.SMEM)]
+        + [pl.BlockSpec(memory_space=pltpu.VMEM)] * 2,
+        out_specs=[pl.BlockSpec(memory_space=pltpu.VMEM)] * len(shapes),
+        out_shape=shapes,
+        compiler_params=pltpu.CompilerParams(vmem_limit_bytes=32 * 1024 * 1024),
+    )(jnp.stack([head % 2, head // 2]).astype(jnp.int32), mine, theirs)
 
 
 def normalize(values):
@@ -186,37 +298,56 @@
     )
 
 
-def attend(packed, length):
-    tokens = packed.shape[0]
-    queries, keys, values = packed[:, :, 0], packed[:, :, 1], packed[:, :, 2]
-    scores = jnp.einsum("qhd,khd->hqk", queries, keys, preferred_element_type=F32)
-    scores = scores * HD ** (-0.5)
-    scores = jnp.where(jnp.arange(tokens) < length, scores, -1e30)
-    top = jnp.max(scores, -1, keepdims=True)
-    log_total = top + jnp.log(jnp.sum(jnp.exp(scores - top), -1, keepdims=True))
-    soft = jnp.exp(scores - log_total).astype(BF)
-    blended = jnp.einsum("hqk,khd->qhd", soft, values, preferred_element_type=F32)
-    return blended.astype(BF), log_total, soft
-
-
-def attend_back(packed, length, log_total, soft, grad):
-    tokens = packed.shape[0]
-    queries, keys, values = packed[:, :, 0], packed[:, :, 1], packed[:, :, 2]
-    scale = HD ** (-0.5)
-    grad_values = jnp.einsum("hqk,qhd->khd", soft, grad, preferred_element_type=F32)
-    grad_soft = jnp.einsum("qhd,khd->hqk", grad, values, preferred_element_type=F32)
-    scores = jnp.einsum("qhd,khd->hqk", queries, keys, preferred_element_type=F32) * scale
-    scores = jnp.where(jnp.arange(tokens) < length, scores, -1e30)
-    probs = jnp.exp(scores - log_total)
-    grad_scores = probs * (grad_soft - jnp.sum(probs * grad_soft, -1, keepdims=True))
-    grad_scores = grad_scores.astype(BF)
-    grad_queries = (
-        jnp.einsum("hqk,khd->qhd", grad_scores, keys, preferred_element_type=F32) * scale
-    )
-    grad_keys = (
-        jnp.einsum("hqk,qhd->khd", grad_scores, queries, preferred_element_type=F32) * scale
-    )
-    return jnp.stack([grad_queries, grad_keys, grad_values], 2).astype(BF)
+def soft_columns(keys, queries, length):
+    scores = dot(keys, queries, 1, 1)
+    places = lax.broadcasted_iota(jnp.int32, (keys.shape[0], 1), 0)
+    scores = jnp.where(places < length, scores, -1e30)
+    scores = jnp.exp(scores - jnp.max(scores, 0, keepdims=True))
+    return scores * (1.0 / jnp.sum(scores, 0, keepdims=True))
+
+
+def parts_of(packed, spans):
+    for head in range(packed.shape[1] // (3 * HD)):
+        base = head * 3 * HD
+        for start, rows, length in spans:
+            span = slice(start, start + rows)
+            queries = packed[span, base : base + HD] * HD ** (-0.5)
+            keys = packed[span, base + HD : base + 2 * HD]
+            values = packed[span, base + 2 * HD : base + 3 * HD]
+            yield head, base, span, length, queries, keys, values
+
+
+def attend_kernel(spans, packed, out):
+    for head, _, span, length, queries, keys, values in parts_of(packed, spans):
+        soft = soft_columns(keys, queries, length).astype(BF)
+        out[span, head * HD : (head + 1) * HD] = dot(values, soft, 0, 0).T.astype(BF)
+
+
+def attend_back_kernel(spans, packed, grad, out):
+    for head, base, span, length, queries, keys, values in parts_of(packed, spans):
+        grads = grad[span, head * HD : (head + 1) * HD]
+        soft = soft_columns(keys, queries, length)
+        out[span, base + 2 * HD : base + 3 * HD] = dot(soft.astype(BF), grads).astype(BF)
+        grad_soft = dot(values, grads, 1, 1)
+        grad_scores = soft * (grad_soft - jnp.sum(soft * grad_soft, 0, keepdims=True))
+        grad_scores = grad_scores.astype(BF)
+        grad_queries = dot(keys, grad_scores, 0, 0).T * HD ** (-0.5)
+        out[span, base : base + HD] = grad_queries.astype(BF)
+        out[span, base + HD : base + 2 * HD] = dot(grad_scores, queries).astype(BF)
+
+
+def attention(kernel, spans, packed, *grads):
+    tokens, width = packed.shape
+    wide = pl.BlockSpec((tokens, 6 * HD), lambda step: (0, step))
+    narrow = pl.BlockSpec((tokens, 2 * HD), lambda step: (0, step))
+    return pl.pallas_call(
+        lambda *refs: kernel(spans, *refs),
+        grid=(width // (6 * HD),),
+        in_specs=[wide] + [narrow] * len(grads),
+        out_specs=wide if grads else narrow,
+        out_shape=jax.ShapeDtypeStruct((tokens, width if grads else width // 3), BF),
+        compiler_params=pltpu.CompilerParams(vmem_limit_bytes=40 * 1024 * 1024),
+    )(packed, *grads)
 
 
 def adam_update(weight, gradient, first, second, rate, decay):
@@ -313,24 +444,21 @@
     quarter_table = lax.dynamic_slice_in_dim(table, head * extra_width, extra_width, 1)
     padded_head = jnp.pad(head_w.astype(BF), ((0, 0), (0, head_padded - head_columns)))
     quarter_head = lax.dynamic_slice_in_dim(padded_head, head * head_width, head_width, 1)
-    chunk_one = jnp.concatenate(
-        [quarter_patch.astype(BF), quarter_table, w_qkv.astype(BF), w_out.astype(BF)], 1
-    )
-    chunk_two = w_up.astype(BF)
+    small = patch_width + extra_width
+    chunk_one = jnp.concatenate([quarter_patch.astype(BF), quarter_table, w_qkv.astype(BF)], 1)
+    chunk_two = jnp.concatenate([w_out.astype(BF), w_up.astype(BF)], 1)
     chunk_three = jnp.concatenate([w_down.astype(BF), quarter_head], 1)
-    one = gather_rows(chunk_one)
-    two = gather_rows(chunk_two)
-    three = gather_rows(chunk_three)
-    small = patch_width + extra_width
-    quarters = all_quarters(one[0][:, :small], one[1][:, :small])
-    full_patch = jnp.concatenate([quarter[:, :patch_width] for quarter in quarters], 1)
-    table = jnp.concatenate([quarter[:, patch_width:] for quarter in quarters], 1).T
-    full_qkv = jnp.concatenate([part[:, small : small + qkv_width] for part in one], 1)
-    full_out = jnp.concatenate([part[:, small + qkv_width :] for part in one], 1)
-    full_up = jnp.concatenate(two, 1)
-    full_down = jnp.concatenate([part[:, :hidden] for part in three], 1)
-    quarters = all_quarters(three[0][:, hidden:], three[1][:, hidden:])
-    full_head = jnp.concatenate(quarters, 1)[:, :head_columns]
+    lines = gather_lines(chunk_one)
+    chunk_two, lines = tie(chunk_two, lines)
+    planes = gather_planes(lines)
+    lines_two = gather_lines(chunk_two)
+    planes, lines_two = tie(planes, lines_two)
+    ends = gather_ends(planes)
+    planes_two = gather_planes(lines_two)
+    both_small, full_qkv = gather_last(planes, ends, (small, qkv_width))
+    full_patch, table = all_quarters(both_small, extra_width)
+    chunk_three, full_patch = tie(chunk_three, full_patch)
+    lines_three = gather_lines(chunk_three)
 
     class_row = grid_low
     vec = table[grid_low + 1 : grid_low + 11].astype(F32)
@@ -359,15 +487,22 @@
     initial = dot(patches, full_patch) + added
     unit_one, scale_one = normalize(initial)
     normed = (unit_one * vec[0] + vec[1]).astype(BF)
-    group_heads = 2 * qkv_width // (3 * HD)
-    packed = dot(normed, full_qkv).astype(BF).reshape(tokens, group_heads, 3, HD)
-    blend_low, logs_low, soft_low = attend(packed[:low_rows], grid_low + 1)
-    blend_high, logs_high, soft_high = attend(packed[low_rows:], grid_high + 1)
-    blended = jnp.concatenate([blend_low, blend_high], 0).reshape(tokens, group_heads * HD)
+    packed = dot(normed, full_qkv).astype(BF)
+    packed, planes_two = tie(packed, planes_two)
+    ends_two = gather_ends(planes_two)
+    spans = ((0, low_rows, grid_low + 1), (low_rows, high_rows, grid_high + 1))
+    blended = attention(attend_kernel, spans, packed)
+    blended, ends_two, lines_three = tie(blended, ends_two, lines_three)
+    planes_three = gather_planes(lines_three)
+    full_out, full_up = gather_last(planes_two, ends_two, (out_width, hidden))
     middle = initial + vec[7] + pair_sum(dot(blended, full_out, 1, 1))
     unit_two, scale_two = normalize(middle)
     normed_two = (unit_two * vec[2] + vec[3]).astype(BF)
     upward = dot(normed_two, full_up)
+    upward, planes_three = tie(upward, planes_three)
+    ends_three = gather_ends(planes_three)
+    full_down, both_head = gather_last(planes_three, ends_three, (hidden, head_width))
+    (full_head,) = all_quarters(both_head)
     cumulative = 0.5 * (1.0 + lax.erf(upward * (0.5**0.5)))
     active = (upward * cumulative).astype(BF).astype(F32)
     slope = cumulative + upward * jnp.exp(-0.5 * upward * upward) * (2.0 * math.pi) ** (-0.5)
@@ -387,19 +522,28 @@
     pooled_own = per_image(middle) / lengths + vec[8] + down_part
 
     ids = jnp.stack([side, low_patches.shape[0] + side])
-    tags = jnp.stack([labels[ids], partner[ids]], 1).astype(F32)
-    sent = jnp.concatenate([pooled_own, jnp.pad(tags, ((0, 0), (0, 126)))], 1)
-    both_sides = in_order(jnp.stack([sent, swap_side(sent)]), side, 1)
+    own_labels, own_partners = labels[ids], partner[ids]
+    tags = jnp.stack([own_labels // 8, own_labels % 8, own_partners // 8, own_partners % 8], 1)
+    pooled_high = pooled_own.astype(BF)
+    pooled_low = (pooled_own - pooled_high.astype(F32)).astype(BF)
+    tags = jnp.pad(tags.astype(BF), ((0, 0), (0, 124)))
+    common = jnp.concatenate([pooled_high, pooled_low, tags], 1)
+    active_low = active_sums.astype(BF)
+    came = swap_side(jnp.concatenate([common, active_low[:, hidden:]], 1))
+    mine = jnp.concatenate([common, active_low[:, :hidden]], 1)
+    both_sides = in_order(jnp.stack([mine, came]), side, 1)
     everyone = gather_small(both_sides.transpose(1, 0, 2))
     images = batch_size * 4
-    everyone = everyone.reshape(images, D + 128)
-    pooled = everyone[:, :D]
-    all_labels = everyone[:, D].astype(jnp.int32)
-    all_partners = everyone[:, D + 1].astype(jnp.int32)
+    everyone = everyone.reshape(images, 2 * D + 128 + hidden)
+    pooled = everyone[:, :D].astype(F32) + everyone[:, D : 2 * D].astype(F32)
+    all_tags = everyone[:, 2 * D : 2 * D + 4].astype(jnp.int32)
+    all_labels = all_tags[:, 0] * 8 + all_tags[:, 1]
+    all_partners = all_tags[:, 2] * 8 + all_tags[:, 3]
+    all_sums = everyone[:, 2 * D + 128 :]
     unit_final, scale_final = normalize(pooled)
     features = (unit_final * vec[4] + vec[5]).astype(BF)
     outputs = dot(features, full_head)
-    logits, projected = outputs[:, :CLS], outputs[:, CLS:]
+    logits, projected = outputs[:, :CLS], outputs[:, CLS:head_columns]
     picked = jnp.arange(CLS)[None, :] == all_labels[:, None]
     logit_top = jnp.max(logits, -1, keepdims=True)
     logit_log = logit_top + jnp.log(jnp.sum(jnp.exp(logits - logit_top), -1, keepdims=True))
@@ -422,8 +566,9 @@
         length_inverse**3 * jnp.sum(grad_embedded * projected, -1, keepdims=True)
     )
     grad_outputs = jnp.concatenate([grad_logits, grad_projected], 1).astype(BF)
+    grad_outputs = jnp.pad(grad_outputs, ((0, 0), (0, head_padded - head_columns)))
     features_here = lax.dynamic_slice_in_dim(features, batch * rows_here, rows_here, 1)
-    grad_head = dot(features_here, grad_outputs, 0, 0)
+    grad_head = dot(features_here, grad_outputs, 0, 0)[:, :head_columns]
     grad_features = dot(grad_outputs, full_head, 1, 1)
     grad_pooled = normalize_back(grad_features, unit_final, scale_final, vec[4])
     complete_rows = jnp.stack(
@@ -449,28 +594,41 @@
         )
         return jnp.where(mask, rows, 0.0)
 
+    held = jnp.concatenate([mom_qkv, mom_out, mom_up, mom_down], 1).astype(BF)
+    held, _ = tie(held, full_down)
+    full_old = lax.all_gather(held, "batch", axis=0, tiled=True)
     grad_active = dot(grad_own_low, full_down)
     grad_upward = (spread(grad_active, is_token) * slope).astype(BF)
-    grad_up = dot(normed_two, grad_upward, 0, 0)
+    grad_up = dot(normed_two, grad_upward, 0, 0).astype(BF)
+    sums_up = reduce_start(grad_up[:, :hidden], grad_up[:, hidden:])
     grad_normed_two = pair_sum(dot(grad_upward, full_up, 1, 1))
     gain_two = jnp.sum(grad_normed_two * unit_two, 0)
     shift_two = jnp.sum(grad_normed_two, 0)
     grad_middle = normalize_back(grad_normed_two, unit_two, scale_two, vec[2])
     grad_middle = grad_middle + spread(grad_own, is_token)
     grad_middle_low = grad_middle.astype(BF)
-    grad_out = dot(grad_middle_low, blended, 0, 0)
-    grad_blend = dot(grad_middle_low, full_out).astype(BF).reshape(tokens, group_heads, HD)
-    grad_packed = jnp.concatenate(
-        [
-            attend_back(packed[:low_rows], grid_low + 1, logs_low, soft_low, grad_blend[:low_rows]),
-            attend_back(
-                packed[low_rows:], grid_high + 1, logs_high, soft_high, grad_blend[low_rows:]
-            ),
-        ],
-        0,
-    ).reshape(tokens, 2 * qkv_width)
-    grad_qkv = dot(normed, grad_packed, 0, 0)
+    grad_middle_low, sums_up = tie(grad_middle_low, sums_up)
+    sums_up = reduce_middle(*sums_up)
+    grad_out = dot(grad_middle_low, blended, 0, 0).astype(BF)
+    grad_blend = dot(grad_middle_low, full_out).astype(BF)
+    grad_packed = attention(attend_back_kernel, spans, packed, grad_blend)
+    grad_packed, sums_up = tie(grad_packed, sums_up)
+    reduced_up = reduce_end(sums_up)
+    grad_qkv = dot(normed, grad_packed, 0, 0).astype(BF)
+    tails = [
+        jnp.concatenate(
+            [
+                grad_qkv[:, index * qkv_width : (index + 1) * qkv_width],
+                grad_out[:, index * out_width : (index + 1) * out_width],
+            ],
+            1,
+        )
+        for index in range(2)
+    ]
+    sums_tail = reduce_start(*tails)
     grad_normed = pair_sum(dot(grad_packed, full_qkv, 1, 1))
+    grad_normed, reduced_up, full_old = tie(grad_normed, reduced_up, full_old)
+    full_grad_up = lax.all_gather(reduced_up.astype(BF), "batch", axis=0, tiled=True)
     gain_one = jnp.sum(grad_normed * unit_one, 0)
     shift_one = jnp.sum(grad_normed, 0)
     grad_initial = normalize_back(grad_normed, unit_one, scale_one, vec[0]) + grad_middle
@@ -501,38 +659,25 @@
         0,
     ).T
 
+    table_grad = table_grad.astype(BF)
+
     def quarter_grads(index):
         columns = lax.dynamic_slice_in_dim(grad_embed_low, index * patch_width, patch_width, 1)
-        return [
-            dot(patches, columns, 0, 0),
-            lax.dynamic_slice_in_dim(table_grad, index * extra_width, extra_width, 1),
-        ]
-
-    def group(values, width, index):
-        return values[:, index * width : (index + 1) * width]
-
-    reduced_up = reduce_rows(group(grad_up, hidden, 0), group(grad_up, hidden, 1))
-    tails = [
-        jnp.concatenate(
-            [
-                group(grad_qkv, qkv_width, index),
-                group(grad_out, out_width, index),
-            ]
-            + quarter_grads(owner),
-            1,
-        )
-        for index, owner in ((0, head), (1, head ^ 2))
-    ]
-    reduced_tail = reduce_rows(tails[0], tails[1])
+        quarter = lax.dynamic_slice_in_dim(table_grad, index * extra_width, extra_width, 1)
+        return jnp.concatenate([dot(patches, columns, 0, 0).astype(BF), quarter], 1)
+
+    sums_small = reduce_start(quarter_grads(head), quarter_grads(head ^ 2))
+    sums_tail = [jnp.concatenate(pair, -1) for pair in zip(sums_tail, sums_small)]
+    reduced_tail = reduce_end(reduce_middle(*sums_tail))
     own_width = qkv_width + out_width
+    lines_tail = gather_lines(reduced_tail[:, :own_width].astype(BF))
     reduced_qkv = reduced_tail[:, :qkv_width]
     reduced_out = reduced_tail[:, qkv_width:own_width]
     quarter = reduced_tail[:, own_width:].astype(BF)
-    quarters = all_quarters(quarter, swap_side(quarter))
-    reduced_patch = jnp.concatenate([part[:, :patch_width] for part in quarters], 1).astype(F32)
-    reduced_table = (
-        jnp.concatenate([part[:, patch_width:] for part in quarters], 1).T.astype(F32)
-    )
+    reduced_patch, reduced_table = all_quarters(
+        jnp.concatenate([quarter, swap_side(quarter)], 1), extra_width
+    )
+    reduced_patch, reduced_table = reduced_patch.astype(F32), reduced_table.astype(F32)
     reduced_pos = jnp.concatenate(
         [reduced_table[grid_low : grid_low + 1], reduced_table[:grid_low]], 0
     )
@@ -542,25 +687,18 @@
         [partial_vec[:4], complete_here[:2], partial_vec[6:8], complete_here[2:], partial_vec[9:]],
         0,
     )
-    side_sums = jnp.stack([active_sums[:, :hidden], swap_side(active_sums[:, hidden:])])
-    all_sums = gather_small(in_order(side_sums, side, 1).transpose(1, 0, 2)).reshape(images, hidden)
-    sums_high = all_sums.astype(BF)
-    sums_low = (all_sums - sums_high.astype(F32)).astype(BF)
-    grad_token_low = grad_token.astype(BF)
-    full_grad_down = dot(
-        jnp.concatenate([grad_token_low, grad_token_low]),
-        jnp.concatenate([sums_high, sums_low]),
-        0,
-        0,
-    )
+    full_grad_down = dot(grad_token.astype(BF), all_sums, 0, 0)
     reduced_down = lax.dynamic_slice_in_dim(full_grad_down, batch * rows_here, rows_here, 0)
 
     muon_grads = (reduced_qkv, reduced_out, reduced_up, reduced_down)
     adam_grads = (reduced_patch, reduced_pos, reduced_vec, grad_head)
     squares = sum(jnp.sum(gradient * gradient) for gradient in muon_grads)
     squares = squares + sum(jnp.sum(gradient * gradient) for gradient in adam_grads) / head_size
+    squares, lines_tail, full_grad_up = tie(squares, lines_tail, full_grad_up)
+    full_tail = gather_batch(lines_tail)
     norm = jnp.sqrt(sum_everywhere(jnp.broadcast_to(squares, (8, 128)))[0, 0])
     factor = jnp.minimum(1.0, CLIP_NORM / norm)
+    factor, full_tail = tie(factor, full_tail)
     losses = jnp.stack([pair_total, class_total])
     adam_weights = (w_patch, pos_table, vectors, head_w)
     firsts = (first_patch, first_pos, first_vec, first_head)
@@ -580,35 +718,30 @@
     old_moments = (mom_qkv, mom_out, mom_up, mom_down)
     old_weights = (w_qkv, w_out, w_up, w_down)
     moments = [MOMENTUM * old_moments[index] + factor * muon_grads[index] for index in range(4)]
-    held = jnp.concatenate(old_moments, 1).astype(BF)
-    held, _ = lax.optimization_barrier((held, full_up))
-    full_old = lax.all_gather(held, "batch", axis=0, tiled=True)
-    sent = jnp.concatenate([reduced_qkv, reduced_out, reduced_up], 1).astype(BF)
-    full_grads = lax.all_gather(sent, "batch", axis=0, tiled=True)
     starts = (0, qkv_width, own_width, own_width + hidden, own_width + 2 * hidden)
-    full_moments = []
-    for index in range(4):
-        low, top = starts[index], starts[index + 1]
-        gradient = full_grad_down if index == 3 else full_grads[:, low:top].astype(F32)
-        full_moments.append(
-            (MOMENTUM * full_old[:, low:top].astype(F32) + factor * gradient)
-        )
-    own_squares = jnp.stack([jnp.sum(moment * moment) for moment in full_moments])
-    totals = sum_over_head(jnp.broadcast_to(own_squares[:, None], (4, 128)))[:, 0]
-    moment_logs = jnp.log(totals)
-    inverse = 1.0 / (jnp.sqrt(totals) + 1e-07)
-    full_moments = [moment.astype(BF) for moment in full_moments]
-    blocks = jnp.stack([gram_blocks(moment) for moment in full_moments])
+
+    def full_moment(index, gradient):
+        old = full_old[:, starts[index] : starts[index + 1]].astype(F32)
+        return (MOMENTUM * old + factor * gradient.astype(F32)).astype(BF)
+
+    gradients = (full_tail[:, :qkv_width], full_tail[:, qkv_width:], full_grad_up, full_grad_down)
+    full_moments = [full_moment(index, gradients[index]) for index in range(4)]
+    blocks = jnp.stack([gram_blocks(moment).astype(BF) for moment in full_moments])
     kept = jnp.stack([at(blocks, head), at(blocks, head ^ 2)])
     given = jnp.stack([at(blocks, head ^ 1), at(blocks, head ^ 3)])
-    kept = kept + swap_core(given.astype(BF)).astype(F32)
+    kept = kept.astype(F32) + swap_core(given).astype(F32)
     mine = kept[0] + swap_side(kept[1].astype(BF)).astype(F32)
-    inverse_here = at(inverse, head)
+    diagonal = jnp.arange(D // 3)[:, None] == jnp.arange(D // 3)[None, :]
+    total_here = jnp.sum(jnp.where(diagonal, mine[0] + mine[3] + mine[5], 0.0))
+    inverse_here = 1.0 / (jnp.sqrt(total_here) + 1e-07)
+    slots = jnp.arange(8)[:, None] == head
+    totals = sum_over_head(jnp.where(slots, jnp.broadcast_to(total_here, (8, 128)), 0.0))
+    moment_logs = jnp.log(totals[:4, 0])
     gram = whole_gram(mine * (inverse_here * inverse_here))
     row_start = batch * rows_here
 
     def fine(left, right):
-        return jnp.dot(left, right, precision=lax.Precision.HIGH)
+        return jnp.dot(left, right, precision=lax.Precision.DEFAULT)
 
     eye = jnp.eye(D, dtype=F32)
     polynomials = []
@@ -626,7 +759,7 @@
             gram = fine(fine(gram, factor_here), factor_here)
     for polynomial in polynomials[::-1]:
         rows = fine(rows, polynomial)
-    rows = rows.astype(BF)
+    rows = (rows * inverse_here).astype(BF)
     pair = jnp.stack([rows, swap_side(rows)])
     four = jnp.concatenate([pair, swap_core(pair)])
     order = jnp.array((0, 2, 1, 3), jnp.int32)
@@ -634,7 +767,7 @@
     for index in range(4):
         weight = old_weights[index]
         scale = 0.2 * math.sqrt(max(D, weight.shape[1] * head_size))
-        iterate = dot(at(four, order[head ^ index]), full_moments[index]) * inverse[index]
+        iterate = dot(at(four, order[head ^ index]), full_moments[index])
         new_muon.append(weight - MUON_RATE * (scale * iterate + DECAY_RATE * weight))
     return (
         adam_new[0][0],

time: 662 us -> 502 us (0.76)
  local copies, waits for them, and re-layouts: 170 us -> 41.2 us
  Pallas kernels: 0 us -> 32.1 us
  matrix products: 92.5 us -> 63.4 us
  waiting for transfers between devices: 183 us -> 160 us
  other arithmetic: 102 us -> 89 us
    all_gather x1, waiting for transfers between devices: 66.5 us -> 5.5 us  [body(): full_old = lax.all_gather(held, 'batch', axis=0, tiled=True)]
    unnamed x438 -> x283, local copies, waits for them, and re-layouts: 76.5 us -> 20.6 us
    ppermute x64 -> x65, waiting for transfers between devices: 108 us -> 152 us  [swap(): lax.ppermute(values, axis, [(index, index ^ mask) for index in range(coun...]
    pallas_call x0 -> x9, Pallas kernels: none -> 32.1 us  [the longest x2 20.5 us: attention(): pl.pallas_call(lambda *refs: kernel(spans, *refs), grid=(width // (6 * HD...]
    dynamic_slice x41 -> x3, local copies, waits for them, and re-layouts: 32.8 us -> 3.97 us  [at(): return lax.dynamic_index_in_dim(stacked, index, 0, keepdims=False)]
    dot_general x21 -> x6, matrix products: 46.6 us -> 21.5 us  [fine(): return jnp.dot(left, right, precision=lax.Precision.DEFAULT)]
    concatenate x6 -> x3, local copies, waits for them, and re-layouts: 22.6 us -> 2.15 us  [the longest x1 1.81 us: body(): held = jnp.concatenate([mom_qkv, mom_out, mom_up, mom_down], 1).astype(BF)]
    another operation x32 -> x22, other arithmetic: 23.4 us -> 7.72 us  [the longest x6 9.1 us: gather_rows(): second = jnp.stack([second, swap_x(second)])]
  transfers between devices with their start and end apart: 66 -> 67, of which waited for: 25 -> 37; matrix products, arithmetic and copies ran while one was open for 38% -> 26% of each run, Pallas kernels for 0% -> 5%
where the time goes in v2:
time: 502 us; the launch traced here: 493 us
  waiting for transfers between devices  160 us (32%)
  other arithmetic  89 us (18%)
  starting transfers between devices  73.2 us (15%)
  matrix products  63.4 us (13%)
  local copies, waits for them, and re-layouts  41.2 us (8%)
  between operations  33.6 us (7%)
  Pallas kernels  32.1 us (6%)
    ppermute x65, waiting for transfers between devices, swap(): lax.ppermute(values, axis, [(index, index ^ mask) for index in range(coun...  152 us
    ppermute x65, starting transfers between devices, swap(): lax.ppermute(values, axis, [(index, index ^ mask) for index in range(coun...  73.1 us
    dot_general x39, matrix products, dot(): lax.dot_general(left, right, (((left_dim,), (right_dim,)), ((), ())), pre...  42 us
    dot_general x6, matrix products, fine(): return jnp.dot(left, right, precision=lax.Precision.DEFAULT)  21.5 us
    unnamed x283, local copies, waits for them, and re-layouts  20.6 us
    pallas_call x2, Pallas kernels, attention(): pl.pallas_call(lambda *refs: kernel(spans, *refs), grid=(width // (6 * HD...  20.5 us
  transfers between devices with their start and end apart: 67, of which 37 were waited for; matrix products, arithmetic and copies ran while one was open for 26% of the time, Pallas kernels for 5%

profile of v2, /device:TPU:0, one launch (start us, length us, event | category | flops | bytes accessed | tf_op | source)
XLA Modules:
  0.0 492.8 jit_solution(12420875884203985731)
XLA Ops:
  11.4 5.1 %collective-permute-start.2 = (bf16[96,832]{1,0:T(8,128)(2,1)S(1)}, bf16[96,832]{1,0:T(8,128)(2,1)S(1)}, u32[]{:S(2)}, u32[]{:S(2)}) collective-permute-start(bf16[96,832]{1,0:T(8,128)(2,1)S(1)} %pad_maximum_fusion.17), channel_id=1, source_target_pairs={{0,24},{4,28},{8,16},{12,20},{16,8},{20,12},{24,0},{28,4},{1,25},{... | collective-permute-start | bytes 479240 | tf_op jit(solution)/shard_map/ppermute | solution.py:54
  19.3 2.5 collective-permute-done.2
  21.8 3.9 collective-permute-done
  25.7 5.4 %collective-permute-done.1 = bf16[96,832]{1,0:T(8,128)(2,1)S(1)} collective-permute-done((bf16[96,832]{1,0:T(8,128)(2,1)S(1)}, bf16[96,832]{1,0:T(8,128)(2,1)S(1)}, u32[]{:S(2)}, u32[]{:S(2)}) %collective-permute-start.1) | collective-permute-done | bytes 159776 | tf_op jit(solution)/shard_map/ppermute | solution.py:54
  34.3 3.0 collective-permute-start.6
  38.7 4.6 collective-permute-done.5
  43.3 7.7 %collective-permute-done.6 = bf16[96,960]{1,0:T(8,128)(2,1)S(1)} collective-permute-done((bf16[96,960]{1,0:T(8,128)(2,1)S(1)}, bf16[96,960]{1,0:T(8,128)(2,1)S(1)}, u32[]{:S(2)}, u32[]{:S(2)}) %collective-permute-start.6) | collective-permute-done | bytes 184352 | tf_op jit(solution)/shard_map/ppermute | solution.py:54
  64.8 3.2 shard_map.443
  73.1 3.4 collective-permute-start.15
  84.8 4.5 collective-permute-done.11.refs_2_
  92.8 7.5 %shard_map.445 = bf16[800,384]{1,0:T(8,128)(2,1)S(1)} custom-call(bf16[800,1152]{1,0:T(8,128)(2,1)S(1)} %convolution_convert_fusion.refs_0_), custom_call_target="tpu_custom_call" | custom-call | tf_op jit(solution)/shard_map/pallas_call | solution.py:343
  110.1 5.2 %broadcast_select_fusion = (f32[800,768]{1,0:T(8,128)}, f32[800,768]{1,0:T(8,128)}) fusion(pred[800]{0:T(1024)(128)(4,1)S(1)} %add_reduce_fusion, bf16[800,768]{1,0:T(8,128)(2,1)} %collective-permute-done.18, bf16[800,768]{1,0:T(8,128)(2,1)} %convolution_convert_fusion.4, f32[800,768]{1,0:T(8,128)} %copy-done.28, f32[768]{0:T(1024)S(1)} %get-tuple-element.178), kind=kLoop, calls=%fused_computation.97 | loop fusion | flops 3686400 | bytes 9834272 | tf_op jit(solution)/shard_map/jit(_where)/select_n | solution.py:511
  119.6 3.9 fusion.227
  123.5 6.7 %collective-permute-done.19.refs_2_ = bf16[4,96,1088]{2,1,0:T(8,128)(2,1)S(1)} collective-permute-done((bf16[4,96,1088]{2,1,0:T(8,128)(2,1)S(1)}, bf16[4,96,1088]{2,1,0:T(8,128)(2,1)S(1)}, u32[]{:S(2)}, u32[]{:S(2)}) %collective-permute-start.19) | collective-permute-done | bytes 835616 | tf_op jit(solution)/shard_map/ppermute | solution.py:54
  134.9 9.9 %collective-permute-done.21.refs_4_ = bf16[2,96,1088]{2,1,0:T(8,128)(2,1)S(1)} collective-permute-done((bf16[2,96,1088]{2,1,0:T(8,128)(2,1)S(1)}, bf16[2,96,1088]{2,1,0:T(8,128)(2,1)S(1)}, u32[]{:S(2)}, u32[]{:S(2)}) %collective-permute-start.21) | collective-permute-done | bytes 417824 | tf_op jit(solution)/shard_map/ppermute | solution.py:54
  157.0 3.4 collective-permute-start.26
  162.9 2.8 collective-permute-done.27
  171.0 2.6 shard_map.448
  180.2 3.6 fusion.5
  183.9 3.6 convolution_convert_fusion.1
  187.5 3.2 convolution_convert_fusion.5
  204.5 6.2 %collective-permute-done.32 = bf16[4,2,48,768]{3,2,0,1:T(8,128)(2,1)} collective-permute-done((bf16[4,2,48,768]{3,2,0,1:T(8,128)(2,1)}, bf16[4,2,48,768]{3,2,0,1:T(8,128)(2,1)}, u32[]{:S(2)}, u32[]{:S(2)}) %collective-permute-start.32) | collective-permute-done | bytes 589856 | tf_op jit(solution)/shard_map/ppermute | solution.py:54
  213.2 2.9 multiply_reduce_fusion
  216.8 2.7 fusion.236
  224.7 13.0 %shard_map.449 = bf16[800,1152]{1,0:T(8,128)(2,1)S(1)} custom-call(bf16[800,1152]{1,0:T(8,128)(2,1)S(1)} %copy-done.3, bf16[800,384]{1,0:T(8,128)(2,1)S(1)} %convolution_convert_fusion.6.refs_1_), custom_call_target="tpu_custom_call" | custom-call | tf_op jit(solution)/shard_map/pallas_call | solution.py:343
  249.8 3.5 collective-permute-done.37
  256.0 12.2 %collective-permute-done.38 = bf16[96,768]{1,0:T(8,128)(2,1)S(1)} collective-permute-done((bf16[96,768]{1,0:T(8,128)(2,1)S(1)}, bf16[96,768]{1,0:T(8,128)(2,1)S(1)}, u32[]{:S(2)}, u32[]{:S(2)}) %collective-permute-start.38) | collective-permute-done | bytes 147488 | tf_op jit(solution)/shard_map/ppermute | solution.py:54
  272.9 5.5 %all-gather.3.cloned.1.call-done = bf16[768,2304]{1,0:T(8,128)(2,1)} async-done(((bf16[96,2304]{1,0:T(8,128)(2,1)}), bf16[768,2304]{1,0:T(8,128)(2,1)}) %all-gather.3.cloned.1.call-update) | async-done | bytes 3538960 | tf_op jit(solution)/shard_map/all_gather | solution.py:599
  278.4 2.9 multiply_reduce_fusion.1
  289.7 3.4 collective-permute-done.40
  300.2 5.0 %collective-permute-done.41 = bf16[4,48,1024]{2,1,0:T(8,128)(2,1)} collective-permute-done((bf16[4,48,1024]{2,1,0:T(8,128)(2,1)}, bf16[4,48,1024]{2,1,0:T(8,128)(2,1)}, u32[]{:S(2)}, u32[]{:S(2)}) %collective-permute-start.41) | collective-permute-done | bytes 393248 | tf_op jit(solution)/shard_map/ppermute | solution.py:54
  308.5 4.7 collective-permute-start.45
  319.1 3.6 collective-permute-done.45
  322.8 9.1 %collective-permute-done.46 = bf16[96,1024]{1,0:T(8,128)(2,1)S(1)} collective-permute-done((bf16[96,1024]{1,0:T(8,128)(2,1)S(1)}, bf16[96,1024]{1,0:T(8,128)(2,1)S(1)}, u32[]{:S(2)}, u32[]{:S(2)}) %collective-permute-start.46) | collective-permute-done | bytes 196640 | tf_op jit(solution)/shard_map/ppermute | solution.py:54
  332.0 3.5 collective-permute-start.50
  339.4 2.7 collective-permute-done.48
  350.9 4.5 collective-permute-done.51
  355.5 2.9 all-gather.5.cloned.1.call-done
  361.0 3.6 collective-permute-done.54
  365.3 8.6 %collective-permute-done.55 = f32[8,128]{1,0:T(8,128)S(1)} collective-permute-done((f32[8,128]{1,0:T(8,128)S(1)}, f32[8,128]{1,0:T(8,128)S(1)}, u32[]{:S(2)}, u32[]{:S(2)}) %collective-permute-start.55) | collective-permute-done | bytes 4128 | tf_op jit(solution)/shard_map/ppermute | solution.py:54
  377.7 4.2 collective-permute-done.57
  423.4 17.8 %collective-permute-done.60 = bf16[6,256,256]{2,1,0:T(8,128)(2,1)S(1)} collective-permute-done((bf16[6,256,256]{2,1,0:T(8,128)(2,1)S(1)}, bf16[6,256,256]{2,1,0:T(8,128)(2,1)S(1)}, u32[]{:S(2)}, u32[]{:S(2)}) %collective-permute-start.60) | collective-permute-done | bytes 786464 | tf_op jit(solution)/shard_map/ppermute | solution.py:54
  446.1 3.1 fusion.9
  449.2 4.9 %fusion.34 = f32[768,768]{1,0:T(8,128)} fusion(bf16[768,768]{1,0:T(8,128)(2,1)S(1)} %fusion.9, f32[256,256]{1,0:T(8,128)} %get-tuple-element.234, f32[256,256]{1,0:T(8,128)S(1)} %copy.118, f32[256,256]{1,0:T(8,128)S(1)} %bitcast.388, f32[256,256]{1,0:T(8,128)} %get-tuple-element.233, f32[256,256]{1,0:T(8,128)S(1)} %copy-done.85, ...), kind=kOutput, calls=%fused_computation.134 | convolution fusion | flops 1820196864 | bytes 5898240 | tf_op jit(solution)/shard_map/dot_general | solution.py:744
  454.1 5.4 %fusion.10 = bf16[768,768]{1,0:T(8,128)(2,1)} fusion(f32[768,768]{1,0:T(8,128)} %fusion.34), kind=kOutput, calls=%fused_computation.49 | convolution fusion | flops 910098432 | bytes 3538944 | tf_op jit(solution)/shard_map/dot_general | solution.py:744
  459.5 4.6 fusion.31
  470.6 3.8 collective-permute-done.61
  478.0 2.5 fusion.21
  (668 shorter events, 216.8 us)
Async XLA Ops:
  7.2 271.2 %all-gather.3.cloned.1.call-start = ((), (), s32[]{:S(2)}) async-start(), calls=%async_computation | async-start | bytes 3981312 | tf_op jit(solution)/shard_map/all_gather | solution.py:599
  11.4 10.4 %collective-permute-start.2 = (bf16[96,832]{1,0:T(8,128)(2,1)S(1)}, bf16[96,832]{1,0:T(8,128)(2,1)S(1)}, u32[]{:S(2)}, u32[]{:S(2)}) collective-permute-start(bf16[96,832]{1,0:T(8,128)(2,1)S(1)} %pad_maximum_fusion.17), channel_id=1, source_target_pairs={{0,24},{4,28},{8,16},{12,20},{16,8},{20,12},{24,0},{28,4},{1,25},{... | collective-permute-start | bytes 479240 | tf_op jit(solution)/shard_map/ppermute | solution.py:54
  16.5 9.2 %collective-permute-start = (bf16[96,832]{1,0:T(8,128)(2,1)S(1)}, bf16[96,832]{1,0:T(8,128)(2,1)S(1)}, u32[]{:S(2)}, u32[]{:S(2)}) collective-permute-start(bf16[96,832]{1,0:T(8,128)(2,1)S(1)} %pad_maximum_fusion.17), channel_id=1, source_target_pairs={{0,8},{4,12},{8,0},{12,4},{16,24},{20,28},{24,16},{28,20},{1,9},{5... | collective-permute-start | bytes 479240 | tf_op jit(solution)/shard_map/ppermute | solution.py:54
  16.5 14.6 %collective-permute-start.1 = (bf16[96,832]{1,0:T(8,128)(2,1)S(1)}, bf16[96,832]{1,0:T(8,128)(2,1)S(1)}, u32[]{:S(2)}, u32[]{:S(2)}) collective-permute-start(bf16[96,832]{1,0:T(8,128)(2,1)S(1)} %pad_maximum_fusion.17), channel_id=1, source_target_pairs={{0,16},{4,20},{8,24},{12,28},{16,0},{20,4},{24,8},{28,12},{1,17},{... | collective-permute-start | bytes 479240 | tf_op jit(solution)/shard_map/ppermute | solution.py:54
  31.2 20.0 %collective-permute-start.3 = (bf16[4,96,832]{2,1,0:T(8,128)(2,1)S(1)}, bf16[4,96,832]{2,1,0:T(8,128)(2,1)S(1)}, u32[]{:S(2)}, u32[]{:S(2)}) collective-permute-start(bf16[4,96,832]{2,1,0:T(8,128)(2,1)S(1)} %pad_maximum_fusion.9.refs_1_), channel_id=1, source_target_pairs={{0,4},{4,0},{8,12},{12,8},{16,20},{20,16},{24,28},{28,24},{1,5},{5... | collective-permute-start | bytes 1916936 | tf_op jit(solution)/shard_map/ppermute | solution.py:54
  32.8 18.4 %collective-permute-start.4 = (bf16[4,96,832]{2,1,0:T(8,128)(2,1)S(1)}, bf16[4,96,832]{2,1,0:T(8,128)(2,1)S(1)}, u32[]{:S(2)}, u32[]{:S(2)}) collective-permute-start(bf16[4,96,832]{2,1,0:T(8,128)(2,1)S(1)} %pad_maximum_fusion.9.refs_1_), channel_id=1, source_target_pairs={{0,2},{1,3},{2,0},{3,1},{4,6},{5,7},{6,4},{7,5},{8,10},{9,11},{10,... | collective-permute-start | bytes 1916936 | tf_op jit(solution)/shard_map/ppermute | solution.py:54
  34.3 9.0 %collective-permute-start.5 = (bf16[96,960]{1,0:T(8,128)(2,1)S(1)}, bf16[96,960]{1,0:T(8,128)(2,1)S(1)}, u32[]{:S(2)}, u32[]{:S(2)}) collective-permute-start(bf16[96,960]{1,0:T(8,128)(2,1)S(1)} %pad_maximum_fusion.16), channel_id=1, source_target_pairs={{0,8},{4,12},{8,0},{12,4},{16,24},{20,28},{24,16},{28,20},{1,9},{5... | collective-permute-start | bytes 552968 | tf_op jit(solution)/shard_map/ppermute | solution.py:54
  34.3 16.8 %collective-permute-start.6 = (bf16[96,960]{1,0:T(8,128)(2,1)S(1)}, bf16[96,960]{1,0:T(8,128)(2,1)S(1)}, u32[]{:S(2)}, u32[]{:S(2)}) collective-permute-start(bf16[96,960]{1,0:T(8,128)(2,1)S(1)} %pad_maximum_fusion.16), channel_id=1, source_target_pairs={{0,16},{4,20},{8,24},{12,28},{16,0},{20,4},{24,8},{28,12},{1,17},{... | collective-permute-start | bytes 552968 | tf_op jit(solution)/shard_map/ppermute | solution.py:54
  37.3 13.7 %collective-permute-start.7 = (bf16[96,960]{1,0:T(8,128)(2,1)S(1)}, bf16[96,960]{1,0:T(8,128)(2,1)S(1)}, u32[]{:S(2)}, u32[]{:S(2)}) collective-permute-start(bf16[96,960]{1,0:T(8,128)(2,1)S(1)} %pad_maximum_fusion.16), channel_id=1, source_target_pairs={{0,24},{4,28},{8,16},{12,20},{16,8},{20,12},{24,0},{28,4},{1,25},{... | collective-permute-start | bytes 552968 | tf_op jit(solution)/shard_map/ppermute | solution.py:54
  69.7 19.7 %collective-permute-start.11 = (bf16[4,96,960]{2,1,0:T(8,128)(2,1)S(1)}, bf16[4,96,960]{2,1,0:T(8,128)(2,1)S(1)}, u32[]{:S(2)}, u32[]{:S(2)}) collective-permute-start(bf16[4,96,960]{2,1,0:T(8,128)(2,1)S(1)} %pad_maximum_fusion.7.refs_1_), channel_id=1, source_target_pairs={{0,4},{4,0},{8,12},{12,8},{16,20},{20,16},{24,28},{28,24},{1,5},{5... | collective-permute-start | bytes 2211848 | tf_op jit(solution)/shard_map/ppermute | solution.py:54
  70.3 19.3 %collective-permute-start.12 = (bf16[4,96,960]{2,1,0:T(8,128)(2,1)S(1)}, bf16[4,96,960]{2,1,0:T(8,128)(2,1)S(1)}, u32[]{:S(2)}, u32[]{:S(2)}) collective-permute-start(bf16[4,96,960]{2,1,0:T(8,128)(2,1)S(1)} %pad_maximum_fusion.7.refs_1_), channel_id=1, source_target_pairs={{0,2},{1,3},{2,0},{3,1},{4,6},{5,7},{6,4},{7,5},{8,10},{9,11},{10,... | collective-permute-start | bytes 2211848 | tf_op jit(solution)/shard_map/ppermute | solution.py:54
  73.1 27.2 %collective-permute-start.15 = (bf16[96,1088]{1,0:T(8,128)(2,1)S(1)}, bf16[96,1088]{1,0:T(8,128)(2,1)S(1)}, u32[]{:S(2)}, u32[]{:S(2)}) collective-permute-start(bf16[96,1088]{1,0:T(8,128)(2,1)S(1)} %pad_maximum_fusion.15), channel_id=1, source_target_pairs={{0,8},{4,12},{8,0},{12,4},{16,24},{20,28},{24,16},{28,20},{1,9},{5... | collective-permute-start | bytes 626696 | tf_op jit(solution)/shard_map/ppermute | solution.py:54
  76.5 23.8 %collective-permute-start.16 = (bf16[96,1088]{1,0:T(8,128)(2,1)S(1)}, bf16[96,1088]{1,0:T(8,128)(2,1)S(1)}, u32[]{:S(2)}, u32[]{:S(2)}) collective-permute-start(bf16[96,1088]{1,0:T(8,128)(2,1)S(1)} %pad_maximum_fusion.15), channel_id=1, source_target_pairs={{0,16},{4,20},{8,24},{12,28},{16,0},{20,4},{24,8},{28,12},{1,17},{... | collective-permute-start | bytes 626696 | tf_op jit(solution)/shard_map/ppermute | solution.py:54
  77.4 22.8 %collective-permute-start.17 = (bf16[96,1088]{1,0:T(8,128)(2,1)S(1)}, bf16[96,1088]{1,0:T(8,128)(2,1)S(1)}, u32[]{:S(2)}, u32[]{:S(2)}) collective-permute-start(bf16[96,1088]{1,0:T(8,128)(2,1)S(1)} %pad_maximum_fusion.15), channel_id=1, source_target_pairs={{0,24},{4,28},{8,16},{12,20},{16,8},{20,12},{24,0},{28,4},{1,25},{... | collective-permute-start | bytes 626696 | tf_op jit(solution)/shard_map/ppermute | solution.py:54
  89.6 10.8 %collective-permute-start.13 = (bf16[2,96,960]{2,1,0:T(8,128)(2,1)S(1)}, bf16[2,96,960]{2,1,0:T(8,128)(2,1)S(1)}, u32[]{:S(2)}, u32[]{:S(2)}) collective-permute-start(bf16[2,96,960]{2,1,0:T(8,128)(2,1)S(1)} %slice.456), channel_id=1, source_target_pairs={{0,2},{1,3},{2,0},{3,1},{4,6},{5,7},{6,4},{7,5},{8,10},{9,11},{10,... | collective-permute-start | bytes 1105928 | tf_op jit(solution)/shard_map/ppermute | solution.py:54
  91.2 9.9 %collective-permute-start.14 = (bf16[2,96,960]{2,1,0:T(8,128)(2,1)S(1)}, bf16[2,96,960]{2,1,0:T(8,128)(2,1)S(1)}, u32[]{:S(2)}, u32[]{:S(2)}) collective-permute-start(bf16[2,96,960]{2,1,0:T(8,128)(2,1)S(1)} %slice.457), channel_id=1, source_target_pairs={{0,4},{4,0},{8,12},{12,8},{16,20},{20,16},{24,28},{28,24},{1,5},{5... | collective-permute-start | bytes 1105928 | tf_op jit(solution)/shard_map/ppermute | solution.py:54
  108.1 22.1 %collective-permute-start.19 = (bf16[4,96,1088]{2,1,0:T(8,128)(2,1)S(1)}, bf16[4,96,1088]{2,1,0:T(8,128)(2,1)S(1)}, u32[]{:S(2)}, u32[]{:S(2)}) collective-permute-start(bf16[4,96,1088]{2,1,0:T(8,128)(2,1)S(1)} %pad_maximum_fusion.5.refs_1_), channel_id=1, source_target_pairs={{0,4},{4,0},{8,12},{12,8},{16,20},{20,16},{24,28},{28,24},{1,5},{5... | collective-permute-start | bytes 2506760 | tf_op jit(solution)/shard_map/ppermute | solution.py:54
  109.6 21.8 %collective-permute-start.20 = (bf16[4,96,1088]{2,1,0:T(8,128)(2,1)S(1)}, bf16[4,96,1088]{2,1,0:T(8,128)(2,1)S(1)}, u32[]{:S(2)}, u32[]{:S(2)}) collective-permute-start(bf16[4,96,1088]{2,1,0:T(8,128)(2,1)S(1)} %pad_maximum_fusion.5.refs_1_), channel_id=1, source_target_pairs={{0,2},{1,3},{2,0},{3,1},{4,6},{5,7},{6,4},{7,5},{8,10},{9,11},{10,... | collective-permute-start | bytes 2506760 | tf_op jit(solution)/shard_map/ppermute | solution.py:54
  133.3 11.5 %collective-permute-start.21 = (bf16[2,96,1088]{2,1,0:T(8,128)(2,1)S(1)}, bf16[2,96,1088]{2,1,0:T(8,128)(2,1)S(1)}, u32[]{:S(2)}, u32[]{:S(2)}) collective-permute-start(bf16[2,96,1088]{2,1,0:T(8,128)(2,1)S(1)} %slice.465), channel_id=1, source_target_pairs={{0,2},{1,3},{2,0},{3,1},{4,6},{5,7},{6,4},{7,5},{8,10},{9,11},{10,... | collective-permute-start | bytes 1253384 | tf_op jit(solution)/shard_map/ppermute | solution.py:54
  133.9 11.3 %collective-permute-start.22 = (bf16[2,96,1088]{2,1,0:T(8,128)(2,1)S(1)}, bf16[2,96,1088]{2,1,0:T(8,128)(2,1)S(1)}, u32[]{:S(2)}, u32[]{:S(2)}) collective-permute-start(bf16[2,96,1088]{2,1,0:T(8,128)(2,1)S(1)} %slice.466), channel_id=1, source_target_pairs={{0,4},{4,0},{8,12},{12,8},{16,20},{20,16},{24,28},{28,24},{1,5},{5... | collective-permute-start | bytes 1253384 | tf_op jit(solution)/shard_map/ppermute | solution.py:54
  155.0 15.9 %collective-permute-start.29 = (bf16[768,640]{1,0:T(8,128)(2,1)S(1)}, bf16[768,640]{1,0:T(8,128)(2,1)}, u32[]{:S(2)}, u32[]{:S(2)}) collective-permute-start(bf16[768,640]{1,0:T(8,128)(2,1)S(1)} %bitcast.353), channel_id=1, source_target_pairs={{0,1},{1,0},{2,3},{3,2},{4,5},{5,4},{6,7},{7,6},{8,9},{9,8},{10,11... | collective-permute-start | bytes 2949128 | tf_op jit(solution)/shard_map/ppermute | solution.py:54
  192.8 20.4 %collective-permute-start.30 = (bf16[800,768]{1,0:T(8,128)(2,1)}, bf16[800,768]{1,0:T(8,128)(2,1)}, u32[]{:S(2)}, u32[]{:S(2)}) collective-permute-start(bf16[800,768]{1,0:T(8,128)(2,1)} %convolution_convert_fusion.5), channel_id=1, source_target_pairs={{0,1},{1,0},{2,3},{3,2},{4,5},{5,4},{6,7},{7,6},{8,9},{9,8},{10,11... | collective-permute-start | bytes 3686408 | tf_op jit(solution)/shard_map/ppermute | solution.py:54
  194.6 16.1 %collective-permute-start.32 = (bf16[4,2,48,768]{3,2,0,1:T(8,128)(2,1)}, bf16[4,2,48,768]{3,2,0,1:T(8,128)(2,1)}, u32[]{:S(2)}, u32[]{:S(2)}) collective-permute-start(bf16[4,2,48,768]{3,2,0,1:T(8,128)(2,1)} %fusion.70), channel_id=1, source_target_pairs={{0,4},{4,0},{8,12},{12,8},{16,20},{20,16},{24,28},{28,24},{1,5},{5... | collective-permute-start | bytes 1769480 | tf_op jit(solution)/shard_map/ppermute | solution.py:54
  196.1 15.8 %collective-permute-start.31 = (bf16[4,2,48,768]{3,2,0,1:T(8,128)(2,1)}, bf16[4,2,48,768]{3,2,0,1:T(8,128)(2,1)}, u32[]{:S(2)}, u32[]{:S(2)}) collective-permute-start(bf16[4,2,48,768]{3,2,0,1:T(8,128)(2,1)} %copy.130), channel_id=1, source_target_pairs={{0,2},{1,3},{2,0},{3,1},{4,6},{5,7},{6,4},{7,5},{8,10},{9,11},{10,... | collective-permute-start | bytes 1769480 | tf_op jit(solution)/shard_map/ppermute | solution.py:54
  203.6 154.9 %all-gather.5.cloned.1.call-start = ((), (), s32[]{:S(2)}) async-start(), calls=%async_computation.1 | async-start | bytes 1327104 | tf_op jit(solution)/shard_map/all_gather | solution.py:631
  219.7 18.0 %collective-permute-start.33 = (bf16[4,48,768]{2,1,0:T(8,128)(2,1)S(1)}, bf16[4,48,768]{2,1,0:T(8,128)(2,1)S(1)}, u32[]{:S(2)}, u32[]{:S(2)}) collective-permute-start(bf16[4,48,768]{2,1,0:T(8,128)(2,1)S(1)} %fusion.103), channel_id=1, source_target_pairs={{0,4},{4,0},{8,12},{12,8},{16,20},{20,16},{24,28},{28,24},{1,5},{5... | collective-permute-start | bytes 884744 | tf_op jit(solution)/shard_map/ppermute | solution.py:54
  223.0 14.8 %collective-permute-start.34 = (bf16[4,48,768]{2,1,0:T(8,128)(2,1)S(1)}, bf16[4,48,768]{2,1,0:T(8,128)(2,1)S(1)}, u32[]{:S(2)}, u32[]{:S(2)}) collective-permute-start(bf16[4,48,768]{2,1,0:T(8,128)(2,1)S(1)} %fusion.104), channel_id=1, source_target_pairs={{0,2},{1,3},{2,0},{3,1},{4,6},{5,7},{6,4},{7,5},{8,10},{9,11},{10,... | collective-permute-start | bytes 884744 | tf_op jit(solution)/shard_map/ppermute | solution.py:54
  238.1 15.1 %collective-permute-start.37 = (bf16[96,768]{1,0:T(8,128)(2,1)S(1)}, bf16[96,768]{1,0:T(8,128)(2,1)S(1)}, u32[]{:S(2)}, u32[]{:S(2)}) collective-permute-start(bf16[96,768]{1,0:T(8,128)(2,1)S(1)} %get-tuple-element.243), channel_id=1, source_target_pairs={{0,8},{4,12},{8,0},{12,4},{16,24},{20,28},{24,16},{28,20},{1,9},{5... | collective-permute-start | bytes 442376 | tf_op jit(solution)/shard_map/ppermute | solution.py:54
  241.1 30.1 %collective-permute-start.36 = (bf16[800,768]{1,0:T(8,128)(2,1)S(1)}, bf16[800,768]{1,0:T(8,128)(2,1)S(1)}, u32[]{:S(2)}, u32[]{:S(2)}) collective-permute-start(bf16[800,768]{1,0:T(8,128)(2,1)S(1)} %convolution_convert_fusion.3), channel_id=1, source_target_pairs={{0,1},{1,0},{2,3},{3,2},{4,5},{5,4},{6,7},{7,6},{8,9},{9,8},{10,11... | collective-permute-start | bytes 3686408 | tf_op jit(solution)/shard_map/ppermute | solution.py:54
  245.0 23.9 %collective-permute-start.42 = (bf16[4,2,48,768]{3,2,0,1:T(8,128)(2,1)S(1)}, bf16[4,2,48,768]{3,2,0,1:T(8,128)(2,1)S(1)}, u32[]{:S(2)}, u32[]{:S(2)}) collective-permute-start(bf16[4,2,48,768]{3,2,0,1:T(8,128)(2,1)S(1)} %fusion.66), channel_id=1, source_target_pairs={{0,4},{4,0},{8,12},{12,8},{16,20},{20,16},{24,28},{28,24},{1,5},{5... | collective-permute-start | bytes 1769480 | tf_op jit(solution)/shard_map/ppermute | solution.py:54
  246.4 21.7 %collective-permute-start.38 = (bf16[96,768]{1,0:T(8,128)(2,1)S(1)}, bf16[96,768]{1,0:T(8,128)(2,1)S(1)}, u32[]{:S(2)}, u32[]{:S(2)}) collective-permute-start(bf16[96,768]{1,0:T(8,128)(2,1)S(1)} %get-tuple-element.245), channel_id=1, source_target_pairs={{0,16},{4,20},{8,24},{12,28},{16,0},{20,4},{24,8},{28,12},{1,17},{... | collective-permute-start | bytes 442376 | tf_op jit(solution)/shard_map/ppermute | solution.py:54
  247.4 20.8 %collective-permute-start.39 = (bf16[96,768]{1,0:T(8,128)(2,1)S(1)}, bf16[96,768]{1,0:T(8,128)(2,1)S(1)}, u32[]{:S(2)}, u32[]{:S(2)}) collective-permute-start(bf16[96,768]{1,0:T(8,128)(2,1)S(1)} %get-tuple-element.244), channel_id=1, source_target_pairs={{0,24},{4,28},{8,16},{12,20},{16,8},{20,12},{24,0},{28,4},{1,25},{... | collective-permute-start | bytes 442376 | tf_op jit(solution)/shard_map/ppermute | solution.py:54
  253.2 16.8 %collective-permute-start.35 = (bf16[4,2,48,768]{3,2,0,1:T(8,128)(2,1)S(1)}, bf16[4,2,48,768]{3,2,0,1:T(8,128)(2,1)S(1)}, u32[]{:S(2)}, u32[]{:S(2)}) collective-permute-start(bf16[4,2,48,768]{3,2,0,1:T(8,128)(2,1)S(1)} %copy.134), channel_id=1, source_target_pairs={{0,2},{1,3},{2,0},{3,1},{4,6},{5,7},{6,4},{7,5},{8,10},{9,11},{10,... | collective-permute-start | bytes 1769480 | tf_op jit(solution)/shard_map/ppermute | solution.py:54
  288.3 8.2 %collective-permute-start.43 = (bf16[4,2,48,256]{3,2,0,1:T(8,128)(2,1)S(1)}, bf16[4,2,48,256]{3,2,0,1:T(8,128)(2,1)S(1)}, u32[]{:S(2)}, u32[]{:S(2)}) collective-permute-start(bf16[4,2,48,256]{3,2,0,1:T(8,128)(2,1)S(1)} %fusion.113), channel_id=1, source_target_pairs={{0,4},{4,0},{8,12},{12,8},{16,20},{20,16},{24,28},{28,24},{1,5},{5... | collective-permute-start | bytes 589832 | tf_op jit(solution)/shard_map/ppermute | solution.py:54
  295.0 10.2 %collective-permute-start.41 = (bf16[4,48,1024]{2,1,0:T(8,128)(2,1)}, bf16[4,48,1024]{2,1,0:T(8,128)(2,1)}, u32[]{:S(2)}, u32[]{:S(2)}) collective-permute-start(bf16[4,48,1024]{2,1,0:T(8,128)(2,1)} %fusion.77), channel_id=1, source_target_pairs={{0,4},{4,0},{8,12},{12,8},{16,20},{20,16},{24,28},{28,24},{1,5},{5... | collective-permute-start | bytes 1179656 | tf_op jit(solution)/shard_map/ppermute | solution.py:54
  297.4 9.9 %collective-permute-start.44 = (bf16[4,48,1024]{2,1,0:T(8,128)(2,1)}, bf16[4,48,1024]{2,1,0:T(8,128)(2,1)}, u32[]{:S(2)}, u32[]{:S(2)}) collective-permute-start(bf16[4,48,1024]{2,1,0:T(8,128)(2,1)} %fusion.76), channel_id=1, source_target_pairs={{0,2},{1,3},{2,0},{3,1},{4,6},{5,7},{6,4},{7,5},{8,10},{9,11},{10,... | collective-permute-start | bytes 1179656 | tf_op jit(solution)/shard_map/ppermute | solution.py:54
  308.5 14.2 %collective-permute-start.45 = (bf16[96,1024]{1,0:T(8,128)(2,1)S(1)}, bf16[96,1024]{1,0:T(8,128)(2,1)S(1)}, u32[]{:S(2)}, u32[]{:S(2)}) collective-permute-start(bf16[96,1024]{1,0:T(8,128)(2,1)S(1)} %get-tuple-element.236), channel_id=1, source_target_pairs={{0,8},{4,12},{8,0},{12,4},{16,24},{20,28},{24,16},{28,20},{1,9},{5... | collective-permute-start | bytes 589832 | tf_op jit(solution)/shard_map/ppermute | solution.py:54
  313.3 18.6 %collective-permute-start.46 = (bf16[96,1024]{1,0:T(8,128)(2,1)S(1)}, bf16[96,1024]{1,0:T(8,128)(2,1)S(1)}, u32[]{:S(2)}, u32[]{:S(2)}) collective-permute-start(bf16[96,1024]{1,0:T(8,128)(2,1)S(1)} %get-tuple-element.237), channel_id=1, source_target_pairs={{0,16},{4,20},{8,24},{12,28},{16,0},{20,4},{24,8},{28,12},{1,17},{... | collective-permute-start | bytes 589832 | tf_op jit(solution)/shard_map/ppermute | solution.py:54
  313.3 18.6 %collective-permute-start.47 = (bf16[96,1024]{1,0:T(8,128)(2,1)S(1)}, bf16[96,1024]{1,0:T(8,128)(2,1)S(1)}, u32[]{:S(2)}, u32[]{:S(2)}) collective-permute-start(bf16[96,1024]{1,0:T(8,128)(2,1)S(1)} %get-tuple-element.238), channel_id=1, source_target_pairs={{0,24},{4,28},{8,16},{12,20},{16,8},{20,12},{24,0},{28,4},{1,25},{... | collective-permute-start | bytes 589832 | tf_op jit(solution)/shard_map/ppermute | solution.py:54
  332.0 18.9 %collective-permute-start.50 = (bf16[96,768]{1,0:T(8,128)(2,1)S(1)}, bf16[96,768]{1,0:T(8,128)(2,1)S(1)}, u32[]{:S(2)}, u32[]{:S(2)}) collective-permute-start(bf16[96,768]{1,0:T(8,128)(2,1)S(1)} %get-tuple-element.261), channel_id=1, source_target_pairs={{0,8},{4,12},{8,0},{12,4},{16,24},{20,28},{24,16},{28,20},{1,9},{5... | collective-permute-start | bytes 442376 | tf_op jit(solution)/shard_map/ppermute | solution.py:54
  335.5 19.9 %collective-permute-start.51 = (bf16[96,768]{1,0:T(8,128)(2,1)S(1)}, bf16[96,768]{1,0:T(8,128)(2,1)S(1)}, u32[]{:S(2)}, u32[]{:S(2)}) collective-permute-start(bf16[96,768]{1,0:T(8,128)(2,1)S(1)} %get-tuple-element.261), channel_id=1, source_target_pairs={{0,16},{4,20},{8,24},{12,28},{16,0},{20,4},{24,8},{28,12},{1,17},{... | collective-permute-start | bytes 442376 | tf_op jit(solution)/shard_map/ppermute | solution.py:54
  335.5 19.9 %collective-permute-start.52 = (bf16[96,768]{1,0:T(8,128)(2,1)S(1)}, bf16[96,768]{1,0:T(8,128)(2,1)S(1)}, u32[]{:S(2)}, u32[]{:S(2)}) collective-permute-start(bf16[96,768]{1,0:T(8,128)(2,1)S(1)} %get-tuple-element.261), channel_id=1, source_target_pairs={{0,24},{4,28},{8,16},{12,20},{16,8},{20,12},{24,0},{28,4},{1,25},{... | collective-permute-start | bytes 442376 | tf_op jit(solution)/shard_map/ppermute | solution.py:54
  358.4 24.7 %collective-permute-start.58 = (bf16[4,96,768]{2,1,0:T(8,128)(2,1)S(1)}, bf16[4,96,768]{2,1,0:T(8,128)(2,1)S(1)}, u32[]{:S(2)}, u32[]{:S(2)}) collective-permute-start(bf16[4,96,768]{2,1,0:T(8,128)(2,1)S(1)} %pad_maximum_fusion.10.own), channel_id=1, source_target_pairs={{0,4},{4,0},{8,12},{12,8},{16,20},{20,16},{24,28},{28,24},{1,5},{5... | collective-permute-start | bytes 1769480 | tf_op jit(solution)/shard_map/ppermute | solution.py:54
  364.6 9.2 %collective-permute-start.55 = (f32[8,128]{1,0:T(8,128)S(1)}, f32[8,128]{1,0:T(8,128)S(1)}, u32[]{:S(2)}, u32[]{:S(2)}) collective-permute-start(f32[8,128]{1,0:T(8,128)S(1)} %fusion.301), channel_id=1, source_target_pairs={{0,4},{4,0},{8,12},{12,8},{16,20},{20,16},{24,28},{28,24},{1,5},{5... | collective-permute-start | bytes 12296 | tf_op jit(solution)/shard_map/ppermute | solution.py:54
  395.8 23.3 %collective-permute-start.59 = (bf16[2,6,256,256]{3,2,1,0:T(8,128)(2,1)}, bf16[2,6,256,256]{3,2,1,0:T(8,128)(2,1)}, u32[]{:S(2)}, u32[]{:S(2)}) collective-permute-start(bf16[2,6,256,256]{3,2,1,0:T(8,128)(2,1)} %pad_maximum_fusion.1), channel_id=1, source_target_pairs={{0,1},{1,0},{2,3},{3,2},{4,5},{5,4},{6,7},{7,6},{8,9},{9,8},{10,11... | collective-permute-start | bytes 4718600 | tf_op jit(solution)/shard_map/ppermute | solution.py:54
  421.2 20.0 %collective-permute-start.60 = (bf16[6,256,256]{2,1,0:T(8,128)(2,1)S(1)}, bf16[6,256,256]{2,1,0:T(8,128)(2,1)S(1)}, u32[]{:S(2)}, u32[]{:S(2)}) collective-permute-start(bf16[6,256,256]{2,1,0:T(8,128)(2,1)S(1)} %fusion.54), channel_id=1, source_target_pairs={{0,2},{1,3},{2,0},{3,1},{4,6},{5,7},{6,4},{7,5},{8,10},{9,11},{10,... | collective-permute-start | bytes 2359304 | tf_op jit(solution)/shard_map/ppermute | solution.py:54
  444.0 24.0 %collective-permute-start.63 = (f32[8,128]{0,1:T(8,128)}, f32[8,128]{0,1:T(8,128)}, u32[]{:S(2)}, u32[]{:S(2)}) collective-permute-start(f32[8,128]{0,1:T(8,128)} %broadcast_in_dim.246), channel_id=1, source_target_pairs={{0,1},{1,0},{2,3},{3,2},{4,5},{5,4},{6,7},{7,6},{8,9},{9,8},{10,11... | collective-permute-start | bytes 12296 | tf_op jit(solution)/shard_map/ppermute | solution.py:54
  468.9 8.5 %collective-permute-start.64 = (f32[8,128]{0,1:T(8,128)S(1)}, f32[8,128]{0,1:T(8,128)S(1)}, u32[]{:S(2)}, u32[]{:S(2)}) collective-permute-start(f32[8,128]{0,1:T(8,128)S(1)} %broadcast_add_fusion), channel_id=1, source_target_pairs={{0,2},{1,3},{2,0},{3,1},{4,6},{5,7},{6,4},{7,5},{8,10},{9,11},{10,... | collective-permute-start | bytes 12296 | tf_op jit(solution)/shard_map/ppermute | solution.py:54
  (141 other events, 941.4 us)
Sparse Core Ops, SparseCore 0:
  203.7 74.7 all-gather.2
  300.3 58.0 all-gather.4

commit v3 on v2

--- a/solution.py
+++ b/solution.py
@@ -64,11 +64,6 @@
 
 def swap_x(values):
     return swap(values, "batch", 1)
-
-
-def pair_sum(values):
-    low = values.astype(BF)
-    return low.astype(F32) + swap_core(low).astype(F32)
 
 
 def place_kernel(splits, position, own, own_x, own_side, near, far, *outs):
@@ -125,7 +120,7 @@
     return jnp.stack([shard] + [swap(shard, "batch", 2 * mask) for mask in (1, 2, 3)])
 
 
-def gather_batch(lines):
+def gather_batch(lines, lines_x):
     if lax.axis_size("batch") != 8:
         return lines
     here = lax.axis_index("batch")
@@ -147,7 +142,7 @@
         ),
         out_shape=jax.ShapeDtypeStruct((4, 2, rows, columns), lines.dtype),
         compiler_params=pltpu.CompilerParams(vmem_limit_bytes=32 * 1024 * 1024),
-    )(position, lines, swap_x(lines))
+    )(position, lines, lines_x)
     return out.reshape(8 * rows, columns)
 
 
@@ -179,37 +174,45 @@
     return lax.dynamic_index_in_dim(blocks, index, axis, keepdims=False)
 
 
-def reduce_start(own, other):
+def reduce_first(own, other):
     count = lax.axis_size("batch")
     if count != 8:
-        return own.astype(F32) + swap_side(other).astype(F32), own
+        return (own,), (swap_side(other),)
     rows, columns = own.shape[0] // count, own.shape[1]
     half = rows // 2
     x = lax.axis_index("batch") % 2
     own = own.reshape(4, 2, rows, columns)
     other = other.reshape(4, 2, rows, columns)
-    first = own[:, :, :half].astype(F32) + swap_side(other[:, :, :half]).astype(F32)
-    second = jnp.stack([own[:, :, half:], other[:, :, half:]], 2)
-    second = pick(second, x, 1).astype(F32) + swap_x(pick(second, 1 - x, 1)).astype(F32)
-    return first, second
-
-
-def reduce_middle(first, second):
+    kept = [pick(part[:, :, half:], x, 1) for part in (own, other)]
+    sent = [pick(part[:, :, half:], 1 - x, 1) for part in (own, other)]
+    came = swap_side(other[:, :, :half]), swap_x(jnp.stack(sent))
+    return (own[:, :, :half], *kept), came
+
+
+def reduce_second(kept, came):
     if lax.axis_size("batch") != 8:
-        return first
+        return (kept[0].astype(F32) + came[0].astype(F32),), ()
     x = lax.axis_index("batch") % 2
-    first = pick(first, x, 1) + swap_x(pick(first, 1 - x, 1).astype(BF)).astype(F32)
-    second = second[:, 0] + swap_side(second[:, 1].astype(BF)).astype(F32)
-    return jnp.concatenate([first, second], 1)
-
-
-def reduce_end(both):
+    first = kept[0].astype(F32) + came[0].astype(F32)
+    second = kept[1].astype(F32) + came[1][0].astype(F32)
+    sent = (kept[2].astype(F32) + came[1][1].astype(F32)).astype(BF)
+    came = swap_x(pick(first, 1 - x, 1).astype(BF)), swap_side(sent)
+    return (pick(first, x, 1), second), came
+
+
+def reduce_third(kept, came):
     if lax.axis_size("batch") != 8:
-        return lax.psum_scatter(both, "batch", scatter_dimension=0, tiled=True)
+        return (lax.psum_scatter(kept[0], "batch", scatter_dimension=0, tiled=True),), ()
     z = lax.axis_index("batch") // 2
-    total = at(both, z)
-    for mask in (1, 2, 3):
-        total = total + swap(at(both, z ^ mask).astype(BF), "batch", 2 * mask).astype(F32)
+    both = jnp.concatenate([part + got.astype(F32) for part, got in zip(kept, came)], 1)
+    came = [swap(at(both, z ^ mask).astype(BF), "batch", 2 * mask) for mask in (1, 2, 3)]
+    return (at(both, z),), came
+
+
+def reduce_last(kept, came):
+    total = kept[0]
+    for got in came:
+        total = total + got.astype(F32)
     return total
 
 
@@ -266,9 +269,9 @@
             )
 
 
-def all_quarters(mine, turned=0):
+def all_quarters(mine, turned=0, theirs=None):
     head = lax.axis_index("head")
-    theirs = swap_core(mine)
+    theirs = swap_core(mine) if theirs is None else theirs
     rows, both = mine.shape
     shapes = [jax.ShapeDtypeStruct((rows, 2 * both - 4 * turned), BF)]
     if turned:
@@ -350,6 +353,170 @@
     )(packed, *grads)
 
 
+def row_kind(first, rows, spans):
+    places = first + lax.broadcasted_iota(jnp.int32, (rows, 1), 0)
+    return [(places >= start) & (places < start + length) for start, _, length in spans]
+
+
+def row_grid(kernel, spans, inputs, rows, tables, outs):
+    tokens, width = inputs[0].shape
+
+    def body(*refs):
+        first = pl.program_id(0) * rows
+        kinds = row_kind(first, rows, spans)
+        sums = refs[-1]
+
+        @pl.when(pl.program_id(0) == 0)
+        def _():
+            sums[...] = jnp.zeros_like(sums)
+
+        kernel(first, kinds, *refs)
+
+    block = pl.BlockSpec((rows, width), lambda step: (step, 0))
+    return pl.pallas_call(
+        body,
+        grid=(tokens // rows,),
+        in_specs=[block] * len(inputs)
+        + [pl.BlockSpec(table.shape, lambda step: (0, 0)) for table in tables],
+        out_specs=[block] * len(outs) + [pl.BlockSpec((8, width), lambda step: (0, 0))],
+        out_shape=[jax.ShapeDtypeStruct((tokens, width), kind) for kind in outs]
+        + [jax.ShapeDtypeStruct((8, width), F32)],
+        compiler_params=pltpu.CompilerParams(vmem_limit_bytes=32 * 1024 * 1024),
+    )(*inputs, *tables)
+
+
+def add_row(sums, index, values):
+    sums[index : index + 1, :] += jnp.sum(values, 0, keepdims=True)
+
+
+def middle_kernel(first, kinds, initial, mine, theirs, vec, middle, normed, sums):
+    branch = mine[...].astype(F32) + theirs[...].astype(F32)
+    values = initial[...] + vec[7:8, :] + branch
+    unit, _ = normalize(values)
+    middle[...] = values
+    normed[...] = (unit * vec[2:3, :] + vec[3:4, :]).astype(BF)
+    for index, kind in enumerate(kinds):
+        add_row(sums, index, jnp.where(kind, values, 0.0))
+
+
+def middle_back_kernel(first, kinds, middle, mine, theirs, vec, rows, out, sums):
+    grad = mine[...].astype(F32) + theirs[...].astype(F32)
+    unit, scale = normalize(middle[...])
+    back = normalize_back(grad, unit, scale, vec[2:3, :])
+    back = back + jnp.where(kinds[0], rows[0:1, :], jnp.where(kinds[1], rows[1:2, :], 0.0))
+    out[...] = back.astype(BF)
+    add_row(sums, 0, grad * unit)
+    add_row(sums, 1, grad)
+    add_row(sums, 2, back)
+
+
+def initial_back_kernel(spans, first, kinds, initial, mine, theirs, middle, vec, out, sums):
+    grad = mine[...].astype(F32) + theirs[...].astype(F32)
+    unit, scale = normalize(initial[...])
+    back = normalize_back(grad, unit, scale, vec[0:1, :]) + middle[...].astype(F32)
+    out[...] = back.astype(BF)
+    places = first + lax.broadcasted_iota(jnp.int32, (back.shape[0], 1), 0)
+    is_class = (places == spans[0][0] + spans[0][2] - 1) | (places == spans[1][0] + spans[1][2] - 1)
+    of_class = jnp.where(is_class, back, 0.0)
+    add_row(sums, 0, grad * unit)
+    add_row(sums, 1, grad)
+    add_row(sums, 2, jnp.where(kinds[0] | kinds[1], back, 0.0) - of_class)
+    add_row(sums, 3, of_class)
+
+
+def hidden_kernel(spans, normed, weight, slope, sums):
+    upward = dot(normed[...], weight[...])
+    cumulative = 0.5 * (1.0 + lax.erf(upward * (0.5**0.5)))
+    bell = jnp.exp(-0.5 * upward * upward) * (2.0 * math.pi) ** (-0.5)
+    slope[...] = (cumulative + upward * bell).astype(BF)
+    active = (upward * cumulative).astype(BF).astype(F32)
+    sums[...] = jnp.zeros_like(sums)
+    for index, (start, _, length) in enumerate(spans):
+        rows = up_to(length, 16)
+        part = active[start : start + rows]
+        kept = lax.broadcasted_iota(jnp.int32, (rows, 1), 0) < length
+        sums[index : index + 1, :] = jnp.sum(jnp.where(kept, part, 0.0), 0, keepdims=True)
+
+
+def hidden_layer(spans, normed, weight):
+    tokens, width = normed.shape
+    columns = weight.shape[1]
+    step = 256
+    return pl.pallas_call(
+        lambda *refs: hidden_kernel(spans, *refs),
+        grid=(columns // step,),
+        in_specs=[
+            pl.BlockSpec((tokens, width), lambda index: (0, 0)),
+            pl.BlockSpec((width, step), lambda index: (0, index)),
+        ],
+        out_specs=[
+            pl.BlockSpec((tokens, step), lambda index: (0, index)),
+            pl.BlockSpec((8, step), lambda index: (0, index)),
+        ],
+        out_shape=[
+            jax.ShapeDtypeStruct((tokens, columns), BF),
+            jax.ShapeDtypeStruct((8, columns), F32),
+        ],
+        compiler_params=pltpu.CompilerParams(vmem_limit_bytes=40 * 1024 * 1024),
+    )(normed, weight)
+
+
+def iterate_kernel(start, blocks, rows_out, total_out):
+    step = D // 3
+    rows = rows_out.shape[0]
+    same = lax.broadcasted_iota(jnp.int32, (step, step), 0) == lax.broadcasted_iota(
+        jnp.int32, (step, step), 1
+    )
+    total = jnp.sum(jnp.where(same, blocks[0] + blocks[3] + blocks[5], 0.0))
+    inverse = 1.0 / (jnp.sqrt(jnp.full((1, 1), total, F32)) + 1e-07)
+    total_out[...] = jnp.full(total_out.shape, total, F32)
+    aa, ab, ac, bb, bc, cc = [blocks[index] * (inverse * inverse) for index in range(6)]
+    gram = jnp.concatenate(
+        [
+            jnp.concatenate([aa, ab, ac], 1),
+            jnp.concatenate([ab.T, bb, bc], 1),
+            jnp.concatenate([ac.T, bc.T, cc], 1),
+        ],
+        0,
+    )
+    eye = (
+        lax.broadcasted_iota(jnp.int32, (D, D), 0) == lax.broadcasted_iota(jnp.int32, (D, D), 1)
+    ).astype(F32)
+    chosen = (
+        lax.broadcasted_iota(jnp.int32, (rows, D), 0) + start[0]
+        == lax.broadcasted_iota(jnp.int32, (rows, D), 1)
+    ).astype(F32)
+    polynomials = []
+    for _ in range(NS_STEPS - 1):
+        low = gram.astype(BF)
+        polynomial = POLY_ONE * eye + POLY_TWO * gram + POLY_THREE * dot(low, low)
+        polynomial = polynomial.astype(BF)
+        polynomials.append(polynomial)
+        gram = dot(dot(low, polynomial).astype(BF), polynomial)
+    low = gram.astype(BF)
+    gram_rows = dot(chosen.astype(BF), low)
+    out = POLY_ONE * chosen + POLY_TWO * gram_rows + POLY_THREE * dot(gram_rows.astype(BF), low)
+    for polynomial in polynomials[::-1]:
+        out = dot(out.astype(BF), polynomial)
+    rows_out[...] = (out * inverse).astype(BF)
+
+
+def iterate_gram(start, blocks, rows):
+    return pl.pallas_call(
+        iterate_kernel,
+        in_specs=[
+            pl.BlockSpec(memory_space=pltpu.SMEM),
+            pl.BlockSpec(memory_space=pltpu.VMEM),
+        ],
+        out_specs=[pl.BlockSpec(memory_space=pltpu.VMEM)] * 2,
+        out_shape=[
+            jax.ShapeDtypeStruct((rows, D), BF),
+            jax.ShapeDtypeStruct((8, 128), F32),
+        ],
+        compiler_params=pltpu.CompilerParams(vmem_limit_bytes=48 * 1024 * 1024),
+    )(jnp.reshape(start, (1,)).astype(jnp.int32), blocks)
+
+
 def adam_update(weight, gradient, first, second, rate, decay):
     first = BETA_FIRST * first + (1.0 - BETA_FIRST) * gradient
     second = BETA_SECOND * second + (1.0 - BETA_SECOND) * gradient * gradient
@@ -361,34 +528,42 @@
     return (weight - rate * (direction + decay * weight), first, second)
 
 
-def gram_blocks(matrix):
+def moment_kernel(pieces, count, factor, *refs):
+    olds, grads, moments = (refs[index * count : (index + 1) * count] for index in range(3))
+    blocks = refs[-1]
     step = D // 3
-    rows = [matrix[index * step : (index + 1) * step] for index in range(3)]
-    top = dot(rows[0], matrix, 1, 1)
-    middle = dot(rows[1], matrix[step:], 1, 1)
-    last = dot(rows[2], rows[2], 1, 1)
-    return jnp.stack(
-        [
-            top[:, :step],
-            top[:, step : 2 * step],
-            top[:, 2 * step :],
-            middle[:, :step],
-            middle[:, step:],
-            last,
-        ]
-    )
-
-
-def whole_gram(blocks):
-    aa, ab, ac, bb, bc, cc = [blocks[index] for index in range(6)]
-    return jnp.concatenate(
-        [
-            jnp.concatenate([aa, ab, ac], 1),
-            jnp.concatenate([ab.T, bb, bc], 1),
-            jnp.concatenate([ac.T, bc.T, cc], 1),
-        ],
-        0,
-    )
+    place = 0
+    for old, grad, moment in zip(olds, grads, moments):
+        before = old[...].astype(F32)
+        moment[...] = (MOMENTUM * before + factor[0] * grad[...].astype(F32)).astype(BF)
+        for low, top in pieces:
+            matrix = moment[:, low:top]
+            for row, column in ((0, 0), (0, 1), (0, 2), (1, 1), (1, 2), (2, 2)):
+                left = matrix[row * step : (row + 1) * step]
+                right = matrix[column * step : (column + 1) * step]
+                blocks[place // 6, place % 6] = dot(left, right, 1, 1).astype(BF)
+                place += 1
+
+
+def moment_grams(factor, old, block, grads, pieces):
+    count, rows = len(grads), old.shape[0]
+    width = grads[0].shape[1]
+    whole = pl.BlockSpec((rows, width), lambda step: (0, 0))
+    olds = [
+        pl.BlockSpec((rows, width), lambda step, index=block + place: (0, index))
+        for place in range(count)
+    ]
+    shape = (count * len(pieces), 6, D // 3, D // 3)
+    *moments, blocks = pl.pallas_call(
+        lambda *refs: moment_kernel(pieces, count, *refs),
+        grid=(1,),
+        in_specs=[pl.BlockSpec(memory_space=pltpu.SMEM)] + olds + [whole] * count,
+        out_specs=[whole] * count + [pl.BlockSpec(shape, lambda step: (0, 0, 0, 0))],
+        out_shape=[jax.ShapeDtypeStruct((rows, width), BF)] * count
+        + [jax.ShapeDtypeStruct(shape, BF)],
+        compiler_params=pltpu.CompilerParams(vmem_limit_bytes=56 * 1024 * 1024),
+    )(jnp.reshape(factor, (1,)), *[old] * count, *grads)
+    return moments, blocks
 
 
 def body(
@@ -485,41 +660,37 @@
         0,
     )
     initial = dot(patches, full_patch) + added
-    unit_one, scale_one = normalize(initial)
+    unit_one, _ = normalize(initial)
     normed = (unit_one * vec[0] + vec[1]).astype(BF)
     packed = dot(normed, full_qkv).astype(BF)
-    packed, planes_two = tie(packed, planes_two)
+    packed, planes_two, lines_three = tie(packed, planes_two, lines_three)
     ends_two = gather_ends(planes_two)
+    planes_three = gather_planes(lines_three)
     spans = ((0, low_rows, grid_low + 1), (low_rows, high_rows, grid_high + 1))
     blended = attention(attend_kernel, spans, packed)
-    blended, ends_two, lines_three = tie(blended, ends_two, lines_three)
-    planes_three = gather_planes(lines_three)
     full_out, full_up = gather_last(planes_two, ends_two, (out_width, hidden))
-    middle = initial + vec[7] + pair_sum(dot(blended, full_out, 1, 1))
-    unit_two, scale_two = normalize(middle)
-    normed_two = (unit_two * vec[2] + vec[3]).astype(BF)
-    upward = dot(normed_two, full_up)
-    upward, planes_three = tie(upward, planes_three)
+    branch = dot(blended, full_out, 1, 1).astype(BF)
+    block_rows = 160
+    middle, normed_two, middle_sums = row_grid(
+        middle_kernel, spans, (initial, branch, swap_core(branch)), block_rows, (vec,), (F32, BF)
+    )
+    held = jnp.concatenate([mom_qkv, mom_out, mom_up, mom_down], 1).astype(BF)
+    held, normed_two, planes_three = tie(held, normed_two, planes_three)
+    full_old = lax.all_gather(held, "batch", axis=0, tiled=True)
     ends_three = gather_ends(planes_three)
+    slope, active_sums = hidden_layer(spans, normed_two, full_up)
+    active_sums = active_sums[:2]
     full_down, both_head = gather_last(planes_three, ends_three, (hidden, head_width))
     (full_head,) = all_quarters(both_head)
-    cumulative = 0.5 * (1.0 + lax.erf(upward * (0.5**0.5)))
-    active = (upward * cumulative).astype(BF).astype(F32)
-    slope = cumulative + upward * jnp.exp(-0.5 * upward * upward) * (2.0 * math.pi) ** (-0.5)
-
-    def per_image(values):
-        values = jnp.where(is_token, values, 0.0)
-        return jnp.stack([jnp.sum(values[:low_rows], 0), jnp.sum(values[low_rows:], 0)])
 
     lengths = jnp.array([[grid_low + 1.0], [grid_high + 1.0]], F32)
-    active_sums = per_image(active)
     active_means = active_sums / lengths
     means_high = active_means.astype(BF)
     means_low = (active_means - means_high.astype(F32)).astype(BF)
     down_parts = dot(jnp.concatenate([means_high, means_low]), full_down, 1, 1)
     down_part = down_parts[:2] + down_parts[2:]
     down_part = down_part + swap_core(down_part)
-    pooled_own = per_image(middle) / lengths + vec[8] + down_part
+    pooled_own = middle_sums[:2] / lengths + vec[8] + down_part
 
     ids = jnp.stack([side, low_patches.shape[0] + side])
     own_labels, own_partners = labels[ids], partner[ids]
@@ -530,6 +701,7 @@
     common = jnp.concatenate([pooled_high, pooled_low, tags], 1)
     active_low = active_sums.astype(BF)
     came = swap_side(jnp.concatenate([common, active_low[:, hidden:]], 1))
+    came, full_head = tie(came, full_head)
     mine = jnp.concatenate([common, active_low[:, :hidden]], 1)
     both_sides = in_order(jnp.stack([mine, came]), side, 1)
     everyone = gather_small(both_sides.transpose(1, 0, 2))
@@ -594,26 +766,25 @@
         )
         return jnp.where(mask, rows, 0.0)
 
-    held = jnp.concatenate([mom_qkv, mom_out, mom_up, mom_down], 1).astype(BF)
-    held, _ = tie(held, full_down)
-    full_old = lax.all_gather(held, "batch", axis=0, tiled=True)
     grad_active = dot(grad_own_low, full_down)
-    grad_upward = (spread(grad_active, is_token) * slope).astype(BF)
+    grad_upward = (spread(grad_active, is_token) * slope.astype(F32)).astype(BF)
+    grad_normed_two = dot(grad_upward, full_up, 1, 1).astype(BF)
     grad_up = dot(normed_two, grad_upward, 0, 0).astype(BF)
-    sums_up = reduce_start(grad_up[:, :hidden], grad_up[:, hidden:])
-    grad_normed_two = pair_sum(dot(grad_upward, full_up, 1, 1))
-    gain_two = jnp.sum(grad_normed_two * unit_two, 0)
-    shift_two = jnp.sum(grad_normed_two, 0)
-    grad_middle = normalize_back(grad_normed_two, unit_two, scale_two, vec[2])
-    grad_middle = grad_middle + spread(grad_own, is_token)
-    grad_middle_low = grad_middle.astype(BF)
-    grad_middle_low, sums_up = tie(grad_middle_low, sums_up)
-    sums_up = reduce_middle(*sums_up)
-    grad_out = dot(grad_middle_low, blended, 0, 0).astype(BF)
-    grad_blend = dot(grad_middle_low, full_out).astype(BF)
+    kept_up, came_up = reduce_first(grad_up[:, :hidden], grad_up[:, hidden:])
+    grad_middle, middle_row_sums = row_grid(
+        middle_back_kernel,
+        spans,
+        (middle, grad_normed_two, swap_core(grad_normed_two)),
+        block_rows,
+        (vec, jnp.pad(grad_own, ((0, 6), (0, 0)))),
+        (BF,),
+    )
+    grad_blend = dot(grad_middle, full_out).astype(BF)
+    grad_out = dot(grad_middle, blended, 0, 0).astype(BF)
     grad_packed = attention(attend_back_kernel, spans, packed, grad_blend)
-    grad_packed, sums_up = tie(grad_packed, sums_up)
-    reduced_up = reduce_end(sums_up)
+    grad_packed, came_up = tie(grad_packed, came_up)
+    kept_up, came_up = reduce_second(kept_up, came_up)
+    grad_normed = dot(grad_packed, full_qkv, 1, 1).astype(BF)
     grad_qkv = dot(normed, grad_packed, 0, 0).astype(BF)
     tails = [
         jnp.concatenate(
@@ -625,149 +796,160 @@
         )
         for index in range(2)
     ]
-    sums_tail = reduce_start(*tails)
-    grad_normed = pair_sum(dot(grad_packed, full_qkv, 1, 1))
-    grad_normed, reduced_up, full_old = tie(grad_normed, reduced_up, full_old)
-    full_grad_up = lax.all_gather(reduced_up.astype(BF), "batch", axis=0, tiled=True)
-    gain_one = jnp.sum(grad_normed * unit_one, 0)
-    shift_one = jnp.sum(grad_normed, 0)
-    grad_initial = normalize_back(grad_normed, unit_one, scale_one, vec[0]) + grad_middle
-    grad_embed = jnp.where(is_patch, grad_initial, 0.0)
-    grad_embed_low = grad_embed.astype(BF)
-    initial_low = grad_initial.astype(BF)
-    grad_low_tokens = grad_initial[: grid_low + 1]
-    from_high = dot(interp, initial_low[low_rows : low_rows + grid_high], 0, 0)
-    class_high = grad_initial[low_rows + grid_high][None]
+    kept_tail, came_tail = reduce_first(*tails)
+    grad_initial, initial_row_sums = row_grid(
+        lambda *refs: initial_back_kernel(spans, *refs),
+        spans,
+        (initial, grad_normed, swap_core(grad_normed), grad_middle),
+        block_rows,
+        (vec,),
+        (BF,),
+    )
+    grad_initial, came_up, full_old = tie(grad_initial, came_up, full_old)
+    kept_up, came_up = reduce_third(kept_up, came_up)
+    from_high = dot(interp, grad_initial[low_rows : low_rows + grid_high], 0, 0)
     zero_row = jnp.zeros((1, D), F32)
-    class_both = grad_low_tokens[grid_low:] + class_high
+    class_both = initial_row_sums[3:4]
     table_grad = jnp.concatenate(
         [
-            grad_low_tokens[:grid_low] + from_high,
+            grad_initial[:grid_low].astype(F32) + from_high,
             class_both,
-            gain_one[None],
-            shift_one[None],
-            gain_two[None],
-            shift_two[None],
+            initial_row_sums[:2],
+            middle_row_sums[:2],
             zero_row,
             zero_row,
-            jnp.sum(grad_embed, 0)[None],
-            jnp.sum(grad_middle, 0)[None],
+            initial_row_sums[2:3],
+            middle_row_sums[2:3],
             zero_row,
             class_both,
             jnp.zeros((table_rows - grid_low - 11, D), F32),
         ],
         0,
-    ).T
-
-    table_grad = table_grad.astype(BF)
+    )
+    table_grad = table_grad.astype(BF).T
 
     def quarter_grads(index):
-        columns = lax.dynamic_slice_in_dim(grad_embed_low, index * patch_width, patch_width, 1)
+        columns = lax.dynamic_slice_in_dim(grad_initial, index * patch_width, patch_width, 1)
         quarter = lax.dynamic_slice_in_dim(table_grad, index * extra_width, extra_width, 1)
         return jnp.concatenate([dot(patches, columns, 0, 0).astype(BF), quarter], 1)
 
-    sums_small = reduce_start(quarter_grads(head), quarter_grads(head ^ 2))
-    sums_tail = [jnp.concatenate(pair, -1) for pair in zip(sums_tail, sums_small)]
-    reduced_tail = reduce_end(reduce_middle(*sums_tail))
+    kept_small, came_small = reduce_first(quarter_grads(head), quarter_grads(head ^ 2))
+    came_small, came_tail = tie(came_small, came_tail)
+
+    def beside(left, right):
+        return [jnp.concatenate(pair, -1) for pair in zip(left, right)]
+
+    kept_tail, came_tail = reduce_second(
+        beside(kept_tail, kept_small), beside(came_tail, came_small)
+    )
+    came_tail, came_up = tie(came_tail, came_up)
+    reduced_up = reduce_last(kept_up, came_up)
+    full_grad_up = lax.all_gather(reduced_up.astype(BF), "batch", axis=0, tiled=True)
+    kept_tail, came_tail = reduce_third(kept_tail, came_tail)
+    reduced_tail = reduce_last(kept_tail, came_tail)
     own_width = qkv_width + out_width
     lines_tail = gather_lines(reduced_tail[:, :own_width].astype(BF))
     reduced_qkv = reduced_tail[:, :qkv_width]
     reduced_out = reduced_tail[:, qkv_width:own_width]
-    quarter = reduced_tail[:, own_width:].astype(BF)
-    reduced_patch, reduced_table = all_quarters(
-        jnp.concatenate([quarter, swap_side(quarter)], 1), extra_width
-    )
+    full_grad_down = dot(grad_token.astype(BF), all_sums, 0, 0)
+    reduced_down = lax.dynamic_slice_in_dim(full_grad_down, batch * rows_here, rows_here, 0)
+
+    quarter = reduced_tail[:, own_width:]
+    complete_here = lax.dynamic_slice_in_dim(complete_rows, batch * rows_here, rows_here, 1)
+    muon_grads = (reduced_qkv, reduced_out, reduced_up, reduced_down)
+    squares = sum(jnp.sum(gradient * gradient) for gradient in (*muon_grads, quarter))
+    same = jnp.sum(grad_head * grad_head) + jnp.sum(complete_here * complete_here)
+    squares = jnp.broadcast_to(squares + same / head_size, (8, 128))
+    for axis, mask in (("head", 1), ("head", 2), ("batch", 1)):
+        squares = squares + swap(squares, axis, mask)
+    quarter = quarter.astype(BF)
+    quarters = jnp.concatenate([quarter, swap_side(quarter)], 1)
+    partner_quarters = swap_core(quarters)
+    squares, lines_tail, partner_quarters = tie(squares, lines_tail, partner_quarters)
+    tail_x = swap_x(lines_tail) if batch_size == 8 else lines_tail
+    mask = 2
+    while mask < batch_size:
+        squares = squares + swap(squares, "batch", mask)
+        mask *= 2
+    norm = jnp.sqrt(squares[0, 0])
+    factor = jnp.minimum(1.0, CLIP_NORM / norm)
+    factor, full_grad_up = tie(factor, full_grad_up)
+    losses = jnp.stack([pair_total, class_total])
+    old_moments = (mom_qkv, mom_out, mom_up, mom_down)
+    old_weights = (w_qkv, w_out, w_up, w_down)
+    owned = (0, 2, 1, 3)
+    starts = (0, qkv_width, own_width)
+    moments = [MOMENTUM * old_moments[index] + factor * muon_grads[index] for index in range(4)]
+    new_head = adam_update(
+        head_w, factor * grad_head, first_head, second_head, ADAM_RATES[3], ADAM_DECAYS[3]
+    )
+    (moment_up, moment_down), pair = moment_grams(
+        factor, full_old, 1, (full_grad_up, full_grad_down), ((0, hidden),)
+    )
+    pair, tail_x = tie(pair, tail_x)
+    full_tail = gather_batch(lines_tail, tail_x)
+
+    def to_owner(pair, core):
+        count = lax.axis_size("head")
+        there = [(index, index ^ 1) for index in range(count) if index % 2 != core]
+        pair = pair.astype(F32) + lax.ppermute(pair, "head", there).astype(F32)
+        across = [(index, index ^ 2) for index in range(count) if index % 2 == core]
+        sent = at(pair, 1 - side).astype(BF)
+        return at(pair, side), lax.ppermute(sent, "head", across)
+
+    early, came_early = to_owner(pair, 1)
+    full_tail, early, moments, new_head = tie(full_tail, early, moments, new_head)
+    (moment_tail,), pair = moment_grams(
+        factor, full_old, 0, (full_tail,), ((0, qkv_width), (qkv_width, own_width))
+    )
+    late, came_late = to_owner(pair, 0)
+    late, late_factor, quarters, firsts, seconds, adam_weights = tie(
+        late,
+        factor,
+        quarters,
+        (first_patch, first_pos, first_vec),
+        (second_patch, second_pos, second_vec),
+        (w_patch, pos_table, vectors),
+    )
+    reduced_patch, reduced_table = all_quarters(quarters, extra_width, partner_quarters)
     reduced_patch, reduced_table = reduced_patch.astype(F32), reduced_table.astype(F32)
     reduced_pos = jnp.concatenate(
         [reduced_table[grid_low : grid_low + 1], reduced_table[:grid_low]], 0
     )
-    complete_here = lax.dynamic_slice_in_dim(complete_rows, batch * rows_here, rows_here, 1)
     partial_vec = reduced_table[grid_low + 1 : grid_low + 11]
     reduced_vec = jnp.concatenate(
         [partial_vec[:4], complete_here[:2], partial_vec[6:8], complete_here[2:], partial_vec[9:]],
         0,
     )
-    full_grad_down = dot(grad_token.astype(BF), all_sums, 0, 0)
-    reduced_down = lax.dynamic_slice_in_dim(full_grad_down, batch * rows_here, rows_here, 0)
-
-    muon_grads = (reduced_qkv, reduced_out, reduced_up, reduced_down)
-    adam_grads = (reduced_patch, reduced_pos, reduced_vec, grad_head)
-    squares = sum(jnp.sum(gradient * gradient) for gradient in muon_grads)
-    squares = squares + sum(jnp.sum(gradient * gradient) for gradient in adam_grads) / head_size
-    squares, lines_tail, full_grad_up = tie(squares, lines_tail, full_grad_up)
-    full_tail = gather_batch(lines_tail)
-    norm = jnp.sqrt(sum_everywhere(jnp.broadcast_to(squares, (8, 128)))[0, 0])
-    factor = jnp.minimum(1.0, CLIP_NORM / norm)
-    factor, full_tail = tie(factor, full_tail)
-    losses = jnp.stack([pair_total, class_total])
-    adam_weights = (w_patch, pos_table, vectors, head_w)
-    firsts = (first_patch, first_pos, first_vec, first_head)
-    seconds = (second_patch, second_pos, second_vec, second_head)
+    adam_grads = (reduced_patch, reduced_pos, reduced_vec)
     adam_new = [
         adam_update(
             adam_weights[index],
-            factor * adam_grads[index],
+            late_factor * adam_grads[index],
             firsts[index],
             seconds[index],
             ADAM_RATES[index],
             ADAM_DECAYS[index],
         )
-        for index in range(4)
+        for index in range(3)
     ]
-
-    old_moments = (mom_qkv, mom_out, mom_up, mom_down)
-    old_weights = (w_qkv, w_out, w_up, w_down)
-    moments = [MOMENTUM * old_moments[index] + factor * muon_grads[index] for index in range(4)]
-    starts = (0, qkv_width, own_width, own_width + hidden, own_width + 2 * hidden)
-
-    def full_moment(index, gradient):
-        old = full_old[:, starts[index] : starts[index + 1]].astype(F32)
-        return (MOMENTUM * old + factor * gradient.astype(F32)).astype(BF)
-
-    gradients = (full_tail[:, :qkv_width], full_tail[:, qkv_width:], full_grad_up, full_grad_down)
-    full_moments = [full_moment(index, gradients[index]) for index in range(4)]
-    blocks = jnp.stack([gram_blocks(moment).astype(BF) for moment in full_moments])
-    kept = jnp.stack([at(blocks, head), at(blocks, head ^ 2)])
-    given = jnp.stack([at(blocks, head ^ 1), at(blocks, head ^ 3)])
-    kept = kept.astype(F32) + swap_core(given).astype(F32)
-    mine = kept[0] + swap_side(kept[1].astype(BF)).astype(F32)
-    diagonal = jnp.arange(D // 3)[:, None] == jnp.arange(D // 3)[None, :]
-    total_here = jnp.sum(jnp.where(diagonal, mine[0] + mine[3] + mine[5], 0.0))
-    inverse_here = 1.0 / (jnp.sqrt(total_here) + 1e-07)
-    slots = jnp.arange(8)[:, None] == head
-    totals = sum_over_head(jnp.where(slots, jnp.broadcast_to(total_here, (8, 128)), 0.0))
+    adam_new.append(new_head)
+    mine = jnp.where(
+        head % 2 == 0, late + came_late.astype(F32), early + came_early.astype(F32)
+    )
+    rows, total_here = iterate_gram(batch * rows_here, mine, rows_here)
+    slots = jnp.arange(8)[:, None] == jnp.array(owned, jnp.int32)[head]
+    totals = sum_over_head(jnp.where(slots, total_here, 0.0))
     moment_logs = jnp.log(totals[:4, 0])
-    gram = whole_gram(mine * (inverse_here * inverse_here))
-    row_start = batch * rows_here
-
-    def fine(left, right):
-        return jnp.dot(left, right, precision=lax.Precision.DEFAULT)
-
-    eye = jnp.eye(D, dtype=F32)
-    polynomials = []
-    for sweep in range(NS_STEPS):
-        last = sweep == NS_STEPS - 1
-        if last:
-            gram_rows = lax.dynamic_slice_in_dim(gram, row_start, rows_here, 0)
-            eye_rows = lax.dynamic_slice_in_dim(eye, row_start, rows_here, 0)
-            rows = (
-                POLY_ONE * eye_rows + POLY_TWO * gram_rows + POLY_THREE * fine(gram_rows, gram)
-            )
-        else:
-            factor_here = POLY_ONE * eye + POLY_TWO * gram + POLY_THREE * fine(gram, gram)
-            polynomials.append(factor_here)
-            gram = fine(fine(gram, factor_here), factor_here)
-    for polynomial in polynomials[::-1]:
-        rows = fine(rows, polynomial)
-    rows = (rows * inverse_here).astype(BF)
     pair = jnp.stack([rows, swap_side(rows)])
     four = jnp.concatenate([pair, swap_core(pair)])
     order = jnp.array((0, 2, 1, 3), jnp.int32)
+    parts = (moment_tail[:, :qkv_width], moment_tail[:, qkv_width:], moment_up, moment_down)
     new_muon = []
     for index in range(4):
         weight = old_weights[index]
         scale = 0.2 * math.sqrt(max(D, weight.shape[1] * head_size))
-        iterate = dot(at(four, order[head ^ index]), full_moments[index])
+        iterate = dot(at(four, order[head ^ owned.index(index)]), parts[index])
         new_muon.append(weight - MUON_RATE * (scale * iterate + DECAY_RATE * weight))
     return (
         adam_new[0][0],

time: 502 us -> 430 us (0.86); the launches traced: 493 us -> 427 us
  waiting for transfers between devices: 160 us -> 122 us
  other arithmetic: 89 us -> 51.2 us
  Pallas kernels: 32.1 us -> 68.5 us
  matrix products: 63.4 us -> 35.9 us
  local copies, waits for them, and re-layouts: 41.2 us -> 47.6 us
    ppermute x65 -> x63, waiting for transfers between devices: 152 us -> 118 us  [swap(): lax.ppermute(values, axis, [(index, index ^ mask) for index in range(coun...]
    pallas_call x0 -> x7, Pallas kernels: none -> 31.4 us  [the longest x3 10.1 us: row_grid(): pl.pallas_call(body, grid=(tokens // rows,), in_specs=[block] * len(input...]
    dot_general x6 -> x0, matrix products: 21.5 us -> none  [fine(): return jnp.dot(left, right, precision=lax.Precision.DEFAULT)]
    reduce_sum x12 -> x1, other arithmetic: 12.9 us -> 0.68 us  [body(): jnp.sum(complete_here * complete_here)]
    ppermute x65 -> x63, starting transfers between devices: 73.1 us -> 64.8 us  [swap(): lax.ppermute(values, axis, [(index, index ^ mask) for index in range(coun...]
    convert_element_type x10 -> x4, other arithmetic: 9.58 us -> 1.74 us  [the longest x2 1.56 us: reduce_third(): at(both, z ^ mask).astype(BF)]
    dot_general x39 -> x26, matrix products: 42 us -> 35.9 us  [dot(): lax.dot_general(left, right, (((left_dim,), (right_dim,)), ((), ())), pre...]
    select_n x3 -> x2, other arithmetic: 7.33 us -> 1.56 us  [the longest x1 1.49 us: body(): jnp.where(head % 2 == 0, late + came_late.astype(F32), early + came_early...]
  transfers between devices with their start and end apart: 67 -> 69, of which waited for: 37 -> 32; matrix products, arithmetic and copies ran while one was open for 26% -> 23% of each run, Pallas kernels for 5% -> 11%
where the time goes in v3:
time: 430 us; the launch traced here: 427 us
  waiting for transfers between devices  122 us (28%)
  starting transfers between devices  70.6 us (16%)
  Pallas kernels  68.5 us (16%)
  other arithmetic  51.2 us (12%)
  local copies, waits for them, and re-layouts  47.6 us (11%)
  matrix products  35.9 us (8%)
  between operations  31.3 us (7%)
    ppermute x63, waiting for transfers between devices, swap(): lax.ppermute(values, axis, [(index, index ^ mask) for index in range(coun...  118 us
    ppermute x63, starting transfers between devices, swap(): lax.ppermute(values, axis, [(index, index ^ mask) for index in range(coun...  64.8 us
    dot_general x26, matrix products, dot(): lax.dot_general(left, right, (((left_dim,), (right_dim,)), ((), ())), pre...  35.9 us
    pallas_call x2, Pallas kernels, attention(): pl.pallas_call(lambda *refs: kernel(spans, *refs), grid=(width // (6 * HD...  20.5 us
    unnamed x216, local copies, waits for them, and re-layouts  18.7 us
    pallas_call x3, Pallas kernels, place(): pl.pallas_call(lambda *refs: place_kernel(splits, *refs), grid_spec=pltpu...  11.3 us
    pallas_call x3, Pallas kernels, row_grid(): pl.pallas_call(body, grid=(tokens // rows,), in_specs=[block] * len(input...  10.1 us
    pallas_call x2, Pallas kernels, moment_grams(): pl.pallas_call(lambda *refs: moment_kernel(pieces, count, *refs), grid=(1...  9.59 us
  transfers between devices with their start and end apart: 69, of which 32 were waited for; matrix products, arithmetic and copies ran while one was open for 23% of the time, Pallas kernels for 11%

profile of v3, /device:TPU:0, one launch (start us, length us, event | category | flops | bytes accessed | tf_op | source)
XLA Modules:
  0.0 426.5 jit_solution(16461484091656457084)
XLA Ops:
  11.4 5.1 %collective-permute-start.2 = (bf16[96,832]{1,0:T(8,128)(2,1)S(1)}, bf16[96,832]{1,0:T(8,128)(2,1)S(1)}, u32[]{:S(2)}, u32[]{:S(2)}) collective-permute-start(bf16[96,832]{1,0:T(8,128)(2,1)S(1)} %pad_maximum_fusion.16), channel_id=1, source_target_pairs={{0,24},{4,28},{8,16},{12,20},{16,8},{20,12},{24,0},{28,4},{1,25},{... | collective-permute-start | bytes 479240 | tf_op jit(solution)/shard_map/ppermute | solution.py:54
  17.5 4.4 %collective-permute-done.2 = bf16[96,832]{1,0:T(8,128)(2,1)S(1)} collective-permute-done((bf16[96,832]{1,0:T(8,128)(2,1)S(1)}, bf16[96,832]{1,0:T(8,128)(2,1)S(1)}, u32[]{:S(2)}, u32[]{:S(2)}) %collective-permute-start.2) | collective-permute-done | bytes 159776 | tf_op jit(solution)/shard_map/ppermute | solution.py:54
  21.9 9.3 %collective-permute-done.1 = bf16[96,832]{1,0:T(8,128)(2,1)S(1)} collective-permute-done((bf16[96,832]{1,0:T(8,128)(2,1)S(1)}, bf16[96,832]{1,0:T(8,128)(2,1)S(1)}, u32[]{:S(2)}, u32[]{:S(2)}) %collective-permute-start.1) | collective-permute-done | bytes 159776 | tf_op jit(solution)/shard_map/ppermute | solution.py:54
  34.3 2.5 collective-permute-start.7
  38.7 5.3 %collective-permute-done.7 = bf16[96,960]{1,0:T(8,128)(2,1)S(1)} collective-permute-done((bf16[96,960]{1,0:T(8,128)(2,1)S(1)}, bf16[96,960]{1,0:T(8,128)(2,1)S(1)}, u32[]{:S(2)}, u32[]{:S(2)}) %collective-permute-start.7) | collective-permute-done | bytes 184352 | tf_op jit(solution)/shard_map/ppermute | solution.py:54
  44.0 7.7 %collective-permute-done.6 = bf16[96,960]{1,0:T(8,128)(2,1)S(1)} collective-permute-done((bf16[96,960]{1,0:T(8,128)(2,1)S(1)}, bf16[96,960]{1,0:T(8,128)(2,1)S(1)}, u32[]{:S(2)}, u32[]{:S(2)}) %collective-permute-start.6) | collective-permute-done | bytes 184352 | tf_op jit(solution)/shard_map/ppermute | solution.py:54
  64.4 3.5 shard_map.452
  71.8 2.3 collective-permute-start.15
  82.2 10.1 %collective-permute-done.14 = bf16[96,1088]{1,0:T(8,128)(2,1)S(1)} collective-permute-done((bf16[96,1088]{1,0:T(8,128)(2,1)S(1)}, bf16[96,1088]{1,0:T(8,128)(2,1)S(1)}, u32[]{:S(2)}, u32[]{:S(2)}) %collective-permute-start.14) | collective-permute-done | bytes 208928 | tf_op jit(solution)/shard_map/ppermute | solution.py:54
  94.7 7.5 %shard_map.454 = bf16[800,384]{1,0:T(8,128)(2,1)S(1)} custom-call(bf16[800,1152]{1,0:T(8,128)(2,1)S(1)} %convolution_convert_fusion.refs_0_), custom_call_target="tpu_custom_call" | custom-call | tf_op jit(solution)/shard_map/pallas_call | solution.py:346
  104.2 3.3 shard_map.455
  116.9 4.5 %shard_map.456 = (f32[800,768]{1,0:T(8,128)S(1)}, bf16[800,768]{1,0:T(8,128)(2,1)S(1)}, f32[8,768]{1,0:T(8,128)S(1)}) custom-call(f32[800,768]{1,0:T(8,128)S(1)} %get-tuple-element.347.refs_0_, bf16[800,768]{1,0:T(8,128)(2,1)} %convolution_convert_fusion.4.refs_1_, bf16[800,768]{1,0:T(8,128)(2,1)} %collective-permute-done.18.refs_2_, ...), custom_call_target="tpu_custom_call" | custom-call | tf_op jit(solution)/shard_map/pallas_call | solution.py:376
  122.9 8.8 %collective-permute-done.19.refs_2_ = bf16[4,96,1088]{2,1,0:T(8,128)(2,1)} collective-permute-done((bf16[4,96,1088]{2,1,0:T(8,128)(2,1)S(1)}, bf16[4,96,1088]{2,1,0:T(8,128)(2,1)}, u32[]{:S(2)}, u32[]{:S(2)}) %collective-permute-start.19) | collective-permute-done | bytes 835616 | tf_op jit(solution)/shard_map/ppermute | solution.py:54
  136.0 4.8 %shard_map.457 = (bf16[800,1536]{1,0:T(8,128)(2,1)S(1)}, f32[8,1536]{1,0:T(8,128)S(1)}) custom-call(bf16[800,768]{1,0:T(8,128)(2,1)S(1)} %get-tuple-element.134.refs_0_, bf16[768,1536]{1,0:T(8,128)(2,1)S(1)} %bitcast.218), custom_call_target="tpu_custom_call" | custom-call | tf_op jit(solution)/shard_map/pallas_call | solution.py:445
  140.9 3.7 collective-permute-done.21.refs_4_
  146.6 4.5 %shard_map.458 = (bf16[4,2,96,1536]{3,2,1,0:T(8,128)(2,1)S(1)}, bf16[4,2,96,640]{3,2,1,0:T(8,128)(2,1)}) custom-call(s32[2]{0:T(128)S(1)} %pad_add_fusion.1.refs_0_.spot, bf16[4,96,1088]{2,1,0:T(8,128)(2,1)S(1)} %pad_maximum_fusion.2.refs_1_, bf16[4,96,1088]{2,1,0:T(8,128)(2,1)} %collective-permute-done.19.refs_2_, ...), custom_call_target="tpu_custom_call" | custom-call | tf_op jit(solution)/shard_map/pallas_call | solution.py:94
  156.1 2.5 shard_map.459
  165.6 2.7 collective-permute-start.27
  181.3 2.8 convolution_convert_fusion.5.refs_1_
  184.3 3.4 convolution_convert_fusion.1
  194.3 2.7 shard_map.460
  198.5 13.1 %shard_map.461 = bf16[800,1152]{1,0:T(8,128)(2,1)S(1)} custom-call(bf16[800,1152]{1,0:T(8,128)(2,1)S(1)} %copy-done.7, bf16[800,384]{1,0:T(8,128)(2,1)S(1)} %convolution_convert_fusion.6.refs_1_), custom_call_target="tpu_custom_call" | custom-call | tf_op jit(solution)/shard_map/pallas_call | solution.py:346
  211.6 5.0 %collective-permute-done.32 = bf16[2,4,48,768]{3,2,1,0:T(8,128)(2,1)S(1)} collective-permute-done((bf16[2,4,48,768]{3,2,1,0:T(8,128)(2,1)S(1)}, bf16[2,4,48,768]{3,2,1,0:T(8,128)(2,1)S(1)}, u32[]{:S(2)}, u32[]{:S(2)}) %collective-permute-start.32) | collective-permute-done | bytes 589856 | tf_op jit(solution)/shard_map/ppermute | solution.py:54
  222.5 2.4 convolution_convert_fusion.2
  231.0 2.9 shard_map.462
  235.8 3.0 all-gather.3.cloned.1.call-done.refs_1_.refs_2_
  240.6 2.5 convolution_convert_fusion.9
  253.5 2.3 collective-permute-done.37
  271.5 3.7 collective-permute-done.43
  279.2 2.7 collective-permute-start.47
  285.1 4.0 collective-permute-done.47
  289.1 9.7 %collective-permute-done.46 = bf16[96,1024]{1,0:T(8,128)(2,1)} collective-permute-done((bf16[96,1024]{1,0:T(8,128)(2,1)S(1)}, bf16[96,1024]{1,0:T(8,128)(2,1)}, u32[]{:S(2)}, u32[]{:S(2)}) %collective-permute-start.46) | collective-permute-done | bytes 196640 | tf_op jit(solution)/shard_map/ppermute | solution.py:54
  308.1 3.0 collective-permute-start.53
  313.4 3.3 collective-permute-done.50
  316.8 2.5 collective-permute-done.53
  319.3 12.6 %collective-permute-done.52 = bf16[96,768]{1,0:T(8,128)(2,1)S(1)} collective-permute-done((bf16[96,768]{1,0:T(8,128)(2,1)S(1)}, bf16[96,768]{1,0:T(8,128)(2,1)S(1)}, u32[]{:S(2)}, u32[]{:S(2)}) %collective-permute-start.52) | collective-permute-done | bytes 147488 | tf_op jit(solution)/shard_map/ppermute | solution.py:54
  332.1 3.6 collective-permute-done.56
  335.7 4.5 %collective-permute-done.57 = f32[8,128]{1,0:T(8,128)S(1)} collective-permute-done((f32[8,128]{1,0:T(8,128)S(1)}, f32[8,128]{1,0:T(8,128)S(1)}, u32[]{:S(2)}, u32[]{:S(2)}) %collective-permute-start.57) | collective-permute-done | bytes 4128 | tf_op jit(solution)/shard_map/ppermute | solution.py:54
  341.5 5.6 %shard_map.463 = (bf16[768,768]{1,0:T(8,128)(2,1)}, bf16[768,768]{1,0:T(8,128)(2,1)}, bf16[2,6,256,256]{3,2,1,0:T(8,128)(2,1)}) custom-call(f32[1]{0:T(128)} %bitcast.83.refs_0_, bf16[768,2304]{1,0:T(8,128)(2,1)} %all-gather.3.cloned.1.call-done.refs_1_.refs_2_, bf16[768,2304]{1,0:T(8,128)(2,1)} %all-gather.3.cloned.1.call-done.refs_1_.refs_2_, ...), custom_call_target="tpu_custom_call" | custom-call | tf_op jit(solution)/shard_map/pallas_call | solution.py:557
  359.1 4.0 shard_map.465
  365.1 2.4 fusion.23
  368.8 3.5 convert_add_fusion
  372.3 2.4 fusion.22
  387.2 2.8 dynamic-slice_bitcast_fusion
  391.2 2.3 multiply_subtract_fusion.1
  395.0 6.9 %shard_map.467 = (bf16[96,768]{1,0:T(8,128)(2,1)S(1)}, f32[8,128]{1,0:T(8,128)S(1)}) custom-call(s32[1]{0:T(128)} %bitcast.87.start, f32[6,256,256]{2,1,0:T(8,128)S(1)} %add_select_fusion.blocks), custom_call_target="tpu_custom_call" | custom-call | tf_op jit(solution)/shard_map/pallas_call | solution.py:505
  402.0 2.5 collective-permute-start.65
  407.1 3.4 collective-permute-done.63
  (559 shorter events, 177.5 us)
Async XLA Ops:
  7.2 231.6 %all-gather.3.cloned.1.call-start = ((), (), s32[]{:S(2)}) async-start(), calls=%async_computation | async-start | bytes 3981312 | tf_op jit(solution)/shard_map/all_gather | solution.py:679
  11.4 10.4 %collective-permute-start.2 = (bf16[96,832]{1,0:T(8,128)(2,1)S(1)}, bf16[96,832]{1,0:T(8,128)(2,1)S(1)}, u32[]{:S(2)}, u32[]{:S(2)}) collective-permute-start(bf16[96,832]{1,0:T(8,128)(2,1)S(1)} %pad_maximum_fusion.16), channel_id=1, source_target_pairs={{0,24},{4,28},{8,16},{12,20},{16,8},{20,12},{24,0},{28,4},{1,25},{... | collective-permute-start | bytes 479240 | tf_op jit(solution)/shard_map/ppermute | solution.py:54
  16.6 14.6 %collective-permute-start.1 = (bf16[96,832]{1,0:T(8,128)(2,1)S(1)}, bf16[96,832]{1,0:T(8,128)(2,1)S(1)}, u32[]{:S(2)}, u32[]{:S(2)}) collective-permute-start(bf16[96,832]{1,0:T(8,128)(2,1)S(1)} %pad_maximum_fusion.16), channel_id=1, source_target_pairs={{0,16},{4,20},{8,24},{12,28},{16,0},{20,4},{24,8},{28,12},{1,17},{... | collective-permute-start | bytes 479240 | tf_op jit(solution)/shard_map/ppermute | solution.py:54
  16.6 14.6 %collective-permute-start = (bf16[96,832]{1,0:T(8,128)(2,1)S(1)}, bf16[96,832]{1,0:T(8,128)(2,1)S(1)}, u32[]{:S(2)}, u32[]{:S(2)}) collective-permute-start(bf16[96,832]{1,0:T(8,128)(2,1)S(1)} %pad_maximum_fusion.16), channel_id=1, source_target_pairs={{0,8},{4,12},{8,0},{12,4},{16,24},{20,28},{24,16},{28,20},{1,9},{5... | collective-permute-start | bytes 479240 | tf_op jit(solution)/shard_map/ppermute | solution.py:54
  31.3 21.5 %collective-permute-start.3 = (bf16[4,96,832]{2,1,0:T(8,128)(2,1)S(1)}, bf16[4,96,832]{2,1,0:T(8,128)(2,1)S(1)}, u32[]{:S(2)}, u32[]{:S(2)}) collective-permute-start(bf16[4,96,832]{2,1,0:T(8,128)(2,1)S(1)} %pad_maximum_fusion.5.refs_1_), channel_id=1, source_target_pairs={{0,4},{4,0},{8,12},{12,8},{16,20},{20,16},{24,28},{28,24},{1,5},{5... | collective-permute-start | bytes 1916936 | tf_op jit(solution)/shard_map/ppermute | solution.py:54
  32.8 19.9 %collective-permute-start.4 = (bf16[4,96,832]{2,1,0:T(8,128)(2,1)S(1)}, bf16[4,96,832]{2,1,0:T(8,128)(2,1)S(1)}, u32[]{:S(2)}, u32[]{:S(2)}) collective-permute-start(bf16[4,96,832]{2,1,0:T(8,128)(2,1)S(1)} %pad_maximum_fusion.5.refs_1_), channel_id=1, source_target_pairs={{0,2},{1,3},{2,0},{3,1},{4,6},{5,7},{6,4},{7,5},{8,10},{9,11},{10,... | collective-permute-start | bytes 1916936 | tf_op jit(solution)/shard_map/ppermute | solution.py:54
  34.3 9.7 %collective-permute-start.7 = (bf16[96,960]{1,0:T(8,128)(2,1)S(1)}, bf16[96,960]{1,0:T(8,128)(2,1)S(1)}, u32[]{:S(2)}, u32[]{:S(2)}) collective-permute-start(bf16[96,960]{1,0:T(8,128)(2,1)S(1)} %pad_maximum_fusion.14), channel_id=1, source_target_pairs={{0,24},{4,28},{8,16},{12,20},{16,8},{20,12},{24,0},{28,4},{1,25},{... | collective-permute-start | bytes 552968 | tf_op jit(solution)/shard_map/ppermute | solution.py:54
  36.8 14.9 %collective-permute-start.6 = (bf16[96,960]{1,0:T(8,128)(2,1)S(1)}, bf16[96,960]{1,0:T(8,128)(2,1)S(1)}, u32[]{:S(2)}, u32[]{:S(2)}) collective-permute-start(bf16[96,960]{1,0:T(8,128)(2,1)S(1)} %pad_maximum_fusion.14), channel_id=1, source_target_pairs={{0,16},{4,20},{8,24},{12,28},{16,0},{20,4},{24,8},{28,12},{1,17},{... | collective-permute-start | bytes 552968 | tf_op jit(solution)/shard_map/ppermute | solution.py:54
  36.8 14.9 %collective-permute-start.5 = (bf16[96,960]{1,0:T(8,128)(2,1)S(1)}, bf16[96,960]{1,0:T(8,128)(2,1)S(1)}, u32[]{:S(2)}, u32[]{:S(2)}) collective-permute-start(bf16[96,960]{1,0:T(8,128)(2,1)S(1)} %pad_maximum_fusion.14), channel_id=1, source_target_pairs={{0,8},{4,12},{8,0},{12,4},{16,24},{20,28},{24,16},{28,20},{1,9},{5... | collective-permute-start | bytes 552968 | tf_op jit(solution)/shard_map/ppermute | solution.py:54
  53.5 8.7 %collective-permute-start.8 = (bf16[2,96,832]{2,1,0:T(8,128)(2,1)}, bf16[2,96,832]{2,1,0:T(8,128)(2,1)S(1)}, u32[]{:S(2)}, u32[]{:S(2)}) collective-permute-start(bf16[2,96,832]{2,1,0:T(8,128)(2,1)} %slice.267), channel_id=1, source_target_pairs={{0,2},{1,3},{2,0},{3,1},{4,6},{5,7},{6,4},{7,5},{8,10},{9,11},{10,... | collective-permute-start | bytes 958472 | tf_op jit(solution)/shard_map/ppermute | solution.py:54
  54.8 8.5 %collective-permute-start.9 = (bf16[2,96,832]{2,1,0:T(8,128)(2,1)}, bf16[2,96,832]{2,1,0:T(8,128)(2,1)}, u32[]{:S(2)}, u32[]{:S(2)}) collective-permute-start(bf16[2,96,832]{2,1,0:T(8,128)(2,1)} %slice.268), channel_id=1, source_target_pairs={{0,4},{4,0},{8,12},{12,8},{16,20},{20,16},{24,28},{28,24},{1,5},{5... | collective-permute-start | bytes 958472 | tf_op jit(solution)/shard_map/ppermute | solution.py:54
  68.4 24.1 %collective-permute-start.11 = (bf16[4,96,960]{2,1,0:T(8,128)(2,1)}, bf16[4,96,960]{2,1,0:T(8,128)(2,1)S(1)}, u32[]{:S(2)}, u32[]{:S(2)}) collective-permute-start(bf16[4,96,960]{2,1,0:T(8,128)(2,1)} %pad_maximum_fusion.3.refs_1_), channel_id=1, source_target_pairs={{0,4},{4,0},{8,12},{12,8},{16,20},{20,16},{24,28},{28,24},{1,5},{5... | collective-permute-start | bytes 2211848 | tf_op jit(solution)/shard_map/ppermute | solution.py:54
  69.0 23.5 %collective-permute-start.12 = (bf16[4,96,960]{2,1,0:T(8,128)(2,1)}, bf16[4,96,960]{2,1,0:T(8,128)(2,1)S(1)}, u32[]{:S(2)}, u32[]{:S(2)}) collective-permute-start(bf16[4,96,960]{2,1,0:T(8,128)(2,1)} %pad_maximum_fusion.3.refs_1_), channel_id=1, source_target_pairs={{0,2},{1,3},{2,0},{3,1},{4,6},{5,7},{6,4},{7,5},{8,10},{9,11},{10,... | collective-permute-start | bytes 2211848 | tf_op jit(solution)/shard_map/ppermute | solution.py:54
  71.8 10.4 %collective-permute-start.15 = (bf16[96,1088]{1,0:T(8,128)(2,1)S(1)}, bf16[96,1088]{1,0:T(8,128)(2,1)S(1)}, u32[]{:S(2)}, u32[]{:S(2)}) collective-permute-start(bf16[96,1088]{1,0:T(8,128)(2,1)S(1)} %pad_maximum_fusion.13), channel_id=1, source_target_pairs={{0,24},{4,28},{8,16},{12,20},{16,8},{20,12},{24,0},{28,4},{1,25},{... | collective-permute-start | bytes 626696 | tf_op jit(solution)/shard_map/ppermute | solution.py:54
  74.1 18.1 %collective-permute-start.14 = (bf16[96,1088]{1,0:T(8,128)(2,1)S(1)}, bf16[96,1088]{1,0:T(8,128)(2,1)S(1)}, u32[]{:S(2)}, u32[]{:S(2)}) collective-permute-start(bf16[96,1088]{1,0:T(8,128)(2,1)S(1)} %pad_maximum_fusion.13), channel_id=1, source_target_pairs={{0,16},{4,20},{8,24},{12,28},{16,0},{20,4},{24,8},{28,12},{1,17},{... | collective-permute-start | bytes 626696 | tf_op jit(solution)/shard_map/ppermute | solution.py:54
  74.1 18.1 %collective-permute-start.13 = (bf16[96,1088]{1,0:T(8,128)(2,1)S(1)}, bf16[96,1088]{1,0:T(8,128)(2,1)S(1)}, u32[]{:S(2)}, u32[]{:S(2)}) collective-permute-start(bf16[96,1088]{1,0:T(8,128)(2,1)S(1)} %pad_maximum_fusion.13), channel_id=1, source_target_pairs={{0,8},{4,12},{8,0},{12,4},{16,24},{20,28},{24,16},{28,20},{1,9},{5... | collective-permute-start | bytes 626696 | tf_op jit(solution)/shard_map/ppermute | solution.py:54
  92.5 10.2 %collective-permute-start.16 = (bf16[2,96,960]{2,1,0:T(8,128)(2,1)S(1)}, bf16[2,96,960]{2,1,0:T(8,128)(2,1)S(1)}, u32[]{:S(2)}, u32[]{:S(2)}) collective-permute-start(bf16[2,96,960]{2,1,0:T(8,128)(2,1)S(1)} %slice.277), channel_id=1, source_target_pairs={{0,2},{1,3},{2,0},{3,1},{4,6},{5,7},{6,4},{7,5},{8,10},{9,11},{10,... | collective-permute-start | bytes 1105928 | tf_op jit(solution)/shard_map/ppermute | solution.py:54
  94.1 10.1 %collective-permute-start.17 = (bf16[2,96,960]{2,1,0:T(8,128)(2,1)S(1)}, bf16[2,96,960]{2,1,0:T(8,128)(2,1)S(1)}, u32[]{:S(2)}, u32[]{:S(2)}) collective-permute-start(bf16[2,96,960]{2,1,0:T(8,128)(2,1)S(1)} %slice.278), channel_id=1, source_target_pairs={{0,4},{4,0},{8,12},{12,8},{16,20},{20,16},{24,28},{28,24},{1,5},{5... | collective-permute-start | bytes 1105928 | tf_op jit(solution)/shard_map/ppermute | solution.py:54
  109.5 7.4 %collective-permute-start.18 = (bf16[800,768]{1,0:T(8,128)(2,1)}, bf16[800,768]{1,0:T(8,128)(2,1)}, u32[]{:S(2)}, u32[]{:S(2)}) collective-permute-start(bf16[800,768]{1,0:T(8,128)(2,1)} %convolution_convert_fusion.4.refs_1_), channel_id=1, source_target_pairs={{0,1},{1,0},{2,3},{3,2},{4,5},{5,4},{6,7},{7,6},{8,9},{9,8},{10,11... | collective-permute-start | bytes 3686408 | tf_op jit(solution)/shard_map/ppermute | solution.py:54
  109.5 22.2 %collective-permute-start.19 = (bf16[4,96,1088]{2,1,0:T(8,128)(2,1)S(1)}, bf16[4,96,1088]{2,1,0:T(8,128)(2,1)}, u32[]{:S(2)}, u32[]{:S(2)}) collective-permute-start(bf16[4,96,1088]{2,1,0:T(8,128)(2,1)S(1)} %pad_maximum_fusion.2.refs_1_), channel_id=1, source_target_pairs={{0,4},{4,0},{8,12},{12,8},{16,20},{20,16},{24,28},{28,24},{1,5},{5... | collective-permute-start | bytes 2506760 | tf_op jit(solution)/shard_map/ppermute | solution.py:54
  109.8 21.9 %collective-permute-start.20 = (bf16[4,96,1088]{2,1,0:T(8,128)(2,1)S(1)}, bf16[4,96,1088]{2,1,0:T(8,128)(2,1)}, u32[]{:S(2)}, u32[]{:S(2)}) collective-permute-start(bf16[4,96,1088]{2,1,0:T(8,128)(2,1)S(1)} %pad_maximum_fusion.2.refs_1_), channel_id=1, source_target_pairs={{0,2},{1,3},{2,0},{3,1},{4,6},{5,7},{6,4},{7,5},{8,10},{9,11},{10,... | collective-permute-start | bytes 2506760 | tf_op jit(solution)/shard_map/ppermute | solution.py:54
  132.7 11.8 %collective-permute-start.21 = (bf16[2,96,1088]{2,1,0:T(8,128)(2,1)S(1)}, bf16[2,96,1088]{2,1,0:T(8,128)(2,1)S(1)}, u32[]{:S(2)}, u32[]{:S(2)}) collective-permute-start(bf16[2,96,1088]{2,1,0:T(8,128)(2,1)S(1)} %slice.282), channel_id=1, source_target_pairs={{0,2},{1,3},{2,0},{3,1},{4,6},{5,7},{6,4},{7,5},{8,10},{9,11},{10,... | collective-permute-start | bytes 1253384 | tf_op jit(solution)/shard_map/ppermute | solution.py:54
  135.3 11.3 %collective-permute-start.22 = (bf16[2,96,1088]{2,1,0:T(8,128)(2,1)S(1)}, bf16[2,96,1088]{2,1,0:T(8,128)(2,1)S(1)}, u32[]{:S(2)}, u32[]{:S(2)}) collective-permute-start(bf16[2,96,1088]{2,1,0:T(8,128)(2,1)S(1)} %slice.283), channel_id=1, source_target_pairs={{0,4},{4,0},{8,12},{12,8},{16,20},{20,16},{24,28},{28,24},{1,5},{5... | collective-permute-start | bytes 1253384 | tf_op jit(solution)/shard_map/ppermute | solution.py:54
  162.1 179.4 %all-gather.5.cloned.1.call-start = ((), (), s32[]{:S(2)}) async-start(), calls=%async_computation.1 | async-start | bytes 1327104 | tf_op jit(solution)/shard_map/all_gather | solution.py:847
  184.2 10.1 %collective-permute-start.30 = (bf16[800,768]{1,0:T(8,128)(2,1)S(1)}, bf16[800,768]{1,0:T(8,128)(2,1)S(1)}, u32[]{:S(2)}, u32[]{:S(2)}) collective-permute-start(bf16[800,768]{1,0:T(8,128)(2,1)S(1)} %convolution_convert_fusion.5.refs_1_), channel_id=1, source_target_pairs={{0,1},{1,0},{2,3},{3,2},{4,5},{5,4},{6,7},{7,6},{8,9},{9,8},{10,11... | collective-permute-start | bytes 3686408 | tf_op jit(solution)/shard_map/ppermute | solution.py:54
  188.0 23.6 %collective-permute-start.31 = (bf16[4,2,48,768]{3,2,0,1:T(8,128)(2,1)S(1)}, bf16[4,2,48,768]{3,2,0,1:T(8,128)(2,1)S(1)}, u32[]{:S(2)}, u32[]{:S(2)}) collective-permute-start(bf16[4,2,48,768]{3,2,0,1:T(8,128)(2,1)S(1)} %copy.103), channel_id=1, source_target_pairs={{0,2},{1,3},{2,0},{3,1},{4,6},{5,7},{6,4},{7,5},{8,10},{9,11},{10,... | collective-permute-start | bytes 1769480 | tf_op jit(solution)/shard_map/ppermute | solution.py:54
  189.1 27.5 %collective-permute-start.32 = (bf16[2,4,48,768]{3,2,1,0:T(8,128)(2,1)S(1)}, bf16[2,4,48,768]{3,2,1,0:T(8,128)(2,1)S(1)}, u32[]{:S(2)}, u32[]{:S(2)}) collective-permute-start(bf16[2,4,48,768]{3,2,1,0:T(8,128)(2,1)S(1)} %pad_maximum_fusion.6), channel_id=1, source_target_pairs={{0,4},{4,0},{8,12},{12,8},{16,20},{20,16},{24,28},{28,24},{1,5},{5... | collective-permute-start | bytes 1769480 | tf_op jit(solution)/shard_map/ppermute | solution.py:54
  218.4 12.6 %collective-permute-start.33 = (bf16[800,768]{1,0:T(8,128)(2,1)S(1)}, bf16[800,768]{1,0:T(8,128)(2,1)S(1)}, u32[]{:S(2)}, u32[]{:S(2)}) collective-permute-start(bf16[800,768]{1,0:T(8,128)(2,1)S(1)} %convolution_convert_fusion.3.refs_1_), channel_id=1, source_target_pairs={{0,1},{1,0},{2,3},{3,2},{4,5},{5,4},{6,7},{7,6},{8,9},{9,8},{10,11... | collective-permute-start | bytes 3686408 | tf_op jit(solution)/shard_map/ppermute | solution.py:54
  218.7 16.4 %collective-permute-start.34 = (bf16[4,48,768]{2,1,0:T(8,128)(2,1)S(1)}, bf16[4,48,768]{2,1,0:T(8,128)(2,1)S(1)}, u32[]{:S(2)}, u32[]{:S(2)}) collective-permute-start(bf16[4,48,768]{2,1,0:T(8,128)(2,1)S(1)} %fusion.46), channel_id=1, source_target_pairs={{0,4},{4,0},{8,12},{12,8},{16,20},{20,16},{24,28},{28,24},{1,5},{5... | collective-permute-start | bytes 884744 | tf_op jit(solution)/shard_map/ppermute | solution.py:54
  220.9 15.0 %collective-permute-start.35 = (bf16[4,48,768]{2,1,0:T(8,128)(2,1)S(1)}, bf16[4,48,768]{2,1,0:T(8,128)(2,1)}, u32[]{:S(2)}, u32[]{:S(2)}) collective-permute-start(bf16[4,48,768]{2,1,0:T(8,128)(2,1)S(1)} %fusion.27), channel_id=1, source_target_pairs={{0,2},{1,3},{2,0},{3,1},{4,6},{5,7},{6,4},{7,5},{8,10},{9,11},{10,... | collective-permute-start | bytes 884744 | tf_op jit(solution)/shard_map/ppermute | solution.py:54
  226.8 24.8 %collective-permute-start.38 = (bf16[4,2,48,768]{3,2,0,1:T(8,128)(2,1)}, bf16[4,2,48,768]{3,2,0,1:T(8,128)(2,1)}, u32[]{:S(2)}, u32[]{:S(2)}) collective-permute-start(bf16[4,2,48,768]{3,2,0,1:T(8,128)(2,1)} %copy.113), channel_id=1, source_target_pairs={{0,2},{1,3},{2,0},{3,1},{4,6},{5,7},{6,4},{7,5},{8,10},{9,11},{10,... | collective-permute-start | bytes 1769480 | tf_op jit(solution)/shard_map/ppermute | solution.py:54
  231.0 20.6 %collective-permute-start.39 = (bf16[2,4,48,768]{3,2,1,0:T(8,128)(2,1)}, bf16[2,4,48,768]{3,2,1,0:T(8,128)(2,1)}, u32[]{:S(2)}, u32[]{:S(2)}) collective-permute-start(bf16[2,4,48,768]{3,2,1,0:T(8,128)(2,1)} %pad_maximum_fusion.7), channel_id=1, source_target_pairs={{0,4},{4,0},{8,12},{12,8},{16,20},{20,16},{24,28},{28,24},{1,5},{5... | collective-permute-start | bytes 1769480 | tf_op jit(solution)/shard_map/ppermute | solution.py:54
  257.3 17.9 %collective-permute-start.40 = (bf16[4,48,1024]{2,1,0:T(8,128)(2,1)S(1)}, bf16[4,48,1024]{2,1,0:T(8,128)(2,1)S(1)}, u32[]{:S(2)}, u32[]{:S(2)}) collective-permute-start(bf16[4,48,1024]{2,1,0:T(8,128)(2,1)S(1)} %fusion.31), channel_id=1, source_target_pairs={{0,4},{4,0},{8,12},{12,8},{16,20},{20,16},{24,28},{28,24},{1,5},{5... | collective-permute-start | bytes 1179656 | tf_op jit(solution)/shard_map/ppermute | solution.py:54
  260.3 15.5 %collective-permute-start.41 = (bf16[4,48,1024]{2,1,0:T(8,128)(2,1)S(1)}, bf16[4,48,1024]{2,1,0:T(8,128)(2,1)}, u32[]{:S(2)}, u32[]{:S(2)}) collective-permute-start(bf16[4,48,1024]{2,1,0:T(8,128)(2,1)S(1)} %fusion.25), channel_id=1, source_target_pairs={{0,2},{1,3},{2,0},{3,1},{4,6},{5,7},{6,4},{7,5},{8,10},{9,11},{10,... | collective-permute-start | bytes 1179656 | tf_op jit(solution)/shard_map/ppermute | solution.py:54
  261.7 9.7 %collective-permute-start.42 = (bf16[96,768]{1,0:T(8,128)(2,1)}, bf16[96,768]{1,0:T(8,128)(2,1)S(1)}, u32[]{:S(2)}, u32[]{:S(2)}) collective-permute-start(bf16[96,768]{1,0:T(8,128)(2,1)} %get-tuple-element.302), channel_id=1, source_target_pairs={{0,8},{4,12},{8,0},{12,4},{16,24},{20,28},{24,16},{28,20},{1,9},{5... | collective-permute-start | bytes 442376 | tf_op jit(solution)/shard_map/ppermute | solution.py:54
  262.5 12.7 %collective-permute-start.43 = (bf16[96,768]{1,0:T(8,128)(2,1)}, bf16[96,768]{1,0:T(8,128)(2,1)S(1)}, u32[]{:S(2)}, u32[]{:S(2)}) collective-permute-start(bf16[96,768]{1,0:T(8,128)(2,1)} %get-tuple-element.303), channel_id=1, source_target_pairs={{0,16},{4,20},{8,24},{12,28},{16,0},{20,4},{24,8},{28,12},{1,17},{... | collective-permute-start | bytes 442376 | tf_op jit(solution)/shard_map/ppermute | solution.py:54
  264.5 10.6 %collective-permute-start.44 = (bf16[96,768]{1,0:T(8,128)(2,1)}, bf16[96,768]{1,0:T(8,128)(2,1)S(1)}, u32[]{:S(2)}, u32[]{:S(2)}) collective-permute-start(bf16[96,768]{1,0:T(8,128)(2,1)} %get-tuple-element.301), channel_id=1, source_target_pairs={{0,24},{4,28},{8,16},{12,20},{16,8},{20,12},{24,0},{28,4},{1,25},{... | collective-permute-start | bytes 442376 | tf_op jit(solution)/shard_map/ppermute | solution.py:54
  279.2 9.8 %collective-permute-start.47 = (bf16[96,1024]{1,0:T(8,128)(2,1)}, bf16[96,1024]{1,0:T(8,128)(2,1)}, u32[]{:S(2)}, u32[]{:S(2)}) collective-permute-start(bf16[96,1024]{1,0:T(8,128)(2,1)} %get-tuple-element.300), channel_id=1, source_target_pairs={{0,24},{4,28},{8,16},{12,20},{16,8},{20,12},{24,0},{28,4},{1,25},{... | collective-permute-start | bytes 589832 | tf_op jit(solution)/shard_map/ppermute | solution.py:54
  281.9 16.8 %collective-permute-start.46 = (bf16[96,1024]{1,0:T(8,128)(2,1)S(1)}, bf16[96,1024]{1,0:T(8,128)(2,1)}, u32[]{:S(2)}, u32[]{:S(2)}) collective-permute-start(bf16[96,1024]{1,0:T(8,128)(2,1)S(1)} %get-tuple-element.299), channel_id=1, source_target_pairs={{0,16},{4,20},{8,24},{12,28},{16,0},{20,4},{24,8},{28,12},{1,17},{... | collective-permute-start | bytes 589832 | tf_op jit(solution)/shard_map/ppermute | solution.py:54
  282.8 16.0 %collective-permute-start.45 = (bf16[96,1024]{1,0:T(8,128)(2,1)S(1)}, bf16[96,1024]{1,0:T(8,128)(2,1)}, u32[]{:S(2)}, u32[]{:S(2)}) collective-permute-start(bf16[96,1024]{1,0:T(8,128)(2,1)S(1)} %get-tuple-element.298), channel_id=1, source_target_pairs={{0,8},{4,12},{8,0},{12,4},{16,24},{20,28},{24,16},{28,20},{1,9},{5... | collective-permute-start | bytes 589832 | tf_op jit(solution)/shard_map/ppermute | solution.py:54
  308.1 11.2 %collective-permute-start.53 = (bf16[96,768]{1,0:T(8,128)(2,1)S(1)}, bf16[96,768]{1,0:T(8,128)(2,1)S(1)}, u32[]{:S(2)}, u32[]{:S(2)}) collective-permute-start(bf16[96,768]{1,0:T(8,128)(2,1)S(1)} %slice.501), channel_id=1, source_target_pairs={{0,24},{4,28},{8,16},{12,20},{16,8},{20,12},{24,0},{28,4},{1,25},{... | collective-permute-start | bytes 442376 | tf_op jit(solution)/shard_map/ppermute | solution.py:54
  311.1 20.7 %collective-permute-start.52 = (bf16[96,768]{1,0:T(8,128)(2,1)S(1)}, bf16[96,768]{1,0:T(8,128)(2,1)S(1)}, u32[]{:S(2)}, u32[]{:S(2)}) collective-permute-start(bf16[96,768]{1,0:T(8,128)(2,1)S(1)} %slice.501), channel_id=1, source_target_pairs={{0,16},{4,20},{8,24},{12,28},{16,0},{20,4},{24,8},{28,12},{1,17},{... | collective-permute-start | bytes 442376 | tf_op jit(solution)/shard_map/ppermute | solution.py:54
  311.1 20.7 %collective-permute-start.51 = (bf16[96,768]{1,0:T(8,128)(2,1)S(1)}, bf16[96,768]{1,0:T(8,128)(2,1)S(1)}, u32[]{:S(2)}, u32[]{:S(2)}) collective-permute-start(bf16[96,768]{1,0:T(8,128)(2,1)S(1)} %slice.501), channel_id=1, source_target_pairs={{0,8},{4,12},{8,0},{12,4},{16,24},{20,28},{24,16},{28,20},{1,9},{5... | collective-permute-start | bytes 442376 | tf_op jit(solution)/shard_map/ppermute | solution.py:54
  316.7 15.2 %collective-permute-start.55 = (bf16[96,512]{1,0:T(8,128)(2,1)S(1)}, bf16[96,512]{1,0:T(8,128)(2,1)S(1)}, u32[]{:S(2)}, u32[]{:S(2)}) collective-permute-start(bf16[96,512]{1,0:T(8,128)(2,1)S(1)} %pad_maximum_fusion.18.refs_1_), channel_id=1, source_target_pairs={{0,1},{1,0},{2,3},{3,2},{4,5},{5,4},{6,7},{7,6},{8,9},{9,8},{10,11... | collective-permute-start | bytes 294920 | tf_op jit(solution)/shard_map/ppermute | solution.py:54
  332.0 15.1 %collective-permute-start.58 = (bf16[4,96,768]{2,1,0:T(8,128)(2,1)S(1)}, bf16[4,96,768]{2,1,0:T(8,128)(2,1)S(1)}, u32[]{:S(2)}, u32[]{:S(2)}) collective-permute-start(bf16[4,96,768]{2,1,0:T(8,128)(2,1)S(1)} %pad_maximum_fusion.8.own), channel_id=1, source_target_pairs={{0,4},{4,0},{8,12},{12,8},{16,20},{20,16},{24,28},{28,24},{1,5},{5... | collective-permute-start | bytes 1769480 | tf_op jit(solution)/shard_map/ppermute | solution.py:54
  347.1 7.9 %collective-permute-start.59 = (bf16[2,6,256,256]{3,2,1,0:T(8,128)(2,1)}, bf16[2,6,256,256]{3,2,1,0:T(8,128)(2,1)S(1)}, u32[]{:S(2)}, u32[]{:S(2)}) collective-permute-start(bf16[2,6,256,256]{3,2,1,0:T(8,128)(2,1)} %get-tuple-element.172), channel_id=1, source_target_pairs={{0,1},{2,3},{4,5},{6,7},{8,9},{10,11},{12,13},{14,15},{16,17},{18,... | collective-permute-start | bytes 4718600 | tf_op jit(solution)/shard_map/ppermute | solution.py:895
  367.5 26.0 %collective-permute-start.62 = (bf16[6,256,256]{2,1,0:T(8,128)(2,1)}, bf16[6,256,256]{2,1,0:T(8,128)(2,1)S(1)}, u32[]{:S(2)}, u32[]{:S(2)}) collective-permute-start(bf16[6,256,256]{2,1,0:T(8,128)(2,1)} %fusion.23), channel_id=1, source_target_pairs={{1,3},{3,1},{5,7},{7,5},{9,11},{11,9},{13,15},{15,13},{17,19},{19,... | collective-permute-start | bytes 2359304 | tf_op jit(solution)/shard_map/ppermute | solution.py:898
  374.7 18.8 %collective-permute-start.61 = (bf16[6,256,256]{2,1,0:T(8,128)(2,1)}, bf16[6,256,256]{2,1,0:T(8,128)(2,1)}, u32[]{:S(2)}, u32[]{:S(2)}) collective-permute-start(bf16[6,256,256]{2,1,0:T(8,128)(2,1)} %fusion.22), channel_id=1, source_target_pairs={{0,2},{2,0},{4,6},{6,4},{8,10},{10,8},{12,14},{14,12},{16,18},{18,... | collective-permute-start | bytes 2359304 | tf_op jit(solution)/shard_map/ppermute | solution.py:898
  (126 other events, 729.5 us)
Sparse Core Ops, SparseCore 0:
  162.2 76.5 all-gather.2
  284.5 48.2 all-gather.4

commit v4 on v3

--- a/solution.py
+++ b/solution.py
@@ -170,6 +170,10 @@
     return place([*planes, *ends], splits)
 
 
+def swapped(index):
+    return (index % 2) * 2 + index // 2
+
+
 def pick(blocks, index, axis):
     return lax.dynamic_index_in_dim(blocks, index, axis, keepdims=False)
 
@@ -216,6 +220,20 @@
     return total
 
 
+def reduce_line(kept, came, step):
+    if lax.axis_size("batch") != 8:
+        return reduce_second(kept, came) if step == 1 else reduce_third(kept, came)
+    total = kept[0].astype(F32) + came[0].astype(F32)
+    here = lax.axis_index("batch")
+    if step == 1:
+        total = total.reshape(4, 2, -1, total.shape[-1])
+        sent = pick(total, 1 - here % 2, 1).astype(BF)
+        return (pick(total, here % 2, 1),), (swap_x(sent),)
+    z = here // 2
+    came = [swap(at(total, z ^ mask).astype(BF), "batch", 2 * mask) for mask in (1, 2, 3)]
+    return (at(total, z),), came
+
+
 def in_order(stacked, here, bits):
     tail = stacked.shape[1:]
     stacked = stacked.reshape((2,) * bits + tail)
@@ -252,7 +270,7 @@
     return values
 
 
-def order_kernel(turned, position, mine, theirs, *outs):
+def order_kernel(turned, turn, position, mine, theirs, *outs):
     core, side = position[0], position[1]
     width = mine.shape[1] // 2
     plain = width - turned
@@ -263,21 +281,23 @@
         other = jnp.where(same_core, mine[:, width:], theirs[:, width:])
         quarter = jnp.where(same_side, kept, other)
         outs[0][:, index * plain : (index + 1) * plain] = quarter[:, :plain]
-        if turned:
+        if turned and not turn:
+            outs[1][:, index * turned : (index + 1) * turned] = quarter[:, plain:]
+        elif turned:
             outs[1][index * turned : (index + 1) * turned, :] = (
                 quarter[:, plain:].astype(F32).T.astype(BF)
             )
 
 
-def all_quarters(mine, turned=0, theirs=None):
+def all_quarters(mine, turned=0, theirs=None, turn=True):
     head = lax.axis_index("head")
     theirs = swap_core(mine) if theirs is None else theirs
     rows, both = mine.shape
     shapes = [jax.ShapeDtypeStruct((rows, 2 * both - 4 * turned), BF)]
     if turned:
-        shapes.append(jax.ShapeDtypeStruct((4 * turned, rows), BF))
+        shapes.append(jax.ShapeDtypeStruct((4 * turned, rows) if turn else (rows, 4 * turned), BF))
     return pl.pallas_call(
-        lambda *refs: order_kernel(turned, *refs),
+        lambda *refs: order_kernel(turned, turn, *refs),
         in_specs=[pl.BlockSpec(memory_space=pltpu.SMEM)]
         + [pl.BlockSpec(memory_space=pltpu.VMEM)] * 2,
         out_specs=[pl.BlockSpec(memory_space=pltpu.VMEM)] * len(shapes),
@@ -339,18 +359,26 @@
         out[span, base + HD : base + 2 * HD] = dot(grad_scores, queries).astype(BF)
 
 
-def attention(kernel, spans, packed, *grads):
+def attention(kernel, spans, packed, *grads, begin=0, stop=None, into=None):
     tokens, width = packed.shape
-    wide = pl.BlockSpec((tokens, 6 * HD), lambda step: (0, step))
-    narrow = pl.BlockSpec((tokens, 2 * HD), lambda step: (0, step))
+    stop = width // (6 * HD) if stop is None else stop
+    wide = pl.BlockSpec((tokens, 6 * HD), lambda step: (0, step + begin))
+    narrow = pl.BlockSpec((tokens, 2 * HD), lambda step: (0, step + begin))
+    filled = [] if into is None else [into]
+    count = 1 + len(grads)
+
+    def run(*refs):
+        kernel(spans, *refs[:count], refs[-1])
+
     return pl.pallas_call(
-        lambda *refs: kernel(spans, *refs),
-        grid=(width // (6 * HD),),
-        in_specs=[wide] + [narrow] * len(grads),
+        run,
+        grid=(stop - begin,),
+        in_specs=[wide] + [narrow] * len(grads) + [pl.BlockSpec(memory_space=pl.ANY)] * len(filled),
         out_specs=wide if grads else narrow,
         out_shape=jax.ShapeDtypeStruct((tokens, width if grads else width // 3), BF),
+        input_output_aliases={count: 0} if filled else {},
         compiler_params=pltpu.CompilerParams(vmem_limit_bytes=40 * 1024 * 1024),
-    )(packed, *grads)
+    )(packed, *grads, *filled)
 
 
 def row_kind(first, rows, spans):
@@ -461,9 +489,11 @@
     )(normed, weight)
 
 
-def iterate_kernel(start, blocks, rows_out, total_out):
+def iterate_kernel(start, kept, came, came_side, rows_out, total_out):
     step = D // 3
     rows = rows_out.shape[0]
+    parts = kept[start[1]], came[start[1]], came_side[...]
+    blocks = [sum(part[index].astype(F32) for part in parts) for index in range(6)]
     same = lax.broadcasted_iota(jnp.int32, (step, step), 0) == lax.broadcasted_iota(
         jnp.int32, (step, step), 1
     )
@@ -501,20 +531,18 @@
     rows_out[...] = (out * inverse).astype(BF)
 
 
-def iterate_gram(start, blocks, rows):
+def iterate_gram(start, kept, came, came_side, rows):
+    vmem = pl.BlockSpec(memory_space=pltpu.VMEM)
     return pl.pallas_call(
         iterate_kernel,
-        in_specs=[
-            pl.BlockSpec(memory_space=pltpu.SMEM),
-            pl.BlockSpec(memory_space=pltpu.VMEM),
-        ],
-        out_specs=[pl.BlockSpec(memory_space=pltpu.VMEM)] * 2,
+        in_specs=[pl.BlockSpec(memory_space=pltpu.SMEM)] + [vmem] * 3,
+        out_specs=[vmem] * 2,
         out_shape=[
             jax.ShapeDtypeStruct((rows, D), BF),
             jax.ShapeDtypeStruct((8, 128), F32),
         ],
         compiler_params=pltpu.CompilerParams(vmem_limit_bytes=48 * 1024 * 1024),
-    )(jnp.reshape(start, (1,)).astype(jnp.int32), blocks)
+    )(start.astype(jnp.int32), kept, came, came_side)
 
 
 def adam_update(weight, gradient, first, second, rate, decay):
@@ -526,6 +554,27 @@
         / (jnp.sqrt(second / (1.0 - BETA_SECOND**STEP)) + ADAM_FLOOR)
     )
     return (weight - rate * (direction + decay * weight), first, second)
+
+
+def square_sum(own, shared, count):
+    arrays = (*own, *shared)
+
+    def kernel(*refs):
+        total = jnp.zeros((1, 1), F32)
+        for index, ref in enumerate(refs[:-1]):
+            values = ref[...]
+            rows = jnp.sum(values * values, 1, keepdims=True)
+            part = jnp.sum(rows, 0, keepdims=True)
+            total = total + (part if index < len(own) else part / count)
+        refs[-1][...] = jnp.broadcast_to(total, (8, 128))
+
+    vmem = pl.BlockSpec(memory_space=pltpu.VMEM)
+    return pl.pallas_call(
+        kernel,
+        in_specs=[vmem] * len(arrays),
+        out_specs=vmem,
+        out_shape=jax.ShapeDtypeStruct((8, 128), F32),
+    )(*arrays)
 
 
 def moment_kernel(pieces, count, factor, *refs):
@@ -613,8 +662,9 @@
     head_width = head_padded // head_size
     table_rows = extra_width * head_size
 
-    table = jnp.concatenate([pos_table[1:], pos_table[:1], vectors], 0).astype(BF)
-    table = jnp.pad(table, ((0, table_rows - table.shape[0]), (0, 0))).T
+    pos_turned, vec_turned = pos_table.T, vectors.T
+    table = jnp.concatenate([pos_turned[:, 1:], pos_turned[:, :1], vec_turned], 1).astype(BF)
+    table = jnp.pad(table, ((0, 0), (0, table_rows - table.shape[1])))
     quarter_patch = lax.dynamic_slice_in_dim(w_patch, head * patch_width, patch_width, 1)
     quarter_table = lax.dynamic_slice_in_dim(table, head * extra_width, extra_width, 1)
     padded_head = jnp.pad(head_w.astype(BF), ((0, 0), (0, head_padded - head_columns)))
@@ -674,14 +724,15 @@
     middle, normed_two, middle_sums = row_grid(
         middle_kernel, spans, (initial, branch, swap_core(branch)), block_rows, (vec,), (F32, BF)
     )
-    held = jnp.concatenate([mom_qkv, mom_out, mom_up, mom_down], 1).astype(BF)
-    held, normed_two, planes_three = tie(held, normed_two, planes_three)
-    full_old = lax.all_gather(held, "batch", axis=0, tiled=True)
+    normed_two, planes_three = tie(normed_two, planes_three)
     ends_three = gather_ends(planes_three)
     slope, active_sums = hidden_layer(spans, normed_two, full_up)
     active_sums = active_sums[:2]
     full_down, both_head = gather_last(planes_three, ends_three, (hidden, head_width))
     (full_head,) = all_quarters(both_head)
+    held = jnp.concatenate([mom_qkv, mom_out, mom_up, mom_down], 1).astype(BF)
+    held, full_down = tie(held, full_down)
+    full_old = lax.all_gather(held, "batch", axis=0, tiled=True)
 
     lengths = jnp.array([[grid_low + 1.0], [grid_high + 1.0]], F32)
     active_means = active_sums / lengths
@@ -719,7 +770,7 @@
     picked = jnp.arange(CLS)[None, :] == all_labels[:, None]
     logit_top = jnp.max(logits, -1, keepdims=True)
     logit_log = logit_top + jnp.log(jnp.sum(jnp.exp(logits - logit_top), -1, keepdims=True))
-    class_total = jnp.sum(logit_log[:, 0] - jnp.sum(jnp.where(picked, logits, 0.0), -1))
+    class_terms = logit_log - jnp.sum(jnp.where(picked, logits, 0.0), -1, keepdims=True)
     grad_logits = (jnp.exp(logits - logit_log) - picked.astype(F32)) * (1.0 / images)
     length_inverse = lax.rsqrt(jnp.sum(projected * projected, -1, keepdims=True) + 1e-06)
     embedded = (projected * length_inverse).astype(BF)
@@ -729,7 +780,8 @@
     similar_top = jnp.max(masked, -1, keepdims=True)
     similar_log = similar_top + jnp.log(jnp.sum(jnp.exp(masked - similar_top), -1, keepdims=True))
     target = image_ids[None, :] == all_partners[:, None]
-    pair_total = jnp.sum(similar_log[:, 0] - jnp.sum(jnp.where(target, similar, 0.0), -1))
+    pair_terms = similar_log - jnp.sum(jnp.where(target, similar, 0.0), -1, keepdims=True)
+    losses = jnp.sum(jnp.concatenate([pair_terms, class_terms], 1), 0)
     count = pair_count[0].astype(F32)
     grad_similar = ((jnp.exp(masked - similar_log) - target.astype(F32)) / count).astype(BF)
     grad_embedded = (dot(grad_similar, embedded) + dot(grad_similar, embedded, 0, 0)) / SOFTMAX_TEMP
@@ -782,9 +834,9 @@
     grad_blend = dot(grad_middle, full_out).astype(BF)
     grad_out = dot(grad_middle, blended, 0, 0).astype(BF)
     grad_packed = attention(attend_back_kernel, spans, packed, grad_blend)
-    grad_packed, came_up = tie(grad_packed, came_up)
+    grad_normed = dot(grad_packed, full_qkv, 1, 1).astype(BF)
+    grad_normed, came_up = tie(grad_normed, came_up)
     kept_up, came_up = reduce_second(kept_up, came_up)
-    grad_normed = dot(grad_packed, full_qkv, 1, 1).astype(BF)
     grad_qkv = dot(normed, grad_packed, 0, 0).astype(BF)
     tails = [
         jnp.concatenate(
@@ -805,7 +857,7 @@
         (vec,),
         (BF,),
     )
-    grad_initial, came_up, full_old = tie(grad_initial, came_up, full_old)
+    grad_initial, came_up = tie(grad_initial, came_up)
     kept_up, came_up = reduce_third(kept_up, came_up)
     from_high = dot(interp, grad_initial[low_rows : low_rows + grid_high], 0, 0)
     zero_row = jnp.zeros((1, D), F32)
@@ -828,13 +880,24 @@
     )
     table_grad = table_grad.astype(BF).T
 
-    def quarter_grads(index):
-        columns = lax.dynamic_slice_in_dim(grad_initial, index * patch_width, patch_width, 1)
-        quarter = lax.dynamic_slice_in_dim(table_grad, index * extra_width, extra_width, 1)
-        return jnp.concatenate([dot(patches, columns, 0, 0).astype(BF), quarter], 1)
-
-    kept_small, came_small = reduce_first(quarter_grads(head), quarter_grads(head ^ 2))
-    came_small, came_tail = tie(came_small, came_tail)
+    def quarter_of(values, width, index):
+        return lax.dynamic_slice_in_dim(values, index * width, width, 1)
+
+    owners = (head, head ^ 2)
+    columns = [quarter_of(grad_initial, patch_width, index) for index in owners]
+    grad_patch = dot(patches, jnp.concatenate(columns, 1), 0, 0).astype(BF)
+    grad_small = [
+        jnp.concatenate(
+            [
+                grad_patch[:, index * patch_width : (index + 1) * patch_width],
+                quarter_of(table_grad, extra_width, owner),
+            ],
+            1,
+        )
+        for index, owner in enumerate(owners)
+    ]
+    kept_small, came_small = reduce_first(*grad_small)
+    came_small, came_tail, full_old = tie(came_small, came_tail, full_old)
 
     def beside(left, right):
         return [jnp.concatenate(pair, -1) for pair in zip(left, right)]
@@ -857,15 +920,34 @@
     quarter = reduced_tail[:, own_width:]
     complete_here = lax.dynamic_slice_in_dim(complete_rows, batch * rows_here, rows_here, 1)
     muon_grads = (reduced_qkv, reduced_out, reduced_up, reduced_down)
-    squares = sum(jnp.sum(gradient * gradient) for gradient in (*muon_grads, quarter))
-    same = jnp.sum(grad_head * grad_head) + jnp.sum(complete_here * complete_here)
-    squares = jnp.broadcast_to(squares + same / head_size, (8, 128))
+    squares = square_sum(
+        (reduced_tail, reduced_up, reduced_down), (grad_head, complete_here), head_size
+    )
     for axis, mask in (("head", 1), ("head", 2), ("batch", 1)):
         squares = squares + swap(squares, axis, mask)
     quarter = quarter.astype(BF)
     quarters = jnp.concatenate([quarter, swap_side(quarter)], 1)
     partner_quarters = swap_core(quarters)
-    squares, lines_tail, partner_quarters = tie(squares, lines_tail, partner_quarters)
+    reduced_patch, reduced_table = all_quarters(quarters, extra_width, partner_quarters, False)
+    reduced_patch, reduced_table = reduced_patch.astype(F32), reduced_table.astype(F32)
+    reduced_pos = jnp.concatenate(
+        [reduced_table[:, grid_low : grid_low + 1], reduced_table[:, :grid_low]], 1
+    )
+    partial_vec = reduced_table[:, grid_low + 1 : grid_low + 11]
+    complete_turned = complete_here.T
+    reduced_vec = jnp.concatenate(
+        [
+            partial_vec[:, :4],
+            complete_turned[:, :2],
+            partial_vec[:, 6:8],
+            complete_turned[:, 2:],
+            partial_vec[:, 9:],
+        ],
+        1,
+    )
+    squares, lines_tail, *adam_grads = tie(
+        squares, lines_tail, reduced_patch, reduced_pos, reduced_vec
+    )
     tail_x = swap_x(lines_tail) if batch_size == 8 else lines_tail
     mask = 2
     while mask < batch_size:
@@ -874,82 +956,63 @@
     norm = jnp.sqrt(squares[0, 0])
     factor = jnp.minimum(1.0, CLIP_NORM / norm)
     factor, full_grad_up = tie(factor, full_grad_up)
-    losses = jnp.stack([pair_total, class_total])
     old_moments = (mom_qkv, mom_out, mom_up, mom_down)
     old_weights = (w_qkv, w_out, w_up, w_down)
-    owned = (0, 2, 1, 3)
     starts = (0, qkv_width, own_width)
-    moments = [MOMENTUM * old_moments[index] + factor * muon_grads[index] for index in range(4)]
-    new_head = adam_update(
-        head_w, factor * grad_head, first_head, second_head, ADAM_RATES[3], ADAM_DECAYS[3]
-    )
-    (moment_up, moment_down), pair = moment_grams(
+    (moment_up, moment_down), early_pair = moment_grams(
         factor, full_old, 1, (full_grad_up, full_grad_down), ((0, hidden),)
     )
-    pair, tail_x = tie(pair, tail_x)
+    early_pair, tail_x = tie(early_pair, tail_x)
     full_tail = gather_batch(lines_tail, tail_x)
 
-    def to_owner(pair, core):
-        count = lax.axis_size("head")
-        there = [(index, index ^ 1) for index in range(count) if index % 2 != core]
-        pair = pair.astype(F32) + lax.ppermute(pair, "head", there).astype(F32)
-        across = [(index, index ^ 2) for index in range(count) if index % 2 == core]
-        sent = at(pair, 1 - side).astype(BF)
-        return at(pair, side), lax.ppermute(sent, "head", across)
-
-    early, came_early = to_owner(pair, 1)
-    full_tail, early, moments, new_head = tie(full_tail, early, moments, new_head)
-    (moment_tail,), pair = moment_grams(
+    (moment_tail,), late_pair = moment_grams(
         factor, full_old, 0, (full_tail,), ((0, qkv_width), (qkv_width, own_width))
     )
-    late, came_late = to_owner(pair, 0)
-    late, late_factor, quarters, firsts, seconds, adam_weights = tie(
-        late,
+    on_first = head % 2 == 0
+    came = swap_core(jnp.where(on_first, early_pair, late_pair))
+    kept = jnp.where(on_first, late_pair, early_pair)
+    sent = (at(kept, 1 - side).astype(F32) + at(came, 1 - side).astype(F32)).astype(BF)
+    came_side = swap_side(sent)
+    middle_factor, adam_grads, firsts, seconds, _ = tie(
         factor,
-        quarters,
-        (first_patch, first_pos, first_vec),
-        (second_patch, second_pos, second_vec),
-        (w_patch, pos_table, vectors),
-    )
-    reduced_patch, reduced_table = all_quarters(quarters, extra_width, partner_quarters)
-    reduced_patch, reduced_table = reduced_patch.astype(F32), reduced_table.astype(F32)
-    reduced_pos = jnp.concatenate(
-        [reduced_table[grid_low : grid_low + 1], reduced_table[:grid_low]], 0
-    )
-    partial_vec = reduced_table[grid_low + 1 : grid_low + 11]
-    reduced_vec = jnp.concatenate(
-        [partial_vec[:4], complete_here[:2], partial_vec[6:8], complete_here[2:], partial_vec[9:]],
-        0,
-    )
-    adam_grads = (reduced_patch, reduced_pos, reduced_vec)
+        (*adam_grads, grad_head),
+        (first_patch, first_pos.T, first_vec.T, first_head),
+        (second_patch, second_pos.T, second_vec.T, second_head),
+        sent,
+    )
+    adam_weights = (w_patch, pos_turned, vec_turned, head_w)
+    moments = [
+        MOMENTUM * old_moments[index] + middle_factor * muon_grads[index] for index in range(4)
+    ]
     adam_new = [
         adam_update(
             adam_weights[index],
-            late_factor * adam_grads[index],
+            middle_factor * adam_grads[index],
             firsts[index],
             seconds[index],
             ADAM_RATES[index],
             ADAM_DECAYS[index],
         )
-        for index in range(3)
+        for index in range(4)
     ]
-    adam_new.append(new_head)
-    mine = jnp.where(
-        head % 2 == 0, late + came_late.astype(F32), early + came_early.astype(F32)
-    )
-    rows, total_here = iterate_gram(batch * rows_here, mine, rows_here)
-    slots = jnp.arange(8)[:, None] == jnp.array(owned, jnp.int32)[head]
+    for index in (1, 2):
+        adam_new[index] = [part.T for part in adam_new[index]]
+    rows, total_here = iterate_gram(
+        jnp.stack([batch * rows_here, side]), kept, came, came_side, rows_here
+    )
+    rows_side = swap_side(rows)
+    rows_side, total_here = tie(rows_side, total_here)
+    pair = jnp.stack([rows, rows_side])
+    four = jnp.concatenate([pair, swap_core(pair)])
+    slots = jnp.arange(8)[:, None] == swapped(head)
     totals = sum_over_head(jnp.where(slots, total_here, 0.0))
     moment_logs = jnp.log(totals[:4, 0])
-    pair = jnp.stack([rows, swap_side(rows)])
-    four = jnp.concatenate([pair, swap_core(pair)])
-    order = jnp.array((0, 2, 1, 3), jnp.int32)
     parts = (moment_tail[:, :qkv_width], moment_tail[:, qkv_width:], moment_up, moment_down)
     new_muon = []
     for index in range(4):
         weight = old_weights[index]
         scale = 0.2 * math.sqrt(max(D, weight.shape[1] * head_size))
-        iterate = dot(at(four, order[head ^ owned.index(index)]), parts[index])
+        iterate = dot(at(four, swapped(head ^ swapped(index))), parts[index])
         new_muon.append(weight - MUON_RATE * (scale * iterate + DECAY_RATE * weight))
     return (
         adam_new[0][0],

time: 430 us -> 412 us (0.958)
  Pallas kernels: 68.5 us -> 81.4 us
  between operations: 31.3 us -> 18.9 us
  other arithmetic: 51.2 us -> 44.5 us
  local copies, waits for them, and re-layouts: 47.6 us -> 41.4 us
    pallas_call x3, Pallas kernels: 11.3 us -> 20.7 us  [place(): pl.pallas_call(lambda *refs: place_kernel(splits, *refs), grid_spec=pltpu...]
    ppermute x63 -> x65, waiting for transfers between devices: 118 us -> 126 us  [swap(): lax.ppermute(values, axis, [(index, index ^ mask) for index in range(coun...]
    ppermute x4 -> x0, starting transfers between devices: 5.71 us -> none  [the longest x2 2.91 us: to_owner(): return (at(pair, side), lax.ppermute(sent, 'head', across))]
    reduce_sum x10 -> x3, other arithmetic: 6.5 us -> 0.89 us  [the longest x1 0.63 us: body(): losses = jnp.sum(jnp.concatenate([pair_terms, class_terms], 1), 0)]
    convert_element_type x2 -> x0, local copies, waits for them, and re-layouts: 4.76 us -> none  [to_owner(): sent = at(pair, 1 - side).astype(BF)]
    squeeze x3 -> x1, local copies, waits for them, and re-layouts: 4.4 us -> 0.07 us  [at(): return lax.dynamic_index_in_dim(stacked, index, 0, keepdims=False)]
    dot_general x26 -> x25, matrix products: 35.9 us -> 31.7 us  [dot(): lax.dot_general(left, right, (((left_dim,), (right_dim,)), ((), ())), pre...]
    ppermute x63 -> x65, starting transfers between devices: 64.8 us -> 68.8 us  [swap(): lax.ppermute(values, axis, [(index, index ^ mask) for index in range(coun...]
  transfers between devices with their start and end apart: 69 -> 67, of which waited for: 32 -> 33; matrix products, arithmetic and copies ran while one was open for 23% -> 21% of each run, Pallas kernels for 11% -> 12%
where the time goes in v4:
time: 412 us
  waiting for transfers between devices  126 us (31%)
  Pallas kernels  81.4 us (20%)
  starting transfers between devices  68.9 us (17%)
  other arithmetic  44.5 us (11%)
  local copies, waits for them, and re-layouts  41.4 us (10%)
  matrix products  31.7 us (8%)
  between operations  18.9 us (5%)
    ppermute x65, waiting for transfers between devices, swap(): lax.ppermute(values, axis, [(index, index ^ mask) for index in range(coun...  126 us
    ppermute x65, starting transfers between devices, swap(): lax.ppermute(values, axis, [(index, index ^ mask) for index in range(coun...  68.8 us
    dot_general x25, matrix products, dot(): lax.dot_general(left, right, (((left_dim,), (right_dim,)), ((), ())), pre...  31.7 us
    pallas_call x3, Pallas kernels, place(): pl.pallas_call(lambda *refs: place_kernel(splits, *refs), grid_spec=pltpu...  20.7 us
    pallas_call x2, Pallas kernels, attention(): pl.pallas_call(run, grid=(stop - begin,), in_specs=[wide] + [narrow] * le...  20.5 us
    unnamed x219, local copies, waits for them, and re-layouts  19.7 us
    pallas_call x3, Pallas kernels, row_grid(): pl.pallas_call(body, grid=(tokens // rows,), in_specs=[block] * len(input...  10.1 us
    pallas_call x2, Pallas kernels, moment_grams(): pl.pallas_call(lambda *refs: moment_kernel(pieces, count, *refs), grid=(1...  9.7 us
  transfers between devices with their start and end apart: 67, of which 33 were waited for; matrix products, arithmetic and copies ran while one was open for 21% of the time, Pallas kernels for 12%

profile of v4, /device:TPU:0, one launch (start us, length us, event | category | flops | bytes accessed | tf_op | source)
XLA Modules:
  0.0 412.4 jit_solution(12007537281446246541)
XLA Ops:
  11.4 5.1 %collective-permute-start.2 = (bf16[96,832]{1,0:T(8,128)(2,1)S(1)}, bf16[96,832]{1,0:T(8,128)(2,1)S(1)}, u32[]{:S(2)}, u32[]{:S(2)}) collective-permute-start(bf16[96,832]{1,0:T(8,128)(2,1)S(1)} %pad_maximum_fusion.16), channel_id=1, source_target_pairs={{0,24},{4,28},{8,16},{12,20},{16,8},{20,12},{24,0},{28,4},{1,25},{... | collective-permute-start | bytes 479240 | tf_op jit(solution)/shard_map/ppermute | solution.py:54
  17.5 4.4 %collective-permute-done.2 = bf16[96,832]{1,0:T(8,128)(2,1)S(1)} collective-permute-done((bf16[96,832]{1,0:T(8,128)(2,1)S(1)}, bf16[96,832]{1,0:T(8,128)(2,1)S(1)}, u32[]{:S(2)}, u32[]{:S(2)}) %collective-permute-start.2) | collective-permute-done | bytes 159776 | tf_op jit(solution)/shard_map/ppermute | solution.py:54
  21.9 9.3 %collective-permute-done.1 = bf16[96,832]{1,0:T(8,128)(2,1)S(1)} collective-permute-done((bf16[96,832]{1,0:T(8,128)(2,1)S(1)}, bf16[96,832]{1,0:T(8,128)(2,1)S(1)}, u32[]{:S(2)}, u32[]{:S(2)}) %collective-permute-start.1) | collective-permute-done | bytes 159776 | tf_op jit(solution)/shard_map/ppermute | solution.py:54
  34.3 2.5 collective-permute-start.7
  38.7 5.3 %collective-permute-done.7 = bf16[96,960]{1,0:T(8,128)(2,1)S(1)} collective-permute-done((bf16[96,960]{1,0:T(8,128)(2,1)S(1)}, bf16[96,960]{1,0:T(8,128)(2,1)S(1)}, u32[]{:S(2)}, u32[]{:S(2)}) %collective-permute-start.7) | collective-permute-done | bytes 184352 | tf_op jit(solution)/shard_map/ppermute | solution.py:54
  44.0 7.7 %collective-permute-done.6 = bf16[96,960]{1,0:T(8,128)(2,1)S(1)} collective-permute-done((bf16[96,960]{1,0:T(8,128)(2,1)S(1)}, bf16[96,960]{1,0:T(8,128)(2,1)S(1)}, u32[]{:S(2)}, u32[]{:S(2)}) %collective-permute-start.6) | collective-permute-done | bytes 184352 | tf_op jit(solution)/shard_map/ppermute | solution.py:54
  64.4 3.3 shard_map.434
  71.7 2.3 collective-permute-start.15
  74.0 2.1 collective-permute-start.13
  81.9 10.2 %collective-permute-done.14 = bf16[96,1088]{1,0:T(8,128)(2,1)S(1)} collective-permute-done((bf16[96,1088]{1,0:T(8,128)(2,1)S(1)}, bf16[96,1088]{1,0:T(8,128)(2,1)S(1)}, u32[]{:S(2)}, u32[]{:S(2)}) %collective-permute-start.14) | collective-permute-done | bytes 208928 | tf_op jit(solution)/shard_map/ppermute | solution.py:54
  94.5 7.5 %shard_map.436 = bf16[800,384]{1,0:T(8,128)(2,1)S(1)} custom-call(bf16[800,1152]{1,0:T(8,128)(2,1)S(1)} %convolution_convert_fusion.refs_0_), custom_call_target="tpu_custom_call" | custom-call | tf_op jit(solution)/shard_map/pallas_call | solution.py:373
  104.0 3.3 shard_map.437
  116.8 4.5 %shard_map.438 = (f32[800,768]{1,0:T(8,128)S(1)}, bf16[800,768]{1,0:T(8,128)(2,1)S(1)}, f32[8,768]{1,0:T(8,128)S(1)}) custom-call(f32[800,768]{1,0:T(8,128)S(1)} %get-tuple-element.368.refs_0_, bf16[800,768]{1,0:T(8,128)(2,1)} %convolution_convert_fusion.4.refs_1_, bf16[800,768]{1,0:T(8,128)(2,1)} %collective-permute-done.18.refs_2_, ...), custom_call_target="tpu_custom_call" | custom-call | tf_op jit(solution)/shard_map/pallas_call | solution.py:404
  122.7 8.7 %collective-permute-done.19.refs_2_ = bf16[4,96,1088]{2,1,0:T(8,128)(2,1)} collective-permute-done((bf16[4,96,1088]{2,1,0:T(8,128)(2,1)S(1)}, bf16[4,96,1088]{2,1,0:T(8,128)(2,1)}, u32[]{:S(2)}, u32[]{:S(2)}) %collective-permute-start.19) | collective-permute-done | bytes 835616 | tf_op jit(solution)/shard_map/ppermute | solution.py:54
  135.8 4.8 %shard_map.439 = (bf16[800,1536]{1,0:T(8,128)(2,1)S(1)}, f32[8,1536]{1,0:T(8,128)S(1)}) custom-call(bf16[800,768]{1,0:T(8,128)(2,1)S(1)} %get-tuple-element.131.refs_0_, bf16[768,1536]{1,0:T(8,128)(2,1)S(1)} %bitcast.251), custom_call_target="tpu_custom_call" | custom-call | tf_op jit(solution)/shard_map/pallas_call | solution.py:473
  140.7 3.7 collective-permute-done.21.refs_4_
  144.4 2.0 collective-permute-done.22.refs_5_
  146.4 14.1 %shard_map.440 = (bf16[4,2,96,1536]{3,2,1,0:T(8,128)(2,1)S(1)}, bf16[4,2,96,640]{3,2,1,0:T(8,128)(2,1)}) custom-call(s32[2]{0:T(128)S(1)} %pad_add_fusion.1.refs_0_.spot, bf16[4,96,1088]{2,1,0:T(8,128)(2,1)S(1)} %pad_maximum_fusion.2.refs_1_, bf16[4,96,1088]{2,1,0:T(8,128)(2,1)} %collective-permute-done.19.refs_2_, ...), custom_call_target="tpu_custom_call" | custom-call | tf_op jit(solution)/shard_map/pallas_call | solution.py:94
  165.5 2.5 shard_map.441
  175.0 2.8 collective-permute-start.27
  181.6 2.1 fusion.168
  191.6 2.9 convolution_convert_fusion.5.refs_1_
  194.4 3.4 convolution_convert_fusion.1
  201.3 2.7 shard_map.442
  205.5 13.0 %shard_map.443 = bf16[800,1152]{1,0:T(8,128)(2,1)S(1)} custom-call(bf16[800,1152]{1,0:T(8,128)(2,1)S(1)} %copy-done.7, bf16[800,384]{1,0:T(8,128)(2,1)S(1)} %convolution_convert_fusion.6.refs_1_), custom_call_target="tpu_custom_call" | custom-call | tf_op jit(solution)/shard_map/pallas_call | solution.py:373
  220.4 7.2 %collective-permute-done.32 = bf16[2,4,48,768]{3,2,1,0:T(8,128)(2,1)S(1)} collective-permute-done((bf16[2,4,48,768]{3,2,1,0:T(8,128)(2,1)S(1)}, bf16[2,4,48,768]{3,2,1,0:T(8,128)(2,1)S(1)}, u32[]{:S(2)}, u32[]{:S(2)}) %collective-permute-start.32) | collective-permute-done | bytes 589856 | tf_op jit(solution)/shard_map/ppermute | solution.py:54
  231.3 2.4 convolution_convert_fusion.2
  240.3 2.9 shard_map.444
  255.7 2.2 collective-permute-start.42
  257.9 2.4 collective-permute-start.44
  271.2 2.8 collective-permute-done.41
  279.7 2.1 collective-permute-start.45
  283.6 3.5 collective-permute-done.47
  287.1 12.1 %collective-permute-done.46 = bf16[96,1024]{1,0:T(8,128)(2,1)S(1)} collective-permute-done((bf16[96,1024]{1,0:T(8,128)(2,1)S(1)}, bf16[96,1024]{1,0:T(8,128)(2,1)S(1)}, u32[]{:S(2)}, u32[]{:S(2)}) %collective-permute-start.46) | collective-permute-done | bytes 196640 | tf_op jit(solution)/shard_map/ppermute | solution.py:54
  300.1 2.1 shard_map.445
  306.0 2.2 collective-permute-done.49
  311.5 2.7 collective-permute-start.51
  316.9 4.4 %collective-permute-done.53 = bf16[96,768]{1,0:T(8,128)(2,1)S(1)} collective-permute-done((bf16[96,768]{1,0:T(8,128)(2,1)S(1)}, bf16[96,768]{1,0:T(8,128)(2,1)S(1)}, u32[]{:S(2)}, u32[]{:S(2)}) %collective-permute-start.53) | collective-permute-done | bytes 147488 | tf_op jit(solution)/shard_map/ppermute | solution.py:54
  321.2 8.6 %collective-permute-done.52 = bf16[96,768]{1,0:T(8,128)(2,1)S(1)} collective-permute-done((bf16[96,768]{1,0:T(8,128)(2,1)S(1)}, bf16[96,768]{1,0:T(8,128)(2,1)S(1)}, u32[]{:S(2)}, u32[]{:S(2)}) %collective-permute-start.52) | collective-permute-done | bytes 147488 | tf_op jit(solution)/shard_map/ppermute | solution.py:54
  331.0 3.6 collective-permute-done.56
  334.8 4.4 %collective-permute-done.57 = f32[8,128]{1,0:T(8,128)S(1)} collective-permute-done((f32[8,128]{1,0:T(8,128)S(1)}, f32[8,128]{1,0:T(8,128)S(1)}, u32[]{:S(2)}, u32[]{:S(2)}) %collective-permute-start.57) | collective-permute-done | bytes 4128 | tf_op jit(solution)/shard_map/ppermute | solution.py:54
  340.4 5.6 %shard_map.447 = (bf16[768,768]{1,0:T(8,128)(2,1)}, bf16[768,768]{1,0:T(8,128)(2,1)}, bf16[2,6,256,256]{3,2,1,0:T(8,128)(2,1)}) custom-call(f32[1]{0:T(128)} %bitcast.89.refs_0_, bf16[768,2304]{1,0:T(8,128)(2,1)} %all-gather.3.cloned.1.call-done.refs_1_.refs_2_, bf16[768,2304]{1,0:T(8,128)(2,1)} %all-gather.3.cloned.1.call-done.refs_1_.refs_2_, ...), custom_call_target="tpu_custom_call" | custom-call | tf_op jit(solution)/shard_map/pallas_call | solution.py:606
  347.9 4.1 shard_map.449
  352.0 2.9 broadcast_select_fusion.1
  364.8 2.4 multiply_subtract_fusion.1
  371.2 8.4 %collective-permute-done.60.came_side = bf16[6,256,256]{2,1,0:T(8,128)(2,1)} collective-permute-done((bf16[6,256,256]{2,1,0:T(8,128)(2,1)}, bf16[6,256,256]{2,1,0:T(8,128)(2,1)}, u32[]{:S(2)}, u32[]{:S(2)}) %collective-permute-start.60) | collective-permute-done | bytes 786464 | tf_op jit(solution)/shard_map/ppermute | solution.py:54
  379.6 8.2 %shard_map.450 = (bf16[96,768]{1,0:T(8,128)(2,1)S(1)}, f32[8,128]{1,0:T(8,128)S(1)}) custom-call(s32[2]{0:T(128)S(1)} %pad_add_fusion.2.start, bf16[2,6,256,256]{3,2,1,0:T(8,128)(2,1)S(1)} %get-tuple-element.305.kept, bf16[2,6,256,256]{3,2,1,0:T(8,128)(2,1)S(1)} %collective-permute-done.59.came, bf16[6,256,256]{2,1,0:T(8,128)(2,1)} %collective-permute-done.60.came_side), custom_call_target="tpu_custom_call" | custom-call | tf_op jit(solution)/shard_map/pallas_call | solution.py:536
  389.3 3.7 collective-permute-done.61
  (552 shorter events, 162.5 us)
Async XLA Ops:
  7.2 253.1 %all-gather.3.cloned.1.call-start = ((), (), s32[]{:S(2)}) async-start(), calls=%async_computation | async-start | bytes 3981312 | tf_op jit(solution)/shard_map/all_gather | solution.py:735
  11.4 10.4 %collective-permute-start.2 = (bf16[96,832]{1,0:T(8,128)(2,1)S(1)}, bf16[96,832]{1,0:T(8,128)(2,1)S(1)}, u32[]{:S(2)}, u32[]{:S(2)}) collective-permute-start(bf16[96,832]{1,0:T(8,128)(2,1)S(1)} %pad_maximum_fusion.16), channel_id=1, source_target_pairs={{0,24},{4,28},{8,16},{12,20},{16,8},{20,12},{24,0},{28,4},{1,25},{... | collective-permute-start | bytes 479240 | tf_op jit(solution)/shard_map/ppermute | solution.py:54
  16.6 14.6 %collective-permute-start.1 = (bf16[96,832]{1,0:T(8,128)(2,1)S(1)}, bf16[96,832]{1,0:T(8,128)(2,1)S(1)}, u32[]{:S(2)}, u32[]{:S(2)}) collective-permute-start(bf16[96,832]{1,0:T(8,128)(2,1)S(1)} %pad_maximum_fusion.16), channel_id=1, source_target_pairs={{0,16},{4,20},{8,24},{12,28},{16,0},{20,4},{24,8},{28,12},{1,17},{... | collective-permute-start | bytes 479240 | tf_op jit(solution)/shard_map/ppermute | solution.py:54
  16.6 14.6 %collective-permute-start = (bf16[96,832]{1,0:T(8,128)(2,1)S(1)}, bf16[96,832]{1,0:T(8,128)(2,1)S(1)}, u32[]{:S(2)}, u32[]{:S(2)}) collective-permute-start(bf16[96,832]{1,0:T(8,128)(2,1)S(1)} %pad_maximum_fusion.16), channel_id=1, source_target_pairs={{0,8},{4,12},{8,0},{12,4},{16,24},{20,28},{24,16},{28,20},{1,9},{5... | collective-permute-start | bytes 479240 | tf_op jit(solution)/shard_map/ppermute | solution.py:54
  31.3 21.5 %collective-permute-start.3 = (bf16[4,96,832]{2,1,0:T(8,128)(2,1)S(1)}, bf16[4,96,832]{2,1,0:T(8,128)(2,1)S(1)}, u32[]{:S(2)}, u32[]{:S(2)}) collective-permute-start(bf16[4,96,832]{2,1,0:T(8,128)(2,1)S(1)} %pad_maximum_fusion.5.refs_1_), channel_id=1, source_target_pairs={{0,4},{4,0},{8,12},{12,8},{16,20},{20,16},{24,28},{28,24},{1,5},{5... | collective-permute-start | bytes 1916936 | tf_op jit(solution)/shard_map/ppermute | solution.py:54
  32.8 19.9 %collective-permute-start.4 = (bf16[4,96,832]{2,1,0:T(8,128)(2,1)S(1)}, bf16[4,96,832]{2,1,0:T(8,128)(2,1)S(1)}, u32[]{:S(2)}, u32[]{:S(2)}) collective-permute-start(bf16[4,96,832]{2,1,0:T(8,128)(2,1)S(1)} %pad_maximum_fusion.5.refs_1_), channel_id=1, source_target_pairs={{0,2},{1,3},{2,0},{3,1},{4,6},{5,7},{6,4},{7,5},{8,10},{9,11},{10,... | collective-permute-start | bytes 1916936 | tf_op jit(solution)/shard_map/ppermute | solution.py:54
  34.3 9.7 %collective-permute-start.7 = (bf16[96,960]{1,0:T(8,128)(2,1)S(1)}, bf16[96,960]{1,0:T(8,128)(2,1)S(1)}, u32[]{:S(2)}, u32[]{:S(2)}) collective-permute-start(bf16[96,960]{1,0:T(8,128)(2,1)S(1)} %pad_maximum_fusion.14), channel_id=1, source_target_pairs={{0,24},{4,28},{8,16},{12,20},{16,8},{20,12},{24,0},{28,4},{1,25},{... | collective-permute-start | bytes 552968 | tf_op jit(solution)/shard_map/ppermute | solution.py:54
  36.8 14.9 %collective-permute-start.6 = (bf16[96,960]{1,0:T(8,128)(2,1)S(1)}, bf16[96,960]{1,0:T(8,128)(2,1)S(1)}, u32[]{:S(2)}, u32[]{:S(2)}) collective-permute-start(bf16[96,960]{1,0:T(8,128)(2,1)S(1)} %pad_maximum_fusion.14), channel_id=1, source_target_pairs={{0,16},{4,20},{8,24},{12,28},{16,0},{20,4},{24,8},{28,12},{1,17},{... | collective-permute-start | bytes 552968 | tf_op jit(solution)/shard_map/ppermute | solution.py:54
  36.8 14.9 %collective-permute-start.5 = (bf16[96,960]{1,0:T(8,128)(2,1)S(1)}, bf16[96,960]{1,0:T(8,128)(2,1)S(1)}, u32[]{:S(2)}, u32[]{:S(2)}) collective-permute-start(bf16[96,960]{1,0:T(8,128)(2,1)S(1)} %pad_maximum_fusion.14), channel_id=1, source_target_pairs={{0,8},{4,12},{8,0},{12,4},{16,24},{20,28},{24,16},{28,20},{1,9},{5... | collective-permute-start | bytes 552968 | tf_op jit(solution)/shard_map/ppermute | solution.py:54
  53.6 8.7 %collective-permute-start.8 = (bf16[2,96,832]{2,1,0:T(8,128)(2,1)}, bf16[2,96,832]{2,1,0:T(8,128)(2,1)S(1)}, u32[]{:S(2)}, u32[]{:S(2)}) collective-permute-start(bf16[2,96,832]{2,1,0:T(8,128)(2,1)} %slice.274), channel_id=1, source_target_pairs={{0,2},{1,3},{2,0},{3,1},{4,6},{5,7},{6,4},{7,5},{8,10},{9,11},{10,... | collective-permute-start | bytes 958472 | tf_op jit(solution)/shard_map/ppermute | solution.py:54
  54.8 8.5 %collective-permute-start.9 = (bf16[2,96,832]{2,1,0:T(8,128)(2,1)}, bf16[2,96,832]{2,1,0:T(8,128)(2,1)}, u32[]{:S(2)}, u32[]{:S(2)}) collective-permute-start(bf16[2,96,832]{2,1,0:T(8,128)(2,1)} %slice.275), channel_id=1, source_target_pairs={{0,4},{4,0},{8,12},{12,8},{16,20},{20,16},{24,28},{28,24},{1,5},{5... | collective-permute-start | bytes 958472 | tf_op jit(solution)/shard_map/ppermute | solution.py:54
  68.2 24.1 %collective-permute-start.11 = (bf16[4,96,960]{2,1,0:T(8,128)(2,1)}, bf16[4,96,960]{2,1,0:T(8,128)(2,1)S(1)}, u32[]{:S(2)}, u32[]{:S(2)}) collective-permute-start(bf16[4,96,960]{2,1,0:T(8,128)(2,1)} %pad_maximum_fusion.3.refs_1_), channel_id=1, source_target_pairs={{0,4},{4,0},{8,12},{12,8},{16,20},{20,16},{24,28},{28,24},{1,5},{5... | collective-permute-start | bytes 2211848 | tf_op jit(solution)/shard_map/ppermute | solution.py:54
  68.8 23.5 %collective-permute-start.12 = (bf16[4,96,960]{2,1,0:T(8,128)(2,1)}, bf16[4,96,960]{2,1,0:T(8,128)(2,1)S(1)}, u32[]{:S(2)}, u32[]{:S(2)}) collective-permute-start(bf16[4,96,960]{2,1,0:T(8,128)(2,1)} %pad_maximum_fusion.3.refs_1_), channel_id=1, source_target_pairs={{0,2},{1,3},{2,0},{3,1},{4,6},{5,7},{6,4},{7,5},{8,10},{9,11},{10,... | collective-permute-start | bytes 2211848 | tf_op jit(solution)/shard_map/ppermute | solution.py:54
  71.7 10.3 %collective-permute-start.15 = (bf16[96,1088]{1,0:T(8,128)(2,1)S(1)}, bf16[96,1088]{1,0:T(8,128)(2,1)S(1)}, u32[]{:S(2)}, u32[]{:S(2)}) collective-permute-start(bf16[96,1088]{1,0:T(8,128)(2,1)S(1)} %pad_maximum_fusion.13), channel_id=1, source_target_pairs={{0,24},{4,28},{8,16},{12,20},{16,8},{20,12},{24,0},{28,4},{1,25},{... | collective-permute-start | bytes 626696 | tf_op jit(solution)/shard_map/ppermute | solution.py:54
  74.0 18.1 %collective-permute-start.14 = (bf16[96,1088]{1,0:T(8,128)(2,1)S(1)}, bf16[96,1088]{1,0:T(8,128)(2,1)S(1)}, u32[]{:S(2)}, u32[]{:S(2)}) collective-permute-start(bf16[96,1088]{1,0:T(8,128)(2,1)S(1)} %pad_maximum_fusion.13), channel_id=1, source_target_pairs={{0,16},{4,20},{8,24},{12,28},{16,0},{20,4},{24,8},{28,12},{1,17},{... | collective-permute-start | bytes 626696 | tf_op jit(solution)/shard_map/ppermute | solution.py:54
  74.0 18.1 %collective-permute-start.13 = (bf16[96,1088]{1,0:T(8,128)(2,1)S(1)}, bf16[96,1088]{1,0:T(8,128)(2,1)S(1)}, u32[]{:S(2)}, u32[]{:S(2)}) collective-permute-start(bf16[96,1088]{1,0:T(8,128)(2,1)S(1)} %pad_maximum_fusion.13), channel_id=1, source_target_pairs={{0,8},{4,12},{8,0},{12,4},{16,24},{20,28},{24,16},{28,20},{1,9},{5... | collective-permute-start | bytes 626696 | tf_op jit(solution)/shard_map/ppermute | solution.py:54
  92.4 10.2 %collective-permute-start.16 = (bf16[2,96,960]{2,1,0:T(8,128)(2,1)S(1)}, bf16[2,96,960]{2,1,0:T(8,128)(2,1)S(1)}, u32[]{:S(2)}, u32[]{:S(2)}) collective-permute-start(bf16[2,96,960]{2,1,0:T(8,128)(2,1)S(1)} %slice.284), channel_id=1, source_target_pairs={{0,2},{1,3},{2,0},{3,1},{4,6},{5,7},{6,4},{7,5},{8,10},{9,11},{10,... | collective-permute-start | bytes 1105928 | tf_op jit(solution)/shard_map/ppermute | solution.py:54
  93.9 10.1 %collective-permute-start.17 = (bf16[2,96,960]{2,1,0:T(8,128)(2,1)S(1)}, bf16[2,96,960]{2,1,0:T(8,128)(2,1)S(1)}, u32[]{:S(2)}, u32[]{:S(2)}) collective-permute-start(bf16[2,96,960]{2,1,0:T(8,128)(2,1)S(1)} %slice.285), channel_id=1, source_target_pairs={{0,4},{4,0},{8,12},{12,8},{16,20},{20,16},{24,28},{28,24},{1,5},{5... | collective-permute-start | bytes 1105928 | tf_op jit(solution)/shard_map/ppermute | solution.py:54
  109.3 7.5 %collective-permute-start.18 = (bf16[800,768]{1,0:T(8,128)(2,1)}, bf16[800,768]{1,0:T(8,128)(2,1)}, u32[]{:S(2)}, u32[]{:S(2)}) collective-permute-start(bf16[800,768]{1,0:T(8,128)(2,1)} %convolution_convert_fusion.4.refs_1_), channel_id=1, source_target_pairs={{0,1},{1,0},{2,3},{3,2},{4,5},{5,4},{6,7},{7,6},{8,9},{9,8},{10,11... | collective-permute-start | bytes 3686408 | tf_op jit(solution)/shard_map/ppermute | solution.py:54
  109.3 22.2 %collective-permute-start.19 = (bf16[4,96,1088]{2,1,0:T(8,128)(2,1)S(1)}, bf16[4,96,1088]{2,1,0:T(8,128)(2,1)}, u32[]{:S(2)}, u32[]{:S(2)}) collective-permute-start(bf16[4,96,1088]{2,1,0:T(8,128)(2,1)S(1)} %pad_maximum_fusion.2.refs_1_), channel_id=1, source_target_pairs={{0,4},{4,0},{8,12},{12,8},{16,20},{20,16},{24,28},{28,24},{1,5},{5... | collective-permute-start | bytes 2506760 | tf_op jit(solution)/shard_map/ppermute | solution.py:54
  109.6 21.9 %collective-permute-start.20 = (bf16[4,96,1088]{2,1,0:T(8,128)(2,1)S(1)}, bf16[4,96,1088]{2,1,0:T(8,128)(2,1)}, u32[]{:S(2)}, u32[]{:S(2)}) collective-permute-start(bf16[4,96,1088]{2,1,0:T(8,128)(2,1)S(1)} %pad_maximum_fusion.2.refs_1_), channel_id=1, source_target_pairs={{0,2},{1,3},{2,0},{3,1},{4,6},{5,7},{6,4},{7,5},{8,10},{9,11},{10,... | collective-permute-start | bytes 2506760 | tf_op jit(solution)/shard_map/ppermute | solution.py:54
  132.5 11.8 %collective-permute-start.21 = (bf16[2,96,1088]{2,1,0:T(8,128)(2,1)S(1)}, bf16[2,96,1088]{2,1,0:T(8,128)(2,1)S(1)}, u32[]{:S(2)}, u32[]{:S(2)}) collective-permute-start(bf16[2,96,1088]{2,1,0:T(8,128)(2,1)S(1)} %slice.289), channel_id=1, source_target_pairs={{0,2},{1,3},{2,0},{3,1},{4,6},{5,7},{6,4},{7,5},{8,10},{9,11},{10,... | collective-permute-start | bytes 1253384 | tf_op jit(solution)/shard_map/ppermute | solution.py:54
  135.1 11.3 %collective-permute-start.22 = (bf16[2,96,1088]{2,1,0:T(8,128)(2,1)S(1)}, bf16[2,96,1088]{2,1,0:T(8,128)(2,1)S(1)}, u32[]{:S(2)}, u32[]{:S(2)}) collective-permute-start(bf16[2,96,1088]{2,1,0:T(8,128)(2,1)S(1)} %slice.290), channel_id=1, source_target_pairs={{0,4},{4,0},{8,12},{12,8},{16,20},{20,16},{24,28},{28,24},{1,5},{5... | collective-permute-start | bytes 1253384 | tf_op jit(solution)/shard_map/ppermute | solution.py:54
  171.5 168.9 %all-gather.5.cloned.1.call-start = ((), (), s32[]{:S(2)}) async-start(), calls=%async_computation.1 | async-start | bytes 1327104 | tf_op jit(solution)/shard_map/all_gather | solution.py:910
  198.2 22.1 %collective-permute-start.31 = (bf16[4,2,48,768]{3,2,0,1:T(8,128)(2,1)S(1)}, bf16[4,2,48,768]{3,2,0,1:T(8,128)(2,1)S(1)}, u32[]{:S(2)}, u32[]{:S(2)}) collective-permute-start(bf16[4,2,48,768]{3,2,0,1:T(8,128)(2,1)S(1)} %copy.135), channel_id=1, source_target_pairs={{0,2},{1,3},{2,0},{3,1},{4,6},{5,7},{6,4},{7,5},{8,10},{9,11},{10,... | collective-permute-start | bytes 1769480 | tf_op jit(solution)/shard_map/ppermute | solution.py:54
  199.4 28.1 %collective-permute-start.32 = (bf16[2,4,48,768]{3,2,1,0:T(8,128)(2,1)S(1)}, bf16[2,4,48,768]{3,2,1,0:T(8,128)(2,1)S(1)}, u32[]{:S(2)}, u32[]{:S(2)}) collective-permute-start(bf16[2,4,48,768]{3,2,1,0:T(8,128)(2,1)S(1)} %pad_maximum_fusion.6), channel_id=1, source_target_pairs={{0,4},{4,0},{8,12},{12,8},{16,20},{20,16},{24,28},{28,24},{1,5},{5... | collective-permute-start | bytes 1769480 | tf_op jit(solution)/shard_map/ppermute | solution.py:54
  227.5 12.8 %collective-permute-start.33 = (bf16[800,768]{1,0:T(8,128)(2,1)S(1)}, bf16[800,768]{1,0:T(8,128)(2,1)S(1)}, u32[]{:S(2)}, u32[]{:S(2)}) collective-permute-start(bf16[800,768]{1,0:T(8,128)(2,1)S(1)} %convolution_convert_fusion.3.refs_1_), channel_id=1, source_target_pairs={{0,1},{1,0},{2,3},{3,2},{4,5},{5,4},{6,7},{7,6},{8,9},{9,8},{10,11... | collective-permute-start | bytes 3686408 | tf_op jit(solution)/shard_map/ppermute | solution.py:54
  227.7 15.6 %collective-permute-start.34 = (bf16[4,48,768]{2,1,0:T(8,128)(2,1)S(1)}, bf16[4,48,768]{2,1,0:T(8,128)(2,1)S(1)}, u32[]{:S(2)}, u32[]{:S(2)}) collective-permute-start(bf16[4,48,768]{2,1,0:T(8,128)(2,1)S(1)} %fusion.46), channel_id=1, source_target_pairs={{0,4},{4,0},{8,12},{12,8},{16,20},{20,16},{24,28},{28,24},{1,5},{5... | collective-permute-start | bytes 884744 | tf_op jit(solution)/shard_map/ppermute | solution.py:54
  229.5 13.9 %collective-permute-start.35 = (bf16[4,48,768]{2,1,0:T(8,128)(2,1)S(1)}, bf16[4,48,768]{2,1,0:T(8,128)(2,1)S(1)}, u32[]{:S(2)}, u32[]{:S(2)}) collective-permute-start(bf16[4,48,768]{2,1,0:T(8,128)(2,1)S(1)} %fusion.29), channel_id=1, source_target_pairs={{0,2},{1,3},{2,0},{3,1},{4,6},{5,7},{6,4},{7,5},{8,10},{9,11},{10,... | collective-permute-start | bytes 884744 | tf_op jit(solution)/shard_map/ppermute | solution.py:54
  235.6 22.3 %collective-permute-start.38 = (bf16[4,2,48,768]{3,2,0,1:T(8,128)(2,1)}, bf16[4,2,48,768]{3,2,0,1:T(8,128)(2,1)}, u32[]{:S(2)}, u32[]{:S(2)}) collective-permute-start(bf16[4,2,48,768]{3,2,0,1:T(8,128)(2,1)} %copy.144), channel_id=1, source_target_pairs={{0,2},{1,3},{2,0},{3,1},{4,6},{5,7},{6,4},{7,5},{8,10},{9,11},{10,... | collective-permute-start | bytes 1769480 | tf_op jit(solution)/shard_map/ppermute | solution.py:54
  239.8 18.1 %collective-permute-start.39 = (bf16[2,4,48,768]{3,2,1,0:T(8,128)(2,1)}, bf16[2,4,48,768]{3,2,1,0:T(8,128)(2,1)}, u32[]{:S(2)}, u32[]{:S(2)}) collective-permute-start(bf16[2,4,48,768]{3,2,1,0:T(8,128)(2,1)} %pad_maximum_fusion.7), channel_id=1, source_target_pairs={{0,4},{4,0},{8,12},{12,8},{16,20},{20,16},{24,28},{28,24},{1,5},{5... | collective-permute-start | bytes 1769480 | tf_op jit(solution)/shard_map/ppermute | solution.py:54
  249.7 10.6 %collective-permute-start.36 = (bf16[4,2,48,256]{3,2,0,1:T(8,128)(2,1)}, bf16[4,2,48,256]{3,2,0,1:T(8,128)(2,1)}, u32[]{:S(2)}, u32[]{:S(2)}) collective-permute-start(bf16[4,2,48,256]{3,2,0,1:T(8,128)(2,1)} %copy.143), channel_id=1, source_target_pairs={{0,2},{1,3},{2,0},{3,1},{4,6},{5,7},{6,4},{7,5},{8,10},{9,11},{10,... | collective-permute-start | bytes 589832 | tf_op jit(solution)/shard_map/ppermute | solution.py:54
  252.5 7.8 %collective-permute-start.37 = (bf16[2,4,48,256]{3,2,1,0:T(8,128)(2,1)S(1)}, bf16[2,4,48,256]{3,2,1,0:T(8,128)(2,1)}, u32[]{:S(2)}, u32[]{:S(2)}) collective-permute-start(bf16[2,4,48,256]{3,2,1,0:T(8,128)(2,1)S(1)} %pad_maximum_fusion.15), channel_id=1, source_target_pairs={{0,4},{4,0},{8,12},{12,8},{16,20},{20,16},{24,28},{28,24},{1,5},{5... | collective-permute-start | bytes 589832 | tf_op jit(solution)/shard_map/ppermute | solution.py:54
  255.7 13.5 %collective-permute-start.42 = (bf16[96,768]{1,0:T(8,128)(2,1)}, bf16[96,768]{1,0:T(8,128)(2,1)}, u32[]{:S(2)}, u32[]{:S(2)}) collective-permute-start(bf16[96,768]{1,0:T(8,128)(2,1)} %get-tuple-element.317), channel_id=1, source_target_pairs={{0,8},{4,12},{8,0},{12,4},{16,24},{20,28},{24,16},{28,20},{1,9},{5... | collective-permute-start | bytes 442376 | tf_op jit(solution)/shard_map/ppermute | solution.py:54
  257.9 12.8 %collective-permute-start.43 = (bf16[96,768]{1,0:T(8,128)(2,1)}, bf16[96,768]{1,0:T(8,128)(2,1)}, u32[]{:S(2)}, u32[]{:S(2)}) collective-permute-start(bf16[96,768]{1,0:T(8,128)(2,1)} %get-tuple-element.318), channel_id=1, source_target_pairs={{0,16},{4,20},{8,24},{12,28},{16,0},{20,4},{24,8},{28,12},{1,17},{... | collective-permute-start | bytes 442376 | tf_op jit(solution)/shard_map/ppermute | solution.py:54
  257.9 12.8 %collective-permute-start.44 = (bf16[96,768]{1,0:T(8,128)(2,1)}, bf16[96,768]{1,0:T(8,128)(2,1)}, u32[]{:S(2)}, u32[]{:S(2)}) collective-permute-start(bf16[96,768]{1,0:T(8,128)(2,1)} %get-tuple-element.316), channel_id=1, source_target_pairs={{0,24},{4,28},{8,16},{12,20},{16,8},{20,12},{24,0},{28,4},{1,25},{... | collective-permute-start | bytes 442376 | tf_op jit(solution)/shard_map/ppermute | solution.py:54
  261.8 9.3 %collective-permute-start.40 = (bf16[4,48,1024]{2,1,0:T(8,128)(2,1)S(1)}, bf16[4,48,1024]{2,1,0:T(8,128)(2,1)S(1)}, u32[]{:S(2)}, u32[]{:S(2)}) collective-permute-start(bf16[4,48,1024]{2,1,0:T(8,128)(2,1)S(1)} %fusion.31), channel_id=1, source_target_pairs={{0,4},{4,0},{8,12},{12,8},{16,20},{20,16},{24,28},{28,24},{1,5},{5... | collective-permute-start | bytes 1179656 | tf_op jit(solution)/shard_map/ppermute | solution.py:54
  264.9 9.1 %collective-permute-start.41 = (bf16[4,48,1024]{2,1,0:T(8,128)(2,1)S(1)}, bf16[4,48,1024]{2,1,0:T(8,128)(2,1)S(1)}, u32[]{:S(2)}, u32[]{:S(2)}) collective-permute-start(bf16[4,48,1024]{2,1,0:T(8,128)(2,1)S(1)} %fusion.24), channel_id=1, source_target_pairs={{0,2},{1,3},{2,0},{3,1},{4,6},{5,7},{6,4},{7,5},{8,10},{9,11},{10,... | collective-permute-start | bytes 1179656 | tf_op jit(solution)/shard_map/ppermute | solution.py:54
  277.4 9.7 %collective-permute-start.47 = (bf16[96,1024]{1,0:T(8,128)(2,1)S(1)}, bf16[96,1024]{1,0:T(8,128)(2,1)S(1)}, u32[]{:S(2)}, u32[]{:S(2)}) collective-permute-start(bf16[96,1024]{1,0:T(8,128)(2,1)S(1)} %get-tuple-element.313), channel_id=1, source_target_pairs={{0,24},{4,28},{8,16},{12,20},{16,8},{20,12},{24,0},{28,4},{1,25},{... | collective-permute-start | bytes 589832 | tf_op jit(solution)/shard_map/ppermute | solution.py:54
  278.9 20.2 %collective-permute-start.46 = (bf16[96,1024]{1,0:T(8,128)(2,1)S(1)}, bf16[96,1024]{1,0:T(8,128)(2,1)S(1)}, u32[]{:S(2)}, u32[]{:S(2)}) collective-permute-start(bf16[96,1024]{1,0:T(8,128)(2,1)S(1)} %get-tuple-element.312), channel_id=1, source_target_pairs={{0,16},{4,20},{8,24},{12,28},{16,0},{20,4},{24,8},{28,12},{1,17},{... | collective-permute-start | bytes 589832 | tf_op jit(solution)/shard_map/ppermute | solution.py:54
  279.7 19.5 %collective-permute-start.45 = (bf16[96,1024]{1,0:T(8,128)(2,1)S(1)}, bf16[96,1024]{1,0:T(8,128)(2,1)S(1)}, u32[]{:S(2)}, u32[]{:S(2)}) collective-permute-start(bf16[96,1024]{1,0:T(8,128)(2,1)S(1)} %get-tuple-element.311), channel_id=1, source_target_pairs={{0,8},{4,12},{8,0},{12,4},{16,24},{20,28},{24,16},{28,20},{1,9},{5... | collective-permute-start | bytes 589832 | tf_op jit(solution)/shard_map/ppermute | solution.py:54
  302.2 7.4 %collective-permute-start.54 = (bf16[96,256]{1,0:T(8,128)(2,1)S(1)}, bf16[96,256]{1,0:T(8,128)(2,1)S(1)}, u32[]{:S(2)}, u32[]{:S(2)}) collective-permute-start(bf16[96,256]{1,0:T(8,128)(2,1)S(1)} %slice.413), channel_id=1, source_target_pairs={{0,2},{1,3},{2,0},{3,1},{4,6},{5,7},{6,4},{7,5},{8,10},{9,11},{10,... | collective-permute-start | bytes 147464 | tf_op jit(solution)/shard_map/ppermute | solution.py:54
  309.7 11.5 %collective-permute-start.53 = (bf16[96,768]{1,0:T(8,128)(2,1)S(1)}, bf16[96,768]{1,0:T(8,128)(2,1)S(1)}, u32[]{:S(2)}, u32[]{:S(2)}) collective-permute-start(bf16[96,768]{1,0:T(8,128)(2,1)S(1)} %get-tuple-element.345), channel_id=1, source_target_pairs={{0,24},{4,28},{8,16},{12,20},{16,8},{20,12},{24,0},{28,4},{1,25},{... | collective-permute-start | bytes 442376 | tf_op jit(solution)/shard_map/ppermute | solution.py:54
  311.5 18.4 %collective-permute-start.52 = (bf16[96,768]{1,0:T(8,128)(2,1)S(1)}, bf16[96,768]{1,0:T(8,128)(2,1)S(1)}, u32[]{:S(2)}, u32[]{:S(2)}) collective-permute-start(bf16[96,768]{1,0:T(8,128)(2,1)S(1)} %get-tuple-element.345), channel_id=1, source_target_pairs={{0,16},{4,20},{8,24},{12,28},{16,0},{20,4},{24,8},{28,12},{1,17},{... | collective-permute-start | bytes 442376 | tf_op jit(solution)/shard_map/ppermute | solution.py:54
  311.5 18.4 %collective-permute-start.51 = (bf16[96,768]{1,0:T(8,128)(2,1)S(1)}, bf16[96,768]{1,0:T(8,128)(2,1)S(1)}, u32[]{:S(2)}, u32[]{:S(2)}) collective-permute-start(bf16[96,768]{1,0:T(8,128)(2,1)S(1)} %get-tuple-element.345), channel_id=1, source_target_pairs={{0,8},{4,12},{8,0},{12,4},{16,24},{20,28},{24,16},{28,20},{1,9},{5... | collective-permute-start | bytes 442376 | tf_op jit(solution)/shard_map/ppermute | solution.py:54
  329.9 16.1 %collective-permute-start.58 = (bf16[4,96,768]{2,1,0:T(8,128)(2,1)S(1)}, bf16[4,96,768]{2,1,0:T(8,128)(2,1)S(1)}, u32[]{:S(2)}, u32[]{:S(2)}) collective-permute-start(bf16[4,96,768]{2,1,0:T(8,128)(2,1)S(1)} %pad_maximum_fusion.8.own), channel_id=1, source_target_pairs={{0,4},{4,0},{8,12},{12,8},{16,20},{20,16},{24,28},{28,24},{1,5},{5... | collective-permute-start | bytes 1769480 | tf_op jit(solution)/shard_map/ppermute | solution.py:54
  359.7 19.9 %collective-permute-start.60 = (bf16[6,256,256]{2,1,0:T(8,128)(2,1)}, bf16[6,256,256]{2,1,0:T(8,128)(2,1)}, u32[]{:S(2)}, u32[]{:S(2)}) collective-permute-start(bf16[6,256,256]{2,1,0:T(8,128)(2,1)} %fusion.22), channel_id=1, source_target_pairs={{0,2},{1,3},{2,0},{3,1},{4,6},{5,7},{6,4},{7,5},{8,10},{9,11},{10,... | collective-permute-start | bytes 2359304 | tf_op jit(solution)/shard_map/ppermute | solution.py:54
  393.1 6.9 %collective-permute-start.62 = (bf16[2,96,768]{2,1,0:T(8,128)(2,1)S(1)}, bf16[2,96,768]{2,1,0:T(8,128)(2,1)S(1)}, u32[]{:S(2)}, u32[]{:S(2)}) collective-permute-start(bf16[2,96,768]{2,1,0:T(8,128)(2,1)S(1)} %pad_maximum_fusion.12), channel_id=1, source_target_pairs={{0,1},{1,0},{2,3},{3,2},{4,5},{5,4},{6,7},{7,6},{8,9},{9,8},{10,11... | collective-permute-start | bytes 884744 | tf_op jit(solution)/shard_map/ppermute | solution.py:54
  (124 other events, 699.6 us)
Sparse Core Ops, SparseCore 0:
  171.6 78.5 all-gather.2
  276.2 51.4 all-gather.4

commit v5 on v4

--- a/solution.py
+++ b/solution.py
@@ -144,6 +144,12 @@
         compiler_params=pltpu.CompilerParams(vmem_limit_bytes=32 * 1024 * 1024),
     )(position, lines, lines_x)
     return out.reshape(8 * rows, columns)
+
+
+def gather_came(shard):
+    if lax.axis_size("batch") != 8:
+        return [gather_lines(shard)]
+    return [swap(shard, "batch", 2 * mask) for mask in (1, 2, 3)]
 
 
 def gather_planes(lines):
@@ -672,9 +678,16 @@
     small = patch_width + extra_width
     chunk_one = jnp.concatenate([quarter_patch.astype(BF), quarter_table, w_qkv.astype(BF)], 1)
     chunk_two = jnp.concatenate([w_out.astype(BF), w_up.astype(BF)], 1)
-    chunk_three = jnp.concatenate([w_down.astype(BF), quarter_head], 1)
+    chunk_three, chunk_four = w_down.astype(BF), quarter_head
     lines = gather_lines(chunk_one)
-    chunk_two, lines = tie(chunk_two, lines)
+    patches = jnp.concatenate(
+        [
+            jnp.pad(at(low_patches, side), ((0, low_rows - grid_low), (0, 0))),
+            jnp.pad(at(high_patches, side), ((0, high_rows - grid_high), (0, 0))),
+        ],
+        0,
+    )
+    chunk_two, chunk_four, lines, patches = tie(chunk_two, chunk_four, lines, patches)
     planes = gather_planes(lines)
     lines_two = gather_lines(chunk_two)
     planes, lines_two = tie(planes, lines_two)
@@ -702,18 +715,14 @@
     added = jnp.concatenate([add_low, add_high], 0)
     is_patch = jnp.concatenate([row_low < grid_low, row_high < grid_high], 0)
     is_token = jnp.concatenate([row_low <= grid_low, row_high <= grid_high], 0)
-    patches = jnp.concatenate(
-        [
-            jnp.pad(at(low_patches, side), ((0, low_rows - grid_low), (0, 0))),
-            jnp.pad(at(high_patches, side), ((0, high_rows - grid_high), (0, 0))),
-        ],
-        0,
-    )
     initial = dot(patches, full_patch) + added
     unit_one, _ = normalize(initial)
     normed = (unit_one * vec[0] + vec[1]).astype(BF)
     packed = dot(normed, full_qkv).astype(BF)
-    packed, planes_two, lines_three = tie(packed, planes_two, lines_three)
+    packed, planes_two, lines_three, chunk_four = tie(
+        packed, planes_two, lines_three, chunk_four
+    )
+    came_four = gather_came(chunk_four)
     ends_two = gather_ends(planes_two)
     planes_three = gather_planes(lines_three)
     spans = ((0, low_rows, grid_low + 1), (low_rows, high_rows, grid_high + 1))
@@ -728,7 +737,10 @@
     ends_three = gather_ends(planes_three)
     slope, active_sums = hidden_layer(spans, normed_two, full_up)
     active_sums = active_sums[:2]
-    full_down, both_head = gather_last(planes_three, ends_three, (hidden, head_width))
+    slope, ends_three, came_four = tie(slope, ends_three, came_four)
+    planes_four = gather_planes(jnp.stack([chunk_four, *came_four]) if batch_size == 8 else came_four[0])
+    (full_down,) = gather_last(planes_three, ends_three, (hidden,))
+    (both_head,) = gather_last(planes_four, gather_ends(planes_four), (head_width,))
     (full_head,) = all_quarters(both_head)
     held = jnp.concatenate([mom_qkv, mom_out, mom_up, mom_down], 1).astype(BF)
     held, full_down = tie(held, full_down)
@@ -752,10 +764,10 @@
     common = jnp.concatenate([pooled_high, pooled_low, tags], 1)
     active_low = active_sums.astype(BF)
     came = swap_side(jnp.concatenate([common, active_low[:, hidden:]], 1))
-    came, full_head = tie(came, full_head)
     mine = jnp.concatenate([common, active_low[:, :hidden]], 1)
     both_sides = in_order(jnp.stack([mine, came]), side, 1)
     everyone = gather_small(both_sides.transpose(1, 0, 2))
+    everyone, full_head = tie(everyone, full_head)
     images = batch_size * 4
     everyone = everyone.reshape(images, 2 * D + 128 + hidden)
     pooled = everyone[:, :D].astype(F32) + everyone[:, D : 2 * D].astype(F32)

time: 412 us -> 402 us (0.976)
  waiting for transfers between devices: 126 us -> 111 us
  Pallas kernels: 81.4 us -> 72 us
  starting transfers between devices: 68.9 us -> 76.3 us
    ppermute x65 -> x72, waiting for transfers between devices: 126 us -> 111 us  [swap(): lax.ppermute(values, axis, [(index, index ^ mask) for index in range(coun...]
    pallas_call x3 -> x4, Pallas kernels: 20.7 us -> 11.4 us  [place(): pl.pallas_call(lambda *refs: place_kernel(splits, *refs), grid_spec=pltpu...]
    ppermute x65 -> x72, starting transfers between devices: 68.8 us -> 75.7 us  [swap(): lax.ppermute(values, axis, [(index, index ^ mask) for index in range(coun...]
    unnamed x219 -> x203, local copies, waits for them, and re-layouts: 19.7 us -> 21.1 us
  transfers between devices with their start and end apart: 67 -> 74, of which waited for: 33 -> 37; matrix products, arithmetic and copies ran while one was open for 21% -> 22% of each run, Pallas kernels for 12% -> 13%
where the time goes in v5:
time: 402 us; the launch traced here: 398 us
  waiting for transfers between devices  111 us (28%)
  starting transfers between devices  76.3 us (19%)
  Pallas kernels  72 us (18%)
  other arithmetic  44.6 us (11%)
  local copies, waits for them, and re-layouts  43.5 us (11%)
  matrix products  32.3 us (8%)
  between operations  19 us (5%)
    ppermute x72, waiting for transfers between devices, swap(): lax.ppermute(values, axis, [(index, index ^ mask) for index in range(coun...  111 us
    ppermute x72, starting transfers between devices, swap(): lax.ppermute(values, axis, [(index, index ^ mask) for index in range(coun...  75.7 us
    dot_general x25, matrix products, dot(): lax.dot_general(left, right, (((left_dim,), (right_dim,)), ((), ())), pre...  32.3 us
    unnamed x203, local copies, waits for them, and re-layouts  21.1 us
    pallas_call x2, Pallas kernels, attention(): pl.pallas_call(run, grid=(stop - begin,), in_specs=[wide] + [narrow] * le...  20.5 us
    pallas_call x4, Pallas kernels, place(): pl.pallas_call(lambda *refs: place_kernel(splits, *refs), grid_spec=pltpu...  11.4 us
    pallas_call x3, Pallas kernels, row_grid(): pl.pallas_call(body, grid=(tokens // rows,), in_specs=[block] * len(input...  10.1 us
    pallas_call x2, Pallas kernels, moment_grams(): pl.pallas_call(lambda *refs: moment_kernel(pieces, count, *refs), grid=(1...  9.68 us
  transfers between devices with their start and end apart: 74, of which 37 were waited for; matrix products, arithmetic and copies ran while one was open for 22% of the time, Pallas kernels for 13%

profile of v5, /device:TPU:0, one launch (start us, length us, event | category | flops | bytes accessed | tf_op | source)
XLA Modules:
  0.0 398.3 jit_solution(12924480707864681093)
XLA Ops:
  12.1 5.0 %collective-permute-start.2 = (bf16[96,832]{1,0:T(8,128)(2,1)}, bf16[96,832]{1,0:T(8,128)(2,1)}, u32[]{:S(2)}, u32[]{:S(2)}) collective-permute-start(bf16[96,832]{1,0:T(8,128)(2,1)} %pad_maximum_fusion.16), channel_id=1, source_target_pairs={{0,24},{4,28},{8,16},{12,20},{16,8},{20,12},{24,0},{28,4},{1,25},{... | collective-permute-start | bytes 479240 | tf_op jit(solution)/shard_map/ppermute | solution.py:54
  22.8 9.3 %collective-permute-done.1 = bf16[96,832]{1,0:T(8,128)(2,1)} collective-permute-done((bf16[96,832]{1,0:T(8,128)(2,1)}, bf16[96,832]{1,0:T(8,128)(2,1)}, u32[]{:S(2)}, u32[]{:S(2)}) %collective-permute-start.1) | collective-permute-done | bytes 159776 | tf_op jit(solution)/shard_map/ppermute | solution.py:54
  36.3 2.5 collective-permute-start.7
  40.7 5.3 %collective-permute-done.7 = bf16[96,960]{1,0:T(8,128)(2,1)S(1)} collective-permute-done((bf16[96,960]{1,0:T(8,128)(2,1)S(1)}, bf16[96,960]{1,0:T(8,128)(2,1)S(1)}, u32[]{:S(2)}, u32[]{:S(2)}) %collective-permute-start.7) | collective-permute-done | bytes 184352 | tf_op jit(solution)/shard_map/ppermute | solution.py:54
  46.0 7.7 %collective-permute-done.6 = bf16[96,960]{1,0:T(8,128)(2,1)S(1)} collective-permute-done((bf16[96,960]{1,0:T(8,128)(2,1)S(1)}, bf16[96,960]{1,0:T(8,128)(2,1)S(1)}, u32[]{:S(2)}, u32[]{:S(2)}) %collective-permute-start.6) | collective-permute-done | bytes 184352 | tf_op jit(solution)/shard_map/ppermute | solution.py:54
  56.5 6.8 %collective-permute-done.8.refs_4_ = bf16[2,96,832]{2,1,0:T(8,128)(2,1)S(1)} collective-permute-done((bf16[2,96,832]{2,1,0:T(8,128)(2,1)}, bf16[2,96,832]{2,1,0:T(8,128)(2,1)S(1)}, u32[]{:S(2)}, u32[]{:S(2)}) %collective-permute-start.8) | collective-permute-done | bytes 319520 | tf_op jit(solution)/shard_map/ppermute | solution.py:54
  64.4 4.2 %shard_map.434 = (bf16[4,2,96,512]{3,2,1,0:T(8,128)(2,1)}, bf16[4,2,96,1152]{3,2,1,0:T(8,128)(2,1)S(1)}) custom-call(s32[2]{0:T(128)S(1)} %pad_add_fusion.1.refs_0_.spot, bf16[4,96,832]{2,1,0:T(8,128)(2,1)S(1)} %pad_maximum_fusion.4.refs_1_, bf16[4,96,832]{2,1,0:T(8,128)(2,1)S(1)} %collective-permute-done.3.refs_2_, ...), custom_call_target="tpu_custom_call" | custom-call | tf_op jit(solution)/shard_map/pallas_call | solution.py:94
  74.9 2.3 collective-permute-start.15
  77.2 2.1 collective-permute-start.13
  87.0 2.0 collective-permute-done.14
  94.4 7.5 %shard_map.436 = bf16[800,384]{1,0:T(8,128)(2,1)S(1)} custom-call(bf16[800,1152]{1,0:T(8,128)(2,1)S(1)} %convolution_convert_fusion.refs_0_), custom_call_target="tpu_custom_call" | custom-call | tf_op jit(solution)/shard_map/pallas_call | solution.py:379
  113.7 2.8 collective-permute-start.24
  118.1 4.5 %shard_map.438 = (f32[800,768]{1,0:T(8,128)S(1)}, bf16[800,768]{1,0:T(8,128)(2,1)S(1)}, f32[8,768]{1,0:T(8,128)S(1)}) custom-call(f32[800,768]{1,0:T(8,128)S(1)} %get-tuple-element.382.refs_0_, bf16[800,768]{1,0:T(8,128)(2,1)} %convolution_convert_fusion.4.refs_1_, bf16[800,768]{1,0:T(8,128)(2,1)} %collective-permute-done.18.refs_2_, ...), custom_call_target="tpu_custom_call" | custom-call | tf_op jit(solution)/shard_map/pallas_call | solution.py:410
  127.3 4.8 %shard_map.439 = (bf16[800,1536]{1,0:T(8,128)(2,1)S(1)}, f32[8,1536]{1,0:T(8,128)S(1)}) custom-call(bf16[800,768]{1,0:T(8,128)(2,1)S(1)} %get-tuple-element.140.refs_0_, bf16[768,1536]{1,0:T(8,128)(2,1)S(1)} %bitcast.260), custom_call_target="tpu_custom_call" | custom-call | tf_op jit(solution)/shard_map/pallas_call | solution.py:479
  134.4 2.8 shard_map.440
  148.6 2.3 collective-permute-start.31
  150.9 2.1 collective-permute-start.29
  158.7 2.6 collective-permute-done.34.refs_4_
  161.4 3.7 collective-permute-done.35.refs_5_
  165.0 2.7 shard_map.441
  168.2 2.2 collective-permute-done.36.refs_2_
  174.0 2.1 fusion.161
  184.0 2.9 convolution_convert_fusion.5.refs_1_
  186.9 3.4 convolution_convert_fusion.1
  193.9 2.7 shard_map.443
  198.1 13.0 %shard_map.444 = bf16[800,1152]{1,0:T(8,128)(2,1)S(1)} custom-call(bf16[800,1152]{1,0:T(8,128)(2,1)S(1)} %copy-done.7, bf16[800,384]{1,0:T(8,128)(2,1)S(1)} %convolution_convert_fusion.6.refs_1_), custom_call_target="tpu_custom_call" | custom-call | tf_op jit(solution)/shard_map/pallas_call | solution.py:379
  215.9 2.4 convolution_convert_fusion.2
  226.4 2.9 shard_map.445
  231.6 2.6 concatenate.135
  256.6 3.6 collective-permute-done.48
  263.5 2.3 collective-permute-start.54
  265.8 2.2 collective-permute-start.52
  270.5 2.8 collective-permute-done.54
  273.2 11.1 %collective-permute-done.53 = bf16[96,1024]{1,0:T(8,128)(2,1)S(1)} collective-permute-done((bf16[96,1024]{1,0:T(8,128)(2,1)S(1)}, bf16[96,1024]{1,0:T(8,128)(2,1)S(1)}, u32[]{:S(2)}, u32[]{:S(2)}) %collective-permute-start.53) | collective-permute-done | bytes 196640 | tf_op jit(solution)/shard_map/ppermute | solution.py:54
  285.2 2.1 shard_map.446
  290.5 2.4 collective-permute-done.56
  294.4 2.7 collective-permute-start.60
  301.5 4.0 %collective-permute-done.60 = bf16[96,768]{1,0:T(8,128)(2,1)S(1)} collective-permute-done((bf16[96,768]{1,0:T(8,128)(2,1)S(1)}, bf16[96,768]{1,0:T(8,128)(2,1)S(1)}, u32[]{:S(2)}, u32[]{:S(2)}) %collective-permute-start.60) | collective-permute-done | bytes 147488 | tf_op jit(solution)/shard_map/ppermute | solution.py:54
  305.6 9.9 %collective-permute-done.59 = bf16[96,768]{1,0:T(8,128)(2,1)S(1)} collective-permute-done((bf16[96,768]{1,0:T(8,128)(2,1)S(1)}, bf16[96,768]{1,0:T(8,128)(2,1)S(1)}, u32[]{:S(2)}, u32[]{:S(2)}) %collective-permute-start.59) | collective-permute-done | bytes 147488 | tf_op jit(solution)/shard_map/ppermute | solution.py:54
  316.9 3.6 collective-permute-done.63
  320.5 4.5 %collective-permute-done.64 = f32[8,128]{1,0:T(8,128)S(1)} collective-permute-done((f32[8,128]{1,0:T(8,128)S(1)}, f32[8,128]{1,0:T(8,128)S(1)}, u32[]{:S(2)}, u32[]{:S(2)}) %collective-permute-start.64) | collective-permute-done | bytes 4128 | tf_op jit(solution)/shard_map/ppermute | solution.py:54
  326.3 5.6 %shard_map.448 = (bf16[768,768]{1,0:T(8,128)(2,1)}, bf16[768,768]{1,0:T(8,128)(2,1)}, bf16[2,6,256,256]{3,2,1,0:T(8,128)(2,1)}) custom-call(f32[1]{0:T(128)} %bitcast.94.refs_0_, bf16[768,2304]{1,0:T(8,128)(2,1)} %all-gather.3.cloned.1.call-done.refs_1_.refs_2_, bf16[768,2304]{1,0:T(8,128)(2,1)} %all-gather.3.cloned.1.call-done.refs_1_.refs_2_, ...), custom_call_target="tpu_custom_call" | custom-call | tf_op jit(solution)/shard_map/pallas_call | solution.py:612
  333.9 4.1 %shard_map.450 = (bf16[768,768]{1,0:T(8,128)(2,1)}, bf16[2,6,256,256]{3,2,1,0:T(8,128)(2,1)}) custom-call(f32[1]{0:T(128)} %bitcast.94.refs_0_, bf16[768,2304]{1,0:T(8,128)(2,1)} %all-gather.3.cloned.1.call-done.refs_1_.refs_2_, bf16[768,768]{1,0:T(8,128)(2,1)} %bitcast.257), custom_call_target="tpu_custom_call" | custom-call | tf_op jit(solution)/shard_map/pallas_call | solution.py:612
  338.0 2.9 broadcast_select_fusion.1
  350.6 2.4 multiply_subtract_fusion.1
  357.0 8.5 %collective-permute-done.67.came_side = bf16[6,256,256]{2,1,0:T(8,128)(2,1)} collective-permute-done((bf16[6,256,256]{2,1,0:T(8,128)(2,1)}, bf16[6,256,256]{2,1,0:T(8,128)(2,1)}, u32[]{:S(2)}, u32[]{:S(2)}) %collective-permute-start.67) | collective-permute-done | bytes 786464 | tf_op jit(solution)/shard_map/ppermute | solution.py:54
  365.5 8.2 %shard_map.451 = (bf16[96,768]{1,0:T(8,128)(2,1)S(1)}, f32[8,128]{1,0:T(8,128)S(1)}) custom-call(s32[2]{0:T(128)S(1)} %pad_add_fusion.2.start, bf16[2,6,256,256]{3,2,1,0:T(8,128)(2,1)S(1)} %get-tuple-element.319.kept, bf16[2,6,256,256]{3,2,1,0:T(8,128)(2,1)S(1)} %collective-permute-done.66.came, bf16[6,256,256]{2,1,0:T(8,128)(2,1)} %collective-permute-done.67.came_side), custom_call_target="tpu_custom_call" | custom-call | tf_op jit(solution)/shard_map/pallas_call | solution.py:542
  375.1 3.8 collective-permute-done.68
  (554 shorter events, 175.2 us)
Async XLA Ops:
  7.2 238.8 %all-gather.3.cloned.1.call-start = ((), (), s32[]{:S(2)}) async-start(), calls=%async_computation | async-start | bytes 3981312 | tf_op jit(solution)/shard_map/all_gather | solution.py:747
  12.1 10.7 %collective-permute-start.2 = (bf16[96,832]{1,0:T(8,128)(2,1)}, bf16[96,832]{1,0:T(8,128)(2,1)}, u32[]{:S(2)}, u32[]{:S(2)}) collective-permute-start(bf16[96,832]{1,0:T(8,128)(2,1)} %pad_maximum_fusion.16), channel_id=1, source_target_pairs={{0,24},{4,28},{8,16},{12,20},{16,8},{20,12},{24,0},{28,4},{1,25},{... | collective-permute-start | bytes 479240 | tf_op jit(solution)/shard_map/ppermute | solution.py:54
  17.2 14.9 %collective-permute-start.1 = (bf16[96,832]{1,0:T(8,128)(2,1)}, bf16[96,832]{1,0:T(8,128)(2,1)}, u32[]{:S(2)}, u32[]{:S(2)}) collective-permute-start(bf16[96,832]{1,0:T(8,128)(2,1)} %pad_maximum_fusion.16), channel_id=1, source_target_pairs={{0,16},{4,20},{8,24},{12,28},{16,0},{20,4},{24,8},{28,12},{1,17},{... | collective-permute-start | bytes 479240 | tf_op jit(solution)/shard_map/ppermute | solution.py:54
  17.2 14.9 %collective-permute-start = (bf16[96,832]{1,0:T(8,128)(2,1)}, bf16[96,832]{1,0:T(8,128)(2,1)}, u32[]{:S(2)}, u32[]{:S(2)}) collective-permute-start(bf16[96,832]{1,0:T(8,128)(2,1)} %pad_maximum_fusion.16), channel_id=1, source_target_pairs={{0,8},{4,12},{8,0},{12,4},{16,24},{20,28},{24,16},{28,20},{1,9},{5... | collective-permute-start | bytes 479240 | tf_op jit(solution)/shard_map/ppermute | solution.py:54
  33.3 20.6 %collective-permute-start.3 = (bf16[4,96,832]{2,1,0:T(8,128)(2,1)S(1)}, bf16[4,96,832]{2,1,0:T(8,128)(2,1)S(1)}, u32[]{:S(2)}, u32[]{:S(2)}) collective-permute-start(bf16[4,96,832]{2,1,0:T(8,128)(2,1)S(1)} %pad_maximum_fusion.4.refs_1_), channel_id=1, source_target_pairs={{0,4},{4,0},{8,12},{12,8},{16,20},{20,16},{24,28},{28,24},{1,5},{5... | collective-permute-start | bytes 1916936 | tf_op jit(solution)/shard_map/ppermute | solution.py:54
  34.8 19.0 %collective-permute-start.4 = (bf16[4,96,832]{2,1,0:T(8,128)(2,1)S(1)}, bf16[4,96,832]{2,1,0:T(8,128)(2,1)S(1)}, u32[]{:S(2)}, u32[]{:S(2)}) collective-permute-start(bf16[4,96,832]{2,1,0:T(8,128)(2,1)S(1)} %pad_maximum_fusion.4.refs_1_), channel_id=1, source_target_pairs={{0,2},{1,3},{2,0},{3,1},{4,6},{5,7},{6,4},{7,5},{8,10},{9,11},{10,... | collective-permute-start | bytes 1916936 | tf_op jit(solution)/shard_map/ppermute | solution.py:54
  36.3 9.7 %collective-permute-start.7 = (bf16[96,960]{1,0:T(8,128)(2,1)S(1)}, bf16[96,960]{1,0:T(8,128)(2,1)S(1)}, u32[]{:S(2)}, u32[]{:S(2)}) collective-permute-start(bf16[96,960]{1,0:T(8,128)(2,1)S(1)} %pad_maximum_fusion.14), channel_id=1, source_target_pairs={{0,24},{4,28},{8,16},{12,20},{16,8},{20,12},{24,0},{28,4},{1,25},{... | collective-permute-start | bytes 552968 | tf_op jit(solution)/shard_map/ppermute | solution.py:54
  38.8 14.9 %collective-permute-start.6 = (bf16[96,960]{1,0:T(8,128)(2,1)S(1)}, bf16[96,960]{1,0:T(8,128)(2,1)S(1)}, u32[]{:S(2)}, u32[]{:S(2)}) collective-permute-start(bf16[96,960]{1,0:T(8,128)(2,1)S(1)} %pad_maximum_fusion.14), channel_id=1, source_target_pairs={{0,16},{4,20},{8,24},{12,28},{16,0},{20,4},{24,8},{28,12},{1,17},{... | collective-permute-start | bytes 552968 | tf_op jit(solution)/shard_map/ppermute | solution.py:54
  38.8 14.9 %collective-permute-start.5 = (bf16[96,960]{1,0:T(8,128)(2,1)S(1)}, bf16[96,960]{1,0:T(8,128)(2,1)S(1)}, u32[]{:S(2)}, u32[]{:S(2)}) collective-permute-start(bf16[96,960]{1,0:T(8,128)(2,1)S(1)} %pad_maximum_fusion.14), channel_id=1, source_target_pairs={{0,8},{4,12},{8,0},{12,4},{16,24},{20,28},{24,16},{28,20},{1,9},{5... | collective-permute-start | bytes 552968 | tf_op jit(solution)/shard_map/ppermute | solution.py:54
  54.6 8.7 %collective-permute-start.8 = (bf16[2,96,832]{2,1,0:T(8,128)(2,1)}, bf16[2,96,832]{2,1,0:T(8,128)(2,1)S(1)}, u32[]{:S(2)}, u32[]{:S(2)}) collective-permute-start(bf16[2,96,832]{2,1,0:T(8,128)(2,1)} %slice.280), channel_id=1, source_target_pairs={{0,2},{1,3},{2,0},{3,1},{4,6},{5,7},{6,4},{7,5},{8,10},{9,11},{10,... | collective-permute-start | bytes 958472 | tf_op jit(solution)/shard_map/ppermute | solution.py:54
  55.9 8.5 %collective-permute-start.9 = (bf16[2,96,832]{2,1,0:T(8,128)(2,1)}, bf16[2,96,832]{2,1,0:T(8,128)(2,1)}, u32[]{:S(2)}, u32[]{:S(2)}) collective-permute-start(bf16[2,96,832]{2,1,0:T(8,128)(2,1)} %slice.281), channel_id=1, source_target_pairs={{0,4},{4,0},{8,12},{12,8},{16,20},{20,16},{24,28},{28,24},{1,5},{5... | collective-permute-start | bytes 958472 | tf_op jit(solution)/shard_map/ppermute | solution.py:54
  70.9 20.0 %collective-permute-start.11 = (bf16[4,96,960]{2,1,0:T(8,128)(2,1)S(1)}, bf16[4,96,960]{2,1,0:T(8,128)(2,1)S(1)}, u32[]{:S(2)}, u32[]{:S(2)}) collective-permute-start(bf16[4,96,960]{2,1,0:T(8,128)(2,1)S(1)} %pad_maximum_fusion.2.refs_1_), channel_id=1, source_target_pairs={{0,4},{4,0},{8,12},{12,8},{16,20},{20,16},{24,28},{28,24},{1,5},{5... | collective-permute-start | bytes 2211848 | tf_op jit(solution)/shard_map/ppermute | solution.py:54
  71.5 19.7 %collective-permute-start.12 = (bf16[4,96,960]{2,1,0:T(8,128)(2,1)S(1)}, bf16[4,96,960]{2,1,0:T(8,128)(2,1)S(1)}, u32[]{:S(2)}, u32[]{:S(2)}) collective-permute-start(bf16[4,96,960]{2,1,0:T(8,128)(2,1)S(1)} %pad_maximum_fusion.2.refs_1_), channel_id=1, source_target_pairs={{0,2},{1,3},{2,0},{3,1},{4,6},{5,7},{6,4},{7,5},{8,10},{9,11},{10,... | collective-permute-start | bytes 2211848 | tf_op jit(solution)/shard_map/ppermute | solution.py:54
  74.9 12.1 %collective-permute-start.15 = (bf16[96,768]{1,0:T(8,128)(2,1)S(1)}, bf16[96,768]{1,0:T(8,128)(2,1)S(1)}, u32[]{:S(2)}, u32[]{:S(2)}) collective-permute-start(bf16[96,768]{1,0:T(8,128)(2,1)S(1)} %convert_element_type.319), channel_id=1, source_target_pairs={{0,24},{4,28},{8,16},{12,20},{16,8},{20,12},{24,0},{28,4},{1,25},{... | collective-permute-start | bytes 442376 | tf_op jit(solution)/shard_map/ppermute | solution.py:54
  77.2 11.8 %collective-permute-start.14 = (bf16[96,768]{1,0:T(8,128)(2,1)S(1)}, bf16[96,768]{1,0:T(8,128)(2,1)S(1)}, u32[]{:S(2)}, u32[]{:S(2)}) collective-permute-start(bf16[96,768]{1,0:T(8,128)(2,1)S(1)} %convert_element_type.319), channel_id=1, source_target_pairs={{0,16},{4,20},{8,24},{12,28},{16,0},{20,4},{24,8},{28,12},{1,17},{... | collective-permute-start | bytes 442376 | tf_op jit(solution)/shard_map/ppermute | solution.py:54
  77.2 11.8 %collective-permute-start.13 = (bf16[96,768]{1,0:T(8,128)(2,1)S(1)}, bf16[96,768]{1,0:T(8,128)(2,1)S(1)}, u32[]{:S(2)}, u32[]{:S(2)}) collective-permute-start(bf16[96,768]{1,0:T(8,128)(2,1)S(1)} %convert_element_type.319), channel_id=1, source_target_pairs={{0,8},{4,12},{8,0},{12,4},{16,24},{20,28},{24,16},{28,20},{1,9},{5... | collective-permute-start | bytes 442376 | tf_op jit(solution)/shard_map/ppermute | solution.py:54
  91.2 10.7 %collective-permute-start.16 = (bf16[2,96,960]{2,1,0:T(8,128)(2,1)S(1)}, bf16[2,96,960]{2,1,0:T(8,128)(2,1)S(1)}, u32[]{:S(2)}, u32[]{:S(2)}) collective-permute-start(bf16[2,96,960]{2,1,0:T(8,128)(2,1)S(1)} %slice.290), channel_id=1, source_target_pairs={{0,2},{1,3},{2,0},{3,1},{4,6},{5,7},{6,4},{7,5},{8,10},{9,11},{10,... | collective-permute-start | bytes 1105928 | tf_op jit(solution)/shard_map/ppermute | solution.py:54
  92.8 10.3 %collective-permute-start.17 = (bf16[2,96,960]{2,1,0:T(8,128)(2,1)S(1)}, bf16[2,96,960]{2,1,0:T(8,128)(2,1)S(1)}, u32[]{:S(2)}, u32[]{:S(2)}) collective-permute-start(bf16[2,96,960]{2,1,0:T(8,128)(2,1)S(1)} %slice.291), channel_id=1, source_target_pairs={{0,4},{4,0},{8,12},{12,8},{16,20},{20,16},{24,28},{28,24},{1,5},{5... | collective-permute-start | bytes 1105928 | tf_op jit(solution)/shard_map/ppermute | solution.py:54
  106.7 9.8 %collective-permute-start.18 = (bf16[800,768]{1,0:T(8,128)(2,1)}, bf16[800,768]{1,0:T(8,128)(2,1)}, u32[]{:S(2)}, u32[]{:S(2)}) collective-permute-start(bf16[800,768]{1,0:T(8,128)(2,1)} %convolution_convert_fusion.4.refs_1_), channel_id=1, source_target_pairs={{0,1},{1,0},{2,3},{3,2},{4,5},{5,4},{6,7},{7,6},{8,9},{9,8},{10,11... | collective-permute-start | bytes 3686408 | tf_op jit(solution)/shard_map/ppermute | solution.py:54
  106.9 17.1 %collective-permute-start.19 = (bf16[4,96,768]{2,1,0:T(8,128)(2,1)}, bf16[4,96,768]{2,1,0:T(8,128)(2,1)S(1)}, u32[]{:S(2)}, u32[]{:S(2)}) collective-permute-start(bf16[4,96,768]{2,1,0:T(8,128)(2,1)} %pad_maximum_fusion.5.refs_1_), channel_id=1, source_target_pairs={{0,4},{4,0},{8,12},{12,8},{16,20},{20,16},{24,28},{28,24},{1,5},{5... | collective-permute-start | bytes 1769480 | tf_op jit(solution)/shard_map/ppermute | solution.py:54
  108.4 15.8 %collective-permute-start.20 = (bf16[4,96,768]{2,1,0:T(8,128)(2,1)}, bf16[4,96,768]{2,1,0:T(8,128)(2,1)}, u32[]{:S(2)}, u32[]{:S(2)}) collective-permute-start(bf16[4,96,768]{2,1,0:T(8,128)(2,1)} %pad_maximum_fusion.5.refs_1_), channel_id=1, source_target_pairs={{0,2},{1,3},{2,0},{3,1},{4,6},{5,7},{6,4},{7,5},{8,10},{9,11},{10,... | collective-permute-start | bytes 1769480 | tf_op jit(solution)/shard_map/ppermute | solution.py:54
  113.6 18.6 %collective-permute-start.23 = (bf16[96,320]{1,0:T(8,128)(2,1)S(1)}, bf16[96,320]{1,0:T(8,128)(2,1)S(1)}, u32[]{:S(2)}, u32[]{:S(2)}) collective-permute-start(bf16[96,320]{1,0:T(8,128)(2,1)S(1)} %pad_dynamic-slice_fusion.16), channel_id=1, source_target_pairs={{0,8},{4,12},{8,0},{12,4},{16,24},{20,28},{24,16},{28,20},{1,9},{5... | collective-permute-start | bytes 184328 | tf_op jit(solution)/shard_map/ppermute | solution.py:54
  113.7 18.5 %collective-permute-start.24 = (bf16[96,320]{1,0:T(8,128)(2,1)S(1)}, bf16[96,320]{1,0:T(8,128)(2,1)S(1)}, u32[]{:S(2)}, u32[]{:S(2)}) collective-permute-start(bf16[96,320]{1,0:T(8,128)(2,1)S(1)} %pad_dynamic-slice_fusion.16), channel_id=1, source_target_pairs={{0,16},{4,20},{8,24},{12,28},{16,0},{20,4},{24,8},{28,12},{1,17},{... | collective-permute-start | bytes 184328 | tf_op jit(solution)/shard_map/ppermute | solution.py:54
  116.6 15.6 %collective-permute-start.25 = (bf16[96,320]{1,0:T(8,128)(2,1)S(1)}, bf16[96,320]{1,0:T(8,128)(2,1)S(1)}, u32[]{:S(2)}, u32[]{:S(2)}) collective-permute-start(bf16[96,320]{1,0:T(8,128)(2,1)S(1)} %pad_dynamic-slice_fusion.16), channel_id=1, source_target_pairs={{0,24},{4,28},{8,16},{12,20},{16,8},{20,12},{24,0},{28,4},{1,25},{... | collective-permute-start | bytes 184328 | tf_op jit(solution)/shard_map/ppermute | solution.py:54
  145.2 10.9 %collective-permute-start.32 = (bf16[4,96,320]{2,1,0:T(8,128)(2,1)S(1)}, bf16[4,96,320]{2,1,0:T(8,128)(2,1)S(1)}, u32[]{:S(2)}, u32[]{:S(2)}) collective-permute-start(bf16[4,96,320]{2,1,0:T(8,128)(2,1)S(1)} %pad_maximum_fusion.12.refs_1_), channel_id=1, source_target_pairs={{0,4},{4,0},{8,12},{12,8},{16,20},{20,16},{24,28},{28,24},{1,5},{5... | collective-permute-start | bytes 737288 | tf_op jit(solution)/shard_map/ppermute | solution.py:54
  146.7 10.4 %collective-permute-start.33 = (bf16[4,96,320]{2,1,0:T(8,128)(2,1)S(1)}, bf16[4,96,320]{2,1,0:T(8,128)(2,1)}, u32[]{:S(2)}, u32[]{:S(2)}) collective-permute-start(bf16[4,96,320]{2,1,0:T(8,128)(2,1)S(1)} %pad_maximum_fusion.12.refs_1_), channel_id=1, source_target_pairs={{0,2},{1,3},{2,0},{3,1},{4,6},{5,7},{6,4},{7,5},{8,10},{9,11},{10,... | collective-permute-start | bytes 737288 | tf_op jit(solution)/shard_map/ppermute | solution.py:54
  147.6 178.7 %all-gather.5.cloned.1.call-start = ((), (), s32[]{:S(2)}) async-start(), calls=%async_computation.1 | async-start | bytes 1327104 | tf_op jit(solution)/shard_map/all_gather | solution.py:922
  190.8 22.2 %collective-permute-start.38 = (bf16[4,2,48,768]{3,2,0,1:T(8,128)(2,1)S(1)}, bf16[4,2,48,768]{3,2,0,1:T(8,128)(2,1)S(1)}, u32[]{:S(2)}, u32[]{:S(2)}) collective-permute-start(bf16[4,2,48,768]{3,2,0,1:T(8,128)(2,1)S(1)} %copy.132), channel_id=1, source_target_pairs={{0,2},{1,3},{2,0},{3,1},{4,6},{5,7},{6,4},{7,5},{8,10},{9,11},{10,... | collective-permute-start | bytes 1769480 | tf_op jit(solution)/shard_map/ppermute | solution.py:54
  192.2 20.7 %collective-permute-start.39 = (bf16[2,4,48,768]{3,2,1,0:T(8,128)(2,1)S(1)}, bf16[2,4,48,768]{3,2,1,0:T(8,128)(2,1)S(1)}, u32[]{:S(2)}, u32[]{:S(2)}) collective-permute-start(bf16[2,4,48,768]{3,2,1,0:T(8,128)(2,1)S(1)} %pad_maximum_fusion.6), channel_id=1, source_target_pairs={{0,4},{4,0},{8,12},{12,8},{16,20},{20,16},{24,28},{28,24},{1,5},{5... | collective-permute-start | bytes 1769480 | tf_op jit(solution)/shard_map/ppermute | solution.py:54
  213.0 13.5 %collective-permute-start.40 = (bf16[800,768]{1,0:T(8,128)(2,1)S(1)}, bf16[800,768]{1,0:T(8,128)(2,1)S(1)}, u32[]{:S(2)}, u32[]{:S(2)}) collective-permute-start(bf16[800,768]{1,0:T(8,128)(2,1)S(1)} %convolution_convert_fusion.3.refs_1_), channel_id=1, source_target_pairs={{0,1},{1,0},{2,3},{3,2},{4,5},{5,4},{6,7},{7,6},{8,9},{9,8},{10,11... | collective-permute-start | bytes 3686408 | tf_op jit(solution)/shard_map/ppermute | solution.py:54
  213.3 16.2 %collective-permute-start.41 = (bf16[4,48,768]{2,1,0:T(8,128)(2,1)S(1)}, bf16[4,48,768]{2,1,0:T(8,128)(2,1)S(1)}, u32[]{:S(2)}, u32[]{:S(2)}) collective-permute-start(bf16[4,48,768]{2,1,0:T(8,128)(2,1)S(1)} %fusion.46), channel_id=1, source_target_pairs={{0,4},{4,0},{8,12},{12,8},{16,20},{20,16},{24,28},{28,24},{1,5},{5... | collective-permute-start | bytes 884744 | tf_op jit(solution)/shard_map/ppermute | solution.py:54
  214.0 15.5 %collective-permute-start.42 = (bf16[4,48,768]{2,1,0:T(8,128)(2,1)S(1)}, bf16[4,48,768]{2,1,0:T(8,128)(2,1)S(1)}, u32[]{:S(2)}, u32[]{:S(2)}) collective-permute-start(bf16[4,48,768]{2,1,0:T(8,128)(2,1)S(1)} %fusion.29), channel_id=1, source_target_pairs={{0,2},{1,3},{2,0},{3,1},{4,6},{5,7},{6,4},{7,5},{8,10},{9,11},{10,... | collective-permute-start | bytes 884744 | tf_op jit(solution)/shard_map/ppermute | solution.py:54
  220.2 22.9 %collective-permute-start.45 = (bf16[4,2,48,768]{3,2,0,1:T(8,128)(2,1)}, bf16[4,2,48,768]{3,2,0,1:T(8,128)(2,1)}, u32[]{:S(2)}, u32[]{:S(2)}) collective-permute-start(bf16[4,2,48,768]{3,2,0,1:T(8,128)(2,1)} %copy.141), channel_id=1, source_target_pairs={{0,2},{1,3},{2,0},{3,1},{4,6},{5,7},{6,4},{7,5},{8,10},{9,11},{10,... | collective-permute-start | bytes 1769480 | tf_op jit(solution)/shard_map/ppermute | solution.py:54
  224.9 19.6 %collective-permute-start.46 = (bf16[2,4,48,768]{3,2,1,0:T(8,128)(2,1)}, bf16[2,4,48,768]{3,2,1,0:T(8,128)(2,1)}, u32[]{:S(2)}, u32[]{:S(2)}) collective-permute-start(bf16[2,4,48,768]{3,2,1,0:T(8,128)(2,1)} %pad_maximum_fusion.7), channel_id=1, source_target_pairs={{0,4},{4,0},{8,12},{12,8},{16,20},{20,16},{24,28},{28,24},{1,5},{5... | collective-permute-start | bytes 1769480 | tf_op jit(solution)/shard_map/ppermute | solution.py:54
  236.6 9.4 %collective-permute-start.43 = (bf16[4,2,48,256]{3,2,0,1:T(8,128)(2,1)}, bf16[4,2,48,256]{3,2,0,1:T(8,128)(2,1)}, u32[]{:S(2)}, u32[]{:S(2)}) collective-permute-start(bf16[4,2,48,256]{3,2,0,1:T(8,128)(2,1)} %copy.140), channel_id=1, source_target_pairs={{0,2},{1,3},{2,0},{3,1},{4,6},{5,7},{6,4},{7,5},{8,10},{9,11},{10,... | collective-permute-start | bytes 589832 | tf_op jit(solution)/shard_map/ppermute | solution.py:54
  241.6 13.7 %collective-permute-start.49 = (bf16[96,768]{1,0:T(8,128)(2,1)}, bf16[96,768]{1,0:T(8,128)(2,1)}, u32[]{:S(2)}, u32[]{:S(2)}) collective-permute-start(bf16[96,768]{1,0:T(8,128)(2,1)} %get-tuple-element.331), channel_id=1, source_target_pairs={{0,8},{4,12},{8,0},{12,4},{16,24},{20,28},{24,16},{28,20},{1,9},{5... | collective-permute-start | bytes 442376 | tf_op jit(solution)/shard_map/ppermute | solution.py:54
  243.0 13.3 %collective-permute-start.50 = (bf16[96,768]{1,0:T(8,128)(2,1)}, bf16[96,768]{1,0:T(8,128)(2,1)}, u32[]{:S(2)}, u32[]{:S(2)}) collective-permute-start(bf16[96,768]{1,0:T(8,128)(2,1)} %get-tuple-element.332), channel_id=1, source_target_pairs={{0,16},{4,20},{8,24},{12,28},{16,0},{20,4},{24,8},{28,12},{1,17},{... | collective-permute-start | bytes 442376 | tf_op jit(solution)/shard_map/ppermute | solution.py:54
  244.6 11.8 %collective-permute-start.51 = (bf16[96,768]{1,0:T(8,128)(2,1)}, bf16[96,768]{1,0:T(8,128)(2,1)}, u32[]{:S(2)}, u32[]{:S(2)}) collective-permute-start(bf16[96,768]{1,0:T(8,128)(2,1)} %get-tuple-element.330), channel_id=1, source_target_pairs={{0,24},{4,28},{8,16},{12,20},{16,8},{20,12},{24,0},{28,4},{1,25},{... | collective-permute-start | bytes 442376 | tf_op jit(solution)/shard_map/ppermute | solution.py:54
  247.5 9.0 %collective-permute-start.47 = (bf16[4,48,1024]{2,1,0:T(8,128)(2,1)S(1)}, bf16[4,48,1024]{2,1,0:T(8,128)(2,1)S(1)}, u32[]{:S(2)}, u32[]{:S(2)}) collective-permute-start(bf16[4,48,1024]{2,1,0:T(8,128)(2,1)S(1)} %fusion.31), channel_id=1, source_target_pairs={{0,4},{4,0},{8,12},{12,8},{16,20},{20,16},{24,28},{28,24},{1,5},{5... | collective-permute-start | bytes 1179656 | tf_op jit(solution)/shard_map/ppermute | solution.py:54
  251.5 8.7 %collective-permute-start.48 = (bf16[4,48,1024]{2,1,0:T(8,128)(2,1)S(1)}, bf16[4,48,1024]{2,1,0:T(8,128)(2,1)S(1)}, u32[]{:S(2)}, u32[]{:S(2)}) collective-permute-start(bf16[4,48,1024]{2,1,0:T(8,128)(2,1)S(1)} %fusion.24), channel_id=1, source_target_pairs={{0,2},{1,3},{2,0},{3,1},{4,6},{5,7},{6,4},{7,5},{8,10},{9,11},{10,... | collective-permute-start | bytes 1179656 | tf_op jit(solution)/shard_map/ppermute | solution.py:54
  263.5 9.7 %collective-permute-start.54 = (bf16[96,1024]{1,0:T(8,128)(2,1)S(1)}, bf16[96,1024]{1,0:T(8,128)(2,1)S(1)}, u32[]{:S(2)}, u32[]{:S(2)}) collective-permute-start(bf16[96,1024]{1,0:T(8,128)(2,1)S(1)} %get-tuple-element.327), channel_id=1, source_target_pairs={{0,24},{4,28},{8,16},{12,20},{16,8},{20,12},{24,0},{28,4},{1,25},{... | collective-permute-start | bytes 589832 | tf_op jit(solution)/shard_map/ppermute | solution.py:54
  265.8 18.5 %collective-permute-start.53 = (bf16[96,1024]{1,0:T(8,128)(2,1)S(1)}, bf16[96,1024]{1,0:T(8,128)(2,1)S(1)}, u32[]{:S(2)}, u32[]{:S(2)}) collective-permute-start(bf16[96,1024]{1,0:T(8,128)(2,1)S(1)} %get-tuple-element.326), channel_id=1, source_target_pairs={{0,16},{4,20},{8,24},{12,28},{16,0},{20,4},{24,8},{28,12},{1,17},{... | collective-permute-start | bytes 589832 | tf_op jit(solution)/shard_map/ppermute | solution.py:54
  265.8 18.5 %collective-permute-start.52 = (bf16[96,1024]{1,0:T(8,128)(2,1)S(1)}, bf16[96,1024]{1,0:T(8,128)(2,1)S(1)}, u32[]{:S(2)}, u32[]{:S(2)}) collective-permute-start(bf16[96,1024]{1,0:T(8,128)(2,1)S(1)} %get-tuple-element.325), channel_id=1, source_target_pairs={{0,8},{4,12},{8,0},{12,4},{16,24},{20,28},{24,16},{28,20},{1,9},{5... | collective-permute-start | bytes 589832 | tf_op jit(solution)/shard_map/ppermute | solution.py:54
  294.4 11.2 %collective-permute-start.60 = (bf16[96,768]{1,0:T(8,128)(2,1)S(1)}, bf16[96,768]{1,0:T(8,128)(2,1)S(1)}, u32[]{:S(2)}, u32[]{:S(2)}) collective-permute-start(bf16[96,768]{1,0:T(8,128)(2,1)S(1)} %get-tuple-element.359), channel_id=1, source_target_pairs={{0,24},{4,28},{8,16},{12,20},{16,8},{20,12},{24,0},{28,4},{1,25},{... | collective-permute-start | bytes 442376 | tf_op jit(solution)/shard_map/ppermute | solution.py:54
  297.1 18.4 %collective-permute-start.59 = (bf16[96,768]{1,0:T(8,128)(2,1)S(1)}, bf16[96,768]{1,0:T(8,128)(2,1)S(1)}, u32[]{:S(2)}, u32[]{:S(2)}) collective-permute-start(bf16[96,768]{1,0:T(8,128)(2,1)S(1)} %get-tuple-element.359), channel_id=1, source_target_pairs={{0,16},{4,20},{8,24},{12,28},{16,0},{20,4},{24,8},{28,12},{1,17},{... | collective-permute-start | bytes 442376 | tf_op jit(solution)/shard_map/ppermute | solution.py:54
  297.1 18.4 %collective-permute-start.58 = (bf16[96,768]{1,0:T(8,128)(2,1)S(1)}, bf16[96,768]{1,0:T(8,128)(2,1)S(1)}, u32[]{:S(2)}, u32[]{:S(2)}) collective-permute-start(bf16[96,768]{1,0:T(8,128)(2,1)S(1)} %get-tuple-element.359), channel_id=1, source_target_pairs={{0,8},{4,12},{8,0},{12,4},{16,24},{20,28},{24,16},{28,20},{1,9},{5... | collective-permute-start | bytes 442376 | tf_op jit(solution)/shard_map/ppermute | solution.py:54
  315.6 16.3 %collective-permute-start.65 = (bf16[4,96,768]{2,1,0:T(8,128)(2,1)S(1)}, bf16[4,96,768]{2,1,0:T(8,128)(2,1)S(1)}, u32[]{:S(2)}, u32[]{:S(2)}) collective-permute-start(bf16[4,96,768]{2,1,0:T(8,128)(2,1)S(1)} %pad_maximum_fusion.8.own), channel_id=1, source_target_pairs={{0,4},{4,0},{8,12},{12,8},{16,20},{20,16},{24,28},{28,24},{1,5},{5... | collective-permute-start | bytes 1769480 | tf_op jit(solution)/shard_map/ppermute | solution.py:54
  345.6 19.9 %collective-permute-start.67 = (bf16[6,256,256]{2,1,0:T(8,128)(2,1)}, bf16[6,256,256]{2,1,0:T(8,128)(2,1)}, u32[]{:S(2)}, u32[]{:S(2)}) collective-permute-start(bf16[6,256,256]{2,1,0:T(8,128)(2,1)} %fusion.22), channel_id=1, source_target_pairs={{0,2},{1,3},{2,0},{3,1},{4,6},{5,7},{6,4},{7,5},{8,10},{9,11},{10,... | collective-permute-start | bytes 2359304 | tf_op jit(solution)/shard_map/ppermute | solution.py:54
  (123 other events, 597.8 us)
Sparse Core Ops, SparseCore 0:
  147.7 67.3 all-gather.2
  262.4 50.4 all-gather.4
